TPU v7x, 32 devices: a whole 2x2x4 slice. The times are simulated.
32 devices in a mesh: sp: 4 (over z), fsdp: 2 (over x), rep: 4 (over y, core).
Axes of the slice: x: 2, y: 2, z: 4, core: 2. Of those that a mesh axis runs over, the one named last changes fastest.
Arguments:
- hidden: bfloat16 [16, 256, 4096], P(('fsdp', 'rep'), 'sp'), may hold values from -6 to 6
- query_base: bfloat16 [16, 256, 4096], P(('fsdp', 'rep'), 'sp'), may hold values from -6 to 6
- key_span: bfloat16 [16, 256, 1024], P(('fsdp', 'rep'), 'sp'), may hold values from -6 to 6
- value_base: bfloat16 [16, 256, 1024], P(('fsdp', 'rep'), 'sp'), may hold values from -6 to 6
- past_keys: bfloat16 [16, 16, 1024], P(('fsdp', 'rep'), 'sp'), may hold values from -6 to 6
- past_values: bfloat16 [16, 16, 1024], P(('fsdp', 'rep'), 'sp'), may hold values from -6 to 6
- grad_out: bfloat16 [16, 256, 4096], P(('fsdp', 'rep'), 'sp'), may hold values from -6 to 6
- adapter_down: bfloat16 [4096, 128], P(('sp', 'fsdp')), may hold values from -0.09375 to 0.09375
- adapter_up: bfloat16 [64, 5120], P(None, ('sp', 'fsdp')), may hold values from -0.75 to 0.75
Outputs:
- attended: bfloat16 [16, 256, 4096], P(('fsdp', 'rep'), 'sp')
- grad_query: bfloat16 [16, 256, 4096], P(('fsdp', 'rep'), 'sp')
- grad_value: bfloat16 [16, 256, 1024], P(('fsdp', 'rep'), 'sp')
- grad_hidden: bfloat16 [16, 256, 4096], P(('fsdp', 'rep'), 'sp')
- grad_down: float32 [4096, 128], P(('sp', 'fsdp'))
- grad_up: float32 [64, 5120], P(None, ('sp', 'fsdp'))
All inputs are finite; a program needn't handle non-finite values.
Results may differ from a plain program's by a relative error of at most 0.02.
Values may be sent and summed in bfloat16 or wider, within the bound.
No kernel may reach another device: no remote copies, remote signals or barrier semaphores. Data moves between devices by JAX's collectives and lax.ppermute only.
A program may use at most 128 MiB of HBM per device.

v0:
```python
import math

import jax
import jax.numpy as jnp
from jax import lax
from jax.sharding import PartitionSpec as P

D = 4096
HEADS = 32
KV_HEADS = 8
HEAD_DIM = 128
RANK = 64
KV = 1024


rope_base = 500000.0


def rotary_tables(row_count, offset, head_dim):
    half_dim = head_dim // 2
    position = (jnp.arange(row_count, dtype=jnp.int32) + offset).astype(jnp.float32)
    inverse = jnp.exp(
        jnp.arange(half_dim, dtype=jnp.float32) * (-2.0 * math.log(rope_base) / head_dim)
    )
    angle_table = position[:, None] * inverse[None, :]
    return (jnp.cos(angle_table), jnp.sin(angle_table))


def rotate(source, cosine, sine_table, head_dim, backward):
    full_shape = source.shape
    half_dim = head_dim // 2
    split_pairs = source.reshape(full_shape[:-1] + (full_shape[-1] // head_dim, 2, half_dim))
    first_half = split_pairs[..., 0, :]
    second_half = split_pairs[..., 1, :]
    cos_wide = cosine[:, None, :]
    sin_wide = sine_table[:, None, :]
    if backward:
        new_first = first_half * cos_wide + second_half * sin_wide
        new_second = second_half * cos_wide - first_half * sin_wide
    else:
        new_first = first_half * cos_wide - second_half * sin_wide
        new_second = second_half * cos_wide + first_half * sin_wide
    return jnp.stack([new_first, new_second], axis=-2).reshape(full_shape)


def widen_heads(source, group_size):
    return jnp.repeat(source.reshape(source.shape[:-1] + (KV_HEADS, HEAD_DIM)), group_size, axis=-2)


def attend_one(queries, key_rows, all_values, grad_rows, past_len, span_len, score_scale):
    local_heads = queries.shape[0]
    key_len = past_len + span_len
    block_len = min(256, span_len)
    block_count = span_len // block_len
    key_index = jnp.arange(key_len, dtype=jnp.int32)
    value_acc = jnp.zeros((local_heads, span_len, HEAD_DIM), jnp.float32)
    out_parts = []
    query_grad_parts = []
    for block_index in range(block_count):
        block_start = block_index * block_len
        key_stop = past_len + block_start + block_len
        query_part = queries[:, block_start : block_start + block_len]
        grad_part = grad_rows[:, block_start : block_start + block_len]
        keys_seen = key_rows[:, :key_stop]
        values_seen = all_values[:, :key_stop]
        scores = (
            jnp.einsum("hqd,hkd->hqk", query_part, keys_seen, preferred_element_type=jnp.float32)
            * score_scale
        )
        visible = (
            key_index[None, :key_stop]
            <= past_len + block_start + jnp.arange(block_len, dtype=jnp.int32)[:, None]
        )
        masked = jnp.where(visible[None], scores, -jnp.inf)
        row_max = jnp.max(masked, axis=-1, keepdims=True)
        exp_scores = jnp.exp(masked - row_max)
        probability = exp_scores / jnp.sum(exp_scores, axis=-1, keepdims=True)
        weights = probability.astype(jnp.bfloat16)
        out_block = jnp.einsum(
            "hqk,hkd->hqd", weights, values_seen, preferred_element_type=jnp.float32
        ).astype(jnp.bfloat16)
        prob_grad = jnp.einsum(
            "hqd,hkd->hqk", grad_part, values_seen, preferred_element_type=jnp.float32
        )
        row_delta = jnp.sum(
            grad_part.astype(jnp.float32) * out_block.astype(jnp.float32), axis=-1, keepdims=True
        )
        score_grad = (probability * (prob_grad - row_delta)).astype(jnp.bfloat16)
        query_grad = (
            jnp.einsum("hqk,hkd->hqd", score_grad, keys_seen, preferred_element_type=jnp.float32)
            * score_scale
        ).astype(jnp.bfloat16)
        value_acc = value_acc.at[:, : block_start + block_len].add(
            jnp.einsum(
                "hqk,hqd->hkd",
                weights[:, :, past_len:],
                grad_part,
                preferred_element_type=jnp.float32,
            )
        )
        out_parts.append(out_block)
        query_grad_parts.append(query_grad)
    head_outs = jnp.concatenate(out_parts, axis=1).transpose(1, 0, 2)
    query_grads = jnp.concatenate(query_grad_parts, axis=1).transpose(1, 0, 2)
    value_terms = value_acc.astype(jnp.bfloat16).transpose(1, 0, 2)
    return (head_outs, query_grads, value_terms)


def body(
    hidden,
    query_base,
    key_span,
    value_base,
    past_keys,
    past_values,
    grad_out,
    adapter_down,
    adapter_up,
):
    group_size = HEADS // KV_HEADS
    sp_size = lax.axis_size("sp")
    seq_count = hidden.shape[0]
    tokens = hidden.shape[1]
    span_len = tokens * sp_size
    past_len = past_keys.shape[1] * sp_size
    score_scale = 1.0 / math.sqrt(HEAD_DIM)
    own_rows = hidden.reshape(seq_count * tokens, D)
    own_grads = grad_out.reshape(seq_count, tokens, HEADS, HEAD_DIM)
    past_wide_k = widen_heads(past_keys, group_size)
    past_wide_v = widen_heads(past_values, group_size)
    down_full, up_full = (
        lax.all_gather(adapter_down, ("sp", "fsdp"), axis=0, tiled=True),
        lax.all_gather(adapter_up, ("sp", "fsdp"), axis=1, tiled=True),
    )
    low_rank = jnp.dot(own_rows, down_full, preferred_element_type=jnp.float32).astype(jnp.bfloat16)
    query_delta = jnp.dot(
        low_rank[:, :RANK], up_full[:, :D], preferred_element_type=jnp.float32
    ).reshape(seq_count, tokens, D)
    value_delta = jnp.dot(
        low_rank[:, RANK:], up_full[:, D:], preferred_element_type=jnp.float32
    ).reshape(seq_count, tokens, KV)
    offset = past_len + lax.axis_index("sp") * tokens
    cosine, sine_table = rotary_tables(tokens, offset, HEAD_DIM)
    query_rows = (
        query_base.astype(jnp.float32) + rotate(query_delta, cosine, sine_table, HEAD_DIM, False)
    ).astype(jnp.bfloat16)
    value_rows = (value_base.astype(jnp.float32) + value_delta).astype(jnp.bfloat16)
    query_wide = query_rows.reshape(seq_count, tokens, HEADS, HEAD_DIM)
    key_wide = widen_heads(key_span, group_size)
    value_wide = widen_heads(value_rows, group_size)
    query_heads, key_heads, value_heads, past_k, past_v, grads_heads = (
        lax.all_to_all(query_wide, "sp", split_axis=2, concat_axis=1, tiled=True),
        lax.all_to_all(key_wide, "sp", split_axis=2, concat_axis=1, tiled=True),
        lax.all_to_all(value_wide, "sp", split_axis=2, concat_axis=1, tiled=True),
        lax.all_to_all(past_wide_k, "sp", split_axis=2, concat_axis=1, tiled=True),
        lax.all_to_all(past_wide_v, "sp", split_axis=2, concat_axis=1, tiled=True),
        lax.all_to_all(own_grads, "sp", split_axis=2, concat_axis=1, tiled=True),
    )
    out_list = []
    query_grad_list = []
    value_term_list = []
    for seq_index in range(seq_count):
        queries = query_heads[seq_index].transpose(1, 0, 2)
        key_rows = jnp.concatenate([past_k[seq_index], key_heads[seq_index]], axis=0).transpose(
            1, 0, 2
        )
        all_values = jnp.concatenate([past_v[seq_index], value_heads[seq_index]], axis=0).transpose(
            1, 0, 2
        )
        grad_rows = grads_heads[seq_index].transpose(1, 0, 2)
        head_outs, query_grads, value_terms = attend_one(
            queries, key_rows, all_values, grad_rows, past_len, span_len, score_scale
        )
        out_list.append(head_outs)
        query_grad_list.append(query_grads)
        value_term_list.append(value_terms)
    out_rows = jnp.stack(out_list, axis=0)
    query_grad_rows = jnp.stack(query_grad_list, axis=0)
    value_term_rows = jnp.stack(value_term_list, axis=0)
    attended_tok, query_grad_tok, value_term_tok = (
        lax.all_to_all(out_rows, "sp", split_axis=1, concat_axis=2, tiled=True),
        lax.all_to_all(query_grad_rows, "sp", split_axis=1, concat_axis=2, tiled=True),
        lax.all_to_all(value_term_rows, "sp", split_axis=1, concat_axis=2, tiled=True),
    )
    attended = attended_tok.reshape(seq_count, tokens, D)
    grad_query = query_grad_tok.reshape(seq_count, tokens, D)
    grad_value = (
        value_term_tok.reshape(seq_count, tokens, KV_HEADS, group_size, HEAD_DIM)
        .astype(jnp.float32)
        .sum(axis=3)
        .astype(jnp.bfloat16)
        .reshape(seq_count * tokens, KV)
    )
    query_back = (
        rotate(grad_query.astype(jnp.float32), cosine, sine_table, HEAD_DIM, True)
        .astype(jnp.bfloat16)
        .reshape(seq_count * tokens, D)
    )
    low_grad = jnp.concatenate(
        [
            jnp.dot(query_back, up_full[:, :D].T, preferred_element_type=jnp.float32),
            jnp.dot(grad_value, up_full[:, D:].T, preferred_element_type=jnp.float32),
        ],
        axis=1,
    ).astype(jnp.bfloat16)
    grad_hidden = jnp.dot(low_grad, down_full.T, preferred_element_type=jnp.float32).astype(
        jnp.bfloat16
    )
    column_grads = jnp.concatenate([query_back, grad_value], axis=1)
    hidden_cols, grad_cols = (
        lax.all_to_all(own_rows, ("sp", "fsdp"), split_axis=1, concat_axis=0, tiled=True),
        lax.all_to_all(column_grads, ("sp", "fsdp"), split_axis=1, concat_axis=0, tiled=True),
    )
    all_low, all_low_grad = (
        lax.all_gather(low_rank, ("sp", "fsdp"), axis=0, tiled=True),
        lax.all_gather(low_grad, ("sp", "fsdp"), axis=0, tiled=True),
    )
    down_shard = jnp.dot(hidden_cols.T, all_low_grad, preferred_element_type=jnp.float32)
    col_width = grad_cols.shape[1]
    column = lax.axis_index(("sp", "fsdp")) * col_width + jnp.arange(col_width, dtype=jnp.int32)
    from_query = jnp.dot(all_low[:, :RANK].T, grad_cols, preferred_element_type=jnp.float32)
    from_value = jnp.dot(all_low[:, RANK:].T, grad_cols, preferred_element_type=jnp.float32)
    up_shard = jnp.where(column[None, :] < D, from_query, from_value)
    grad_down, grad_up = lax.psum((down_shard, up_shard), "rep")
    return (
        attended,
        grad_query,
        grad_value.reshape(seq_count, tokens, KV),
        grad_hidden.reshape(seq_count, tokens, D),
        grad_down,
        grad_up,
    )


def solution(mesh):
    in_specs = (
        P(("fsdp", "rep"), "sp", None),
        P(("fsdp", "rep"), "sp", None),
        P(("fsdp", "rep"), "sp", None),
        P(("fsdp", "rep"), "sp", None),
        P(("fsdp", "rep"), "sp", None),
        P(("fsdp", "rep"), "sp", None),
        P(("fsdp", "rep"), "sp", None),
        P(("sp", "fsdp"), None),
        P(None, ("sp", "fsdp")),
    )
    out_specs = (
        P(("fsdp", "rep"), "sp", None),
        P(("fsdp", "rep"), "sp", None),
        P(("fsdp", "rep"), "sp", None),
        P(("fsdp", "rep"), "sp", None),
        P(("sp", "fsdp"), None),
        P(None, ("sp", "fsdp")),
    )
    return jax.shard_map(body, mesh=mesh, in_specs=in_specs, out_specs=out_specs, check_vma=False)
```

profile of v0, /device:TPU:0, one launch (start us, length us, event | category | flops | bytes accessed | tf_op | source)
XLA Modules:
  0.0 451.2 jit_solution(1741259922386973237)
XLA Ops:
  9.3 6.3 %all-to-all-start.1 = ((bf16[2,4,32,128]{3,1,0,2:T(4,128)(2,1)}), bf16[2,4,32,128]{3,1,0,2:T(4,128)(2,1)S(1)}, u32[]{:S(2)}, u32[]{:S(2)}) async-start(bf16[2,4,32,128]{3,1,0,2:T(4,128)(2,1)} %bitcast.5), calls=%async_computation.1 | async-start | bytes 131072 | tf_op jit(solution)/shard_map/all_to_all | solution.py:155
  16.3 5.0 %all-to-all-done.1 = bf16[2,4,32,128]{3,1,0,2:T(4,128)(2,1)S(1)} async-done(((bf16[2,4,32,128]{3,1,0,2:T(4,128)(2,1)}), bf16[2,4,32,128]{3,1,0,2:T(4,128)(2,1)S(1)}, u32[]{:S(2)}, u32[]{:S(2)}) %all-to-all-start.1) | async-done | bytes 65568 | tf_op jit(solution)/shard_map/all_to_all | solution.py:155
  22.0 3.3 all-to-all-start.3
  25.3 1.3 copy_bitcast_fusion
  26.6 4.5 all-to-all-done.3
  31.1 4.2 all-to-all-start.6
  35.7 55.0 %all_gather.13 = bf16[64,5120]{1,0:T(8,128)(2,1)S(1)} all-gather(bf16[64,640]{1,0:T(8,128)(2,1)S(1)} %copy-done.31), channel_id=1, replica_groups=mesh['sp'=4,'fsdp'=2,'rep'=4] {'sp','fsdp'}, dimensions={1}, use_global_device_ids=true | all-gather | bytes 737280 | tf_op jit(solution)/shard_map/all_gather | solution.py:133
  90.6 2.0 convolution_convert_fusion.5
  93.1 4.4 reshape_reshape.6
  97.5 1.2 broadcast_in_dim.55
  98.7 4.4 all-to-all-start.2
  103.1 7.2 %multiply_subtract_fusion = (f32[2,64,32,1,64]{4,3,2,1,0:T(1,128)S(1)}, f32[2,64,32,1,64]{4,3,2,1,0:T(1,128)S(1)}) fusion(f32[2,64,32,2,64]{4,3,2,1,0:T(2,128)} %reshape_reshape.6, f32[64,64]{1,0:T(8,128)S(1)} %get-tuple-element.101, f32[64,64]{1,0:T(8,128)S(1)} %get-tuple-element.100), kind=kLoop, calls=%fused_computation.17 | loop fusion | flops 1572864 | bytes 4227072 | tf_op jit(solution)/shard_map/sub | solution.py:41
  110.3 6.8 %pad_maximum_fusion = f32[2,64,32,2,64]{4,3,2,1,0:T(2,128)} fusion(f32[2,64,32,1,64]{4,3,2,1,0:T(1,128)S(1)} %get-tuple-element.87, f32[2,64,32,1,64]{4,3,2,1,0:T(1,128)S(1)} %get-tuple-element.86), kind=kLoop, calls=%fused_computation.3 | loop fusion | flops 524288 | bytes 4194304 | tf_op jit(solution)/shard_map/stack | solution.py:43
  117.2 5.4 %reshape.272 = f32[2,64,4096]{2,1,0:T(8,128)S(1)} reshape(f32[2,64,32,2,64]{4,3,2,1,0:T(2,128)} %pad_maximum_fusion) | data formatting | bytes 4194304 | tf_op jit(solution)/shard_map/reshape | solution.py:43
  122.6 2.5 copy_bitcast_fusion.1
  125.1 5.2 %all-to-all-start = ((bf16[2,64,32,128]{3,1,0,2:T(8,128)(2,1)}), bf16[2,64,32,128]{3,1,0,2:T(8,128)(2,1)S(1)}, u32[]{:S(2)}, u32[]{:S(2)}) async-start(bf16[2,64,32,128]{3,1,0,2:T(8,128)(2,1)} %copy_bitcast_fusion.1), calls=%async_computation | async-start | bytes 2097152 | tf_op jit(solution)/shard_map/all_to_all | solution.py:152
  130.6 16.8 %all-to-all-done = bf16[2,64,32,128]{3,1,0,2:T(8,128)(2,1)S(1)} async-done(((bf16[2,64,32,128]{3,1,0,2:T(8,128)(2,1)}), bf16[2,64,32,128]{3,1,0,2:T(8,128)(2,1)S(1)}, u32[]{:S(2)}, u32[]{:S(2)}) %all-to-all-start) | async-done | bytes 1048608 | tf_op jit(solution)/shard_map/all_to_all | solution.py:152
  147.4 1.2 broadcast_in_dim.58
  148.6 3.7 all-to-all-start.4
  155.0 1.9 copy.224
  159.0 1.9 copy.226
  164.1 2.1 copy.147
  167.2 1.1 copy.185
  170.1 2.7 all-to-all-done.4
  177.5 1.2 fusion.28
  180.3 1.2 fusion.27
  182.2 1.3 multiply_reduce_fusion
  183.5 3.6 fusion.14
  187.2 2.9 multiply_reduce_fusion.1
  190.1 2.8 fusion.15
  192.9 1.3 pad_maximum_fusion.4
  194.2 1.6 copy.170
  195.8 4.1 all-to-all-start.7
  199.9 1.5 fusion.13
  202.0 1.6 copy.174
  203.7 18.3 %all-to-all-done.7 = bf16[2,256,8,128]{3,2,0,1:T(8,128)(2,1)S(1)} async-done(((bf16[2,256,8,128]{3,2,0,1:T(8,128)(2,1)}), bf16[2,256,8,128]{3,2,0,1:T(8,128)(2,1)S(1)}, u32[]{:S(2)}, u32[]{:S(2)}) %all-to-all-start.7) | async-done | bytes 1048608 | tf_op jit(solution)/shard_map/all_to_all | solution.py:182
  221.9 3.5 all-to-all-start.8
  225.9 1.3 copy.181
  227.2 22.3 %all-to-all-done.8 = bf16[2,256,8,128]{3,2,0,1:T(8,128)(2,1)S(1)} async-done(((bf16[2,256,8,128]{3,2,0,1:T(8,128)(2,1)}), bf16[2,256,8,128]{3,2,0,1:T(8,128)(2,1)S(1)}, u32[]{:S(2)}, u32[]{:S(2)}) %all-to-all-start.8) | async-done | bytes 1048608 | tf_op jit(solution)/shard_map/all_to_all | solution.py:183
  249.4 8.1 %all-to-all-start.9 = ((bf16[128,8,512]{2,0,1:T(8,128)(2,1)}), bf16[128,8,512]{2,0,1:T(8,128)(2,1)}, u32[]{:S(2)}, u32[]{:S(2)}) async-start(bf16[128,8,512]{2,0,1:T(8,128)(2,1)} %copy.181), calls=%async_computation.9 | async-start | bytes 2097152 | tf_op jit(solution)/shard_map/all_to_all | solution.py:211
  257.5 1.3 pad_maximum_fusion.3
  258.8 1.8 copy.159
  262.0 3.7 reshape.289
  265.8 16.1 %all-to-all-done.9 = bf16[128,8,512]{2,0,1:T(8,128)(2,1)} async-done(((bf16[128,8,512]{2,0,1:T(8,128)(2,1)}), bf16[128,8,512]{2,0,1:T(8,128)(2,1)}, u32[]{:S(2)}, u32[]{:S(2)}) %all-to-all-start.9) | async-done | bytes 1048608 | tf_op jit(solution)/shard_map/all_to_all | solution.py:211
  281.9 3.5 all-to-all-start.5
  285.4 7.4 %add_convert_fusion = (bf16[2,64,32,1,64]{4,3,2,1,0:T(2,128)(2,1)S(1)}, bf16[2,64,32,1,64]{4,3,2,1,0:T(2,128)(2,1)S(1)}) fusion(f32[2,64,32,2,64]{4,3,2,1,0:T(2,128)} %reshape.289, f32[64,64]{1,0:T(8,128)S(1)} %get-tuple-element.101, f32[64,64]{1,0:T(8,128)S(1)} %get-tuple-element.100), kind=kLoop, calls=%fused_computation.14 | loop fusion | flops 2097152 | bytes 3178496 | tf_op jit(solution)/shard_map/convert.4
  292.8 6.4 %pad_maximum_fusion.1 = bf16[2,64,32,2,64]{4,3,2,1,0:T(2,128)(2,1)} fusion(bf16[2,64,32,1,64]{4,3,2,1,0:T(2,128)(2,1)S(1)} %get-tuple-element.85, bf16[2,64,32,1,64]{4,3,2,1,0:T(2,128)(2,1)S(1)} %get-tuple-element.84), kind=kLoop, calls=%fused_computation.12 | loop fusion | flops 2097152 | bytes 2097152 | tf_op jit(solution)/shard_map/stack | solution.py:43
  299.2 5.3 %reshape.290 = bf16[128,4096]{1,0:T(8,128)(2,1)S(1)} reshape(bf16[2,64,32,2,64]{4,3,2,1,0:T(2,128)(2,1)} %pad_maximum_fusion.1) | data formatting | bytes 2097152 | tf_op jit(solution)/shard_map/convert_element_type | solution.py:196
  306.4 1.3 copy.199
  307.7 2.4 pad_maximum_fusion.2
  311.1 5.7 %all-to-all-start.10 = ((bf16[128,8,640]{0,2,1:T(8,128)(2,1)}), bf16[128,8,640]{0,2,1:T(8,128)(2,1)S(1)}, u32[]{:S(2)}, u32[]{:S(2)}) async-start(bf16[128,8,640]{0,2,1:T(8,128)(2,1)} %bitcast.76), calls=%async_computation.10 | async-start | bytes 2621440 | tf_op jit(solution)/shard_map/all_to_all | solution.py:212
  316.8 50.8 %all_gather.15 = bf16[1024,128]{0,1:T(8,128)(2,1)} all-gather(bf16[128,128]{0,1:T(8,128)(2,1)S(1)} %convolution_convert_fusion.5), channel_id=1, replica_groups=mesh['sp'=4,'fsdp'=2,'rep'=4] {'sp','fsdp'}, dimensions={0}, use_global_device_ids=true | all-gather | bytes 294912 | tf_op jit(solution)/shard_map/all_gather | solution.py:215
  367.6 1.2 copy.171
  368.8 1.1 copy.161
  370.0 2.4 reshape.283
  372.3 2.3 reshape.285
  375.4 26.8 %all_gather.14 = bf16[1024,128]{0,1:T(8,128)(2,1)S(1)} all-gather(bf16[128,128]{0,1:T(8,128)(2,1)S(1)} %pad_maximum_fusion.6), channel_id=1, replica_groups=mesh['sp'=4,'fsdp'=2,'rep'=4] {'sp','fsdp'}, dimensions={0}, use_global_device_ids=true | all-gather | bytes 294912 | tf_op jit(solution)/shard_map/all_gather | solution.py:216
  402.1 2.2 convolution_bitcast_fusion
  404.4 1.4 convolution_convert_fusion
  406.9 1.7 copy.183
  408.7 1.4 fusion.36
  411.9 29.0 %all-reduce.3.cloned.1.call-done = (f32[512,128]{0,1:T(8,128)}, f32[64,640]{1,0:T(8,128)}) async-done(((f32[512,128]{0,1:T(8,128)}, f32[64,640]{1,0:T(8,128)}), (f32[512,128]{0,1:T(8,128)}, f32[64,640]{1,0:T(8,128)})) %all-reduce.3.cloned.1.call-update) | async-done | bytes 426000 | tf_op jit(solution)/shard_map/psum | solution.py:224
  440.8 1.8 copy.184
  442.6 1.6 copy.233
  (135 shorter events, 31.1 us)
Async XLA Ops:
  7.2 18.1 %copy-start = (bf16[2,64,4096]{2,1,0:T(8,128)(2,1)S(1)}, bf16[2,64,4096]{2,1,0:T(8,128)(2,1)}, u32[]{:S(2)}) copy-start(bf16[2,64,4096]{2,1,0:T(8,128)(2,1)} %param.23) | copy-start | bytes 3145732
  7.2 83.4 %all-gather.2.cloned.1.call-start = ((), (), s32[]{:S(2)}) async-start(), calls=%async_computation.11 | async-start | bytes 1179648 | tf_op jit(solution)/shard_map/all_gather | solution.py:132
  9.3 12.1 %all-to-all-start.1 = ((bf16[2,4,32,128]{3,1,0,2:T(4,128)(2,1)}), bf16[2,4,32,128]{3,1,0,2:T(4,128)(2,1)S(1)}, u32[]{:S(2)}, u32[]{:S(2)}) async-start(bf16[2,4,32,128]{3,1,0,2:T(4,128)(2,1)} %bitcast.5), calls=%async_computation.1 | async-start | bytes 131072 | tf_op jit(solution)/shard_map/all_to_all | solution.py:155
  22.0 9.1 %all-to-all-start.3 = ((bf16[2,4,32,128]{3,1,0,2:T(4,128)(2,1)}), bf16[2,4,32,128]{3,1,0,2:T(4,128)(2,1)S(1)}, u32[]{:S(2)}, u32[]{:S(2)}) async-start(bf16[2,4,32,128]{3,1,0,2:T(4,128)(2,1)} %bitcast.14), calls=%async_computation.3 | async-start | bytes 131072 | tf_op jit(solution)/shard_map/all_to_all | solution.py:156
  25.3 10.3 %copy-start.29 = (bf16[2,64,1024]{2,1,0:T(8,128)(2,1)S(1)}, bf16[2,64,1024]{2,1,0:T(8,128)(2,1)}, u32[]{:S(2)}) copy-start(bf16[2,64,1024]{2,1,0:T(8,128)(2,1)} %param.19) | copy-start | bytes 786436
  25.3 10.3 %copy-start.31 = (bf16[64,640]{1,0:T(8,128)(2,1)S(1)}, bf16[64,640]{1,0:T(8,128)(2,1)}, u32[]{:S(2)}) copy-start(bf16[64,640]{1,0:T(8,128)(2,1)} %param.25) | copy-start | bytes 245764
  26.6 64.0 %copy-start.5 = (bf16[2,64,4096]{2,1,0:T(8,128)(2,1)S(1)}, bf16[2,64,4096]{2,1,0:T(8,128)(2,1)}, u32[]{:S(2)}) copy-start(bf16[2,64,4096]{2,1,0:T(8,128)(2,1)} %param.17) | copy-start | bytes 3145732
  31.1 66.4 %all-to-all-start.6 = ((bf16[2,64,32,128]{3,1,0,2:T(8,128)(2,1)}), bf16[2,64,32,128]{3,1,0,2:T(8,128)(2,1)}, u32[]{:S(2)}, u32[]{:S(2)}) async-start(bf16[2,64,32,128]{3,1,0,2:T(8,128)(2,1)} %copy_bitcast_fusion), calls=%async_computation.6 | async-start | bytes 2097152 | tf_op jit(solution)/shard_map/all_to_all | solution.py:157
  90.6 39.7 %copy-start.3 = (bf16[64,5120]{1,0:T(8,128)(2,1)}, bf16[64,5120]{1,0:T(8,128)(2,1)S(1)}, u32[]{:S(2)}) copy-start(bf16[64,5120]{1,0:T(8,128)(2,1)S(1)} %all_gather.13) | copy-start | bytes 1966084
  98.7 26.3 %all-to-all-start.2 = ((bf16[2,64,32,128]{3,1,0,2:T(8,128)(2,1)}), bf16[2,64,32,128]{3,1,0,2:T(8,128)(2,1)}, u32[]{:S(2)}, u32[]{:S(2)}) async-start(bf16[2,64,32,128]{3,1,0,2:T(8,128)(2,1)} %bitcast.9), calls=%async_computation.2 | async-start | bytes 2097152 | tf_op jit(solution)/shard_map/all_to_all | solution.py:153
  125.1 5.5 %copy-start.30 = (bf16[2,64,1024]{2,1,0:T(8,128)(2,1)S(1)}, bf16[2,64,1024]{2,1,0:T(8,128)(2,1)}, u32[]{:S(2)}) copy-start(bf16[2,64,1024]{2,1,0:T(8,128)(2,1)} %param.20) | copy-start | bytes 786436
  125.1 22.3 %all-to-all-start = ((bf16[2,64,32,128]{3,1,0,2:T(8,128)(2,1)}), bf16[2,64,32,128]{3,1,0,2:T(8,128)(2,1)S(1)}, u32[]{:S(2)}, u32[]{:S(2)}) async-start(bf16[2,64,32,128]{3,1,0,2:T(8,128)(2,1)} %copy_bitcast_fusion.1), calls=%async_computation | async-start | bytes 2097152 | tf_op jit(solution)/shard_map/all_to_all | solution.py:152
  148.6 24.2 %all-to-all-start.4 = ((bf16[2,64,32,128]{3,1,0,2:T(8,128)(2,1)}), bf16[2,64,32,128]{3,1,0,2:T(8,128)(2,1)S(1)}, u32[]{:S(2)}, u32[]{:S(2)}) async-start(bf16[2,64,32,128]{3,1,0,2:T(8,128)(2,1)} %bitcast.19), calls=%async_computation.4 | async-start | bytes 2097152 | tf_op jit(solution)/shard_map/all_to_all | solution.py:154
  160.9 1.9 copy-start.13
  173.6 3.1 copy-start.25
  173.6 3.1 copy-start.27
  173.6 3.0 copy-start.32
  173.6 3.0 copy-start.33
  177.5 1.8 copy-start.12
  177.5 1.8 copy-start.23
  177.5 1.9 copy-start.28
  180.3 1.5 copy-start.14
  180.3 1.8 copy-start.24
  180.3 1.9 copy-start.26
  180.3 1.9 copy-start.35
  181.5 2.0 copy-start.22
  183.5 3.6 copy-start.34
  187.2 2.9 copy-start.20
  194.2 5.7 %copy-start.15 = (bf16[8,256,272]{1,2,0:T(8,128)(2,1)S(1)}, bf16[8,256,272]{1,2,0:T(8,128)(2,1)}, u32[]{:S(2)}) copy-start(bf16[8,256,272]{1,2,0:T(8,128)(2,1)} %fusion.28) | copy-start | bytes 3342340
  195.8 5.6 %copy-start.16 = (bf16[8,256,272]{1,2,0:T(8,128)(2,1)S(1)}, bf16[8,256,272]{1,2,0:T(8,128)(2,1)}, u32[]{:S(2)}) copy-start(bf16[8,256,272]{1,2,0:T(8,128)(2,1)} %fusion.27) | copy-start | bytes 3342340
  195.8 26.1 %all-to-all-start.7 = ((bf16[2,256,8,128]{3,2,0,1:T(8,128)(2,1)}), bf16[2,256,8,128]{3,2,0,1:T(8,128)(2,1)S(1)}, u32[]{:S(2)}, u32[]{:S(2)}) async-start(bf16[2,256,8,128]{3,2,0,1:T(8,128)(2,1)} %copy.170), calls=%async_computation.7 | async-start | bytes 2097152 | tf_op jit(solution)/shard_map/all_to_all | solution.py:182
  199.9 1.6 copy-start.21
  202.0 23.5 %copy-start.6 = (bf16[2,64,4096]{2,1,0:T(8,128)(2,1)S(1)}, bf16[2,64,4096]{2,1,0:T(8,128)(2,1)}, u32[]{:S(2)}) copy-start(bf16[2,64,4096]{2,1,0:T(8,128)(2,1)} %param.17) | copy-start | bytes 3145732
  221.9 27.5 %all-to-all-start.8 = ((bf16[2,256,8,128]{3,2,0,1:T(8,128)(2,1)}), bf16[2,256,8,128]{3,2,0,1:T(8,128)(2,1)S(1)}, u32[]{:S(2)}, u32[]{:S(2)}) async-start(bf16[2,256,8,128]{3,2,0,1:T(8,128)(2,1)} %copy.174), calls=%async_computation.8 | async-start | bytes 2097152 | tf_op jit(solution)/shard_map/all_to_all | solution.py:183
  249.4 32.5 %all-to-all-start.9 = ((bf16[128,8,512]{2,0,1:T(8,128)(2,1)}), bf16[128,8,512]{2,0,1:T(8,128)(2,1)}, u32[]{:S(2)}, u32[]{:S(2)}) async-start(bf16[128,8,512]{2,0,1:T(8,128)(2,1)} %copy.181), calls=%async_computation.9 | async-start | bytes 2097152 | tf_op jit(solution)/shard_map/all_to_all | solution.py:211
  261.1 0.7 copy-start.10
  261.8 42.7 %copy-start.18 = (bf16[2,64,8,128]{3,2,1,0:T(8,128)(2,1)}, bf16[2,64,8,128]{3,2,1,0:T(8,128)(2,1)S(1)}, u32[]{:S(2)}) copy-start(bf16[2,64,8,128]{3,2,1,0:T(8,128)(2,1)S(1)} %copy.177) | copy-start | bytes 786436
  281.9 28.2 %all-to-all-start.5 = ((bf16[2,256,8,128]{3,2,0,1:T(8,128)(2,1)}), bf16[2,256,8,128]{3,2,0,1:T(8,128)(2,1)S(1)}, u32[]{:S(2)}, u32[]{:S(2)}) async-start(bf16[2,256,8,128]{3,2,0,1:T(8,128)(2,1)} %copy.159), calls=%async_computation.5 | async-start | bytes 2097152 | tf_op jit(solution)/shard_map/all_to_all | solution.py:181
  310.1 1.0 copy-start.8
  311.1 94.7 %all-to-all-start.10 = ((bf16[128,8,640]{0,2,1:T(8,128)(2,1)}), bf16[128,8,640]{0,2,1:T(8,128)(2,1)S(1)}, u32[]{:S(2)}, u32[]{:S(2)}) async-start(bf16[128,8,640]{0,2,1:T(8,128)(2,1)} %bitcast.76), calls=%async_computation.10 | async-start | bytes 2621440 | tf_op jit(solution)/shard_map/all_to_all | solution.py:212
  316.8 124.1 %all-reduce.3.cloned.1.call-start = ((), (), s32[]{:S(2)}) async-start(), calls=%async_computation.12 | async-start | bytes 851968 | tf_op jit(solution)/shard_map/psum | solution.py:224
  316.8 52.0 %copy-start.9 = (bf16[2,256,8,128]{3,2,0,1:T(8,128)(2,1)S(1)}, bf16[2,256,8,128]{3,2,0,1:T(8,128)(2,1)}, u32[]{:S(2)}) copy-start(bf16[2,256,8,128]{3,2,0,1:T(8,128)(2,1)} %copy-done.8) | copy-start | bytes 3145732
  370.0 4.7 %copy-start.4 = (bf16[64,5120]{1,0:T(8,128)(2,1)S(1)}, bf16[64,5120]{1,0:T(8,128)(2,1)}, u32[]{:S(2)}) copy-start(bf16[64,5120]{1,0:T(8,128)(2,1)} %copy-done.3) | copy-start | bytes 1966084
  370.0 4.7 %copy-start.19 = (bf16[2,64,8,128]{3,2,1,0:T(8,128)(2,1)S(1)}, bf16[2,64,8,128]{3,2,1,0:T(8,128)(2,1)}, u32[]{:S(2)}) copy-start(bf16[2,64,8,128]{3,2,1,0:T(8,128)(2,1)} %copy-done.18) | copy-start | bytes 786436
  374.6 29.7 %copy-start.7 = (bf16[4096,128]{1,0:T(8,128)(2,1)S(1)}, bf16[4096,128]{1,0:T(8,128)(2,1)}, u32[]{:S(2)}) copy-start(bf16[4096,128]{1,0:T(8,128)(2,1)} %all-gather.2.cloned.1.call-done) | copy-start | bytes 3145732
  405.8 1.1 copy-start.2
  406.9 3.1 copy-start.17
  408.7 2.4 copy-start.11
  408.7 35.5 %copy-start.1 = (bf16[2,64,4096]{2,1,0:T(8,128)(2,1)S(1)}, bf16[2,64,4096]{2,1,0:T(8,128)(2,1)}, u32[]{:S(2)}) copy-start(bf16[2,64,4096]{2,1,0:T(8,128)(2,1)} %param.23) | copy-start | bytes 3145732
Sparse Core Ops, SparseCore 0:
  10.1 49.5 all-gather.1
  411.2 29.5 all-reduce.2
where the time goes:
time: 457 us; the launch traced here: 451 us
  blocking collectives  133 us (29%)
  waiting for transfers between devices  115 us (25%)
  local copies, waits for them, and re-layouts  73.9 us (16%)
  starting transfers between devices  52.1 us (11%)
  other arithmetic  38.9 us (9%)
  matrix products  23.6 us (5%)
  between operations  14.8 us (3%)
    all_gather x1, blocking collectives, body(): lax.all_gather(adapter_up, ('sp', 'fsdp'), axis=1, tiled=True)  55 us
    all_gather x1, blocking collectives, body(): lax.all_gather(low_rank, ('sp', 'fsdp'), axis=0, tiled=True)  50.8 us
    psum x1, waiting for transfers between devices, body(): grad_down, grad_up = lax.psum((down_shard, up_shard), 'rep')  29 us
    all_gather x1, blocking collectives, body(): lax.all_gather(low_grad, ('sp', 'fsdp'), axis=0, tiled=True)  26.8 us
    all_to_all x1, waiting for transfers between devices, body(): lax.all_to_all(value_term_rows, 'sp', split_axis=1, concat_axis=2, tiled=...  22.3 us
    all_to_all x1, waiting for transfers between devices, body(): lax.all_to_all(query_grad_rows, 'sp', split_axis=1, concat_axis=2, tiled=...  18.3 us
    all_to_all x1, waiting for transfers between devices, body(): lax.all_to_all(query_wide, 'sp', split_axis=2, concat_axis=1, tiled=True)  16.8 us
    all_to_all x1, waiting for transfers between devices, body(): lax.all_to_all(own_rows, ('sp', 'fsdp'), split_axis=1, concat_axis=0, til...  16.1 us
  transfers between devices with their start and end apart: 13, of which 8 were waited for; matrix products, arithmetic and copies ran while one was open for 22% of the time, Pallas kernels for 0%

commit v1 on v0

v1 whole, which is shorter than its diff:
```python
import functools
import math

import jax
import jax.numpy as jnp
from jax import lax
from jax.experimental import pallas as pl
from jax.experimental.pallas import tpu as pltpu
from jax.sharding import PartitionSpec as P

D = 4096
HEADS = 32
KV_HEADS = 8
HEAD_DIM = 128
RANK = 64
KV = 1024
GROUP = HEADS // KV_HEADS
WIDE = GROUP * HEAD_DIM
ROPE_BASE = 500000.0
HIDDEN_MASK = -1e30
CHUNKS = 2

f32 = jnp.float32
bf16 = jnp.bfloat16


def rotary_tables(row_count, offset):
    half = HEAD_DIM // 2
    position = (jnp.arange(row_count, dtype=jnp.int32) + offset).astype(f32)
    inverse = jnp.exp(jnp.arange(half, dtype=f32) * (-2.0 * math.log(ROPE_BASE) / HEAD_DIM))
    angle = position[:, None] * inverse[None, :]
    cosine, sine = jnp.cos(angle), jnp.sin(angle)
    return (
        jnp.concatenate([cosine, cosine], axis=1),
        jnp.concatenate([-sine, sine], axis=1),
    )


def cyclic(x, axis, shift):
    n = lax.axis_size(axis)
    return lax.ppermute(x, axis, [(i, (i + shift) % n) for i in range(n)])


def along(x, axis, shift):
    n = lax.axis_size(axis)
    return lax.ppermute(x, axis, [(i, i + shift) for i in range(n) if 0 <= i + shift < n])


def partner(x, axis, mask):
    n = lax.axis_size(axis)
    return lax.ppermute(x, axis, [(i, i ^ mask) for i in range(n)])


def mm(a, b, ca, cb):
    return lax.dot_general(a, b, (((ca,), (cb,)), ((), ())), preferred_element_type=f32)


def attention_kernel(shards, place_ref, *refs, aliased):
    it = iter(refs)
    q_ref, g_ref, upq_ref, upv_ref, pk_ref, pv_ref, cos_ref, sin_ref = (next(it) for _ in range(8))
    low_refs = [next(it) for _ in range(shards)]
    k_refs = [next(it) for _ in range(shards)]
    v_refs = [next(it) for _ in range(shards)]
    if aliased:
        next(it), next(it)
    att_ref, gq_ref, gup_ref, lgq_ref, lgv_ref = (next(it) for _ in range(5))
    gv_refs = [next(it) for _ in range(shards)]

    seqs, tokens = q_ref.shape[0], q_ref.shape[1]
    span = shards * tokens
    past = pk_ref.shape[1]
    scale = 1.0 / math.sqrt(HEAD_DIM)
    place = place_ref[0]
    cos, sin = cos_ref[...], sin_ref[...]
    upq, upv = upq_ref[...], upv_ref[...]

    @pl.when(pl.program_id(0) == 0)
    def _():
        lgq_ref[...] = jnp.zeros_like(lgq_ref)
        lgv_ref[...] = jnp.zeros_like(lgv_ref)

    col = lax.broadcasted_iota(jnp.int32, (tokens, span + past), 1)
    row = lax.broadcasted_iota(jnp.int32, (tokens, span + past), 0)
    seen = (
        (col <= row)
        | ((col >= tokens) & (col < (place + 1) * tokens))
        | (col >= span)
    )
    bias = jnp.where(seen, 0.0, HIDDEN_MASK)
    bias = jnp.concatenate([bias] * GROUP, axis=0)

    def heads(x):
        return jnp.concatenate(
            [x[:, h * HEAD_DIM : (h + 1) * HEAD_DIM] for h in range(GROUP)], axis=0
        )

    def lanes(x):
        return jnp.concatenate([x[h * tokens : (h + 1) * tokens] for h in range(GROUP)], axis=1)

    cos4 = jnp.concatenate([cos] * GROUP, axis=0)
    sin4 = jnp.concatenate([sin] * GROUP, axis=0)
    grad_up_q = None
    for s in range(seqs):
        low = low_refs[0][s]
        low_q = low[:, :RANK]
        delta = heads(mm(low_q, upq, 1, 0))
        delta = delta * cos4 + pltpu.roll(delta, HEAD_DIM // 2, 1) * sin4
        q = (heads(q_ref[s]).astype(f32) + delta).astype(bf16)
        g = heads(g_ref[s])
        low_v = jnp.concatenate([r[s][:, RANK:] for r in low_refs], axis=0)
        keys = jnp.concatenate([r[s] for r in k_refs] + [pk_ref[s]], axis=0)
        base = jnp.concatenate([r[s] for r in v_refs], axis=0).astype(f32)
        vals = jnp.concatenate([(base + mm(low_v, upv, 1, 0)).astype(bf16), pv_ref[s]], axis=0)

        scores = mm(q, keys, 1, 1) * scale + bias
        top = jnp.max(scores, axis=-1, keepdims=True)
        e = jnp.exp(scores - top)
        probs = e / jnp.sum(e, axis=-1, keepdims=True)
        weights = probs.astype(bf16)
        out = mm(weights, vals, 1, 0).astype(bf16)
        att_ref[s] = lanes(out)
        prob_grad = mm(g, vals, 1, 1)
        row_delta = jnp.sum(g.astype(f32) * out.astype(f32), axis=-1, keepdims=True)
        score_grad = (probs * (prob_grad - row_delta)).astype(bf16)
        gq = (mm(score_grad, keys, 1, 0) * scale).astype(bf16)
        gq_ref[s] = lanes(gq)
        gq32 = gq.astype(f32)
        back = (gq32 * cos4 - pltpu.roll(gq32, HEAD_DIM // 2, 1) * sin4).astype(bf16)
        back = lanes(back)
        lgq_ref[s] += mm(back, upq, 1, 1)
        gv = mm(weights[:, :span], g, 0, 0).astype(bf16)
        for k in range(shards):
            gv_refs[k][s] = gv[k * tokens : (k + 1) * tokens]
        lgv_ref[s] += mm(gv, upv, 1, 1)
        up_q = mm(low_q, back, 0, 0)
        up_v = mm(low_v, gv, 0, 0)
        grad_up_q = up_q if s == 0 else grad_up_q + up_q
        grad_up_v = up_v if s == 0 else grad_up_v + up_v
    gup_ref[:, :WIDE] = grad_up_q.astype(bf16)
    gup_ref[:, WIDE:] = grad_up_v.astype(bf16)


def attention_chunk(
    chunk, groups, place, query_base, grad_out, up_full, past, cos, sin, lows, kvs, earlier
):
    shards = len(kvs)
    seqs, tokens = query_base.shape[:2]
    past_len = past.shape[1]
    first = chunk * groups
    q_heads = D // HEAD_DIM
    aliased = earlier is not None

    def at(block, fn):
        return pl.BlockSpec(block, fn)

    def whole(x):
        return pl.BlockSpec(x.shape, lambda g: (0,) * x.ndim)

    token_block = (seqs, tokens, WIDE)
    in_specs = [pl.BlockSpec(memory_space=pltpu.SMEM)]
    in_specs += [at(token_block, lambda g: (0, 0, first + g))] * 2
    in_specs += [at((RANK, WIDE), lambda g: (0, first + g))]
    in_specs += [at((RANK, HEAD_DIM), lambda g: (0, q_heads + first + g))]
    in_specs += [at((seqs, past_len, HEAD_DIM), lambda g: (0, 0, first + g))]
    in_specs += [at((seqs, past_len, HEAD_DIM), lambda g: (0, 0, KV_HEADS + first + g))]
    in_specs += [whole(cos), whole(sin)]
    in_specs += [whole(x) for x in lows]
    in_specs += [at((seqs, tokens, HEAD_DIM), lambda g: (0, 0, g))] * shards
    in_specs += [at((seqs, tokens, HEAD_DIM), lambda g: (0, 0, groups + g))] * shards
    operands = [place, query_base, grad_out, up_full, up_full, past, past, cos, sin]
    operands += list(lows) + list(kvs) + list(kvs)
    aliases = {}
    if aliased:
        aliases = {len(operands): 0, len(operands) + 1: 1}
        in_specs += [pl.BlockSpec(memory_space=pl.ANY)] * 2
        operands += list(earlier)
    shape = jax.ShapeDtypeStruct
    out_shape = [
        shape(query_base.shape, bf16),
        shape(query_base.shape, bf16),
        shape((RANK, groups * (WIDE + HEAD_DIM)), bf16),
        shape((seqs, tokens, RANK), f32),
        shape((seqs, shards * tokens, RANK), f32),
    ] + [shape((seqs, tokens, groups * HEAD_DIM), bf16)] * shards
    out_specs = [
        at(token_block, lambda g: (0, 0, first + g)),
        at(token_block, lambda g: (0, 0, first + g)),
        at((RANK, WIDE + HEAD_DIM), lambda g: (0, g)),
        at((seqs, tokens, RANK), lambda g: (0, 0, 0)),
        at((seqs, shards * tokens, RANK), lambda g: (0, 0, 0)),
    ] + [at((seqs, tokens, HEAD_DIM), lambda g: (0, 0, g))] * shards
    pairs = seqs * groups * GROUP * tokens * (shards * tokens + past_len)
    out = pl.pallas_call(
        functools.partial(attention_kernel, shards, aliased=aliased),
        grid=(groups,),
        in_specs=in_specs,
        out_specs=out_specs,
        out_shape=out_shape,
        input_output_aliases=aliases,
        compiler_params=pltpu.CompilerParams(vmem_limit_bytes=48 * 1024 * 1024),
        cost_estimate=pl.CostEstimate(
            flops=pairs * HEAD_DIM * 14, bytes_accessed=8 * 1024 * 1024, transcendentals=pairs
        ),
        name="attention",
    )(*operands)
    return out[:5], out[5:]


def gather_adapters(adapter_down, adapter_up):
    sp, fs, rp = (lax.axis_size(a) for a in ("sp", "fsdp", "rep"))
    z, x, r = (lax.axis_index(a) for a in ("sp", "fsdp", "rep"))
    split = 2 if rp % 2 == 0 else 1
    half = lax.rem(r, split)

    def gather(shard):
        rows = shard.shape[0] // split
        own = lax.dynamic_slice_in_dim(shard, half * rows, rows, 0)
        parts = [own] + [cyclic(own, "fsdp", k) for k in range(1, fs)]
        ordered = []
        for a in range(fs):
            pick = parts[0]
            for k in range(1, fs):
                pick = jnp.where(lax.rem(x - k + fs, fs) == a, parts[k], pick)
            ordered.append(pick)
        pair = jnp.stack(ordered)
        buf = jnp.zeros((sp,) + pair.shape, pair.dtype)
        for k in range(sp):
            piece = pair if k == 0 else cyclic(pair, "sp", k)
            buf = lax.dynamic_update_index_in_dim(buf, piece, lax.rem(z - k + sp, sp), 0)
        if split == 1:
            return buf.reshape((sp * fs, 1) + own.shape)
        other = partner(buf, "rep", 1)
        both = jnp.stack(
            [jnp.where(half == 0, buf, other), jnp.where(half == 0, other, buf)], axis=2
        )
        return both.reshape((sp * fs, split) + own.shape)

    down = gather(adapter_down).reshape(D, 2 * RANK)
    up = gather(adapter_up)
    up = up.reshape(sp * fs, RANK, -1).transpose(1, 0, 2).reshape(RANK, D + KV)
    return down, up


def halve_over_rep(x):
    rp = lax.axis_size("rep")
    r = lax.axis_index("rep")
    lead = x.shape[:-3]
    at = len(lead)
    bits = rp.bit_length() - 1
    for b in range(bits):
        x = x.reshape(lead + (rp >> (b + 1), 2) + x.shape[-2:])
        mine = lax.rem(lax.div(r, 1 << b), 2)
        send = lax.dynamic_index_in_dim(x, 1 - mine, at + 1, keepdims=False)
        keep = lax.dynamic_index_in_dim(x, mine, at + 1, keepdims=False)
        got = partner(send, "rep", 1 << b)
        x = (keep.astype(f32) + got.astype(f32)).astype(bf16)
    return x.reshape(lead + x.shape[-2:])


def scatter_over(x, axis):
    n = lax.axis_size(axis)
    i = lax.axis_index(axis)
    total = lax.dynamic_index_in_dim(x, i, 0, keepdims=False).astype(f32)
    for k in range(1, n):
        send = lax.dynamic_index_in_dim(x, lax.rem(i + k, n), 0, keepdims=False)
        total = total + cyclic(send, axis, k).astype(f32)
    return total


def gather_rep(own):
    rp = lax.axis_size("rep")
    r = lax.axis_index("rep")
    parts = [own] + [partner(own, "rep", m) for m in range(1, rp)]
    ordered = []
    for q in range(rp):
        pick = parts[0]
        for m in range(1, rp):
            pick = jnp.where((r ^ m) == q, parts[m], pick)
        ordered.append(pick)
    return jnp.concatenate(ordered, axis=0).astype(f32)


def body(
    hidden,
    query_base,
    key_span,
    value_base,
    past_keys,
    past_values,
    grad_out,
    adapter_down,
    adapter_up,
):
    sp, fs, rp = (lax.axis_size(a) for a in ("sp", "fsdp", "rep"))
    z = lax.axis_index("sp")
    seqs, tokens = hidden.shape[:2]
    past_len = past_keys.shape[1] * sp
    groups = KV_HEADS // CHUNKS
    width = groups * HEAD_DIM
    own_rows = hidden.reshape(seqs * tokens, D)

    down_full, up_full = gather_adapters(adapter_down, adapter_up)

    own_past = jnp.concatenate([past_keys, past_values], axis=2)
    past = jnp.concatenate([own_past] + [cyclic(own_past, "sp", k) for k in range(1, sp)], axis=1)

    chunk_kvs = []
    for c in range(CHUNKS):
        cols = slice(c * width, (c + 1) * width)
        own = jnp.concatenate([key_span[:, :, cols], value_base[:, :, cols]], axis=2)
        kvs = [own]
        for k in range(1, sp):
            kvs.append(along(own, "sp", k) if k <= 2 else along(kvs[k - 1], "sp", 1))
        chunk_kvs.append(kvs)

    low_rank = jnp.dot(own_rows, down_full, preferred_element_type=f32).astype(bf16)
    low_own = low_rank.reshape(seqs, tokens, 2 * RANK)
    lows = [low_own] + [along(low_own, "sp", k) for k in range(1, sp)]

    cos, sin = rotary_tables(tokens, past_len + z * tokens)
    place = z.astype(jnp.int32).reshape(1)

    earlier = None
    value_chunks, up_parts, low_grad_q, low_grad_v = [], [], 0.0, 0.0
    for c in range(CHUNKS):
        (att, gq, gup, lgq, lgv), gvs = attention_chunk(
            c, groups, place, query_base, grad_out, up_full, past, cos, sin,
            lows, chunk_kvs[c], earlier,
        )
        earlier = (att, gq)
        low_grad_q = low_grad_q + lgq
        low_grad_v = low_grad_v + lgv
        total = gvs[0].astype(f32)
        for k in range(1, sp):
            total = total + along(gvs[k], "sp", -k).astype(f32)
        value_chunks.append(total.astype(bf16))
        up_parts.append(halve_over_rep(gup.reshape(rp, RANK // rp, gup.shape[1])))
    attended, grad_query = earlier
    grad_value = jnp.concatenate(value_chunks, axis=2)

    low_v_total = low_grad_v[:, :tokens]
    for k in range(1, sp):
        part = low_grad_v[:, k * tokens : (k + 1) * tokens].astype(bf16)
        low_v_total = low_v_total + along(part, "sp", -k).astype(f32)
    low_grad = (
        jnp.concatenate([low_grad_q, low_v_total], axis=2)
        .astype(bf16)
        .reshape(seqs * tokens, 2 * RANK)
    )
    grad_hidden = jnp.dot(low_grad, down_full.T, preferred_element_type=f32).astype(bf16)

    down_part = jnp.dot(own_rows.T, low_grad, preferred_element_type=f32).astype(bf16)
    down_part = down_part.reshape(sp * fs, rp, D // (sp * fs * rp), 2 * RANK)
    down_part = halve_over_rep(down_part)
    up_rows = RANK // rp
    up_part = jnp.concatenate(up_parts, axis=1).reshape(up_rows, KV_HEADS, WIDE + HEAD_DIM)
    up_part = jnp.concatenate(
        [
            up_part[:, :, :WIDE].reshape(up_rows, D),
            up_part[:, :, WIDE:].reshape(up_rows, KV),
        ],
        axis=1,
    )
    up_part = up_part.reshape(up_rows, sp * fs, -1).transpose(1, 0, 2)

    def spread(x):
        x = x.reshape((sp, fs) + x.shape[1:]).swapaxes(0, 1)
        x = scatter_over(x, "fsdp").astype(bf16)
        return gather_rep(scatter_over(x, "sp").astype(bf16))

    grad_down = spread(down_part)
    grad_up = spread(up_part)
    return (
        attended,
        grad_query,
        grad_value,
        grad_hidden.reshape(seqs, tokens, D),
        grad_down,
        grad_up,
    )


def solution(mesh):
    rows = P(("fsdp", "rep"), "sp", None)
    down, up = P(("sp", "fsdp"), None), P(None, ("sp", "fsdp"))
    return jax.shard_map(
        body,
        mesh=mesh,
        in_specs=(rows,) * 7 + (down, up),
        out_specs=(rows,) * 4 + (down, up),
        check_vma=False,
    )
```

time: 457 us -> 198 us (0.43); the launches traced: 451 us -> 197 us
  blocking collectives: 133 us -> 0 us
  waiting for transfers between devices: 115 us -> 58.3 us
  local copies, waits for them, and re-layouts: 73.9 us -> 19.9 us
  other arithmetic: 38.9 us -> 6.66 us
  starting transfers between devices: 52.1 us -> 83.4 us
  Pallas kernels: 0 us -> 22.9 us
  matrix products: 23.6 us -> 4.7 us
  between operations: 14.8 us -> 1.53 us
    all_gather x3 -> x0, blocking collectives: 133 us -> none  [the longest x1 55 us: body(): lax.all_gather(adapter_up, ('sp', 'fsdp'), axis=1, tiled=True)]
    all_to_all x11 -> x0, waiting for transfers between devices: 85.7 us -> none  [the longest x1 22.3 us: body(): lax.all_to_all(value_term_rows, 'sp', split_axis=1, concat_axis=2, tiled=...]
    ppermute x0 -> x51, starting transfers between devices: none -> 83.4 us  [the longest x18 41.6 us: along(): lax.ppermute(x, axis, [(i, i + shift) for i in range(n) if 0 <= i + shift...]
    ppermute x0 -> x51, waiting for transfers between devices: none -> 58.3 us  [the longest x19 36 us: cyclic(): return lax.ppermute(x, axis, [(i, (i + shift) % n) for i in range(n)])]
    all_to_all x11 -> x0, starting transfers between devices: 52 us -> none  [the longest x1 8.07 us: body(): lax.all_to_all(own_rows, ('sp', 'fsdp'), split_axis=1, concat_axis=0, til...]
    psum x1 -> x0, waiting for transfers between devices: 29 us -> none  [body(): grad_down, grad_up = lax.psum((down_shard, up_shard), 'rep')]
    pallas_call x0 -> x2, Pallas kernels: none -> 22.9 us  [attention_chunk(): pl.pallas_call(functools.partial(attention_kernel, shards, aliased=aliase...]
    another operation x6 -> x11, other arithmetic: 23.3 us -> 1.44 us  [the longest x4 1.29 us: gather(): jnp.stack([jnp.where(half == 0, buf, other), jnp.where(half == 0, other,...]
  transfers between devices with their start and end apart: 13 -> 51, of which waited for: 8 -> 23; matrix products, arithmetic and copies ran while one was open for 22% -> 14% of each run, Pallas kernels for 0% -> 12%
where the time goes in v1:
time: 198 us; the launch traced here: 197 us
  starting transfers between devices  83.4 us (42%)
  waiting for transfers between devices  58.3 us (29%)
  Pallas kernels  22.9 us (12%)
  local copies, waits for them, and re-layouts  19.9 us (10%)
  other arithmetic  6.66 us (3%)
  matrix products  4.7 us (2%)
    ppermute x18, starting transfers between devices, along(): lax.ppermute(x, axis, [(i, i + shift) for i in range(n) if 0 <= i + shift...  41.6 us
    ppermute x19, waiting for transfers between devices, cyclic(): return lax.ppermute(x, axis, [(i, (i + shift) % n) for i in range(n)])  36 us
    ppermute x19, starting transfers between devices, cyclic(): return lax.ppermute(x, axis, [(i, (i + shift) % n) for i in range(n)])  34.5 us
    pallas_call x2, Pallas kernels, attention_chunk(): pl.pallas_call(functools.partial(attention_kernel, shards, aliased=aliase...  22.9 us
    ppermute x18, waiting for transfers between devices, along(): lax.ppermute(x, axis, [(i, i + shift) for i in range(n) if 0 <= i + shift...  16 us
    unnamed x22, local copies, waits for them, and re-layouts  9.13 us
    ppermute x14, starting transfers between devices, partner(): return lax.ppermute(x, axis, [(i, i ^ mask) for i in range(n)])  7.35 us
    ppermute x14, waiting for transfers between devices, partner(): return lax.ppermute(x, axis, [(i, i ^ mask) for i in range(n)])  6.34 us
  transfers between devices with their start and end apart: 51, of which 23 were waited for; matrix products, arithmetic and copies ran while one was open for 14% of the time, Pallas kernels for 12%

profile of v1, /device:TPU:0, one launch (start us, length us, event | category | flops | bytes accessed | tf_op | source)
XLA Modules:
  0.0 197.5 jit_solution(15338132893054620832)
XLA Ops:
  2.2 3.1 %collective-permute-start.5 = (bf16[2,4,2048]{2,1,0:T(4,128)(2,1)S(1)}, bf16[2,4,2048]{2,1,0:T(4,128)(2,1)S(1)}, u32[]{:S(2)}, u32[]{:S(2)}) collective-permute-start(bf16[2,4,2048]{2,1,0:T(4,128)(2,1)S(1)} %constant_dynamic-update-slice_fusion), channel_id=1, source_target_pairs={{0,8},{8,16},{16,24},{24,0},{1,9},{9,17},{17,25},{25,1},{2,10},{10... | collective-permute-start | bytes 98312 | tf_op jit(solution)/shard_map/ppermute | solution.py:41
  5.3 2.6 %collective-permute-start.6 = (bf16[2,4,2048]{2,1,0:T(4,128)(2,1)S(1)}, bf16[2,4,2048]{2,1,0:T(4,128)(2,1)S(1)}, u32[]{:S(2)}, u32[]{:S(2)}) collective-permute-start(bf16[2,4,2048]{2,1,0:T(4,128)(2,1)S(1)} %constant_dynamic-update-slice_fusion), channel_id=1, source_target_pairs={{0,16},{8,24},{16,0},{24,8},{1,17},{9,25},{17,1},{25,9},{2,18},{10... | collective-permute-start | bytes 98312 | tf_op jit(solution)/shard_map/ppermute | solution.py:41
  7.9 1.3 collective-permute-start.7
  9.2 0.8 constant_dynamic-slice_fusion.5
  10.0 1.5 collective-permute-start.8
  13.1 1.2 fusion.27
  14.4 2.0 collective-permute-done
  16.3 2.2 %collective-permute-start.20 = (bf16[2,64,1024]{2,1,0:T(8,128)(2,1)S(1)}, bf16[2,64,1024]{2,1,0:T(8,128)(2,1)S(1)}, u32[]{:S(2)}, u32[]{:S(2)}) collective-permute-start(bf16[2,64,1024]{2,1,0:T(8,128)(2,1)S(1)} %pad_maximum_fusion.3.refs_12_.refs_16_), channel_id=1, source_target_pairs={{0,16},{8,24},{1,17},{9,25},{2,18},{10,26},{3,19},{11,27},{4,20},{... | collective-permute-start | bytes 786440 | tf_op jit(solution)/shard_map/ppermute | solution.py:46
  19.6 5.4 %collective-permute-done.1 = bf16[2,32,640]{2,1,0:T(8,128)(2,1)S(1)} collective-permute-done((bf16[2,32,640]{2,1,0:T(8,128)(2,1)S(1)}, bf16[2,32,640]{2,1,0:T(8,128)(2,1)S(1)}, u32[]{:S(2)}, u32[]{:S(2)}) %collective-permute-start.1) | collective-permute-done | bytes 81952 | tf_op jit(solution)/shard_map/ppermute | solution.py:41
  25.0 8.0 %collective-permute-start.2 = (bf16[2,32,640]{2,1,0:T(8,128)(2,1)S(1)}, bf16[2,32,640]{2,1,0:T(8,128)(2,1)S(1)}, u32[]{:S(2)}, u32[]{:S(2)}) collective-permute-start(bf16[2,32,640]{2,1,0:T(8,128)(2,1)S(1)} %pad_maximum_fusion.8), channel_id=1, source_target_pairs={{0,16},{8,24},{16,0},{24,8},{1,17},{9,25},{17,1},{25,9},{2,18},{10... | collective-permute-start | bytes 245768 | tf_op jit(solution)/shard_map/ppermute | solution.py:41
  33.0 3.3 %collective-permute-done.2 = bf16[2,32,640]{2,1,0:T(8,128)(2,1)S(1)} collective-permute-done((bf16[2,32,640]{2,1,0:T(8,128)(2,1)S(1)}, bf16[2,32,640]{2,1,0:T(8,128)(2,1)S(1)}, u32[]{:S(2)}, u32[]{:S(2)}) %collective-permute-start.2) | collective-permute-done | bytes 81952 | tf_op jit(solution)/shard_map/ppermute | solution.py:41
  36.3 4.4 %collective-permute-done.3 = bf16[2,32,640]{2,1,0:T(8,128)(2,1)S(1)} collective-permute-done((bf16[2,32,640]{2,1,0:T(8,128)(2,1)S(1)}, bf16[2,32,640]{2,1,0:T(8,128)(2,1)S(1)}, u32[]{:S(2)}, u32[]{:S(2)}) %collective-permute-start.3) | collective-permute-done | bytes 81952 | tf_op jit(solution)/shard_map/ppermute | solution.py:41
  40.7 1.3 collective-permute-start.9
  42.0 5.9 %collective-permute-done.9 = bf16[2,256,128]{2,1,0:T(8,128)(2,1)S(1)} collective-permute-done((bf16[2,256,128]{2,1,0:T(8,128)(2,1)S(1)}, bf16[2,256,128]{2,1,0:T(8,128)(2,1)S(1)}, u32[]{:S(2)}, u32[]{:S(2)}) %collective-permute-start.9) | collective-permute-done | bytes 131104 | tf_op jit(solution)/shard_map/ppermute | solution.py:41
  47.9 2.9 %collective-permute-start.10 = (bf16[2,256,128]{2,1,0:T(8,128)(2,1)S(1)}, bf16[2,256,128]{2,1,0:T(8,128)(2,1)S(1)}, u32[]{:S(2)}, u32[]{:S(2)}) collective-permute-start(bf16[2,256,128]{2,1,0:T(8,128)(2,1)S(1)} %pad_maximum_fusion.7), channel_id=1, source_target_pairs={{0,16},{8,24},{16,0},{24,8},{1,17},{9,25},{17,1},{25,9},{2,18},{10... | collective-permute-start | bytes 393224 | tf_op jit(solution)/shard_map/ppermute | solution.py:41
  50.8 4.4 %collective-permute-done.10 = bf16[2,256,128]{2,1,0:T(8,128)(2,1)S(1)} collective-permute-done((bf16[2,256,128]{2,1,0:T(8,128)(2,1)S(1)}, bf16[2,256,128]{2,1,0:T(8,128)(2,1)S(1)}, u32[]{:S(2)}, u32[]{:S(2)}) %collective-permute-start.10) | collective-permute-done | bytes 131104 | tf_op jit(solution)/shard_map/ppermute | solution.py:41
  55.2 3.3 %collective-permute-start.11 = (bf16[2,256,128]{2,1,0:T(8,128)(2,1)S(1)}, bf16[2,256,128]{2,1,0:T(8,128)(2,1)S(1)}, u32[]{:S(2)}, u32[]{:S(2)}) collective-permute-start(bf16[2,256,128]{2,1,0:T(8,128)(2,1)S(1)} %pad_maximum_fusion.7), channel_id=1, source_target_pairs={{0,24},{8,0},{16,8},{24,16},{1,25},{9,1},{17,9},{25,17},{2,26},{10... | collective-permute-start | bytes 393224 | tf_op jit(solution)/shard_map/ppermute | solution.py:41
  58.5 2.5 %collective-permute-done.11 = bf16[2,256,128]{2,1,0:T(8,128)(2,1)S(1)} collective-permute-done((bf16[2,256,128]{2,1,0:T(8,128)(2,1)S(1)}, bf16[2,256,128]{2,1,0:T(8,128)(2,1)S(1)}, u32[]{:S(2)}, u32[]{:S(2)}) %collective-permute-start.11) | collective-permute-done | bytes 131104 | tf_op jit(solution)/shard_map/ppermute | solution.py:41
  61.8 1.5 collective-permute-start.19
  63.4 7.1 %collective-permute-start.17 = (bf16[2,64,1024]{2,1,0:T(8,128)(2,1)S(1)}, bf16[2,64,1024]{2,1,0:T(8,128)(2,1)S(1)}, u32[]{:S(2)}, u32[]{:S(2)}) collective-permute-start(bf16[2,64,1024]{2,1,0:T(8,128)(2,1)S(1)} %pad_maximum_fusion.2.refs_12_.refs_16_), channel_id=1, source_target_pairs={{0,16},{8,24},{1,17},{9,25},{2,18},{10,26},{3,19},{11,27},{4,20},{... | collective-permute-start | bytes 786440 | tf_op jit(solution)/shard_map/ppermute | solution.py:46
  70.6 1.3 collective-permute-start.21
  71.9 1.0 select_bitcast_fusion.3
  74.2 2.4 %collective-permute-start.13 = (bf16[2,64,128]{2,1,0:T(8,128)(2,1)S(1)}, bf16[2,64,128]{2,1,0:T(8,128)(2,1)S(1)}, u32[]{:S(2)}, u32[]{:S(2)}) collective-permute-start(bf16[2,64,128]{2,1,0:T(8,128)(2,1)S(1)} %bitcast.127), channel_id=1, source_target_pairs={{0,8},{8,16},{16,24},{1,9},{9,17},{17,25},{2,10},{10,18},{18,26},{... | collective-permute-start | bytes 98312 | tf_op jit(solution)/shard_map/ppermute | solution.py:46
  76.6 1.4 collective-permute-start.14
  78.0 1.9 collective-permute-start.15
  80.2 5.2 %collective-permute-start.16 = (bf16[2,64,1024]{2,1,0:T(8,128)(2,1)S(1)}, bf16[2,64,1024]{2,1,0:T(8,128)(2,1)S(1)}, u32[]{:S(2)}, u32[]{:S(2)}) collective-permute-start(bf16[2,64,1024]{2,1,0:T(8,128)(2,1)S(1)} %pad_maximum_fusion.2.refs_12_.refs_16_), channel_id=1, source_target_pairs={{0,8},{8,16},{16,24},{1,9},{9,17},{17,25},{2,10},{10,18},{18,26},{... | collective-permute-start | bytes 786440 | tf_op jit(solution)/shard_map/ppermute | solution.py:46
  85.4 6.8 %collective-permute-start.18 = (bf16[2,64,1024]{2,1,0:T(8,128)(2,1)S(1)}, bf16[2,64,1024]{2,1,0:T(8,128)(2,1)S(1)}, u32[]{:S(2)}, u32[]{:S(2)}) collective-permute-start(bf16[2,64,1024]{2,1,0:T(8,128)(2,1)S(1)} %collective-permute-done.17.refs_14_.refs_18_), channel_id=1, source_target_pairs={{0,8},{8,16},{16,24},{1,9},{9,17},{17,25},{2,10},{10,18},{18,26},{... | collective-permute-start | bytes 786440 | tf_op jit(solution)/shard_map/ppermute | solution.py:46
  92.2 11.4 %attention.2 = (bf16[2,64,4096]{2,1,0:T(8,128)(2,1)}, bf16[2,64,4096]{2,1,0:T(8,128)(2,1)}, bf16[64,2560]{1,0:T(8,128)(2,1)S(1)}, f32[2,64,64]{2,1,0:T(8,128)S(1...) custom-call(s32[1]{0:T(128)} %bitcast.place_ref, ...), custom_call_target="tpu_custom_call" | custom-call | flops 998244352 | bytes 8388608 | tf_op jit(solution)/shard_map/attention/pallas_call | solution.py:193
  104.3 11.5 %attention.3 = (bf16[2,64,4096]{2,1,0:T(8,128)(2,1)}, bf16[2,64,4096]{2,1,0:T(8,128)(2,1)}, bf16[64,2560]{1,0:T(8,128)(2,1)S(1)}, f32[2,64,64]{2,1,0:T(8,128)S(1...) custom-call(s32[1]{0:T(128)} %bitcast.place_ref, ...), custom_call_target="tpu_custom_call", output_to_operand_aliasing={{0}: (21, {}), {1}: (22, {})} | custom-call | flops 998244352 | bytes 8388608 | tf_op jit(solution)/shard_map/attention/pallas_call | solution.py:193
  116.4 1.3 collective-permute-start.28
  117.7 1.3 collective-permute-start.29
  119.0 1.3 collective-permute-start.30
  120.3 2.3 %collective-permute-done.28 = bf16[2,64,64]{2,1,0:T(8,128)(2,1)S(1)} collective-permute-done((bf16[2,64,64]{2,1,0:T(8,128)(2,1)S(1)}, bf16[2,64,64]{2,1,0:T(8,128)(2,1)S(1)}, u32[]{:S(2)}, u32[]{:S(2)}) %collective-permute-start.28) | collective-permute-done | bytes 16416 | tf_op jit(solution)/shard_map/ppermute | solution.py:46
  122.6 1.3 collective-permute-start.22
  123.9 1.5 collective-permute-done.29
  125.4 1.3 collective-permute-start.23
  126.7 1.7 collective-permute-done.30
  128.3 1.5 collective-permute-start.24
  129.8 1.5 fusion.1
  131.3 2.6 %reshape_reshape.20 = bf16[8,2,2,128,128]{3,2,1,0,4:T(2,128)(2,1)} reshape(bf16[4096,128]{0,1:T(8,128)(2,1)} %fusion.1) | data formatting | bytes 2097152 | tf_op jit(solution)/shard_map/reshape;reshape | solution.py:251
  133.9 2.8 %convolution_convert_fusion = bf16[128,4096]{1,0:T(8,128)(2,1)} fusion(bf16[4096,128]{1,0:T(8,128)(2,1)} %bitcast.133, bf16[128,64]{1,0:T(8,128)(2,1)S(1)} %bitcast.146, bf16[128,64]{1,0:T(8,128)(2,1)S(1)} %bitcast.145), kind=kOutput, calls=%fused_computation.2 | convolution fusion | flops 134807552 | bytes 2129920 | tf_op jit(solution)/shard_map/dot_general | solution.py:350
  136.7 3.5 %constant_dynamic-slice_fusion.4 = (bf16[8,2,1,128,128]{3,2,1,0,4:T(2,128)(2,1)}, bf16[8,2,1,128,128]{3,2,1,0,4:T(2,128)(2,1)}) fusion(bf16[8,2,2,128,128]{3,2,1,0,4:T(2,128)(2,1)S(1)} %copy-done.3, s32[]{:T(128)S(6)} %select_n.291, s32[]{:T(128)S(6)} %select_n.292), kind=kLoop, calls=%fused_computation.98 | loop fusion | bytes 2097160 | tf_op jit(solution)/shard_map/jit(dynamic_index_in_dim)/dynamic_slice | solution.py:254
  140.2 3.5 %copy.28 = bf16[8,2,1,128,128]{4,3,1,0,2:T(8,128)(2,1)} copy(bf16[8,2,1,128,128]{3,2,1,0,4:T(2,128)(2,1)} %get-tuple-element.45) | data formatting | bytes 1048576
  143.7 3.5 %copy.27 = bf16[8,2,1,128,128]{4,3,1,0,2:T(8,128)(2,1)} copy(bf16[8,2,1,128,128]{3,2,1,0,4:T(2,128)(2,1)} %get-tuple-element.44) | data formatting | bytes 1048576
  147.2 1.3 collective-permute-start.25
  148.5 1.3 collective-permute-start.26
  149.8 1.3 collective-permute-start.27
  151.1 1.0 add_convert_fusion.2
  152.1 3.0 %collective-permute-done.25 = bf16[2,64,512]{2,1,0:T(8,128)(2,1)S(1)} collective-permute-done((bf16[2,64,512]{2,1,0:T(8,128)(2,1)S(1)}, bf16[2,64,512]{2,1,0:T(8,128)(2,1)S(1)}, u32[]{:S(2)}, u32[]{:S(2)}) %collective-permute-start.25) | collective-permute-done | bytes 131104 | tf_op jit(solution)/shard_map/ppermute | solution.py:46
  155.1 7.5 %collective-permute-done.26 = bf16[2,64,512]{2,1,0:T(8,128)(2,1)S(1)} collective-permute-done((bf16[2,64,512]{2,1,0:T(8,128)(2,1)S(1)}, bf16[2,64,512]{2,1,0:T(8,128)(2,1)S(1)}, u32[]{:S(2)}, u32[]{:S(2)}) %collective-permute-start.26) | collective-permute-done | bytes 131104 | tf_op jit(solution)/shard_map/ppermute | solution.py:46
  163.5 2.3 %collective-permute-start.41 = (bf16[1,16,2560]{2,1,0:T(8,128)(2,1)S(1)}, bf16[1,16,2560]{2,1,0:T(8,128)(2,1)S(1)}, u32[]{:S(2)}, u32[]{:S(2)}) collective-permute-start(bf16[1,16,2560]{2,1,0:T(8,128)(2,1)S(1)} %constant_dynamic-slice_fusion.1), channel_id=1, source_target_pairs={{0,2},{1,3},{2,0},{3,1},{4,6},{5,7},{6,4},{7,5},{8,10},{9,11},{10,... | collective-permute-start | bytes 245768 | tf_op jit(solution)/shard_map/ppermute | solution.py:51
  165.7 1.0 fusion.3
  166.8 1.3 collective-permute-done.41
  168.2 3.5 %collective-permute-done.43 = bf16[1,16,2560]{2,1,0:T(8,128)(2,1)S(1)} collective-permute-done((bf16[1,16,2560]{2,1,0:T(8,128)(2,1)S(1)}, bf16[1,16,2560]{2,1,0:T(8,128)(2,1)S(1)}, u32[]{:S(2)}, u32[]{:S(2)}) %collective-permute-start.43) | collective-permute-done | bytes 81952 | tf_op jit(solution)/shard_map/ppermute | solution.py:51
  173.0 3.5 %collective-permute-done.44 = bf16[4,16,640]{2,1,0:T(8,128)(2,1)S(1)} collective-permute-done((bf16[4,16,640]{2,1,0:T(8,128)(2,1)S(1)}, bf16[4,16,640]{2,1,0:T(8,128)(2,1)S(1)}, u32[]{:S(2)}, u32[]{:S(2)}) %collective-permute-start.44) | collective-permute-done | bytes 81952 | tf_op jit(solution)/shard_map/ppermute | solution.py:41
  176.7 3.7 %collective-permute-start.47 = (bf16[16,640]{1,0:T(8,128)(2,1)S(1)}, bf16[16,640]{1,0:T(8,128)(2,1)S(1)}, u32[]{:S(2)}, u32[]{:S(2)}) collective-permute-start(bf16[16,640]{1,0:T(8,128)(2,1)S(1)} %get-tuple-element.71), channel_id=1, source_target_pairs={{0,24},{8,0},{16,8},{24,16},{1,25},{9,1},{17,9},{25,17},{2,26},{10... | collective-permute-start | bytes 61448 | tf_op jit(solution)/shard_map/ppermute | solution.py:41
  180.9 1.3 collective-permute-done.45
  182.9 1.8 collective-permute-start.50
  184.7 0.9 collective-permute-done.33
  185.6 1.2 collective-permute-start.34
  186.8 1.8 collective-permute-start.35
  188.7 2.0 %collective-permute-start.36 = (bf16[128,128]{1,0:T(8,128)(2,1)S(1)}, bf16[128,128]{1,0:T(8,128)(2,1)S(1)}, u32[]{:S(2)}, u32[]{:S(2)}) collective-permute-start(bf16[128,128]{1,0:T(8,128)(2,1)S(1)} %get-tuple-element.59), channel_id=1, source_target_pairs={{0,24},{8,0},{16,8},{24,16},{1,25},{9,1},{17,9},{25,17},{2,26},{10... | collective-permute-start | bytes 98312 | tf_op jit(solution)/shard_map/ppermute | solution.py:41
  190.7 0.9 collective-permute-done.34
  193.1 1.4 collective-permute-start.39
  (134 shorter events, 15.8 us)
Async XLA Ops:
  0.6 72.5 %copy-start = (bf16[2,64,4096]{2,1,0:T(8,128)(2,1)S(1)}, bf16[2,64,4096]{2,1,0:T(8,128)(2,1)}, u32[]{:S(2)}) copy-start(bf16[2,64,4096]{2,1,0:T(8,128)(2,1)} %param.9) | copy-start | bytes 3145732
  2.2 58.9 %collective-permute-start.5 = (bf16[2,4,2048]{2,1,0:T(4,128)(2,1)S(1)}, bf16[2,4,2048]{2,1,0:T(4,128)(2,1)S(1)}, u32[]{:S(2)}, u32[]{:S(2)}) collective-permute-start(bf16[2,4,2048]{2,1,0:T(4,128)(2,1)S(1)} %constant_dynamic-update-slice_fusion), channel_id=1, source_target_pairs={{0,8},{8,16},{16,24},{24,0},{1,9},{9,17},{17,25},{25,1},{2,10},{10... | collective-permute-start | bytes 98312 | tf_op jit(solution)/shard_map/ppermute | solution.py:41
  5.3 56.5 %collective-permute-start.6 = (bf16[2,4,2048]{2,1,0:T(4,128)(2,1)S(1)}, bf16[2,4,2048]{2,1,0:T(4,128)(2,1)S(1)}, u32[]{:S(2)}, u32[]{:S(2)}) collective-permute-start(bf16[2,4,2048]{2,1,0:T(4,128)(2,1)S(1)} %constant_dynamic-update-slice_fusion), channel_id=1, source_target_pairs={{0,16},{8,24},{16,0},{24,8},{1,17},{9,25},{17,1},{25,9},{2,18},{10... | collective-permute-start | bytes 98312 | tf_op jit(solution)/shard_map/ppermute | solution.py:41
  7.9 55.5 %collective-permute-start.7 = (bf16[2,4,2048]{2,1,0:T(4,128)(2,1)S(1)}, bf16[2,4,2048]{2,1,0:T(4,128)(2,1)S(1)}, u32[]{:S(2)}, u32[]{:S(2)}) collective-permute-start(bf16[2,4,2048]{2,1,0:T(4,128)(2,1)S(1)} %constant_dynamic-update-slice_fusion), channel_id=1, source_target_pairs={{0,24},{8,0},{16,8},{24,16},{1,25},{9,1},{17,9},{25,17},{2,26},{10... | collective-permute-start | bytes 98312 | tf_op jit(solution)/shard_map/ppermute | solution.py:41
  10.0 8.7 %collective-permute-start.8 = (bf16[256,128]{1,0:T(8,128)(2,1)S(1)}, bf16[256,128]{1,0:T(8,128)(2,1)S(1)}, u32[]{:S(2)}, u32[]{:S(2)}) collective-permute-start(bf16[256,128]{1,0:T(8,128)(2,1)S(1)} %constant_dynamic-slice_fusion.5), channel_id=1, source_target_pairs={{0,4},{4,0},{1,5},{5,1},{2,6},{6,2},{3,7},{7,3},{8,12},{12,8},{9,1... | collective-permute-start | bytes 196616 | tf_op jit(solution)/shard_map/ppermute | solution.py:41
  12.3 4.0 %collective-permute-start = (bf16[32,640]{1,0:T(8,128)(2,1)S(1)}, bf16[32,640]{1,0:T(8,128)(2,1)S(1)}, u32[]{:S(2)}, u32[]{:S(2)}) collective-permute-start(bf16[32,640]{1,0:T(8,128)(2,1)S(1)} %constant_dynamic-slice_fusion.6), channel_id=1, source_target_pairs={{0,4},{4,0},{1,5},{5,1},{2,6},{6,2},{3,7},{7,3},{8,12},{12,8},{9,1... | collective-permute-start | bytes 122888 | tf_op jit(solution)/shard_map/ppermute | solution.py:41
  13.1 5.5 %copy-start.7 = (bf16[64,640]{1,0:T(8,128)(2,1)S(1)}, bf16[64,640]{1,0:T(8,128)(2,1)}, u32[]{:S(2)}) copy-start(bf16[64,640]{1,0:T(8,128)(2,1)} %param.17) | copy-start | bytes 245764
  14.3 5.2 %copy-start.6 = (bf16[512,128]{1,0:T(8,128)(2,1)S(1)}, bf16[512,128]{1,0:T(8,128)(2,1)}, u32[]{:S(2)}) copy-start(bf16[512,128]{1,0:T(8,128)(2,1)} %param.16) | copy-start | bytes 393220
  16.3 54.2 %collective-permute-start.20 = (bf16[2,64,1024]{2,1,0:T(8,128)(2,1)S(1)}, bf16[2,64,1024]{2,1,0:T(8,128)(2,1)S(1)}, u32[]{:S(2)}, u32[]{:S(2)}) collective-permute-start(bf16[2,64,1024]{2,1,0:T(8,128)(2,1)S(1)} %pad_maximum_fusion.3.refs_12_.refs_16_), channel_id=1, source_target_pairs={{0,16},{8,24},{1,17},{9,25},{2,18},{10,26},{3,19},{11,27},{4,20},{... | collective-permute-start | bytes 786440 | tf_op jit(solution)/shard_map/ppermute | solution.py:46
  18.7 6.3 %collective-permute-start.1 = (bf16[2,32,640]{2,1,0:T(8,128)(2,1)S(1)}, bf16[2,32,640]{2,1,0:T(8,128)(2,1)S(1)}, u32[]{:S(2)}, u32[]{:S(2)}) collective-permute-start(bf16[2,32,640]{2,1,0:T(8,128)(2,1)S(1)} %pad_maximum_fusion.8), channel_id=1, source_target_pairs={{0,8},{8,16},{16,24},{24,0},{1,9},{9,17},{17,25},{25,1},{2,10},{10... | collective-permute-start | bytes 245768 | tf_op jit(solution)/shard_map/ppermute | solution.py:41
  25.0 11.3 %collective-permute-start.2 = (bf16[2,32,640]{2,1,0:T(8,128)(2,1)S(1)}, bf16[2,32,640]{2,1,0:T(8,128)(2,1)S(1)}, u32[]{:S(2)}, u32[]{:S(2)}) collective-permute-start(bf16[2,32,640]{2,1,0:T(8,128)(2,1)S(1)} %pad_maximum_fusion.8), channel_id=1, source_target_pairs={{0,16},{8,24},{16,0},{24,8},{1,17},{9,25},{17,1},{25,9},{2,18},{10... | collective-permute-start | bytes 245768 | tf_op jit(solution)/shard_map/ppermute | solution.py:41
  36.3 4.4 %collective-permute-start.3 = (bf16[2,32,640]{2,1,0:T(8,128)(2,1)S(1)}, bf16[2,32,640]{2,1,0:T(8,128)(2,1)S(1)}, u32[]{:S(2)}, u32[]{:S(2)}) collective-permute-start(bf16[2,32,640]{2,1,0:T(8,128)(2,1)S(1)} %pad_maximum_fusion.8), channel_id=1, source_target_pairs={{0,24},{8,0},{16,8},{24,16},{1,25},{9,1},{17,9},{25,17},{2,26},{10... | collective-permute-start | bytes 245768 | tf_op jit(solution)/shard_map/ppermute | solution.py:41
  40.7 7.2 %collective-permute-start.9 = (bf16[2,256,128]{2,1,0:T(8,128)(2,1)S(1)}, bf16[2,256,128]{2,1,0:T(8,128)(2,1)S(1)}, u32[]{:S(2)}, u32[]{:S(2)}) collective-permute-start(bf16[2,256,128]{2,1,0:T(8,128)(2,1)S(1)} %pad_maximum_fusion.7), channel_id=1, source_target_pairs={{0,8},{8,16},{16,24},{24,0},{1,9},{9,17},{17,25},{25,1},{2,10},{10... | collective-permute-start | bytes 393224 | tf_op jit(solution)/shard_map/ppermute | solution.py:41
  47.9 7.3 %collective-permute-start.10 = (bf16[2,256,128]{2,1,0:T(8,128)(2,1)S(1)}, bf16[2,256,128]{2,1,0:T(8,128)(2,1)S(1)}, u32[]{:S(2)}, u32[]{:S(2)}) collective-permute-start(bf16[2,256,128]{2,1,0:T(8,128)(2,1)S(1)} %pad_maximum_fusion.7), channel_id=1, source_target_pairs={{0,16},{8,24},{16,0},{24,8},{1,17},{9,25},{17,1},{25,9},{2,18},{10... | collective-permute-start | bytes 393224 | tf_op jit(solution)/shard_map/ppermute | solution.py:41
  55.2 5.8 %collective-permute-start.11 = (bf16[2,256,128]{2,1,0:T(8,128)(2,1)S(1)}, bf16[2,256,128]{2,1,0:T(8,128)(2,1)S(1)}, u32[]{:S(2)}, u32[]{:S(2)}) collective-permute-start(bf16[2,256,128]{2,1,0:T(8,128)(2,1)S(1)} %pad_maximum_fusion.7), channel_id=1, source_target_pairs={{0,24},{8,0},{16,8},{24,16},{1,25},{9,1},{17,9},{25,17},{2,26},{10... | collective-permute-start | bytes 393224 | tf_op jit(solution)/shard_map/ppermute | solution.py:41
  61.0 10.8 %collective-permute-start.4 = (bf16[4,2,32,640]{3,2,1,0:T(8,128)(2,1)S(1)}, bf16[4,2,32,640]{3,2,1,0:T(8,128)(2,1)}, u32[]{:S(2)}, u32[]{:S(2)}) collective-permute-start(bf16[4,2,32,640]{3,2,1,0:T(8,128)(2,1)S(1)} %bitcast_dynamic-update-slice_fusion.4), channel_id=1, source_target_pairs={{0,1},{1,0},{2,3},{3,2},{4,5},{5,4},{6,7},{7,6},{8,9},{9,8},{10,11... | collective-permute-start | bytes 983048 | tf_op jit(solution)/shard_map/ppermute | solution.py:51
  61.1 11.9 %collective-permute-start.12 = (bf16[4,2,256,128]{3,2,1,0:T(8,128)(2,1)S(1)}, bf16[4,2,256,128]{3,2,1,0:T(8,128)(2,1)S(1)}, u32[]{:S(2)}, u32[]{:S(2)}) collective-permute-start(bf16[4,2,256,128]{3,2,1,0:T(8,128)(2,1)S(1)} %bitcast_dynamic-update-slice_fusion), channel_id=1, source_target_pairs={{0,1},{1,0},{2,3},{3,2},{4,5},{5,4},{6,7},{7,6},{8,9},{9,8},{10,11... | collective-permute-start | bytes 1572872 | tf_op jit(solution)/shard_map/ppermute | solution.py:51
  61.8 16.2 %collective-permute-start.19 = (bf16[2,64,1024]{2,1,0:T(8,128)(2,1)S(1)}, bf16[2,64,1024]{2,1,0:T(8,128)(2,1)S(1)}, u32[]{:S(2)}, u32[]{:S(2)}) collective-permute-start(bf16[2,64,1024]{2,1,0:T(8,128)(2,1)S(1)} %pad_maximum_fusion.3.refs_12_.refs_16_), channel_id=1, source_target_pairs={{0,8},{8,16},{16,24},{1,9},{9,17},{17,25},{2,10},{10,18},{18,26},{... | collective-permute-start | bytes 786440 | tf_op jit(solution)/shard_map/ppermute | solution.py:46
  63.4 16.8 %collective-permute-start.17 = (bf16[2,64,1024]{2,1,0:T(8,128)(2,1)S(1)}, bf16[2,64,1024]{2,1,0:T(8,128)(2,1)S(1)}, u32[]{:S(2)}, u32[]{:S(2)}) collective-permute-start(bf16[2,64,1024]{2,1,0:T(8,128)(2,1)S(1)} %pad_maximum_fusion.2.refs_12_.refs_16_), channel_id=1, source_target_pairs={{0,16},{8,24},{1,17},{9,25},{2,18},{10,26},{3,19},{11,27},{4,20},{... | collective-permute-start | bytes 786440 | tf_op jit(solution)/shard_map/ppermute | solution.py:46
  70.6 14.8 %collective-permute-start.21 = (bf16[2,64,1024]{2,1,0:T(8,128)(2,1)S(1)}, bf16[2,64,1024]{2,1,0:T(8,128)(2,1)S(1)}, u32[]{:S(2)}, u32[]{:S(2)}) collective-permute-start(bf16[2,64,1024]{2,1,0:T(8,128)(2,1)S(1)} %collective-permute-done.20.refs_14_.refs_18_), channel_id=1, source_target_pairs={{0,8},{8,16},{16,24},{1,9},{9,17},{17,25},{2,10},{10,18},{18,26},{... | collective-permute-start | bytes 786440 | tf_op jit(solution)/shard_map/ppermute | solution.py:46
  73.1 1.0 copy-start.4
  74.2 18.0 %collective-permute-start.13 = (bf16[2,64,128]{2,1,0:T(8,128)(2,1)S(1)}, bf16[2,64,128]{2,1,0:T(8,128)(2,1)S(1)}, u32[]{:S(2)}, u32[]{:S(2)}) collective-permute-start(bf16[2,64,128]{2,1,0:T(8,128)(2,1)S(1)} %bitcast.127), channel_id=1, source_target_pairs={{0,8},{8,16},{16,24},{1,9},{9,17},{17,25},{2,10},{10,18},{18,26},{... | collective-permute-start | bytes 98312 | tf_op jit(solution)/shard_map/ppermute | solution.py:46
  76.6 15.6 %collective-permute-start.14 = (bf16[2,64,128]{2,1,0:T(8,128)(2,1)S(1)}, bf16[2,64,128]{2,1,0:T(8,128)(2,1)S(1)}, u32[]{:S(2)}, u32[]{:S(2)}) collective-permute-start(bf16[2,64,128]{2,1,0:T(8,128)(2,1)S(1)} %bitcast.128), channel_id=1, source_target_pairs={{0,16},{8,24},{1,17},{9,25},{2,18},{10,26},{3,19},{11,27},{4,20},{... | collective-permute-start | bytes 98312 | tf_op jit(solution)/shard_map/ppermute | solution.py:46
  78.0 14.2 %collective-permute-start.15 = (bf16[2,64,128]{2,1,0:T(8,128)(2,1)S(1)}, bf16[2,64,128]{2,1,0:T(8,128)(2,1)S(1)}, u32[]{:S(2)}, u32[]{:S(2)}) collective-permute-start(bf16[2,64,128]{2,1,0:T(8,128)(2,1)S(1)} %bitcast.129), channel_id=1, source_target_pairs={{0,24},{1,25},{2,26},{3,27},{4,28},{5,29},{6,30},{7,31}} | collective-permute-start | bytes 98312 | tf_op jit(solution)/shard_map/ppermute | solution.py:46
  80.0 12.2 %copy-start.1 = (bf16[2,64,4096]{2,1,0:T(8,128)(2,1)S(1)}, bf16[2,64,4096]{2,1,0:T(8,128)(2,1)}, u32[]{:S(2)}) copy-start(bf16[2,64,4096]{2,1,0:T(8,128)(2,1)} %refs_0_.3) | copy-start | bytes 3145732
  80.0 12.2 %copy-start.2 = (bf16[2,64,4096]{2,1,0:T(8,128)(2,1)S(1)}, bf16[2,64,4096]{2,1,0:T(8,128)(2,1)}, u32[]{:S(2)}) copy-start(bf16[2,64,4096]{2,1,0:T(8,128)(2,1)} %refs_1_.3) | copy-start | bytes 3145732
  80.2 24.1 %collective-permute-start.16 = (bf16[2,64,1024]{2,1,0:T(8,128)(2,1)S(1)}, bf16[2,64,1024]{2,1,0:T(8,128)(2,1)S(1)}, u32[]{:S(2)}, u32[]{:S(2)}) collective-permute-start(bf16[2,64,1024]{2,1,0:T(8,128)(2,1)S(1)} %pad_maximum_fusion.2.refs_12_.refs_16_), channel_id=1, source_target_pairs={{0,8},{8,16},{16,24},{1,9},{9,17},{17,25},{2,10},{10,18},{18,26},{... | collective-permute-start | bytes 786440 | tf_op jit(solution)/shard_map/ppermute | solution.py:46
  85.4 19.0 %collective-permute-start.18 = (bf16[2,64,1024]{2,1,0:T(8,128)(2,1)S(1)}, bf16[2,64,1024]{2,1,0:T(8,128)(2,1)S(1)}, u32[]{:S(2)}, u32[]{:S(2)}) collective-permute-start(bf16[2,64,1024]{2,1,0:T(8,128)(2,1)S(1)} %collective-permute-done.17.refs_14_.refs_18_), channel_id=1, source_target_pairs={{0,8},{8,16},{16,24},{1,9},{9,17},{17,25},{2,10},{10,18},{18,26},{... | collective-permute-start | bytes 786440 | tf_op jit(solution)/shard_map/ppermute | solution.py:46
  104.3 59.1 %collective-permute-start.40 = (bf16[2,16,2560]{2,1,0:T(8,128)(2,1)}, bf16[2,16,2560]{2,1,0:T(8,128)(2,1)S(1)}, u32[]{:S(2)}, u32[]{:S(2)}) collective-permute-start(bf16[2,16,2560]{2,1,0:T(8,128)(2,1)} %dynamic-slice_bitcast_fusion.1), channel_id=1, source_target_pairs={{0,1},{1,0},{2,3},{3,2},{4,5},{5,4},{6,7},{7,6},{8,9},{9,8},{10,11... | collective-permute-start | bytes 491528 | tf_op jit(solution)/shard_map/ppermute | solution.py:51
  115.8 49.9 %collective-permute-start.42 = (bf16[2,16,2560]{2,1,0:T(8,128)(2,1)S(1)}, bf16[2,16,2560]{2,1,0:T(8,128)(2,1)}, u32[]{:S(2)}, u32[]{:S(2)}) collective-permute-start(bf16[2,16,2560]{2,1,0:T(8,128)(2,1)S(1)} %dynamic-slice_bitcast_fusion), channel_id=1, source_target_pairs={{0,1},{1,0},{2,3},{3,2},{4,5},{5,4},{6,7},{7,6},{8,9},{9,8},{10,11... | collective-permute-start | bytes 491528 | tf_op jit(solution)/shard_map/ppermute | solution.py:51
  116.4 6.3 %collective-permute-start.28 = (bf16[2,64,64]{2,1,0:T(8,128)(2,1)S(1)}, bf16[2,64,64]{2,1,0:T(8,128)(2,1)S(1)}, u32[]{:S(2)}, u32[]{:S(2)}) collective-permute-start(bf16[2,64,64]{2,1,0:T(8,128)(2,1)S(1)} %get-tuple-element.61), channel_id=1, source_target_pairs={{8,0},{16,8},{24,16},{9,1},{17,9},{25,17},{10,2},{18,10},{26,18},{... | collective-permute-start | bytes 49160 | tf_op jit(solution)/shard_map/ppermute | solution.py:46
  117.7 7.7 %collective-permute-start.29 = (bf16[2,64,64]{2,1,0:T(8,128)(2,1)S(1)}, bf16[2,64,64]{2,1,0:T(8,128)(2,1)S(1)}, u32[]{:S(2)}, u32[]{:S(2)}) collective-permute-start(bf16[2,64,64]{2,1,0:T(8,128)(2,1)S(1)} %get-tuple-element.63), channel_id=1, source_target_pairs={{16,0},{24,8},{17,1},{25,9},{18,2},{26,10},{19,3},{27,11},{20,4},{... | collective-permute-start | bytes 49160 | tf_op jit(solution)/shard_map/ppermute | solution.py:46
  119.0 9.4 %collective-permute-start.30 = (bf16[2,64,64]{2,1,0:T(8,128)(2,1)S(1)}, bf16[2,64,64]{2,1,0:T(8,128)(2,1)S(1)}, u32[]{:S(2)}, u32[]{:S(2)}) collective-permute-start(bf16[2,64,64]{2,1,0:T(8,128)(2,1)S(1)} %get-tuple-element.62), channel_id=1, source_target_pairs={{24,0},{25,1},{26,2},{27,3},{28,4},{29,5},{30,6},{31,7}} | collective-permute-start | bytes 49160 | tf_op jit(solution)/shard_map/ppermute | solution.py:46
  122.6 24.6 %collective-permute-start.22 = (bf16[2,64,512]{2,1,0:T(8,128)(2,1)S(1)}, bf16[2,64,512]{2,1,0:T(8,128)(2,1)S(1)}, u32[]{:S(2)}, u32[]{:S(2)}) collective-permute-start(bf16[2,64,512]{2,1,0:T(8,128)(2,1)S(1)} %get-tuple-element.29), channel_id=1, source_target_pairs={{8,0},{16,8},{24,16},{9,1},{17,9},{25,17},{10,2},{18,10},{26,18},{... | collective-permute-start | bytes 393224 | tf_op jit(solution)/shard_map/ppermute | solution.py:46
  125.4 23.1 %collective-permute-start.23 = (bf16[2,64,512]{2,1,0:T(8,128)(2,1)S(1)}, bf16[2,64,512]{2,1,0:T(8,128)(2,1)}, u32[]{:S(2)}, u32[]{:S(2)}) collective-permute-start(bf16[2,64,512]{2,1,0:T(8,128)(2,1)S(1)} %get-tuple-element.30), channel_id=1, source_target_pairs={{16,0},{24,8},{17,1},{25,9},{18,2},{26,10},{19,3},{27,11},{20,4},{... | collective-permute-start | bytes 393224 | tf_op jit(solution)/shard_map/ppermute | solution.py:46
  128.3 21.4 %collective-permute-start.24 = (bf16[2,64,512]{2,1,0:T(8,128)(2,1)S(1)}, bf16[2,64,512]{2,1,0:T(8,128)(2,1)}, u32[]{:S(2)}, u32[]{:S(2)}) collective-permute-start(bf16[2,64,512]{2,1,0:T(8,128)(2,1)S(1)} %get-tuple-element.31), channel_id=1, source_target_pairs={{24,0},{25,1},{26,2},{27,3},{28,4},{29,5},{30,6},{31,7}} | collective-permute-start | bytes 393224 | tf_op jit(solution)/shard_map/ppermute | solution.py:46
  133.9 2.8 %copy-start.3 = (bf16[8,2,2,128,128]{3,2,1,0,4:T(2,128)(2,1)S(1)}, bf16[8,2,2,128,128]{3,2,1,0,4:T(2,128)(2,1)}, u32[]{:S(2)}) copy-start(bf16[8,2,2,128,128]{3,2,1,0,4:T(2,128)(2,1)} %reshape_reshape.20) | copy-start | bytes 3145732
  147.2 7.9 %collective-permute-start.25 = (bf16[2,64,512]{2,1,0:T(8,128)(2,1)S(1)}, bf16[2,64,512]{2,1,0:T(8,128)(2,1)S(1)}, u32[]{:S(2)}, u32[]{:S(2)}) collective-permute-start(bf16[2,64,512]{2,1,0:T(8,128)(2,1)S(1)} %get-tuple-element.33), channel_id=1, source_target_pairs={{8,0},{16,8},{24,16},{9,1},{17,9},{25,17},{10,2},{18,10},{26,18},{... | collective-permute-start | bytes 393224 | tf_op jit(solution)/shard_map/ppermute | solution.py:46
  148.5 14.1 %collective-permute-start.26 = (bf16[2,64,512]{2,1,0:T(8,128)(2,1)S(1)}, bf16[2,64,512]{2,1,0:T(8,128)(2,1)S(1)}, u32[]{:S(2)}, u32[]{:S(2)}) collective-permute-start(bf16[2,64,512]{2,1,0:T(8,128)(2,1)S(1)} %get-tuple-element.34), channel_id=1, source_target_pairs={{16,0},{24,8},{17,1},{25,9},{18,2},{26,10},{19,3},{27,11},{20,4},{... | collective-permute-start | bytes 393224 | tf_op jit(solution)/shard_map/ppermute | solution.py:46
  149.8 12.8 %collective-permute-start.27 = (bf16[2,64,512]{2,1,0:T(8,128)(2,1)S(1)}, bf16[2,64,512]{2,1,0:T(8,128)(2,1)S(1)}, u32[]{:S(2)}, u32[]{:S(2)}) collective-permute-start(bf16[2,64,512]{2,1,0:T(8,128)(2,1)S(1)} %get-tuple-element.35), channel_id=1, source_target_pairs={{24,0},{25,1},{26,2},{27,3},{28,4},{29,5},{30,6},{31,7}} | collective-permute-start | bytes 393224 | tf_op jit(solution)/shard_map/ppermute | solution.py:46
  155.1 17.0 %collective-permute-start.31 = (bf16[8,2,128,128]{3,2,1,0:T(8,128)(2,1)}, bf16[8,2,128,128]{3,2,1,0:T(8,128)(2,1)S(1)}, u32[]{:S(2)}, u32[]{:S(2)}) collective-permute-start(bf16[8,2,128,128]{3,2,1,0:T(8,128)(2,1)} %bitcast.142), channel_id=1, source_target_pairs={{0,1},{1,0},{2,3},{3,2},{4,5},{5,4},{6,7},{7,6},{8,9},{9,8},{10,11... | collective-permute-start | bytes 1572872 | tf_op jit(solution)/shard_map/ppermute | solution.py:51
  163.5 4.7 %collective-permute-start.41 = (bf16[1,16,2560]{2,1,0:T(8,128)(2,1)S(1)}, bf16[1,16,2560]{2,1,0:T(8,128)(2,1)S(1)}, u32[]{:S(2)}, u32[]{:S(2)}) collective-permute-start(bf16[1,16,2560]{2,1,0:T(8,128)(2,1)S(1)} %constant_dynamic-slice_fusion.1), channel_id=1, source_target_pairs={{0,2},{1,3},{2,0},{3,1},{4,6},{5,7},{6,4},{7,5},{8,10},{9,11},{10,... | collective-permute-start | bytes 245768 | tf_op jit(solution)/shard_map/ppermute | solution.py:51
  166.7 5.0 %collective-permute-start.43 = (bf16[1,16,2560]{2,1,0:T(8,128)(2,1)S(1)}, bf16[1,16,2560]{2,1,0:T(8,128)(2,1)S(1)}, u32[]{:S(2)}, u32[]{:S(2)}) collective-permute-start(bf16[1,16,2560]{2,1,0:T(8,128)(2,1)S(1)} %constant_dynamic-slice_fusion), channel_id=1, source_target_pairs={{0,2},{1,3},{2,0},{3,1},{4,6},{5,7},{6,4},{7,5},{8,10},{9,11},{10,... | collective-permute-start | bytes 245768 | tf_op jit(solution)/shard_map/ppermute | solution.py:51
  171.7 1.0 copy-start.5
  172.0 4.5 %collective-permute-start.44 = (bf16[4,16,640]{2,1,0:T(8,128)(2,1)S(1)}, bf16[4,16,640]{2,1,0:T(8,128)(2,1)S(1)}, u32[]{:S(2)}, u32[]{:S(2)}) collective-permute-start(bf16[4,16,640]{2,1,0:T(8,128)(2,1)S(1)} %dynamic-slice_bitcast_fusion.3), channel_id=1, source_target_pairs={{0,4},{4,0},{1,5},{5,1},{2,6},{6,2},{3,7},{7,3},{8,12},{12,8},{9,1... | collective-permute-start | bytes 245768 | tf_op jit(solution)/shard_map/ppermute | solution.py:41
  172.9 7.5 %collective-permute-start.32 = (bf16[8,1,128,128]{3,2,1,0:T(8,128)(2,1)S(1)}, bf16[8,1,128,128]{3,2,1,0:T(8,128)(2,1)S(1)}, u32[]{:S(2)}, u32[]{:S(2)}) collective-permute-start(bf16[8,1,128,128]{3,2,1,0:T(8,128)(2,1)S(1)} %constant_dynamic-slice_fusion.2), channel_id=1, source_target_pairs={{0,2},{1,3},{2,0},{3,1},{4,6},{5,7},{6,4},{7,5},{8,10},{9,11},{10,... | collective-permute-start | bytes 786440 | tf_op jit(solution)/shard_map/ppermute | solution.py:51
  176.6 5.6 %collective-permute-start.45 = (bf16[16,640]{1,0:T(8,128)(2,1)S(1)}, bf16[16,640]{1,0:T(8,128)(2,1)S(1)}, u32[]{:S(2)}, u32[]{:S(2)}) collective-permute-start(bf16[16,640]{1,0:T(8,128)(2,1)S(1)} %get-tuple-element.70), channel_id=1, source_target_pairs={{0,8},{8,16},{16,24},{24,0},{1,9},{9,17},{17,25},{25,1},{2,10},{10... | collective-permute-start | bytes 61448 | tf_op jit(solution)/shard_map/ppermute | solution.py:41
  176.6 5.6 %collective-permute-start.46 = (bf16[16,640]{1,0:T(8,128)(2,1)S(1)}, bf16[16,640]{1,0:T(8,128)(2,1)S(1)}, u32[]{:S(2)}, u32[]{:S(2)}) collective-permute-start(bf16[16,640]{1,0:T(8,128)(2,1)S(1)} %get-tuple-element.72), channel_id=1, source_target_pairs={{0,16},{8,24},{16,0},{24,8},{1,17},{9,25},{17,1},{25,9},{2,18},{10... | collective-permute-start | bytes 61448 | tf_op jit(solution)/shard_map/ppermute | solution.py:41
  176.7 6.1 %collective-permute-start.47 = (bf16[16,640]{1,0:T(8,128)(2,1)S(1)}, bf16[16,640]{1,0:T(8,128)(2,1)S(1)}, u32[]{:S(2)}, u32[]{:S(2)}) collective-permute-start(bf16[16,640]{1,0:T(8,128)(2,1)S(1)} %get-tuple-element.71), channel_id=1, source_target_pairs={{0,24},{8,0},{16,8},{24,16},{1,25},{9,1},{17,9},{25,17},{2,26},{10... | collective-permute-start | bytes 61448 | tf_op jit(solution)/shard_map/ppermute | solution.py:41
  180.5 5.0 %collective-permute-start.33 = (bf16[4,128,128]{2,1,0:T(8,128)(2,1)S(1)}, bf16[4,128,128]{2,1,0:T(8,128)(2,1)S(1)}, u32[]{:S(2)}, u32[]{:S(2)}) collective-permute-start(bf16[4,128,128]{2,1,0:T(8,128)(2,1)S(1)} %dynamic-slice_bitcast_fusion.2), channel_id=1, source_target_pairs={{0,4},{4,0},{1,5},{5,1},{2,6},{6,2},{3,7},{7,3},{8,12},{12,8},{9,1... | collective-permute-start | bytes 393224 | tf_op jit(solution)/shard_map/ppermute | solution.py:41
  182.8 5.9 %collective-permute-start.48 = (bf16[16,640]{1,0:T(8,128)(2,1)S(1)}, bf16[16,640]{1,0:T(8,128)(2,1)S(1)}, u32[]{:S(2)}, u32[]{:S(2)}) collective-permute-start(bf16[16,640]{1,0:T(8,128)(2,1)S(1)} %fusion.16), channel_id=1, source_target_pairs={{0,3},{1,2},{2,1},{3,0},{4,7},{5,6},{6,5},{7,4},{8,11},{9,10},{10,... | collective-permute-start | bytes 61448 | tf_op jit(solution)/shard_map/ppermute | solution.py:51
  182.9 7.8 %collective-permute-start.49 = (bf16[16,640]{1,0:T(8,128)(2,1)S(1)}, bf16[16,640]{1,0:T(8,128)(2,1)S(1)}, u32[]{:S(2)}, u32[]{:S(2)}) collective-permute-start(bf16[16,640]{1,0:T(8,128)(2,1)S(1)} %fusion.16), channel_id=1, source_target_pairs={{0,2},{1,3},{2,0},{3,1},{4,6},{5,7},{6,4},{7,5},{8,10},{9,11},{10,... | collective-permute-start | bytes 61448 | tf_op jit(solution)/shard_map/ppermute | solution.py:51
  182.9 7.7 %collective-permute-start.50 = (bf16[16,640]{1,0:T(8,128)(2,1)S(1)}, bf16[16,640]{1,0:T(8,128)(2,1)S(1)}, u32[]{:S(2)}, u32[]{:S(2)}) collective-permute-start(bf16[16,640]{1,0:T(8,128)(2,1)S(1)} %fusion.16), channel_id=1, source_target_pairs={{0,1},{1,0},{2,3},{3,2},{4,5},{5,4},{6,7},{7,6},{8,9},{9,8},{10,11... | collective-permute-start | bytes 61448 | tf_op jit(solution)/shard_map/ppermute | solution.py:51
  185.6 5.9 %collective-permute-start.34 = (bf16[128,128]{1,0:T(8,128)(2,1)S(1)}, bf16[128,128]{1,0:T(8,128)(2,1)S(1)}, u32[]{:S(2)}, u32[]{:S(2)}) collective-permute-start(bf16[128,128]{1,0:T(8,128)(2,1)S(1)} %get-tuple-element.58), channel_id=1, source_target_pairs={{0,8},{8,16},{16,24},{24,0},{1,9},{9,17},{17,25},{25,1},{2,10},{10... | collective-permute-start | bytes 98312 | tf_op jit(solution)/shard_map/ppermute | solution.py:41
  186.8 4.9 %collective-permute-start.35 = (bf16[128,128]{1,0:T(8,128)(2,1)S(1)}, bf16[128,128]{1,0:T(8,128)(2,1)S(1)}, u32[]{:S(2)}, u32[]{:S(2)}) collective-permute-start(bf16[128,128]{1,0:T(8,128)(2,1)S(1)} %get-tuple-element.60), channel_id=1, source_target_pairs={{0,16},{8,24},{16,0},{24,8},{1,17},{9,25},{17,1},{25,9},{2,18},{10... | collective-permute-start | bytes 98312 | tf_op jit(solution)/shard_map/ppermute | solution.py:41
  188.7 3.9 %collective-permute-start.36 = (bf16[128,128]{1,0:T(8,128)(2,1)S(1)}, bf16[128,128]{1,0:T(8,128)(2,1)S(1)}, u32[]{:S(2)}, u32[]{:S(2)}) collective-permute-start(bf16[128,128]{1,0:T(8,128)(2,1)S(1)} %get-tuple-element.59), channel_id=1, source_target_pairs={{0,24},{8,0},{16,8},{24,16},{1,25},{9,1},{17,9},{25,17},{2,26},{10... | collective-permute-start | bytes 98312 | tf_op jit(solution)/shard_map/ppermute | solution.py:41
  192.6 3.4 %collective-permute-start.37 = (bf16[128,128]{1,0:T(8,128)(2,1)S(1)}, bf16[128,128]{1,0:T(8,128)(2,1)S(1)}, u32[]{:S(2)}, u32[]{:S(2)}) collective-permute-start(bf16[128,128]{1,0:T(8,128)(2,1)S(1)} %fusion.13), channel_id=1, source_target_pairs={{0,3},{1,2},{2,1},{3,0},{4,7},{5,6},{6,5},{7,4},{8,11},{9,10},{10,... | collective-permute-start | bytes 98312 | tf_op jit(solution)/shard_map/ppermute | solution.py:51
  192.7 4.0 %collective-permute-start.38 = (bf16[128,128]{1,0:T(8,128)(2,1)S(1)}, bf16[128,128]{1,0:T(8,128)(2,1)S(1)}, u32[]{:S(2)}, u32[]{:S(2)}) collective-permute-start(bf16[128,128]{1,0:T(8,128)(2,1)S(1)} %fusion.13), channel_id=1, source_target_pairs={{0,2},{1,3},{2,0},{3,1},{4,6},{5,7},{6,4},{7,5},{8,10},{9,11},{10,... | collective-permute-start | bytes 98312 | tf_op jit(solution)/shard_map/ppermute | solution.py:51
  193.1 3.6 %collective-permute-start.39 = (bf16[128,128]{1,0:T(8,128)(2,1)S(1)}, bf16[128,128]{1,0:T(8,128)(2,1)S(1)}, u32[]{:S(2)}, u32[]{:S(2)}) collective-permute-start(bf16[128,128]{1,0:T(8,128)(2,1)S(1)} %fusion.13), channel_id=1, source_target_pairs={{0,1},{1,0},{2,3},{3,2},{4,5},{5,4},{6,7},{7,6},{8,9},{9,8},{10,11... | collective-permute-start | bytes 98312 | tf_op jit(solution)/shard_map/ppermute | solution.py:51

commit v2 on v1

v2 whole, which is shorter than its diff:
```python
import functools
import math

import jax
import jax.numpy as jnp
from jax import lax
from jax.experimental import pallas as pl
from jax.experimental.pallas import tpu as pltpu
from jax.sharding import PartitionSpec as P

D = 4096
HEADS = 32
KV_HEADS = 8
HEAD_DIM = 128
RANK = 64
KV = 1024
GROUP = HEADS // KV_HEADS
WIDE = GROUP * HEAD_DIM
ROPE_BASE = 500000.0
HIDDEN_MASK = -1e30
CHUNKS = 2

f32 = jnp.float32
bf16 = jnp.bfloat16


def rotary_tables(row_count, offset):
    half = HEAD_DIM // 2
    position = (jnp.arange(row_count, dtype=jnp.int32) + offset).astype(f32)
    inverse = jnp.exp(jnp.arange(half, dtype=f32) * (-2.0 * math.log(ROPE_BASE) / HEAD_DIM))
    angle = position[:, None] * inverse[None, :]
    cosine, sine = jnp.cos(angle), jnp.sin(angle)
    return (
        jnp.concatenate([cosine, cosine], axis=1),
        jnp.concatenate([-sine, sine], axis=1),
    )


def cyclic(x, axis, shift):
    n = lax.axis_size(axis)
    return lax.ppermute(x, axis, [(i, (i + shift) % n) for i in range(n)])


def along(x, axis, shift):
    n = lax.axis_size(axis)
    return lax.ppermute(x, axis, [(i, i + shift) for i in range(n) if 0 <= i + shift < n])


def partner(x, axis, mask):
    n = lax.axis_size(axis)
    return lax.ppermute(x, axis, [(i, i ^ mask) for i in range(n)])


def mm(a, b, ca, cb):
    return lax.dot_general(a, b, (((ca,), (cb,)), ((), ())), preferred_element_type=f32)


def attention_kernel(shards, earlier_count, place_ref, *refs):
    it = iter(refs)

    def take(n):
        return [next(it) for _ in range(n)]

    q_ref, g_ref, upq_ref, upv_ref, pk_ref, pv_ref, cos_ref, sin_ref = take(8)
    low_refs, k_refs, v_refs = take(shards), take(shards), take(shards)
    before = take(2) if earlier_count else None
    take(earlier_count)
    att_ref, gq_ref, guq_ref, guv_ref = take(4)
    gv_refs = take(shards)
    lgq_ref, lgv_ref = take(2)

    seqs, tokens = q_ref.shape[0], q_ref.shape[1]
    parts, part_rows = guq_ref.shape[1:3]
    span = shards * tokens
    past = pk_ref.shape[1]
    scale = 1.0 / math.sqrt(HEAD_DIM)
    place = place_ref[0]
    cos, sin = cos_ref[...], sin_ref[...]
    upq = jnp.concatenate([upq_ref[h] for h in range(GROUP)], axis=1)
    upv = upv_ref[0]

    @pl.when(pl.program_id(0) == 0)
    def _():
        if before is None:
            lgq_ref[...] = jnp.zeros_like(lgq_ref)
            lgv_ref[...] = jnp.zeros_like(lgv_ref)
        else:
            lgq_ref[...] = before[0][...]
            lgv_ref[...] = before[1][...]

    col = lax.broadcasted_iota(jnp.int32, (tokens, span + past), 1)
    row = lax.broadcasted_iota(jnp.int32, (tokens, span + past), 0)
    seen = (col <= row) | ((col >= tokens) & (col < (place + 1) * tokens)) | (col >= span)
    bias = jnp.where(seen, 0.0, HIDDEN_MASK)
    bias = jnp.concatenate([bias] * GROUP, axis=0)

    def heads(x):
        return jnp.concatenate(
            [x[:, h * HEAD_DIM : (h + 1) * HEAD_DIM] for h in range(GROUP)], axis=0
        )

    def lanes(x):
        return jnp.concatenate([x[h * tokens : (h + 1) * tokens] for h in range(GROUP)], axis=1)

    cos4 = jnp.concatenate([cos] * GROUP, axis=0)
    sin4 = jnp.concatenate([sin] * GROUP, axis=0)
    for s in range(seqs):
        low = low_refs[0][s]
        low_q = low[:, :RANK]
        delta = heads(mm(low_q, upq, 1, 0))
        delta = delta * cos4 + pltpu.roll(delta, HEAD_DIM // 2, 1) * sin4
        q = (heads(q_ref[s]).astype(f32) + delta).astype(bf16)
        g = heads(g_ref[s])
        low_v = jnp.concatenate([r[s][:, RANK:] for r in low_refs], axis=0)
        keys = jnp.concatenate([r[s] for r in k_refs] + [pk_ref[s]], axis=0)
        base = jnp.concatenate([r[s] for r in v_refs], axis=0).astype(f32)
        vals = jnp.concatenate([(base + mm(low_v, upv, 1, 0)).astype(bf16), pv_ref[s]], axis=0)

        scores = mm(q, keys, 1, 1) * scale + bias
        top = jnp.max(scores, axis=-1, keepdims=True)
        e = jnp.exp(scores - top)
        probs = e / jnp.sum(e, axis=-1, keepdims=True)
        weights = probs.astype(bf16)
        out = mm(weights, vals, 1, 0).astype(bf16)
        att_ref[s] = lanes(out)
        prob_grad = mm(g, vals, 1, 1)
        row_delta = jnp.sum(g.astype(f32) * out.astype(f32), axis=-1, keepdims=True)
        score_grad = (probs * (prob_grad - row_delta)).astype(bf16)
        gq = (mm(score_grad, keys, 1, 0) * scale).astype(bf16)
        gq_ref[s] = lanes(gq)
        gq32 = gq.astype(f32)
        back = (gq32 * cos4 - pltpu.roll(gq32, HEAD_DIM // 2, 1) * sin4).astype(bf16)
        back = lanes(back)
        lgq_ref[s] += mm(back, upq, 1, 1)
        gv = mm(weights[:, :span], g, 0, 0).astype(bf16)
        for k in range(shards):
            gv_refs[k][s] = gv[k * tokens : (k + 1) * tokens]
        lgv_ref[s] += mm(gv, upv, 1, 1)
        up_q = mm(low_q, back, 0, 0)
        up_v = mm(low_v, gv, 0, 0)
        grad_up_q = up_q if s == 0 else grad_up_q + up_q
        grad_up_v = up_v if s == 0 else grad_up_v + up_v
    grad_up_q, grad_up_v = grad_up_q.astype(bf16), grad_up_v.astype(bf16)
    for p in range(parts):
        rows = slice(p * part_rows, (p + 1) * part_rows)
        for h in range(GROUP):
            guq_ref[h, p] = grad_up_q[rows, h * HEAD_DIM : (h + 1) * HEAD_DIM]
        guv_ref[0, p] = grad_up_v[rows]


def attention_chunk(
    chunk, groups, place, query_base, grad_out, up_blocks, past, cos, sin, lows, kvs, earlier
):
    shards = len(kvs)
    parts = lax.axis_size("rep")
    seqs, tokens = query_base.shape[:2]
    past_len = past.shape[1]
    first = chunk * groups

    def whole(x):
        return pl.BlockSpec(x.shape, lambda g: (0,) * len(x.shape))

    spec = pl.BlockSpec
    q_spec = spec((seqs, tokens, WIDE), lambda g: (0, 0, first + g))
    gv_spec = spec((seqs, tokens, HEAD_DIM), lambda g: (0, 0, first + g))
    past_block = (seqs, past_len, HEAD_DIM)
    in_specs = [
        spec(memory_space=pltpu.SMEM),
        q_spec,
        q_spec,
        spec((GROUP, RANK, HEAD_DIM), lambda g: (first + g, 0, 0)),
        spec((1, RANK, HEAD_DIM), lambda g: (HEADS + first + g, 0, 0)),
        spec(past_block, lambda g: (0, 0, first + g)),
        spec(past_block, lambda g: (0, 0, KV_HEADS + first + g)),
        whole(cos),
        whole(sin),
    ]
    in_specs += [whole(x) for x in lows]
    in_specs += [spec((seqs, tokens, HEAD_DIM), lambda g: (0, 0, g))] * shards
    in_specs += [spec((seqs, tokens, HEAD_DIM), lambda g: (0, 0, groups + g))] * shards
    operands = [place, query_base, grad_out, up_blocks, up_blocks, past, past, cos, sin]
    operands += list(lows) + list(kvs) + list(kvs)
    shape = jax.ShapeDtypeStruct
    low_q_shape = shape((seqs, tokens, RANK), f32)
    low_v_shape = shape((seqs, shards * tokens, RANK), f32)
    placed_shapes = [
        shape(query_base.shape, bf16),
        shape(query_base.shape, bf16),
        shape((HEADS, parts, RANK // parts, HEAD_DIM), bf16),
        shape((KV_HEADS, parts, RANK // parts, HEAD_DIM), bf16),
    ] + [shape((seqs, tokens, KV), bf16)] * shards
    placed_specs = [
        q_spec,
        q_spec,
        spec((GROUP, parts, RANK // parts, HEAD_DIM), lambda g: (first + g, 0, 0, 0)),
        spec((1, parts, RANK // parts, HEAD_DIM), lambda g: (first + g, 0, 0, 0)),
    ] + [gv_spec] * shards
    aliases = {}
    placed = len(placed_shapes)
    if earlier is not None:
        in_specs += [whole(low_q_shape), whole(low_v_shape)]
        operands += list(earlier[placed:])
        aliases = {len(operands) + i: i for i in range(placed)}
        in_specs += [spec(memory_space=pl.ANY)] * placed
        operands += list(earlier[:placed])
    pairs = seqs * groups * GROUP * tokens * (shards * tokens + past_len)
    return pl.pallas_call(
        functools.partial(attention_kernel, shards, placed if earlier is not None else 0),
        grid=(groups,),
        in_specs=in_specs,
        out_specs=placed_specs + [whole(low_q_shape), whole(low_v_shape)],
        out_shape=placed_shapes + [low_q_shape, low_v_shape],
        input_output_aliases=aliases,
        compiler_params=pltpu.CompilerParams(vmem_limit_bytes=48 * 1024 * 1024),
        cost_estimate=pl.CostEstimate(
            flops=pairs * HEAD_DIM * 28, bytes_accessed=16 * 1024 * 1024, transcendentals=pairs
        ),
        name="attention",
    )(*operands)


def low_rank_kernel(fs, index_ref, own_ref, other_ref, hidden_ref, down_ref, up_ref, low_ref):
    z, x, c = index_ref[0], index_ref[1], index_ref[2]
    pieces = own_ref.shape[0]
    sp = pieces // fs
    down_rows = D // (2 * pieces)
    blocks = up_ref.shape[0] // pieces
    up_rows = RANK // 2
    for r in range(pieces):
        shard = (z ^ (r % sp)) * fs + (x ^ (r // sp))
        for ref, half in ((own_ref, c), (other_ref, 1 - c)):
            at = pl.multiple_of((shard * 2 + half) * down_rows, down_rows)
            down_ref[pl.ds(at, down_rows), :] = ref[r, :down_rows]
            at = pl.multiple_of(half * up_rows, up_rows)
            for j in range(blocks):
                lo = down_rows + j * up_rows
                up_ref[shard * blocks + j, pl.ds(at, up_rows), :] = ref[r, lo : lo + up_rows]
    rows = jnp.concatenate([hidden_ref[s] for s in range(hidden_ref.shape[0])], axis=0)
    low = mm(rows, down_ref[...], 1, 0).astype(bf16)
    for s in range(low_ref.shape[0]):
        low_ref[s] = low[s * low_ref.shape[1] : (s + 1) * low_ref.shape[1]]


def adapters_packed(hidden, adapter_down, adapter_up, own_past):
    sp, fs = lax.axis_size("sp"), lax.axis_size("fsdp")
    z, x, r = (lax.axis_index(a) for a in ("sp", "fsdp", "rep"))
    c = lax.rem(r, 2)
    down_rows, up_rows = adapter_down.shape[0] // 2, RANK // 2
    blocks = adapter_up.shape[1] // HEAD_DIM
    down = lax.dynamic_slice_in_dim(adapter_down, c * down_rows, down_rows, 0)
    up = lax.dynamic_slice_in_dim(adapter_up, c * up_rows, up_rows, 0)
    up = [up[:, j * HEAD_DIM : (j + 1) * HEAD_DIM] for j in range(blocks)]
    rows = down_rows + blocks * up_rows
    buf = jnp.concatenate([down] + up + [own_past.reshape(-1, 2 * RANK)], axis=0)[None]
    step = 1
    while step < sp:
        buf = jnp.concatenate([buf, partner(buf, "sp", step)], axis=0)
        step *= 2
    seqs, each = own_past.shape[:2]
    past = buf[:, rows:].reshape(sp, seqs, each, -1).swapaxes(0, 1).reshape(seqs, sp * each, -1)
    buf = buf[:, :rows]
    step = 1
    while step < fs:
        buf = jnp.concatenate([buf, partner(buf, "fsdp", step)], axis=0)
        step *= 2
    other = partner(buf, "rep", 1)
    index = jnp.stack([z, x, c]).astype(jnp.int32)
    vmem = pl.BlockSpec(memory_space=pltpu.VMEM)
    seqs, tokens = hidden.shape[:2]
    down_full, up_blocks, low = pl.pallas_call(
        functools.partial(low_rank_kernel, fs),
        in_specs=[pl.BlockSpec(memory_space=pltpu.SMEM)] + [vmem] * 3,
        out_specs=[vmem] * 3,
        out_shape=[
            jax.ShapeDtypeStruct((D, 2 * RANK), bf16),
            jax.ShapeDtypeStruct((HEADS + KV_HEADS, RANK, HEAD_DIM), bf16),
            jax.ShapeDtypeStruct((seqs, tokens, 2 * RANK), bf16),
        ],
        compiler_params=pltpu.CompilerParams(vmem_limit_bytes=32 * 1024 * 1024),
        cost_estimate=pl.CostEstimate(
            flops=2 * seqs * tokens * D * 2 * RANK, bytes_accessed=5 * 2**20, transcendentals=0
        ),
        name="low_rank",
    )(index, buf, other, hidden)
    return down_full, up_blocks, low, past


def adapters_plain(hidden, adapter_down, adapter_up, own_past):
    sp = lax.axis_size("sp")
    seqs, tokens = hidden.shape[:2]
    past = jnp.concatenate([own_past] + [cyclic(own_past, "sp", k) for k in range(1, sp)], axis=1)
    down_full = lax.all_gather(adapter_down, ("sp", "fsdp"), axis=0, tiled=True)
    up_full = lax.all_gather(adapter_up, ("sp", "fsdp"), axis=1, tiled=True)
    rows = hidden.reshape(seqs * tokens, D)
    low = jnp.dot(rows, down_full, preferred_element_type=f32).astype(bf16)
    up_blocks = up_full.reshape(RANK, HEADS + KV_HEADS, HEAD_DIM).swapaxes(0, 1)
    return down_full, up_blocks, low.reshape(seqs, tokens, 2 * RANK), past


def grad_hidden_kernel(low_ref, down_ref, out_ref):
    out = mm(low_ref[...], down_ref[...], 1, 1).astype(bf16)
    tokens = out_ref.shape[1]
    for s in range(out_ref.shape[0]):
        out_ref[s] = out[s * tokens : (s + 1) * tokens]


def grad_hidden_of(low_grad, down_full, seqs, tokens):
    columns = 1024
    return pl.pallas_call(
        grad_hidden_kernel,
        grid=(D // columns,),
        in_specs=[
            pl.BlockSpec(low_grad.shape, lambda i: (0, 0)),
            pl.BlockSpec((columns, 2 * RANK), lambda i: (i, 0)),
        ],
        out_specs=pl.BlockSpec((seqs, tokens, columns), lambda i: (0, 0, i)),
        out_shape=jax.ShapeDtypeStruct((seqs, tokens, D), bf16),
        compiler_params=pltpu.CompilerParams(vmem_limit_bytes=32 * 1024 * 1024),
        cost_estimate=pl.CostEstimate(
            flops=2 * seqs * tokens * D * 2 * RANK, bytes_accessed=2**21, transcendentals=0
        ),
        name="grad_hidden",
    )(low_grad, down_full)


def adapter_grads_kernel(core_ref, hidden_ref, low_ref, guq_ref, guv_ref, send_ref, keep_ref, gd_ref):
    c = core_ref[0]
    shards, pairs = send_ref.shape[:2]
    down_rows = gd_ref.shape[1]
    columns = 2 * pairs * down_rows
    blocks = (HEADS + KV_HEADS) // shards
    up_rows = guq_ref.shape[2]
    low = low_ref[...]
    for b in range(shards):
        cols = [hidden_ref[s, :, b * columns : (b + 1) * columns] for s in range(hidden_ref.shape[0])]
        part = mm(jnp.concatenate(cols, axis=0), low, 0, 0).astype(bf16)
        for q in range(2 * pairs):
            gd_ref[q] = part[q * down_rows : (q + 1) * down_rows]
        for hi in range(pairs):
            for ref, q in ((send_ref, 2 * hi + 1 - c), (keep_ref, 2 * hi + c)):
                ref[b, hi, :down_rows] = gd_ref[q]
                for j in range(blocks):
                    block = b * blocks + j
                    src = guq_ref[block, q] if block < HEADS else guv_ref[block - HEADS, q]
                    lo = down_rows + j * up_rows
                    ref[b, hi, lo : lo + up_rows] = src


def packed_grads(hidden, low_grad, guq, guv, shards):
    rp, r = lax.axis_size("rep"), lax.axis_index("rep")
    c = lax.rem(r, 2)
    down_rows, up_rows = D // (shards * rp), RANK // rp
    up_width = (D + KV) // shards
    rows = down_rows + up_rows * up_width // (2 * RANK)
    if up_width % HEAD_DIM == 0:
        vmem = pl.BlockSpec(memory_space=pltpu.VMEM)
        packed = jax.ShapeDtypeStruct((shards, rp // 2, rows, 2 * RANK), bf16)
        return pl.pallas_call(
            adapter_grads_kernel,
            in_specs=[pl.BlockSpec(memory_space=pltpu.SMEM)] + [vmem] * 4,
            out_specs=[vmem] * 2,
            out_shape=[packed] * 2,
            scratch_shapes=[pltpu.VMEM((rp, down_rows, 2 * RANK), bf16)],
            compiler_params=pltpu.CompilerParams(vmem_limit_bytes=32 * 1024 * 1024),
            cost_estimate=pl.CostEstimate(
                flops=2 * hidden.size * 2 * RANK, bytes_accessed=5 * 2**20, transcendentals=0
            ),
            name="adapter_grads",
        )(c.astype(jnp.int32).reshape(1), hidden, low_grad, guq, guv)
    own_rows = hidden.reshape(-1, D)
    down = jnp.dot(own_rows.T, low_grad, preferred_element_type=f32).astype(bf16)
    down = down.reshape(shards, rp, down_rows, 2 * RANK)
    up = jnp.concatenate([guq, guv], axis=0).transpose(1, 2, 0, 3)
    up = up.reshape(rp, up_rows, shards, up_width).transpose(2, 0, 1, 3)
    up = up.reshape(shards, rp, -1, 2 * RANK)
    both = jnp.concatenate([down, up], axis=2).reshape(shards, rp // 2, 2, rows, 2 * RANK)
    send = lax.dynamic_index_in_dim(both, 1 - c, 2, keepdims=False)
    keep = lax.dynamic_index_in_dim(both, c, 2, keepdims=False)
    return send, keep


def finish_grads(send, keep):
    sp, fs, rp = (lax.axis_size(a) for a in ("sp", "fsdp", "rep"))
    z, x, r = (lax.axis_index(a) for a in ("sp", "fsdp", "rep"))
    shards, _, rows, lanes = send.shape
    got = partner(send, "rep", 1)
    for b in range(1, rp.bit_length() - 1):
        shape = (shards, rp >> (b + 1), 2, rows, lanes)
        mine = lax.rem(lax.div(r, 1 << b), 2)

        def half(i):
            return sum(
                lax.dynamic_index_in_dim(a.reshape(shape), i, 2, keepdims=False).astype(f32)
                for a in (keep, got)
            ).astype(bf16)

        send, keep = half(1 - mine), half(mine)
        got = partner(send, "rep", 1 << b)
    shape = (sp, fs, rows, lanes)

    def over_fsdp(i):
        return sum(
            lax.dynamic_index_in_dim(a.reshape(shape), i, 1, keepdims=False).astype(f32)
            for a in (keep, got)
        ).astype(bf16)

    total = over_fsdp(x).astype(f32)
    for k in range(1, fs):
        total = total + cyclic(over_fsdp(lax.rem(x + k, fs)), "fsdp", k).astype(f32)
    over_sp = total.astype(bf16)
    total = lax.dynamic_index_in_dim(over_sp, z, 0, keepdims=False).astype(f32)
    for k in range(1, sp):
        send = lax.dynamic_index_in_dim(over_sp, lax.rem(z + k, sp), 0, keepdims=False)
        total = total + cyclic(send, "sp", k).astype(f32)
    own = total.astype(bf16)
    parts = [own] + [partner(own, "rep", m) for m in range(1, rp)]
    ordered = []
    for q in range(rp):
        pick = parts[0]
        for m in range(1, rp):
            pick = jnp.where((r ^ m) == q, parts[m], pick)
        ordered.append(pick.astype(f32))
    down_rows, up_rows = D // (shards * rp), RANK // rp
    up_width = (D + KV) // shards
    grad_down = jnp.concatenate([p[:down_rows] for p in ordered], axis=0)
    ups = []
    for p in ordered:
        up = p[down_rows:]
        if up_width % HEAD_DIM == 0:
            up = [up[lo : lo + up_rows] for lo in range(0, up.shape[0], up_rows)]
            up = jnp.concatenate(up, axis=1)
        ups.append(up.reshape(up_rows, up_width))
    return grad_down, jnp.concatenate(ups, axis=0)


def body(
    hidden,
    query_base,
    key_span,
    value_base,
    past_keys,
    past_values,
    grad_out,
    adapter_down,
    adapter_up,
):
    sp, fs = lax.axis_size("sp"), lax.axis_size("fsdp")
    z = lax.axis_index("sp")
    seqs, tokens = hidden.shape[:2]
    past_len = past_keys.shape[1] * sp
    groups = KV_HEADS // CHUNKS
    width = groups * HEAD_DIM

    own_past = jnp.concatenate([past_keys, past_values], axis=2)
    even = adapter_up.shape[1] % HEAD_DIM == 0
    adapters = adapters_packed if even else adapters_plain
    down_full, up_blocks, low_own, past = adapters(hidden, adapter_down, adapter_up, own_past)

    chunk_kvs = []
    for c in range(CHUNKS):
        cols = slice(c * width, (c + 1) * width)
        kvs = [jnp.concatenate([key_span[:, :, cols], value_base[:, :, cols]], axis=2)]
        for k in range(1, sp):
            kvs.append(along(kvs[k - 1], "sp", 1))
        chunk_kvs.append(kvs)

    lows = [low_own] + [along(low_own, "sp", k) for k in range(1, sp)]
    cos, sin = rotary_tables(tokens, past_len + z * tokens)
    place = z.astype(jnp.int32).reshape(1)

    made = None
    for c in range(CHUNKS):
        made = attention_chunk(
            c, groups, place, query_base, grad_out, up_blocks, past, cos, sin,
            lows, chunk_kvs[c], made,
        )
    attended, grad_query, guq, guv = made[:4]
    gvs = made[4 : 4 + sp]
    low_grad_q, low_grad_v = made[4 + sp :]

    low_v_total = low_grad_v[:, :tokens]
    for k in range(1, sp):
        part = low_grad_v[:, k * tokens : (k + 1) * tokens].astype(bf16)
        low_v_total = low_v_total + along(part, "sp", -k).astype(f32)
    low_grad = (
        jnp.concatenate([low_grad_q, low_v_total], axis=2)
        .astype(bf16)
        .reshape(seqs * tokens, 2 * RANK)
    )
    send, keep = packed_grads(hidden, low_grad, guq, guv, sp * fs)
    grad_down, grad_up = finish_grads(send, keep)
    grad_hidden = grad_hidden_of(low_grad, down_full, seqs, tokens)

    grad_value = gvs[0].astype(f32)
    for k in range(1, sp):
        grad_value = grad_value + along(gvs[k], "sp", -k).astype(f32)
    return (
        attended,
        grad_query,
        grad_value.astype(bf16),
        grad_hidden,
        grad_down,
        grad_up,
    )


def solution(mesh):
    rows = P(("fsdp", "rep"), "sp", None)
    down, up = P(("sp", "fsdp"), None), P(None, ("sp", "fsdp"))
    return jax.shard_map(
        body,
        mesh=mesh,
        in_specs=(rows,) * 7 + (down, up),
        out_specs=(rows,) * 4 + (down, up),
        check_vma=False,
    )
```

time: 198 us -> 176 us (0.89)
  starting transfers between devices: 83.4 us -> 56.8 us
  waiting for transfers between devices: 58.3 us -> 75.9 us
  local copies, waits for them, and re-layouts: 19.9 us -> 7.84 us
  Pallas kernels: 22.9 us -> 28.5 us
  matrix products: 4.7 us -> 0 us
    ppermute x14 -> x9, waiting for transfers between devices: 6.34 us -> 37.7 us  [partner(): return lax.ppermute(x, axis, [(i, i ^ mask) for i in range(n)])]
    ppermute x19 -> x4, waiting for transfers between devices: 36 us -> 4.98 us  [cyclic(): return lax.ppermute(x, axis, [(i, (i + shift) % n) for i in range(n)])]
    ppermute x19 -> x4, starting transfers between devices: 34.5 us -> 5.43 us  [cyclic(): return lax.ppermute(x, axis, [(i, (i + shift) % n) for i in range(n)])]
    ppermute x18 -> x15, waiting for transfers between devices: 16 us -> 33.2 us  [along(): lax.ppermute(x, axis, [(i, i + shift) for i in range(n) if 0 <= i + shift...]
    pallas_call x2 -> x5, Pallas kernels: 22.9 us -> 28.5 us  [the longest x2 24 us: attention_chunk(): pl.pallas_call(functools.partial(attention_kernel, shards, placed if earl...]
    dynamic_slice x3 -> x0, local copies, waits for them, and re-layouts: 5.11 us -> none  [the longest x1 3.48 us: halve_over_rep(): keep = lax.dynamic_index_in_dim(x, mine, at + 1, keepdims=False)]
    dot_general x3 -> x0, matrix products: 4.7 us -> none  [the longest x1 2.76 us: body(): jnp.dot(low_grad, down_full.T, preferred_element_type=f32).astype(bf16)]
    ppermute x14 -> x9, starting transfers between devices: 7.35 us -> 10.7 us  [partner(): return lax.ppermute(x, axis, [(i, i ^ mask) for i in range(n)])]
  transfers between devices with their start and end apart: 51 -> 28, of which waited for: 23 -> 17; matrix products, arithmetic and copies ran while one was open for 14% -> 1% of each run, Pallas kernels for 12% -> 9%
where the time goes in v2:
time: 176 us
  waiting for transfers between devices  75.9 us (43%)
  starting transfers between devices  56.8 us (32%)
  Pallas kernels  28.5 us (16%)
  local copies, waits for them, and re-layouts  7.84 us (4%)
  other arithmetic  5.22 us (3%)
    ppermute x15, starting transfers between devices, along(): lax.ppermute(x, axis, [(i, i + shift) for i in range(n) if 0 <= i + shift...  40.7 us
    ppermute x9, waiting for transfers between devices, partner(): return lax.ppermute(x, axis, [(i, i ^ mask) for i in range(n)])  37.7 us
    ppermute x15, waiting for transfers between devices, along(): lax.ppermute(x, axis, [(i, i + shift) for i in range(n) if 0 <= i + shift...  33.2 us
    pallas_call x2, Pallas kernels, attention_chunk(): pl.pallas_call(functools.partial(attention_kernel, shards, placed if earl...  24 us
    ppermute x9, starting transfers between devices, partner(): return lax.ppermute(x, axis, [(i, i ^ mask) for i in range(n)])  10.7 us
    unnamed x74, local copies, waits for them, and re-layouts  7.54 us
    ppermute x4, starting transfers between devices, cyclic(): return lax.ppermute(x, axis, [(i, (i + shift) % n) for i in range(n)])  5.43 us
    ppermute x4, waiting for transfers between devices, cyclic(): return lax.ppermute(x, axis, [(i, (i + shift) % n) for i in range(n)])  4.98 us
  transfers between devices with their start and end apart: 28, of which 17 were waited for; matrix products, arithmetic and copies ran while one was open for 1% of the time, Pallas kernels for 9%

profile of v2, /device:TPU:0, one launch (start us, length us, event | category | flops | bytes accessed | tf_op | source)
XLA Modules:
  0.0 175.7 jit_solution(17758019781991748213)
XLA Ops:
  0.7 0.8 pad_maximum_fusion.8
  1.5 0.8 copy-done.25
  2.5 3.1 %collective-permute-start = (bf16[1,544,128]{2,1,0:T(8,128)(2,1)S(1)}, bf16[1,544,128]{2,1,0:T(8,128)(2,1)S(1)}, u32[]{:S(2)}, u32[]{:S(2)}) collective-permute-start(bf16[1,544,128]{2,1,0:T(8,128)(2,1)S(1)} %bitcast.37), channel_id=1, source_target_pairs={{0,8},{8,0},{16,24},{24,16},{1,9},{9,1},{17,25},{25,17},{2,10},{10... | collective-permute-start | bytes 417800 | tf_op jit(solution)/shard_map/ppermute | solution.py:51
  5.6 3.7 %collective-permute-done = bf16[1,544,128]{2,1,0:T(8,128)(2,1)S(1)} collective-permute-done((bf16[1,544,128]{2,1,0:T(8,128)(2,1)S(1)}, bf16[1,544,128]{2,1,0:T(8,128)(2,1)S(1)}, u32[]{:S(2)}, u32[]{:S(2)}) %collective-permute-start) | collective-permute-done | bytes 139296 | tf_op jit(solution)/shard_map/ppermute | solution.py:51
  9.3 2.8 %collective-permute-start.1 = (bf16[2,544,128]{2,1,0:T(8,128)(2,1)S(1)}, bf16[2,544,128]{2,1,0:T(8,128)(2,1)S(1)}, u32[]{:S(2)}, u32[]{:S(2)}) collective-permute-start(bf16[2,544,128]{2,1,0:T(8,128)(2,1)S(1)} %pad_maximum_fusion.2), channel_id=1, source_target_pairs={{0,16},{8,24},{16,0},{24,8},{1,17},{9,25},{17,1},{25,9},{2,18},{10... | collective-permute-start | bytes 835592 | tf_op jit(solution)/shard_map/ppermute | solution.py:51
  12.1 12.0 %collective-permute-done.1 = bf16[2,544,128]{2,1,0:T(8,128)(2,1)S(1)} collective-permute-done((bf16[2,544,128]{2,1,0:T(8,128)(2,1)S(1)}, bf16[2,544,128]{2,1,0:T(8,128)(2,1)S(1)}, u32[]{:S(2)}, u32[]{:S(2)}) %collective-permute-start.1) | collective-permute-done | bytes 278560 | tf_op jit(solution)/shard_map/ppermute | solution.py:51
  24.1 0.6 copy-done.19
  24.8 1.4 collective-permute-start.2
  26.3 9.4 %collective-permute-done.2 = bf16[4,416,128]{2,1,0:T(8,128)(2,1)S(1)} collective-permute-done((bf16[4,416,128]{2,1,0:T(8,128)(2,1)S(1)}, bf16[4,416,128]{2,1,0:T(8,128)(2,1)S(1)}, u32[]{:S(2)}, u32[]{:S(2)}) %collective-permute-start.2) | collective-permute-done | bytes 426016 | tf_op jit(solution)/shard_map/ppermute | solution.py:51
  35.7 0.1 pad_maximum_fusion.own_ref
  35.9 3.5 %collective-permute-start.10 = (bf16[2,64,1024]{2,1,0:T(8,128)(2,1)S(1)}, bf16[2,64,1024]{2,1,0:T(8,128)(2,1)S(1)}, u32[]{:S(2)}, u32[]{:S(2)}) collective-permute-start(bf16[2,64,1024]{2,1,0:T(8,128)(2,1)S(1)} %pad_maximum_fusion.4.refs_12_.refs_16_), channel_id=1, source_target_pairs={{0,8},{8,16},{16,24},{1,9},{9,17},{17,25},{2,10},{10,18},{18,26},{... | collective-permute-start | bytes 786440 | tf_op jit(solution)/shard_map/ppermute | solution.py:46
  39.5 1.9 %collective-permute-start.7 = (bf16[2,64,1024]{2,1,0:T(8,128)(2,1)S(1)}, bf16[2,64,1024]{2,1,0:T(8,128)(2,1)S(1)}, u32[]{:S(2)}, u32[]{:S(2)}) collective-permute-start(bf16[2,64,1024]{2,1,0:T(8,128)(2,1)S(1)} %pad_maximum_fusion.3.refs_12_.refs_16_), channel_id=1, source_target_pairs={{0,8},{8,16},{16,24},{1,9},{9,17},{17,25},{2,10},{10,18},{18,26},{... | collective-permute-start | bytes 786440 | tf_op jit(solution)/shard_map/ppermute | solution.py:46
  41.4 4.6 %collective-permute-done.10.refs_13_.refs_17_ = bf16[2,64,1024]{2,1,0:T(8,128)(2,1)S(1)} collective-permute-done((bf16[2,64,1024]{2,1,0:T(8,128)(2,1)S(1)}, bf16[2,64,1024]{2,1,0:T(8,128)(2,1)S(1)}, u32[]{:S(2)}, u32[]{:S(2)}) %collective-permute-start.10) | collective-permute-done | bytes 262176 | tf_op jit(solution)/shard_map/ppermute | solution.py:46
  46.0 5.1 %collective-permute-start.11 = (bf16[2,64,1024]{2,1,0:T(8,128)(2,1)S(1)}, bf16[2,64,1024]{2,1,0:T(8,128)(2,1)}, u32[]{:S(2)}, u32[]{:S(2)}) collective-permute-start(bf16[2,64,1024]{2,1,0:T(8,128)(2,1)S(1)} %collective-permute-done.10.refs_13_.refs_17_), channel_id=1, source_target_pairs={{0,8},{8,16},{16,24},{1,9},{9,17},{17,25},{2,10},{10,18},{18,26},{... | collective-permute-start | bytes 786440 | tf_op jit(solution)/shard_map/ppermute | solution.py:46
  51.1 0.5 collective-permute-done.7.refs_13_.refs_17_
  51.6 4.4 %collective-permute-start.8 = (bf16[2,64,1024]{2,1,0:T(8,128)(2,1)S(1)}, bf16[2,64,1024]{2,1,0:T(8,128)(2,1)S(1)}, u32[]{:S(2)}, u32[]{:S(2)}) collective-permute-start(bf16[2,64,1024]{2,1,0:T(8,128)(2,1)S(1)} %collective-permute-done.7.refs_13_.refs_17_), channel_id=1, source_target_pairs={{0,8},{8,16},{16,24},{1,9},{9,17},{17,25},{2,10},{10,18},{18,26},{... | collective-permute-start | bytes 786440 | tf_op jit(solution)/shard_map/ppermute | solution.py:46
  56.0 0.2 fusion.6
  56.2 1.0 collective-permute-done.11.refs_14_.refs_18_
  57.3 5.2 %collective-permute-start.12 = (bf16[2,64,1024]{2,1,0:T(8,128)(2,1)}, bf16[2,64,1024]{2,1,0:T(8,128)(2,1)}, u32[]{:S(2)}, u32[]{:S(2)}) collective-permute-start(bf16[2,64,1024]{2,1,0:T(8,128)(2,1)} %collective-permute-done.11.refs_14_.refs_18_), channel_id=1, source_target_pairs={{0,8},{8,16},{16,24},{1,9},{9,17},{17,25},{2,10},{10,18},{18,26},{... | collective-permute-start | bytes 786440 | tf_op jit(solution)/shard_map/ppermute | solution.py:46
  62.4 0.1 pad_add_fusion.index_ref
  62.5 0.1 pad_maximum_fusion.9
  62.6 0.2 collective-permute-done.8.refs_14_.refs_18_
  62.9 5.1 %collective-permute-start.9 = (bf16[2,64,1024]{2,1,0:T(8,128)(2,1)S(1)}, bf16[2,64,1024]{2,1,0:T(8,128)(2,1)}, u32[]{:S(2)}, u32[]{:S(2)}) collective-permute-start(bf16[2,64,1024]{2,1,0:T(8,128)(2,1)S(1)} %collective-permute-done.8.refs_14_.refs_18_), channel_id=1, source_target_pairs={{0,8},{8,16},{16,24},{1,9},{9,17},{17,25},{2,10},{10,18},{18,26},{... | collective-permute-start | bytes 786440 | tf_op jit(solution)/shard_map/ppermute | solution.py:46
  68.0 1.7 low_rank.1
  69.7 1.0 copy-done.3
  70.7 2.7 %collective-permute-start.4 = (bf16[2,64,128]{2,1,0:T(8,128)(2,1)S(1)}, bf16[2,64,128]{2,1,0:T(8,128)(2,1)S(1)}, u32[]{:S(2)}, u32[]{:S(2)}) collective-permute-start(bf16[2,64,128]{2,1,0:T(8,128)(2,1)S(1)} %get-tuple-element.32.refs_8_), channel_id=1, source_target_pairs={{0,8},{8,16},{16,24},{1,9},{9,17},{17,25},{2,10},{10,18},{18,26},{... | collective-permute-start | bytes 98312 | tf_op jit(solution)/shard_map/ppermute | solution.py:46
  73.4 3.8 %collective-permute-start.5 = (bf16[2,64,128]{2,1,0:T(8,128)(2,1)S(1)}, bf16[2,64,128]{2,1,0:T(8,128)(2,1)S(1)}, u32[]{:S(2)}, u32[]{:S(2)}) collective-permute-start(bf16[2,64,128]{2,1,0:T(8,128)(2,1)S(1)} %get-tuple-element.32.refs_8_), channel_id=1, source_target_pairs={{0,16},{8,24},{1,17},{9,25},{2,18},{10,26},{3,19},{11,27},{4,20},{... | collective-permute-start | bytes 98312 | tf_op jit(solution)/shard_map/ppermute | solution.py:46
  77.2 1.3 collective-permute-start.6
  78.8 1.3 collective-permute-done.6.refs_11_
  80.1 1.2 copy-done.1
  81.3 1.2 copy-done.2
  82.5 0.9 copy-done.14
  83.5 11.8 %attention.2 = (bf16[2,64,4096]{2,1,0:T(8,128)(2,1)}, bf16[2,64,4096]{2,1,0:T(8,128)(2,1)}, bf16[32,4,16,128]{3,2,1,0:T(8,128)(2,1)S(1)}, bf16[8,4,16,128]{3,2,1...) custom-call(s32[1]{0:T(128)} %bitcast.place_ref, ...), custom_call_target="tpu_custom_call" | custom-call | flops 1996488704 | bytes 16777216 | tf_op jit(solution)/shard_map/attention/pallas_call | solution.py:207
  95.3 12.2 %attention.3 = (bf16[2,64,4096]{2,1,0:T(8,128)(2,1)}, bf16[2,64,4096]{2,1,0:T(8,128)(2,1)}, bf16[32,4,16,128]{3,2,1,0:T(8,128)(2,1)S(1)}, bf16[8,4,16,128]{3,2,1...) custom-call(s32[1]{0:T(128)} %bitcast.place_ref, ...), custom_call_target="tpu_custom_call", output_to_operand_aliasing={{0}: (23, {}), {1}: (24, {}), {2}: (25, {}), {3}: (26, {}),... | custom-call | flops 1996488704 | bytes 16777216 | tf_op jit(solution)/shard_map/attention/pallas_call | solution.py:207
  107.5 0.7 copy-done.9
  108.2 0.7 copy-done.5
  108.9 0.1 copy-done.7
  108.9 1.3 collective-permute-start.16
  110.2 1.3 collective-permute-start.17
  111.5 1.3 collective-permute-start.18
  112.8 1.9 %collective-permute-done.16 = bf16[2,64,64]{2,1,0:T(8,128)(2,1)S(1)} collective-permute-done((bf16[2,64,64]{2,1,0:T(8,128)(2,1)S(1)}, bf16[2,64,64]{2,1,0:T(8,128)(2,1)S(1)}, u32[]{:S(2)}, u32[]{:S(2)}) %collective-permute-start.16) | collective-permute-done | bytes 16416 | tf_op jit(solution)/shard_map/ppermute | solution.py:46
  114.7 2.5 %collective-permute-done.17 = bf16[2,64,64]{2,1,0:T(8,128)(2,1)S(1)} collective-permute-done((bf16[2,64,64]{2,1,0:T(8,128)(2,1)S(1)}, bf16[2,64,64]{2,1,0:T(8,128)(2,1)S(1)}, u32[]{:S(2)}, u32[]{:S(2)}) %collective-permute-start.17) | collective-permute-done | bytes 16416 | tf_op jit(solution)/shard_map/ppermute | solution.py:46
  117.3 3.0 %collective-permute-done.18 = bf16[2,64,64]{2,1,0:T(8,128)(2,1)S(1)} collective-permute-done((bf16[2,64,64]{2,1,0:T(8,128)(2,1)S(1)}, bf16[2,64,64]{2,1,0:T(8,128)(2,1)S(1)}, u32[]{:S(2)}, u32[]{:S(2)}) %collective-permute-start.18) | collective-permute-done | bytes 16416 | tf_op jit(solution)/shard_map/ppermute | solution.py:46
  120.3 0.1 pad_maximum_fusion.11.low_ref
  120.4 0.7 adapter_grads.1
  121.2 2.3 %collective-permute-done.19 = bf16[8,2,208,128]{3,2,1,0:T(8,128)(2,1)S(1)} collective-permute-done((bf16[8,2,208,128]{3,2,1,0:T(8,128)(2,1)S(1)}, bf16[8,2,208,128]{3,2,1,0:T(8,128)(2,1)S(1)}, u32[]{:S(2)}, u32[]{:S(2)}) %collective-permute-start.19) | collective-permute-done | bytes 852000 | tf_op jit(solution)/shard_map/ppermute | solution.py:51
  123.6 0.2 add_convert_fusion.1
  123.8 1.6 collective-permute-start.20
  125.4 10.3 %collective-permute-done.20 = bf16[8,1,208,128]{3,2,1,0:T(8,128)(2,1)S(1)} collective-permute-done((bf16[8,1,208,128]{3,2,1,0:T(8,128)(2,1)S(1)}, bf16[8,1,208,128]{3,2,1,0:T(8,128)(2,1)S(1)}, u32[]{:S(2)}, u32[]{:S(2)}) %collective-permute-start.20) | collective-permute-done | bytes 426016 | tf_op jit(solution)/shard_map/ppermute | solution.py:51
  135.8 1.6 collective-permute-start.21
  137.3 5.0 %collective-permute-done.21 = bf16[4,208,128]{2,1,0:T(8,128)(2,1)S(1)} collective-permute-done((bf16[4,208,128]{2,1,0:T(8,128)(2,1)S(1)}, bf16[4,208,128]{2,1,0:T(8,128)(2,1)S(1)}, u32[]{:S(2)}, u32[]{:S(2)}) %collective-permute-start.21) | collective-permute-done | bytes 213024 | tf_op jit(solution)/shard_map/ppermute | solution.py:41
  142.3 1.1 fusion
  143.5 0.3 collective-permute-start.23
  143.8 3.6 %collective-permute-start.24 = (bf16[208,128]{1,0:T(8,128)(2,1)S(1)}, bf16[208,128]{1,0:T(8,128)(2,1)S(1)}, u32[]{:S(2)}, u32[]{:S(2)}) collective-permute-start(bf16[208,128]{1,0:T(8,128)(2,1)S(1)} %get-tuple-element.67), channel_id=1, source_target_pairs={{0,24},{8,0},{16,8},{24,16},{1,25},{9,1},{17,9},{25,17},{2,26},{10... | collective-permute-start | bytes 159752 | tf_op jit(solution)/shard_map/ppermute | solution.py:41
  147.3 1.3 collective-permute-start.13
  148.6 1.3 collective-permute-start.14
  149.9 1.3 collective-permute-start.15
  151.3 2.1 %grad_hidden.1 = bf16[2,64,4096]{2,1,0:T(8,128)(2,1)} custom-call(bf16[128,128]{1,0:T(8,128)(2,1)S(1)} %pad_maximum_fusion.11.low_ref, bf16[4096,128]{1,0:T(8,128)(2,1)S(1)} %copy-done.4), custom_call_target="tpu_custom_call" | custom-call | flops 134217728 | bytes 2097152 | tf_op jit(solution)/shard_map/grad_hidden/pallas_call | solution.py:309
  153.6 1.6 collective-permute-start.26
  155.1 0.8 collective-permute-done.13
  155.9 17.1 %collective-permute-done.14 = bf16[2,64,1024]{2,1,0:T(8,128)(2,1)S(1)} collective-permute-done((bf16[2,64,1024]{2,1,0:T(8,128)(2,1)S(1)}, bf16[2,64,1024]{2,1,0:T(8,128)(2,1)S(1)}, u32[]{:S(2)}, u32[]{:S(2)}) %collective-permute-start.14) | collective-permute-done | bytes 262176 | tf_op jit(solution)/shard_map/ppermute | solution.py:46
  173.1 0.9 add_convert_fusion.2
  174.3 0.7 pad_maximum_fusion.6
  175.0 0.7 pad_maximum_fusion.5
  (112 shorter events, 1.3 us)
Async XLA Ops:
  0.6 0.9 copy-start.24
  1.5 0.9 copy-start.25
  2.5 21.6 %copy-start.15 = (bf16[544,128]{1,0:T(8,128)(2,1)}, bf16[544,128]{1,0:T(8,128)(2,1)S(1)}, u32[]{:S(2)}) copy-start(bf16[544,128]{1,0:T(8,128)(2,1)S(1)} %constant_dynamic-update-slice_fusion) | copy-start | bytes 417796
  2.5 6.8 %collective-permute-start = (bf16[1,544,128]{2,1,0:T(8,128)(2,1)S(1)}, bf16[1,544,128]{2,1,0:T(8,128)(2,1)S(1)}, u32[]{:S(2)}, u32[]{:S(2)}) collective-permute-start(bf16[1,544,128]{2,1,0:T(8,128)(2,1)S(1)} %bitcast.37), channel_id=1, source_target_pairs={{0,8},{8,0},{16,24},{24,16},{1,9},{9,1},{17,25},{25,17},{2,10},{10... | collective-permute-start | bytes 417800 | tf_op jit(solution)/shard_map/ppermute | solution.py:51
  9.3 14.8 %copy-start.17 = (bf16[1,544,128]{2,1,0:T(8,128)(2,1)}, bf16[1,544,128]{2,1,0:T(8,128)(2,1)S(1)}, u32[]{:S(2)}) copy-start(bf16[1,544,128]{2,1,0:T(8,128)(2,1)S(1)} %collective-permute-done) | copy-start | bytes 417796
  9.3 14.8 %collective-permute-start.1 = (bf16[2,544,128]{2,1,0:T(8,128)(2,1)S(1)}, bf16[2,544,128]{2,1,0:T(8,128)(2,1)S(1)}, u32[]{:S(2)}, u32[]{:S(2)}) collective-permute-start(bf16[2,544,128]{2,1,0:T(8,128)(2,1)S(1)} %pad_maximum_fusion.2), channel_id=1, source_target_pairs={{0,16},{8,24},{16,0},{24,8},{1,17},{9,25},{17,1},{25,9},{2,18},{10... | collective-permute-start | bytes 835592 | tf_op jit(solution)/shard_map/ppermute | solution.py:51
  24.1 0.7 copy-start.19
  24.8 1.4 copy-start.22
  24.8 1.4 copy-start.23
  24.8 10.9 %collective-permute-start.2 = (bf16[4,416,128]{2,1,0:T(8,128)(2,1)S(1)}, bf16[4,416,128]{2,1,0:T(8,128)(2,1)S(1)}, u32[]{:S(2)}, u32[]{:S(2)}) collective-permute-start(bf16[4,416,128]{2,1,0:T(8,128)(2,1)S(1)} %slice.183), channel_id=1, source_target_pairs={{0,4},{4,0},{1,5},{5,1},{2,6},{6,2},{3,7},{7,3},{8,12},{12,8},{9,1... | collective-permute-start | bytes 1277960 | tf_op jit(solution)/shard_map/ppermute | solution.py:51
  35.8 32.2 %copy-start = (bf16[2,64,4096]{2,1,0:T(8,128)(2,1)S(1)}, bf16[2,64,4096]{2,1,0:T(8,128)(2,1)}, u32[]{:S(2)}) copy-start(bf16[2,64,4096]{2,1,0:T(8,128)(2,1)} %hidden_ref.3) | copy-start | bytes 3145732
  35.8 32.2 %collective-permute-start.3 = (bf16[8,416,128]{2,1,0:T(8,128)(2,1)S(1)}, bf16[8,416,128]{2,1,0:T(8,128)(2,1)}, u32[]{:S(2)}, u32[]{:S(2)}) collective-permute-start(bf16[8,416,128]{2,1,0:T(8,128)(2,1)S(1)} %pad_maximum_fusion.own_ref), channel_id=1, source_target_pairs={{0,1},{1,0},{2,3},{3,2},{4,5},{5,4},{6,7},{7,6},{8,9},{9,8},{10,11... | collective-permute-start | bytes 2555912 | tf_op jit(solution)/shard_map/ppermute | solution.py:51
  35.9 3.6 %copy-start.11 = (bf16[2,64,1024]{2,1,0:T(8,128)(2,1)}, bf16[2,64,1024]{2,1,0:T(8,128)(2,1)S(1)}, u32[]{:S(2)}) copy-start(bf16[2,64,1024]{2,1,0:T(8,128)(2,1)S(1)} %pad_maximum_fusion.4.refs_12_.refs_16_) | copy-start | bytes 786436
  35.9 10.1 %collective-permute-start.10 = (bf16[2,64,1024]{2,1,0:T(8,128)(2,1)S(1)}, bf16[2,64,1024]{2,1,0:T(8,128)(2,1)S(1)}, u32[]{:S(2)}, u32[]{:S(2)}) collective-permute-start(bf16[2,64,1024]{2,1,0:T(8,128)(2,1)S(1)} %pad_maximum_fusion.4.refs_12_.refs_16_), channel_id=1, source_target_pairs={{0,8},{8,16},{16,24},{1,9},{9,17},{17,25},{2,10},{10,18},{18,26},{... | collective-permute-start | bytes 786440 | tf_op jit(solution)/shard_map/ppermute | solution.py:46
  39.5 12.2 %collective-permute-start.7 = (bf16[2,64,1024]{2,1,0:T(8,128)(2,1)S(1)}, bf16[2,64,1024]{2,1,0:T(8,128)(2,1)S(1)}, u32[]{:S(2)}, u32[]{:S(2)}) collective-permute-start(bf16[2,64,1024]{2,1,0:T(8,128)(2,1)S(1)} %pad_maximum_fusion.3.refs_12_.refs_16_), channel_id=1, source_target_pairs={{0,8},{8,16},{16,24},{1,9},{9,17},{17,25},{2,10},{10,18},{18,26},{... | collective-permute-start | bytes 786440 | tf_op jit(solution)/shard_map/ppermute | solution.py:46
  46.0 21.9 %copy-start.13 = (bf16[2,64,1024]{2,1,0:T(8,128)(2,1)}, bf16[2,64,1024]{2,1,0:T(8,128)(2,1)S(1)}, u32[]{:S(2)}) copy-start(bf16[2,64,1024]{2,1,0:T(8,128)(2,1)S(1)} %collective-permute-done.10.refs_13_.refs_17_) | copy-start | bytes 786436
  46.0 11.2 %collective-permute-start.11 = (bf16[2,64,1024]{2,1,0:T(8,128)(2,1)S(1)}, bf16[2,64,1024]{2,1,0:T(8,128)(2,1)}, u32[]{:S(2)}, u32[]{:S(2)}) collective-permute-start(bf16[2,64,1024]{2,1,0:T(8,128)(2,1)S(1)} %collective-permute-done.10.refs_13_.refs_17_), channel_id=1, source_target_pairs={{0,8},{8,16},{16,24},{1,9},{9,17},{17,25},{2,10},{10,18},{18,26},{... | collective-permute-start | bytes 786440 | tf_op jit(solution)/shard_map/ppermute | solution.py:46
  51.6 11.2 %collective-permute-start.8 = (bf16[2,64,1024]{2,1,0:T(8,128)(2,1)S(1)}, bf16[2,64,1024]{2,1,0:T(8,128)(2,1)S(1)}, u32[]{:S(2)}, u32[]{:S(2)}) collective-permute-start(bf16[2,64,1024]{2,1,0:T(8,128)(2,1)S(1)} %collective-permute-done.7.refs_13_.refs_17_), channel_id=1, source_target_pairs={{0,8},{8,16},{16,24},{1,9},{9,17},{17,25},{2,10},{10,18},{18,26},{... | collective-permute-start | bytes 786440 | tf_op jit(solution)/shard_map/ppermute | solution.py:46
  57.3 21.4 %collective-permute-start.12 = (bf16[2,64,1024]{2,1,0:T(8,128)(2,1)}, bf16[2,64,1024]{2,1,0:T(8,128)(2,1)}, u32[]{:S(2)}, u32[]{:S(2)}) collective-permute-start(bf16[2,64,1024]{2,1,0:T(8,128)(2,1)} %collective-permute-done.11.refs_14_.refs_18_), channel_id=1, source_target_pairs={{0,8},{8,16},{16,24},{1,9},{9,17},{17,25},{2,10},{10,18},{18,26},{... | collective-permute-start | bytes 786440 | tf_op jit(solution)/shard_map/ppermute | solution.py:46
  62.6 15.9 %copy-start.16 = (bf16[544,128]{1,0:T(8,128)(2,1)S(1)}, bf16[544,128]{1,0:T(8,128)(2,1)}, u32[]{:S(2)}) copy-start(bf16[544,128]{1,0:T(8,128)(2,1)} %copy-done.15) | copy-start | bytes 417796
  62.6 15.9 %copy-start.18 = (bf16[1,544,128]{2,1,0:T(8,128)(2,1)S(1)}, bf16[1,544,128]{2,1,0:T(8,128)(2,1)}, u32[]{:S(2)}) copy-start(bf16[1,544,128]{2,1,0:T(8,128)(2,1)} %copy-done.17) | copy-start | bytes 417796
  62.6 15.9 %copy-start.20 = (bf16[2,544,128]{2,1,0:T(8,128)(2,1)S(1)}, bf16[2,544,128]{2,1,0:T(8,128)(2,1)}, u32[]{:S(2)}) copy-start(bf16[2,544,128]{2,1,0:T(8,128)(2,1)} %copy-done.19) | copy-start | bytes 835588
  62.9 32.4 %collective-permute-start.9 = (bf16[2,64,1024]{2,1,0:T(8,128)(2,1)S(1)}, bf16[2,64,1024]{2,1,0:T(8,128)(2,1)}, u32[]{:S(2)}, u32[]{:S(2)}) collective-permute-start(bf16[2,64,1024]{2,1,0:T(8,128)(2,1)S(1)} %collective-permute-done.8.refs_14_.refs_18_), channel_id=1, source_target_pairs={{0,8},{8,16},{16,24},{1,9},{9,17},{17,25},{2,10},{10,18},{18,26},{... | collective-permute-start | bytes 786440 | tf_op jit(solution)/shard_map/ppermute | solution.py:46
  69.7 1.0 copy-start.3
  70.7 8.0 %collective-permute-start.4 = (bf16[2,64,128]{2,1,0:T(8,128)(2,1)S(1)}, bf16[2,64,128]{2,1,0:T(8,128)(2,1)S(1)}, u32[]{:S(2)}, u32[]{:S(2)}) collective-permute-start(bf16[2,64,128]{2,1,0:T(8,128)(2,1)S(1)} %get-tuple-element.32.refs_8_), channel_id=1, source_target_pairs={{0,8},{8,16},{16,24},{1,9},{9,17},{17,25},{2,10},{10,18},{18,26},{... | collective-permute-start | bytes 98312 | tf_op jit(solution)/shard_map/ppermute | solution.py:46
  73.4 5.4 %collective-permute-start.5 = (bf16[2,64,128]{2,1,0:T(8,128)(2,1)S(1)}, bf16[2,64,128]{2,1,0:T(8,128)(2,1)S(1)}, u32[]{:S(2)}, u32[]{:S(2)}) collective-permute-start(bf16[2,64,128]{2,1,0:T(8,128)(2,1)S(1)} %get-tuple-element.32.refs_8_), channel_id=1, source_target_pairs={{0,16},{8,24},{1,17},{9,25},{2,18},{10,26},{3,19},{11,27},{4,20},{... | collective-permute-start | bytes 98312 | tf_op jit(solution)/shard_map/ppermute | solution.py:46
  77.2 2.9 %collective-permute-start.6 = (bf16[2,64,128]{2,1,0:T(8,128)(2,1)S(1)}, bf16[2,64,128]{2,1,0:T(8,128)(2,1)S(1)}, u32[]{:S(2)}, u32[]{:S(2)}) collective-permute-start(bf16[2,64,128]{2,1,0:T(8,128)(2,1)S(1)} %get-tuple-element.32.refs_8_), channel_id=1, source_target_pairs={{0,24},{1,25},{2,26},{3,27},{4,28},{5,29},{6,30},{7,31}} | collective-permute-start | bytes 98312 | tf_op jit(solution)/shard_map/ppermute | solution.py:46
  78.6 1.5 copy-start.12
  80.1 1.2 copy-start.1
  81.3 1.2 copy-start.2
  82.5 0.9 copy-start.14
  107.5 0.7 copy-start.9
  108.2 0.7 copy-start.5
  108.2 0.8 copy-start.7
  108.9 5.8 %collective-permute-start.16 = (bf16[2,64,64]{2,1,0:T(8,128)(2,1)S(1)}, bf16[2,64,64]{2,1,0:T(8,128)(2,1)S(1)}, u32[]{:S(2)}, u32[]{:S(2)}) collective-permute-start(bf16[2,64,64]{2,1,0:T(8,128)(2,1)S(1)} %get-tuple-element.69), channel_id=1, source_target_pairs={{8,0},{16,8},{24,16},{9,1},{17,9},{25,17},{10,2},{18,10},{26,18},{... | collective-permute-start | bytes 49160 | tf_op jit(solution)/shard_map/ppermute | solution.py:46
  110.2 7.1 %collective-permute-start.17 = (bf16[2,64,64]{2,1,0:T(8,128)(2,1)S(1)}, bf16[2,64,64]{2,1,0:T(8,128)(2,1)S(1)}, u32[]{:S(2)}, u32[]{:S(2)}) collective-permute-start(bf16[2,64,64]{2,1,0:T(8,128)(2,1)S(1)} %get-tuple-element.71), channel_id=1, source_target_pairs={{16,0},{24,8},{17,1},{25,9},{18,2},{26,10},{19,3},{27,11},{20,4},{... | collective-permute-start | bytes 49160 | tf_op jit(solution)/shard_map/ppermute | solution.py:46
  111.5 8.8 %collective-permute-start.18 = (bf16[2,64,64]{2,1,0:T(8,128)(2,1)S(1)}, bf16[2,64,64]{2,1,0:T(8,128)(2,1)S(1)}, u32[]{:S(2)}, u32[]{:S(2)}) collective-permute-start(bf16[2,64,64]{2,1,0:T(8,128)(2,1)S(1)} %get-tuple-element.70), channel_id=1, source_target_pairs={{24,0},{25,1},{26,2},{27,3},{28,4},{29,5},{30,6},{31,7}} | collective-permute-start | bytes 49160 | tf_op jit(solution)/shard_map/ppermute | solution.py:46
  121.1 2.4 %collective-permute-start.19 = (bf16[8,2,208,128]{3,2,1,0:T(8,128)(2,1)S(1)}, bf16[8,2,208,128]{3,2,1,0:T(8,128)(2,1)S(1)}, u32[]{:S(2)}, u32[]{:S(2)}) collective-permute-start(bf16[8,2,208,128]{3,2,1,0:T(8,128)(2,1)S(1)} %get-tuple-element.55), channel_id=1, source_target_pairs={{0,1},{1,0},{2,3},{3,2},{4,5},{5,4},{6,7},{7,6},{8,9},{9,8},{10,11... | collective-permute-start | bytes 2555912 | tf_op jit(solution)/shard_map/ppermute | solution.py:51
  123.8 27.5 %copy-start.4 = (bf16[4096,128]{1,0:T(8,128)(2,1)S(1)}, bf16[4096,128]{1,0:T(8,128)(2,1)}, u32[]{:S(2)}) copy-start(bf16[4096,128]{1,0:T(8,128)(2,1)} %copy-done.3) | copy-start | bytes 3145732
  123.8 11.9 %collective-permute-start.20 = (bf16[8,1,208,128]{3,2,1,0:T(8,128)(2,1)S(1)}, bf16[8,1,208,128]{3,2,1,0:T(8,128)(2,1)S(1)}, u32[]{:S(2)}, u32[]{:S(2)}) collective-permute-start(bf16[8,1,208,128]{3,2,1,0:T(8,128)(2,1)S(1)} %get-tuple-element.57), channel_id=1, source_target_pairs={{0,2},{1,3},{2,0},{3,1},{4,6},{5,7},{6,4},{7,5},{8,10},{9,11},{10,... | collective-permute-start | bytes 1277960 | tf_op jit(solution)/shard_map/ppermute | solution.py:51
  135.7 1.6 copy-start.21
  135.8 6.5 %collective-permute-start.21 = (bf16[4,208,128]{2,1,0:T(8,128)(2,1)S(1)}, bf16[4,208,128]{2,1,0:T(8,128)(2,1)S(1)}, u32[]{:S(2)}, u32[]{:S(2)}) collective-permute-start(bf16[4,208,128]{2,1,0:T(8,128)(2,1)S(1)} %fusion.2), channel_id=1, source_target_pairs={{0,4},{4,0},{1,5},{5,1},{2,6},{6,2},{3,7},{7,3},{8,12},{12,8},{9,1... | collective-permute-start | bytes 638984 | tf_op jit(solution)/shard_map/ppermute | solution.py:41
  142.3 6.3 %copy-start.8 = (bf16[2,64,1024]{2,1,0:T(8,128)(2,1)S(1)}, bf16[2,64,1024]{2,1,0:T(8,128)(2,1)}, u32[]{:S(2)}) copy-start(bf16[2,64,1024]{2,1,0:T(8,128)(2,1)} %copy-done.7) | copy-start | bytes 786436
  142.3 7.6 %copy-start.10 = (bf16[2,64,1024]{2,1,0:T(8,128)(2,1)S(1)}, bf16[2,64,1024]{2,1,0:T(8,128)(2,1)}, u32[]{:S(2)}) copy-start(bf16[2,64,1024]{2,1,0:T(8,128)(2,1)} %copy-done.9) | copy-start | bytes 786436
  143.4 3.9 %copy-start.6 = (bf16[2,64,1024]{2,1,0:T(8,128)(2,1)S(1)}, bf16[2,64,1024]{2,1,0:T(8,128)(2,1)}, u32[]{:S(2)}) copy-start(bf16[2,64,1024]{2,1,0:T(8,128)(2,1)} %copy-done.5) | copy-start | bytes 786436
  143.4 6.5 %collective-permute-start.22 = (bf16[208,128]{1,0:T(8,128)(2,1)S(1)}, bf16[208,128]{1,0:T(8,128)(2,1)S(1)}, u32[]{:S(2)}, u32[]{:S(2)}) collective-permute-start(bf16[208,128]{1,0:T(8,128)(2,1)S(1)} %get-tuple-element.66), channel_id=1, source_target_pairs={{0,8},{8,16},{16,24},{24,0},{1,9},{9,17},{17,25},{25,1},{2,10},{10... | collective-permute-start | bytes 159752 | tf_op jit(solution)/shard_map/ppermute | solution.py:41
  143.5 9.9 %collective-permute-start.23 = (bf16[208,128]{1,0:T(8,128)(2,1)S(1)}, bf16[208,128]{1,0:T(8,128)(2,1)S(1)}, u32[]{:S(2)}, u32[]{:S(2)}) collective-permute-start(bf16[208,128]{1,0:T(8,128)(2,1)S(1)} %get-tuple-element.68), channel_id=1, source_target_pairs={{0,16},{8,24},{16,0},{24,8},{1,17},{9,25},{17,1},{25,9},{2,18},{10... | collective-permute-start | bytes 159752 | tf_op jit(solution)/shard_map/ppermute | solution.py:41
  143.8 9.7 %collective-permute-start.24 = (bf16[208,128]{1,0:T(8,128)(2,1)S(1)}, bf16[208,128]{1,0:T(8,128)(2,1)S(1)}, u32[]{:S(2)}, u32[]{:S(2)}) collective-permute-start(bf16[208,128]{1,0:T(8,128)(2,1)S(1)} %get-tuple-element.67), channel_id=1, source_target_pairs={{0,24},{8,0},{16,8},{24,16},{1,25},{9,1},{17,9},{25,17},{2,26},{10... | collective-permute-start | bytes 159752 | tf_op jit(solution)/shard_map/ppermute | solution.py:41
  147.3 8.6 %collective-permute-start.13 = (bf16[2,64,1024]{2,1,0:T(8,128)(2,1)S(1)}, bf16[2,64,1024]{2,1,0:T(8,128)(2,1)S(1)}, u32[]{:S(2)}, u32[]{:S(2)}) collective-permute-start(bf16[2,64,1024]{2,1,0:T(8,128)(2,1)S(1)} %copy-done.6), channel_id=1, source_target_pairs={{8,0},{16,8},{24,16},{9,1},{17,9},{25,17},{10,2},{18,10},{26,18},{... | collective-permute-start | bytes 786440 | tf_op jit(solution)/shard_map/ppermute | solution.py:46
  148.6 24.4 %collective-permute-start.14 = (bf16[2,64,1024]{2,1,0:T(8,128)(2,1)S(1)}, bf16[2,64,1024]{2,1,0:T(8,128)(2,1)S(1)}, u32[]{:S(2)}, u32[]{:S(2)}) collective-permute-start(bf16[2,64,1024]{2,1,0:T(8,128)(2,1)S(1)} %copy-done.8), channel_id=1, source_target_pairs={{16,0},{24,8},{17,1},{25,9},{18,2},{26,10},{19,3},{27,11},{20,4},{... | collective-permute-start | bytes 786440 | tf_op jit(solution)/shard_map/ppermute | solution.py:46
  149.9 23.1 %collective-permute-start.15 = (bf16[2,64,1024]{2,1,0:T(8,128)(2,1)S(1)}, bf16[2,64,1024]{2,1,0:T(8,128)(2,1)S(1)}, u32[]{:S(2)}, u32[]{:S(2)}) collective-permute-start(bf16[2,64,1024]{2,1,0:T(8,128)(2,1)S(1)} %copy-done.10), channel_id=1, source_target_pairs={{24,0},{25,1},{26,2},{27,3},{28,4},{29,5},{30,6},{31,7}} | collective-permute-start | bytes 786440 | tf_op jit(solution)/shard_map/ppermute | solution.py:46
  153.5 20.5 %collective-permute-start.25 = (bf16[208,128]{1,0:T(8,128)(2,1)S(1)}, bf16[208,128]{1,0:T(8,128)(2,1)S(1)}, u32[]{:S(2)}, u32[]{:S(2)}) collective-permute-start(bf16[208,128]{1,0:T(8,128)(2,1)S(1)} %fusion.5), channel_id=1, source_target_pairs={{0,3},{1,2},{2,1},{3,0},{4,7},{5,6},{6,5},{7,4},{8,11},{9,10},{10,... | collective-permute-start | bytes 159752 | tf_op jit(solution)/shard_map/ppermute | solution.py:51
  153.6 20.4 %collective-permute-start.26 = (bf16[208,128]{1,0:T(8,128)(2,1)S(1)}, bf16[208,128]{1,0:T(8,128)(2,1)S(1)}, u32[]{:S(2)}, u32[]{:S(2)}) collective-permute-start(bf16[208,128]{1,0:T(8,128)(2,1)S(1)} %fusion.5), channel_id=1, source_target_pairs={{0,2},{1,3},{2,0},{3,1},{4,6},{5,7},{6,4},{7,5},{8,10},{9,11},{10,... | collective-permute-start | bytes 159752 | tf_op jit(solution)/shard_map/ppermute | solution.py:51
  155.9 18.0 %collective-permute-start.27 = (bf16[208,128]{1,0:T(8,128)(2,1)S(1)}, bf16[208,128]{1,0:T(8,128)(2,1)S(1)}, u32[]{:S(2)}, u32[]{:S(2)}) collective-permute-start(bf16[208,128]{1,0:T(8,128)(2,1)S(1)} %fusion.5), channel_id=1, source_target_pairs={{0,1},{1,0},{2,3},{3,2},{4,5},{5,4},{6,7},{7,6},{8,9},{9,8},{10,11... | collective-permute-start | bytes 159752 | tf_op jit(solution)/shard_map/ppermute | solution.py:51

commit v3 on v2

--- a/solution.py
+++ b/solution.py
@@ -18,7 +18,8 @@
 WIDE = GROUP * HEAD_DIM
 ROPE_BASE = 500000.0
 HIDDEN_MASK = -1e30
-CHUNKS = 2
+CHUNKS = ((0, 5), (5, 8))
+LOG2_E = 1.4426950408889634
 
 f32 = jnp.float32
 bf16 = jnp.bfloat16
@@ -49,6 +50,10 @@
 def partner(x, axis, mask):
     n = lax.axis_size(axis)
     return lax.ppermute(x, axis, [(i, i ^ mask) for i in range(n)])
+
+
+def tie(x, *others):
+    return lax.optimization_barrier((x,) + others)[0]
 
 
 def mm(a, b, ca, cb):
@@ -116,16 +121,17 @@
         base = jnp.concatenate([r[s] for r in v_refs], axis=0).astype(f32)
         vals = jnp.concatenate([(base + mm(low_v, upv, 1, 0)).astype(bf16), pv_ref[s]], axis=0)
 
-        scores = mm(q, keys, 1, 1) * scale + bias
+        scores = mm(q, keys, 1, 1) * (scale * LOG2_E) + bias
         top = jnp.max(scores, axis=-1, keepdims=True)
-        e = jnp.exp(scores - top)
-        probs = e / jnp.sum(e, axis=-1, keepdims=True)
-        weights = probs.astype(bf16)
-        out = mm(weights, vals, 1, 0).astype(bf16)
+        e = jnp.exp2(scores - top)
+        inverse = 1.0 / jnp.sum(e, axis=-1, keepdims=True)
+        weights = e.astype(bf16)
+        out = (mm(weights, vals, 1, 0) * inverse).astype(bf16)
         att_ref[s] = lanes(out)
+        g = (g.astype(f32) * inverse).astype(bf16)
         prob_grad = mm(g, vals, 1, 1)
         row_delta = jnp.sum(g.astype(f32) * out.astype(f32), axis=-1, keepdims=True)
-        score_grad = (probs * (prob_grad - row_delta)).astype(bf16)
+        score_grad = (e * (prob_grad - row_delta)).astype(bf16)
         gq = (mm(score_grad, keys, 1, 0) * scale).astype(bf16)
         gq_ref[s] = lanes(gq)
         gq32 = gq.astype(f32)
@@ -149,13 +155,13 @@
 
 
 def attention_chunk(
-    chunk, groups, place, query_base, grad_out, up_blocks, past, cos, sin, lows, kvs, earlier
+    first, last, place, query_base, grad_out, up_blocks, past, cos, sin, lows, kvs, earlier
 ):
     shards = len(kvs)
     parts = lax.axis_size("rep")
     seqs, tokens = query_base.shape[:2]
     past_len = past.shape[1]
-    first = chunk * groups
+    groups = last - first
 
     def whole(x):
         return pl.BlockSpec(x.shape, lambda g: (0,) * len(x.shape))
@@ -241,7 +247,7 @@
         low_ref[s] = low[s * low_ref.shape[1] : (s + 1) * low_ref.shape[1]]
 
 
-def adapters_packed(hidden, adapter_down, adapter_up, own_past):
+def adapters_packed(hidden, adapter_down, adapter_up, own_past, after):
     sp, fs = lax.axis_size("sp"), lax.axis_size("fsdp")
     z, x, r = (lax.axis_index(a) for a in ("sp", "fsdp", "rep"))
     c = lax.rem(r, 2)
@@ -255,6 +261,8 @@
     step = 1
     while step < sp:
         buf = jnp.concatenate([buf, partner(buf, "sp", step)], axis=0)
+        if step == 1:
+            buf = tie(buf, after[0])
         step *= 2
     seqs, each = own_past.shape[:2]
     past = buf[:, rows:].reshape(sp, seqs, each, -1).swapaxes(0, 1).reshape(seqs, sp * each, -1)
@@ -263,7 +271,7 @@
     while step < fs:
         buf = jnp.concatenate([buf, partner(buf, "fsdp", step)], axis=0)
         step *= 2
-    other = partner(buf, "rep", 1)
+    other = partner(tie(buf, after[1]), "rep", 1)
     index = jnp.stack([z, x, c]).astype(jnp.int32)
     vmem = pl.BlockSpec(memory_space=pltpu.VMEM)
     seqs, tokens = hidden.shape[:2]
@@ -285,7 +293,7 @@
     return down_full, up_blocks, low, past
 
 
-def adapters_plain(hidden, adapter_down, adapter_up, own_past):
+def adapters_plain(hidden, adapter_down, adapter_up, own_past, after):
     sp = lax.axis_size("sp")
     seqs, tokens = hidden.shape[:2]
     past = jnp.concatenate([own_past] + [cyclic(own_past, "sp", k) for k in range(1, sp)], axis=1)
@@ -379,7 +387,7 @@
     return send, keep
 
 
-def finish_grads(send, keep):
+def finish_grads(send, keep, before):
     sp, fs, rp = (lax.axis_size(a) for a in ("sp", "fsdp", "rep"))
     z, x, r = (lax.axis_index(a) for a in ("sp", "fsdp", "rep"))
     shards, _, rows, lanes = send.shape
@@ -395,6 +403,7 @@
             ).astype(bf16)
 
         send, keep = half(1 - mine), half(mine)
+        send = tie(send, before[0])
         got = partner(send, "rep", 1 << b)
     shape = (sp, fs, rows, lanes)
 
@@ -406,8 +415,9 @@
 
     total = over_fsdp(x).astype(f32)
     for k in range(1, fs):
-        total = total + cyclic(over_fsdp(lax.rem(x + k, fs)), "fsdp", k).astype(f32)
-    over_sp = total.astype(bf16)
+        send = tie(over_fsdp(lax.rem(x + k, fs)), *before[:2])
+        total = total + cyclic(send, "fsdp", k).astype(f32)
+    over_sp = tie(total.astype(bf16), *before)
     total = lax.dynamic_index_in_dim(over_sp, z, 0, keepdims=False).astype(f32)
     for k in range(1, sp):
         send = lax.dynamic_index_in_dim(over_sp, lax.rem(z + k, sp), 0, keepdims=False)
@@ -448,31 +458,30 @@
     z = lax.axis_index("sp")
     seqs, tokens = hidden.shape[:2]
     past_len = past_keys.shape[1] * sp
-    groups = KV_HEADS // CHUNKS
-    width = groups * HEAD_DIM
-
     own_past = jnp.concatenate([past_keys, past_values], axis=2)
+    own_kvs = []
+    for first, last in CHUNKS:
+        cols = slice(first * HEAD_DIM, last * HEAD_DIM)
+        own_kvs.append(jnp.concatenate([key_span[:, :, cols], value_base[:, :, cols]], axis=2))
+    early = [own_kvs[0]]
+    for k in range(1, sp):
+        early.append(along(early[k - 1], "sp", 1))
+
     even = adapter_up.shape[1] % HEAD_DIM == 0
     adapters = adapters_packed if even else adapters_plain
-    down_full, up_blocks, low_own, past = adapters(hidden, adapter_down, adapter_up, own_past)
-
-    chunk_kvs = []
-    for c in range(CHUNKS):
-        cols = slice(c * width, (c + 1) * width)
-        kvs = [jnp.concatenate([key_span[:, :, cols], value_base[:, :, cols]], axis=2)]
-        for k in range(1, sp):
-            kvs.append(along(kvs[k - 1], "sp", 1))
-        chunk_kvs.append(kvs)
-
+    down_full, up_blocks, low_own, past = adapters(
+        hidden, adapter_down, adapter_up, own_past, (early[1], early[min(2, sp - 1)])
+    )
+    low_own = tie(low_own, early[-1])
+    late = [own_kvs[1]] + [along(tie(own_kvs[1], low_own), "sp", k) for k in range(1, sp)]
     lows = [low_own] + [along(low_own, "sp", k) for k in range(1, sp)]
     cos, sin = rotary_tables(tokens, past_len + z * tokens)
     place = z.astype(jnp.int32).reshape(1)
 
     made = None
-    for c in range(CHUNKS):
+    for (first, last), kvs in zip(CHUNKS, (early, late)):
         made = attention_chunk(
-            c, groups, place, query_base, grad_out, up_blocks, past, cos, sin,
-            lows, chunk_kvs[c], made,
+            first, last, place, query_base, grad_out, up_blocks, past, cos, sin, lows, kvs, made
         )
     attended, grad_query, guq, guv = made[:4]
     gvs = made[4 : 4 + sp]
@@ -488,12 +497,13 @@
         .reshape(seqs * tokens, 2 * RANK)
     )
     send, keep = packed_grads(hidden, low_grad, guq, guv, sp * fs)
-    grad_down, grad_up = finish_grads(send, keep)
+    value_parts = [along(gvs[k], "sp", -k) for k in range(1, sp)]
+    grad_down, grad_up = finish_grads(send, keep, value_parts)
     grad_hidden = grad_hidden_of(low_grad, down_full, seqs, tokens)
 
     grad_value = gvs[0].astype(f32)
-    for k in range(1, sp):
-        grad_value = grad_value + along(gvs[k], "sp", -k).astype(f32)
+    for part in value_parts:
+        grad_value = grad_value + part.astype(f32)
     return (
         attended,
         grad_query,

time: 176 us -> 165 us (0.938)
  starting transfers between devices: 56.8 us -> 49.2 us
  waiting for transfers between devices: 75.9 us -> 70.3 us
  local copies, waits for them, and re-layouts: 7.84 us -> 9.75 us
    ppermute x15, starting transfers between devices: 40.7 us -> 35.4 us  [along(): lax.ppermute(x, axis, [(i, i + shift) for i in range(n) if 0 <= i + shift...]
    ppermute x15, waiting for transfers between devices: 33.2 us -> 28.3 us  [along(): lax.ppermute(x, axis, [(i, i + shift) for i in range(n) if 0 <= i + shift...]
    pallas_call x2, Pallas kernels: 24 us -> 22.1 us  [attention_chunk(): pl.pallas_call(functools.partial(attention_kernel, shards, placed if earl...]
    unnamed x74 -> x57, local copies, waits for them, and re-layouts: 7.54 us -> 6.65 us
  transfers between devices with their start and end apart: 28 -> 28, of which waited for: 17 -> 18; matrix products, arithmetic and copies ran while one was open for 1% -> 3% of each run, Pallas kernels for 9% -> 10%
where the time goes in v3:
time: 165 us; the launch traced here: 164 us
  waiting for transfers between devices  70.3 us (43%)
  starting transfers between devices  49.2 us (30%)
  Pallas kernels  27.5 us (17%)
  local copies, waits for them, and re-layouts  9.75 us (6%)
  other arithmetic  6.19 us (4%)
    ppermute x9, waiting for transfers between devices, partner(): return lax.ppermute(x, axis, [(i, i ^ mask) for i in range(n)])  36.1 us
    ppermute x15, starting transfers between devices, along(): lax.ppermute(x, axis, [(i, i + shift) for i in range(n) if 0 <= i + shift...  35.4 us
    ppermute x15, waiting for transfers between devices, along(): lax.ppermute(x, axis, [(i, i + shift) for i in range(n) if 0 <= i + shift...  28.3 us
    pallas_call x2, Pallas kernels, attention_chunk(): pl.pallas_call(functools.partial(attention_kernel, shards, placed if earl...  22.1 us
    ppermute x9, starting transfers between devices, partner(): return lax.ppermute(x, axis, [(i, i ^ mask) for i in range(n)])  9.28 us
    unnamed x57, local copies, waits for them, and re-layouts  6.65 us
    ppermute x4, waiting for transfers between devices, cyclic(): return lax.ppermute(x, axis, [(i, (i + shift) % n) for i in range(n)])  5.9 us
    ppermute x4, starting transfers between devices, cyclic(): return lax.ppermute(x, axis, [(i, (i + shift) % n) for i in range(n)])  4.54 us
  transfers between devices with their start and end apart: 28, of which 18 were waited for; matrix products, arithmetic and copies ran while one was open for 3% of the time, Pallas kernels for 10%

profile of v3, /device:TPU:0, one launch (start us, length us, event | category | flops | bytes accessed | tf_op | source)
XLA Modules:
  0.0 164.3 jit_solution(11424286444216833695)
XLA Ops:
  0.7 0.9 slice-done
  1.7 5.1 %collective-permute-start.1 = (bf16[2,64,1280]{2,1,0:T(8,128)(2,1)S(1)}, bf16[2,64,1280]{2,1,0:T(8,128)(2,1)S(1)}, u32[]{:S(2)}, u32[]{:S(2)}) collective-permute-start(bf16[2,64,1280]{2,1,0:T(8,128)(2,1)S(1)} %pad_maximum_fusion.1.refs_12_.refs_16_), channel_id=1, source_target_pairs={{0,8},{8,16},{16,24},{1,9},{9,17},{17,25},{2,10},{10,18},{18,26},{... | collective-permute-start | bytes 983048 | tf_op jit(solution)/shard_map/ppermute | solution.py:47
  6.9 0.8 copy-done.14
  7.8 1.6 collective-permute-start
  9.5 7.2 %collective-permute-done = bf16[1,544,128]{2,1,0:T(8,128)(2,1)S(1)} collective-permute-done((bf16[1,544,128]{2,1,0:T(8,128)(2,1)S(1)}, bf16[1,544,128]{2,1,0:T(8,128)(2,1)S(1)}, u32[]{:S(2)}, u32[]{:S(2)}) %collective-permute-start) | collective-permute-done | bytes 139296 | tf_op jit(solution)/shard_map/ppermute | solution.py:52
  16.7 2.7 %collective-permute-start.2 = (bf16[2,544,128]{2,1,0:T(8,128)(2,1)S(1)}, bf16[2,544,128]{2,1,0:T(8,128)(2,1)S(1)}, u32[]{:S(2)}, u32[]{:S(2)}) collective-permute-start(bf16[2,544,128]{2,1,0:T(8,128)(2,1)S(1)} %pad_maximum_fusion.2), channel_id=1, source_target_pairs={{0,16},{8,24},{16,0},{24,8},{1,17},{9,25},{17,1},{25,9},{2,18},{10... | collective-permute-start | bytes 835592 | tf_op jit(solution)/shard_map/ppermute | solution.py:52
  19.4 11.8 %collective-permute-done.2 = bf16[2,544,128]{2,1,0:T(8,128)(2,1)S(1)} collective-permute-done((bf16[2,544,128]{2,1,0:T(8,128)(2,1)S(1)}, bf16[2,544,128]{2,1,0:T(8,128)(2,1)S(1)}, u32[]{:S(2)}, u32[]{:S(2)}) %collective-permute-start.2) | collective-permute-done | bytes 278560 | tf_op jit(solution)/shard_map/ppermute | solution.py:52
  31.3 1.6 collective-permute-start.3
  32.9 3.3 %collective-permute-start.4 = (bf16[2,64,1280]{2,1,0:T(8,128)(2,1)S(1)}, bf16[2,64,1280]{2,1,0:T(8,128)(2,1)}, u32[]{:S(2)}, u32[]{:S(2)}) collective-permute-start(bf16[2,64,1280]{2,1,0:T(8,128)(2,1)S(1)} %collective-permute-done.1.refs_13_.refs_17_), channel_id=1, source_target_pairs={{0,8},{8,16},{16,24},{1,9},{9,17},{17,25},{2,10},{10,18},{18,26},{... | collective-permute-start | bytes 983048 | tf_op jit(solution)/shard_map/ppermute | solution.py:47
  36.2 5.0 %collective-permute-done.3 = bf16[4,416,128]{2,1,0:T(8,128)(2,1)S(1)} collective-permute-done((bf16[4,416,128]{2,1,0:T(8,128)(2,1)S(1)}, bf16[4,416,128]{2,1,0:T(8,128)(2,1)S(1)}, u32[]{:S(2)}, u32[]{:S(2)}) %collective-permute-start.3) | collective-permute-done | bytes 426016 | tf_op jit(solution)/shard_map/ppermute | solution.py:52
  41.2 1.1 collective-permute-done.4.refs_14_.refs_18_
  42.3 0.9 slice-done.1
  43.2 4.5 %collective-permute-start.6 = (bf16[2,64,1280]{2,1,0:T(8,128)(2,1)}, bf16[2,64,1280]{2,1,0:T(8,128)(2,1)S(1)}, u32[]{:S(2)}, u32[]{:S(2)}) collective-permute-start(bf16[2,64,1280]{2,1,0:T(8,128)(2,1)} %collective-permute-done.4.refs_14_.refs_18_), channel_id=1, source_target_pairs={{0,8},{8,16},{16,24},{1,9},{9,17},{17,25},{2,10},{10,18},{18,26},{... | collective-permute-start | bytes 983048 | tf_op jit(solution)/shard_map/ppermute | solution.py:47
  47.8 0.2 fusion.6
  48.1 1.7 %low_rank.1 = (bf16[4096,128]{1,0:T(8,128)(2,1)S(1)}, bf16[40,64,128]{2,1,0:T(8,128)(2,1)S(1)}, bf16[2,64,128]{2,1,0:T(8,128)(2,1)S(1)}) custom-call(s32[3]{0:T(128)S(1)} %pad_add_fusion.index_ref, bf16[8,416,128]{2,1,0:T(8,128)(2,1)S(1)} %pad_maximum_fusion.own_ref, bf16[8,416,128]{2,1,0:T(8,128)(2,1)} %collective-permute-done.5.other_ref, ...), custom_call_target="tpu_custom_call" | custom-call | flops 134217728 | bytes 5242880 | tf_op jit(solution)/shard_map/low_rank/pallas_call | solution.py:278
  49.8 1.0 copy-done.2
  50.8 4.9 %collective-permute-done.6.refs_15_.refs_19_ = bf16[2,64,1280]{2,1,0:T(8,128)(2,1)S(1)} collective-permute-done((bf16[2,64,1280]{2,1,0:T(8,128)(2,1)}, bf16[2,64,1280]{2,1,0:T(8,128)(2,1)S(1)}, u32[]{:S(2)}, u32[]{:S(2)}) %collective-permute-start.6) | collective-permute-done | bytes 327712 | tf_op jit(solution)/shard_map/ppermute | solution.py:47
  55.7 0.7 copy-done.10
  56.4 4.3 %collective-permute-start.7 = (bf16[2,64,128]{2,1,0:T(8,128)(2,1)S(1)}, bf16[2,64,128]{2,1,0:T(8,128)(2,1)S(1)}, u32[]{:S(2)}, u32[]{:S(2)}) collective-permute-start(bf16[2,64,128]{2,1,0:T(8,128)(2,1)S(1)} %get-tuple-element.42.refs_8_), channel_id=1, source_target_pairs={{0,8},{8,16},{16,24},{1,9},{9,17},{17,25},{2,10},{10,18},{18,26},{... | collective-permute-start | bytes 98312 | tf_op jit(solution)/shard_map/ppermute | solution.py:47
  60.7 5.3 %collective-permute-start.8 = (bf16[2,64,128]{2,1,0:T(8,128)(2,1)S(1)}, bf16[2,64,128]{2,1,0:T(8,128)(2,1)S(1)}, u32[]{:S(2)}, u32[]{:S(2)}) collective-permute-start(bf16[2,64,128]{2,1,0:T(8,128)(2,1)S(1)} %get-tuple-element.42.refs_8_), channel_id=1, source_target_pairs={{0,16},{8,24},{1,17},{9,25},{2,18},{10,26},{3,19},{11,27},{4,20},{... | collective-permute-start | bytes 98312 | tf_op jit(solution)/shard_map/ppermute | solution.py:47
  66.0 1.3 collective-permute-start.9
  67.4 0.9 slice.184
  68.4 1.3 collective-permute-start.10
  69.8 1.3 collective-permute-start.11
  71.1 1.3 collective-permute-start.12
  72.4 1.2 copy-done.1
  73.6 1.0 copy-done.9
  74.6 1.0 copy-done.11
  75.6 13.4 %attention.2 = (bf16[2,64,4096]{2,1,0:T(8,128)(2,1)}, bf16[2,64,4096]{2,1,0:T(8,128)(2,1)}, bf16[32,4,16,128]{3,2,1,0:T(8,128)(2,1)S(1)}, bf16[8,4,16,128]{3,2,1...) custom-call(s32[1]{0:T(128)} %bitcast.place_ref, ...), custom_call_target="tpu_custom_call" | custom-call | flops 2495610880 | bytes 16777216 | tf_op jit(solution)/shard_map/attention/pallas_call | solution.py:213
  89.0 8.7 %attention.3 = (bf16[2,64,4096]{2,1,0:T(8,128)(2,1)}, bf16[2,64,4096]{2,1,0:T(8,128)(2,1)}, bf16[32,4,16,128]{3,2,1,0:T(8,128)(2,1)S(1)}, bf16[8,4,16,128]{3,2,1...) custom-call(s32[1]{0:T(128)} %bitcast.place_ref, ...), custom_call_target="tpu_custom_call", output_to_operand_aliasing={{0}: (23, {}), {1}: (24, {}), {2}: (25, {}), {3}: (26, {}),... | custom-call | flops 1497366528 | bytes 16777216 | tf_op jit(solution)/shard_map/attention/pallas_call | solution.py:213
  97.8 0.7 copy-done.4
  98.5 1.3 collective-permute-start.16
  99.8 1.3 collective-permute-start.17
  101.1 1.3 collective-permute-start.18
  102.4 1.9 %collective-permute-done.16 = bf16[2,64,64]{2,1,0:T(8,128)(2,1)S(1)} collective-permute-done((bf16[2,64,64]{2,1,0:T(8,128)(2,1)S(1)}, bf16[2,64,64]{2,1,0:T(8,128)(2,1)S(1)}, u32[]{:S(2)}, u32[]{:S(2)}) %collective-permute-start.16) | collective-permute-done | bytes 16416 | tf_op jit(solution)/shard_map/ppermute | solution.py:47
  104.3 2.5 %collective-permute-done.17 = bf16[2,64,64]{2,1,0:T(8,128)(2,1)S(1)} collective-permute-done((bf16[2,64,64]{2,1,0:T(8,128)(2,1)S(1)}, bf16[2,64,64]{2,1,0:T(8,128)(2,1)S(1)}, u32[]{:S(2)}, u32[]{:S(2)}) %collective-permute-start.17) | collective-permute-done | bytes 16416 | tf_op jit(solution)/shard_map/ppermute | solution.py:47
  106.9 3.0 %collective-permute-done.18 = bf16[2,64,64]{2,1,0:T(8,128)(2,1)S(1)} collective-permute-done((bf16[2,64,64]{2,1,0:T(8,128)(2,1)S(1)}, bf16[2,64,64]{2,1,0:T(8,128)(2,1)S(1)}, u32[]{:S(2)}, u32[]{:S(2)}) %collective-permute-start.18) | collective-permute-done | bytes 16416 | tf_op jit(solution)/shard_map/ppermute | solution.py:47
  110.0 1.6 adapter_grads.1
  111.6 1.3 collective-permute-start.13
  112.9 1.3 collective-permute-done.19
  114.2 1.2 add_convert_fusion.1
  115.3 6.9 %collective-permute-done.13 = bf16[2,64,1024]{2,1,0:T(8,128)(2,1)S(1)} collective-permute-done((bf16[2,64,1024]{2,1,0:T(8,128)(2,1)S(1)}, bf16[2,64,1024]{2,1,0:T(8,128)(2,1)S(1)}, u32[]{:S(2)}, u32[]{:S(2)}) %collective-permute-start.13) | collective-permute-done | bytes 262176 | tf_op jit(solution)/shard_map/ppermute | solution.py:47
  122.2 1.5 collective-permute-start.20
  123.7 1.3 collective-permute-start.14
  125.0 8.8 %collective-permute-done.20 = bf16[8,1,208,128]{3,2,1,0:T(8,128)(2,1)S(1)} collective-permute-done((bf16[8,1,208,128]{3,2,1,0:T(8,128)(2,1)}, bf16[8,1,208,128]{3,2,1,0:T(8,128)(2,1)S(1)}, u32[]{:S(2)}, u32[]{:S(2)}) %collective-permute-start.20) | collective-permute-done | bytes 426016 | tf_op jit(solution)/shard_map/ppermute | solution.py:52
  133.9 1.0 fusion.2
  134.9 3.9 %collective-permute-done.14 = bf16[2,64,1024]{2,1,0:T(8,128)(2,1)S(1)} collective-permute-done((bf16[2,64,1024]{2,1,0:T(8,128)(2,1)S(1)}, bf16[2,64,1024]{2,1,0:T(8,128)(2,1)S(1)}, u32[]{:S(2)}, u32[]{:S(2)}) %collective-permute-start.14) | collective-permute-done | bytes 262176 | tf_op jit(solution)/shard_map/ppermute | solution.py:47
  138.8 0.7 collective-permute-start.21
  139.4 1.3 collective-permute-start.15
  140.7 5.2 %collective-permute-done.21 = bf16[4,208,128]{2,1,0:T(8,128)(2,1)S(1)} collective-permute-done((bf16[4,208,128]{2,1,0:T(8,128)(2,1)S(1)}, bf16[4,208,128]{2,1,0:T(8,128)(2,1)S(1)}, u32[]{:S(2)}, u32[]{:S(2)}) %collective-permute-start.21) | collective-permute-done | bytes 213024 | tf_op jit(solution)/shard_map/ppermute | solution.py:42
  145.9 1.0 fusion
  147.0 4.1 %collective-permute-done.15 = bf16[2,64,1024]{2,1,0:T(8,128)(2,1)S(1)} collective-permute-done((bf16[2,64,1024]{2,1,0:T(8,128)(2,1)S(1)}, bf16[2,64,1024]{2,1,0:T(8,128)(2,1)S(1)}, u32[]{:S(2)}, u32[]{:S(2)}) %collective-permute-start.15) | collective-permute-done | bytes 262176 | tf_op jit(solution)/shard_map/ppermute | solution.py:47
  151.1 0.1 collective-permute-start.23
  151.2 3.7 %collective-permute-start.24 = (bf16[208,128]{1,0:T(8,128)(2,1)S(1)}, bf16[208,128]{1,0:T(8,128)(2,1)S(1)}, u32[]{:S(2)}, u32[]{:S(2)}) collective-permute-start(bf16[208,128]{1,0:T(8,128)(2,1)S(1)} %get-tuple-element.77), channel_id=1, source_target_pairs={{0,24},{8,0},{16,8},{24,16},{1,25},{9,1},{17,9},{25,17},{2,26},{10... | collective-permute-start | bytes 159752 | tf_op jit(solution)/shard_map/ppermute | solution.py:42
  155.0 2.1 %grad_hidden.1 = bf16[2,64,4096]{2,1,0:T(8,128)(2,1)} custom-call(bf16[128,128]{1,0:T(8,128)(2,1)S(1)} %pad_maximum_fusion.9.low_ref, bf16[4096,128]{1,0:T(8,128)(2,1)S(1)} %copy-done.3), custom_call_target="tpu_custom_call" | custom-call | flops 134217728 | bytes 2097152 | tf_op jit(solution)/shard_map/grad_hidden/pallas_call | solution.py:317
  157.1 0.1 collective-permute-done.22
  157.2 0.6 collective-permute-done.23
  157.9 0.6 collective-permute-start.26
  158.5 1.3 collective-permute-start.27
  159.8 0.9 add_convert_fusion.2
  160.6 0.8 collective-permute-done.25
  161.4 1.1 collective-permute-done.26
  162.9 0.7 pad_maximum_fusion.5
  163.6 0.7 pad_maximum_fusion.3
  (102 shorter events, 1.4 us)
Async XLA Ops:
  0.6 0.9 slice-start
  0.6 1.0 slice-start.2
  1.6 5.1 %copy-start.15 = (bf16[2,4,1024]{2,1,0:T(4,128)(2,1)S(1)}, bf16[2,4,1024]{2,1,0:T(4,128)(2,1)}, u32[]{:S(2)}) copy-start(bf16[2,4,1024]{2,1,0:T(4,128)(2,1)} %param.14) | copy-start | bytes 49156
  1.6 5.2 %copy-start.16 = (bf16[2,4,1024]{2,1,0:T(4,128)(2,1)S(1)}, bf16[2,4,1024]{2,1,0:T(4,128)(2,1)}, u32[]{:S(2)}) copy-start(bf16[2,4,1024]{2,1,0:T(4,128)(2,1)} %param.13) | copy-start | bytes 49156
  1.7 5.2 %copy-start.13 = (bf16[512,128]{1,0:T(8,128)(2,1)S(1)}, bf16[512,128]{1,0:T(8,128)(2,1)}, u32[]{:S(2)}) copy-start(bf16[512,128]{1,0:T(8,128)(2,1)} %param.16) | copy-start | bytes 393220
  1.7 15.0 %collective-permute-start.1 = (bf16[2,64,1280]{2,1,0:T(8,128)(2,1)S(1)}, bf16[2,64,1280]{2,1,0:T(8,128)(2,1)S(1)}, u32[]{:S(2)}, u32[]{:S(2)}) collective-permute-start(bf16[2,64,1280]{2,1,0:T(8,128)(2,1)S(1)} %pad_maximum_fusion.1.refs_12_.refs_16_), channel_id=1, source_target_pairs={{0,8},{8,16},{16,24},{1,9},{9,17},{17,25},{2,10},{10,18},{18,26},{... | collective-permute-start | bytes 983048 | tf_op jit(solution)/shard_map/ppermute | solution.py:47
  6.9 0.9 copy-start.14
  7.8 8.8 %collective-permute-start = (bf16[1,544,128]{2,1,0:T(8,128)(2,1)S(1)}, bf16[1,544,128]{2,1,0:T(8,128)(2,1)S(1)}, u32[]{:S(2)}, u32[]{:S(2)}) collective-permute-start(bf16[1,544,128]{2,1,0:T(8,128)(2,1)S(1)} %bitcast.40), channel_id=1, source_target_pairs={{0,8},{8,0},{16,24},{24,16},{1,9},{9,1},{17,25},{25,17},{2,10},{10... | collective-permute-start | bytes 417800 | tf_op jit(solution)/shard_map/ppermute | solution.py:52
  16.7 16.1 %copy-start.8 = (bf16[2,64,1280]{2,1,0:T(8,128)(2,1)}, bf16[2,64,1280]{2,1,0:T(8,128)(2,1)S(1)}, u32[]{:S(2)}) copy-start(bf16[2,64,1280]{2,1,0:T(8,128)(2,1)S(1)} %collective-permute-done.1.refs_13_.refs_17_) | copy-start | bytes 983044
  16.7 14.5 %collective-permute-start.2 = (bf16[2,544,128]{2,1,0:T(8,128)(2,1)S(1)}, bf16[2,544,128]{2,1,0:T(8,128)(2,1)S(1)}, u32[]{:S(2)}, u32[]{:S(2)}) collective-permute-start(bf16[2,544,128]{2,1,0:T(8,128)(2,1)S(1)} %pad_maximum_fusion.2), channel_id=1, source_target_pairs={{0,16},{8,24},{16,0},{24,8},{1,17},{9,25},{17,1},{25,9},{2,18},{10... | collective-permute-start | bytes 835592 | tf_op jit(solution)/shard_map/ppermute | solution.py:52
  31.2 4.9 %copy-start.12 = (bf16[4,544,128]{2,1,0:T(8,128)(2,1)}, bf16[4,544,128]{2,1,0:T(8,128)(2,1)S(1)}, u32[]{:S(2)}) copy-start(bf16[4,544,128]{2,1,0:T(8,128)(2,1)S(1)} %constant_dynamic-update-slice_fusion.6) | copy-start | bytes 1671172
  31.3 16.8 %copy-start = (bf16[2,64,4096]{2,1,0:T(8,128)(2,1)S(1)}, bf16[2,64,4096]{2,1,0:T(8,128)(2,1)}, u32[]{:S(2)}) copy-start(bf16[2,64,4096]{2,1,0:T(8,128)(2,1)} %hidden_ref.3) | copy-start | bytes 3145732
  31.3 9.8 %collective-permute-start.3 = (bf16[4,416,128]{2,1,0:T(8,128)(2,1)S(1)}, bf16[4,416,128]{2,1,0:T(8,128)(2,1)S(1)}, u32[]{:S(2)}, u32[]{:S(2)}) collective-permute-start(bf16[4,416,128]{2,1,0:T(8,128)(2,1)S(1)} %slice.183), channel_id=1, source_target_pairs={{0,4},{4,0},{1,5},{5,1},{2,6},{6,2},{3,7},{7,3},{8,12},{12,8},{9,1... | collective-permute-start | bytes 1277960 | tf_op jit(solution)/shard_map/ppermute | solution.py:52
  32.9 9.4 %collective-permute-start.4 = (bf16[2,64,1280]{2,1,0:T(8,128)(2,1)S(1)}, bf16[2,64,1280]{2,1,0:T(8,128)(2,1)}, u32[]{:S(2)}, u32[]{:S(2)}) collective-permute-start(bf16[2,64,1280]{2,1,0:T(8,128)(2,1)S(1)} %collective-permute-done.1.refs_13_.refs_17_), channel_id=1, source_target_pairs={{0,8},{8,16},{16,24},{1,9},{9,17},{17,25},{2,10},{10,18},{18,26},{... | collective-permute-start | bytes 983048 | tf_op jit(solution)/shard_map/ppermute | solution.py:47
  42.3 5.8 %collective-permute-start.5 = (bf16[8,416,128]{2,1,0:T(8,128)(2,1)S(1)}, bf16[8,416,128]{2,1,0:T(8,128)(2,1)}, u32[]{:S(2)}, u32[]{:S(2)}) collective-permute-start(bf16[8,416,128]{2,1,0:T(8,128)(2,1)S(1)} %pad_maximum_fusion.own_ref), channel_id=1, source_target_pairs={{0,1},{1,0},{2,3},{3,2},{4,5},{5,4},{6,7},{7,6},{8,9},{9,8},{10,11... | collective-permute-start | bytes 2555912 | tf_op jit(solution)/shard_map/ppermute | solution.py:52
  42.3 0.9 slice-start.1
  42.3 0.9 slice-start.3
  43.2 12.4 %collective-permute-start.6 = (bf16[2,64,1280]{2,1,0:T(8,128)(2,1)}, bf16[2,64,1280]{2,1,0:T(8,128)(2,1)S(1)}, u32[]{:S(2)}, u32[]{:S(2)}) collective-permute-start(bf16[2,64,1280]{2,1,0:T(8,128)(2,1)} %collective-permute-done.4.refs_14_.refs_18_), channel_id=1, source_target_pairs={{0,8},{8,16},{16,24},{1,9},{9,17},{17,25},{2,10},{10,18},{18,26},{... | collective-permute-start | bytes 983048 | tf_op jit(solution)/shard_map/ppermute | solution.py:47
  49.8 1.0 copy-start.2
  55.7 0.7 copy-start.10
  56.4 14.6 %collective-permute-start.7 = (bf16[2,64,128]{2,1,0:T(8,128)(2,1)S(1)}, bf16[2,64,128]{2,1,0:T(8,128)(2,1)S(1)}, u32[]{:S(2)}, u32[]{:S(2)}) collective-permute-start(bf16[2,64,128]{2,1,0:T(8,128)(2,1)S(1)} %get-tuple-element.42.refs_8_), channel_id=1, source_target_pairs={{0,8},{8,16},{16,24},{1,9},{9,17},{17,25},{2,10},{10,18},{18,26},{... | collective-permute-start | bytes 98312 | tf_op jit(solution)/shard_map/ppermute | solution.py:47
  60.7 11.7 %collective-permute-start.8 = (bf16[2,64,128]{2,1,0:T(8,128)(2,1)S(1)}, bf16[2,64,128]{2,1,0:T(8,128)(2,1)S(1)}, u32[]{:S(2)}, u32[]{:S(2)}) collective-permute-start(bf16[2,64,128]{2,1,0:T(8,128)(2,1)S(1)} %get-tuple-element.42.refs_8_), channel_id=1, source_target_pairs={{0,16},{8,24},{1,17},{9,25},{2,18},{10,26},{3,19},{11,27},{4,20},{... | collective-permute-start | bytes 98312 | tf_op jit(solution)/shard_map/ppermute | solution.py:47
  66.0 6.4 %collective-permute-start.9 = (bf16[2,64,128]{2,1,0:T(8,128)(2,1)S(1)}, bf16[2,64,128]{2,1,0:T(8,128)(2,1)S(1)}, u32[]{:S(2)}, u32[]{:S(2)}) collective-permute-start(bf16[2,64,128]{2,1,0:T(8,128)(2,1)S(1)} %get-tuple-element.42.refs_8_), channel_id=1, source_target_pairs={{0,24},{1,25},{2,26},{3,27},{4,28},{5,29},{6,30},{7,31}} | collective-permute-start | bytes 98312 | tf_op jit(solution)/shard_map/ppermute | solution.py:47
  68.4 20.5 %collective-permute-start.10 = (bf16[2,64,768]{2,1,0:T(8,128)(2,1)S(1)}, bf16[2,64,768]{2,1,0:T(8,128)(2,1)S(1)}, u32[]{:S(2)}, u32[]{:S(2)}) collective-permute-start(bf16[2,64,768]{2,1,0:T(8,128)(2,1)S(1)} %pad_maximum_fusion.4.refs_12_.refs_16_), channel_id=1, source_target_pairs={{0,8},{8,16},{16,24},{1,9},{9,17},{17,25},{2,10},{10,18},{18,26},{... | collective-permute-start | bytes 589832 | tf_op jit(solution)/shard_map/ppermute | solution.py:47
  69.8 19.2 %collective-permute-start.11 = (bf16[2,64,768]{2,1,0:T(8,128)(2,1)S(1)}, bf16[2,64,768]{2,1,0:T(8,128)(2,1)S(1)}, u32[]{:S(2)}, u32[]{:S(2)}) collective-permute-start(bf16[2,64,768]{2,1,0:T(8,128)(2,1)S(1)} %pad_maximum_fusion.4.refs_12_.refs_16_), channel_id=1, source_target_pairs={{0,16},{8,24},{1,17},{9,25},{2,18},{10,26},{3,19},{11,27},{4,20},{... | collective-permute-start | bytes 589832 | tf_op jit(solution)/shard_map/ppermute | solution.py:47
  71.1 17.9 %collective-permute-start.12 = (bf16[2,64,768]{2,1,0:T(8,128)(2,1)S(1)}, bf16[2,64,768]{2,1,0:T(8,128)(2,1)S(1)}, u32[]{:S(2)}, u32[]{:S(2)}) collective-permute-start(bf16[2,64,768]{2,1,0:T(8,128)(2,1)S(1)} %pad_maximum_fusion.4.refs_12_.refs_16_), channel_id=1, source_target_pairs={{0,24},{1,25},{2,26},{3,27},{4,28},{5,29},{6,30},{7,31}} | collective-permute-start | bytes 589832 | tf_op jit(solution)/shard_map/ppermute | solution.py:47
  72.4 1.2 copy-start.1
  73.6 1.0 copy-start.9
  74.6 1.0 copy-start.11
  97.8 0.7 copy-start.4
  97.8 0.8 copy-start.6
  98.5 5.8 %collective-permute-start.16 = (bf16[2,64,64]{2,1,0:T(8,128)(2,1)S(1)}, bf16[2,64,64]{2,1,0:T(8,128)(2,1)S(1)}, u32[]{:S(2)}, u32[]{:S(2)}) collective-permute-start(bf16[2,64,64]{2,1,0:T(8,128)(2,1)S(1)} %get-tuple-element.79), channel_id=1, source_target_pairs={{8,0},{16,8},{24,16},{9,1},{17,9},{25,17},{10,2},{18,10},{26,18},{... | collective-permute-start | bytes 49160 | tf_op jit(solution)/shard_map/ppermute | solution.py:47
  99.8 7.1 %collective-permute-start.17 = (bf16[2,64,64]{2,1,0:T(8,128)(2,1)S(1)}, bf16[2,64,64]{2,1,0:T(8,128)(2,1)S(1)}, u32[]{:S(2)}, u32[]{:S(2)}) collective-permute-start(bf16[2,64,64]{2,1,0:T(8,128)(2,1)S(1)} %get-tuple-element.81), channel_id=1, source_target_pairs={{16,0},{24,8},{17,1},{25,9},{18,2},{26,10},{19,3},{27,11},{20,4},{... | collective-permute-start | bytes 49160 | tf_op jit(solution)/shard_map/ppermute | solution.py:47
  101.1 8.8 %collective-permute-start.18 = (bf16[2,64,64]{2,1,0:T(8,128)(2,1)S(1)}, bf16[2,64,64]{2,1,0:T(8,128)(2,1)S(1)}, u32[]{:S(2)}, u32[]{:S(2)}) collective-permute-start(bf16[2,64,64]{2,1,0:T(8,128)(2,1)S(1)} %get-tuple-element.80), channel_id=1, source_target_pairs={{24,0},{25,1},{26,2},{27,3},{28,4},{29,5},{30,6},{31,7}} | collective-permute-start | bytes 49160 | tf_op jit(solution)/shard_map/ppermute | solution.py:47
  111.6 2.6 %collective-permute-start.19 = (bf16[8,2,208,128]{3,2,1,0:T(8,128)(2,1)}, bf16[8,2,208,128]{3,2,1,0:T(8,128)(2,1)S(1)}, u32[]{:S(2)}, u32[]{:S(2)}) collective-permute-start(bf16[8,2,208,128]{3,2,1,0:T(8,128)(2,1)} %get-tuple-element.66), channel_id=1, source_target_pairs={{0,1},{1,0},{2,3},{3,2},{4,5},{5,4},{6,7},{7,6},{8,9},{9,8},{10,11... | collective-permute-start | bytes 2555912 | tf_op jit(solution)/shard_map/ppermute | solution.py:52
  111.6 10.6 %collective-permute-start.13 = (bf16[2,64,1024]{2,1,0:T(8,128)(2,1)S(1)}, bf16[2,64,1024]{2,1,0:T(8,128)(2,1)S(1)}, u32[]{:S(2)}, u32[]{:S(2)}) collective-permute-start(bf16[2,64,1024]{2,1,0:T(8,128)(2,1)S(1)} %get-tuple-element.57), channel_id=1, source_target_pairs={{8,0},{16,8},{24,16},{9,1},{17,9},{25,17},{10,2},{18,10},{26,18},{... | collective-permute-start | bytes 786440 | tf_op jit(solution)/shard_map/ppermute | solution.py:47
  114.2 9.5 %copy-start.5 = (bf16[2,64,1024]{2,1,0:T(8,128)(2,1)S(1)}, bf16[2,64,1024]{2,1,0:T(8,128)(2,1)}, u32[]{:S(2)}) copy-start(bf16[2,64,1024]{2,1,0:T(8,128)(2,1)} %copy-done.4) | copy-start | bytes 786436
  114.2 25.2 %copy-start.7 = (bf16[2,64,1024]{2,1,0:T(8,128)(2,1)S(1)}, bf16[2,64,1024]{2,1,0:T(8,128)(2,1)}, u32[]{:S(2)}) copy-start(bf16[2,64,1024]{2,1,0:T(8,128)(2,1)} %copy-done.6) | copy-start | bytes 786436
  115.3 39.6 %copy-start.3 = (bf16[4096,128]{1,0:T(8,128)(2,1)S(1)}, bf16[4096,128]{1,0:T(8,128)(2,1)}, u32[]{:S(2)}) copy-start(bf16[4096,128]{1,0:T(8,128)(2,1)} %copy-done.2) | copy-start | bytes 3145732
  122.2 11.7 %collective-permute-start.20 = (bf16[8,1,208,128]{3,2,1,0:T(8,128)(2,1)}, bf16[8,1,208,128]{3,2,1,0:T(8,128)(2,1)S(1)}, u32[]{:S(2)}, u32[]{:S(2)}) collective-permute-start(bf16[8,1,208,128]{3,2,1,0:T(8,128)(2,1)} %get-tuple-element.67), channel_id=1, source_target_pairs={{0,2},{1,3},{2,0},{3,1},{4,6},{5,7},{6,4},{7,5},{8,10},{9,11},{10,... | collective-permute-start | bytes 1277960 | tf_op jit(solution)/shard_map/ppermute | solution.py:52
  123.7 15.0 %collective-permute-start.14 = (bf16[2,64,1024]{2,1,0:T(8,128)(2,1)S(1)}, bf16[2,64,1024]{2,1,0:T(8,128)(2,1)S(1)}, u32[]{:S(2)}, u32[]{:S(2)}) collective-permute-start(bf16[2,64,1024]{2,1,0:T(8,128)(2,1)S(1)} %copy-done.5), channel_id=1, source_target_pairs={{16,0},{24,8},{17,1},{25,9},{18,2},{26,10},{19,3},{27,11},{20,4},{... | collective-permute-start | bytes 786440 | tf_op jit(solution)/shard_map/ppermute | solution.py:47
  138.8 7.2 %collective-permute-start.21 = (bf16[4,208,128]{2,1,0:T(8,128)(2,1)S(1)}, bf16[4,208,128]{2,1,0:T(8,128)(2,1)S(1)}, u32[]{:S(2)}, u32[]{:S(2)}) collective-permute-start(bf16[4,208,128]{2,1,0:T(8,128)(2,1)S(1)} %fusion.2), channel_id=1, source_target_pairs={{0,4},{4,0},{1,5},{5,1},{2,6},{6,2},{3,7},{7,3},{8,12},{12,8},{9,1... | collective-permute-start | bytes 638984 | tf_op jit(solution)/shard_map/ppermute | solution.py:42
  139.4 11.6 %collective-permute-start.15 = (bf16[2,64,1024]{2,1,0:T(8,128)(2,1)S(1)}, bf16[2,64,1024]{2,1,0:T(8,128)(2,1)S(1)}, u32[]{:S(2)}, u32[]{:S(2)}) collective-permute-start(bf16[2,64,1024]{2,1,0:T(8,128)(2,1)S(1)} %copy-done.7), channel_id=1, source_target_pairs={{24,0},{25,1},{26,2},{27,3},{28,4},{29,5},{30,6},{31,7}} | collective-permute-start | bytes 786440 | tf_op jit(solution)/shard_map/ppermute | solution.py:47
  151.1 6.1 %collective-permute-start.22 = (bf16[208,128]{1,0:T(8,128)(2,1)S(1)}, bf16[208,128]{1,0:T(8,128)(2,1)S(1)}, u32[]{:S(2)}, u32[]{:S(2)}) collective-permute-start(bf16[208,128]{1,0:T(8,128)(2,1)S(1)} %get-tuple-element.76), channel_id=1, source_target_pairs={{0,8},{8,16},{16,24},{24,0},{1,9},{9,17},{17,25},{25,1},{2,10},{10... | collective-permute-start | bytes 159752 | tf_op jit(solution)/shard_map/ppermute | solution.py:42
  151.1 6.6 %collective-permute-start.23 = (bf16[208,128]{1,0:T(8,128)(2,1)S(1)}, bf16[208,128]{1,0:T(8,128)(2,1)S(1)}, u32[]{:S(2)}, u32[]{:S(2)}) collective-permute-start(bf16[208,128]{1,0:T(8,128)(2,1)S(1)} %get-tuple-element.78), channel_id=1, source_target_pairs={{0,16},{8,24},{16,0},{24,8},{1,17},{9,25},{17,1},{25,9},{2,18},{10... | collective-permute-start | bytes 159752 | tf_op jit(solution)/shard_map/ppermute | solution.py:42
  151.2 6.5 %collective-permute-start.24 = (bf16[208,128]{1,0:T(8,128)(2,1)S(1)}, bf16[208,128]{1,0:T(8,128)(2,1)S(1)}, u32[]{:S(2)}, u32[]{:S(2)}) collective-permute-start(bf16[208,128]{1,0:T(8,128)(2,1)S(1)} %get-tuple-element.77), channel_id=1, source_target_pairs={{0,24},{8,0},{16,8},{24,16},{1,25},{9,1},{17,9},{25,17},{2,26},{10... | collective-permute-start | bytes 159752 | tf_op jit(solution)/shard_map/ppermute | solution.py:42
  157.8 3.6 %collective-permute-start.25 = (bf16[208,128]{1,0:T(8,128)(2,1)S(1)}, bf16[208,128]{1,0:T(8,128)(2,1)S(1)}, u32[]{:S(2)}, u32[]{:S(2)}) collective-permute-start(bf16[208,128]{1,0:T(8,128)(2,1)S(1)} %fusion.5), channel_id=1, source_target_pairs={{0,3},{1,2},{2,1},{3,0},{4,7},{5,6},{6,5},{7,4},{8,11},{9,10},{10,... | collective-permute-start | bytes 159752 | tf_op jit(solution)/shard_map/ppermute | solution.py:52
  157.9 4.7 %collective-permute-start.26 = (bf16[208,128]{1,0:T(8,128)(2,1)S(1)}, bf16[208,128]{1,0:T(8,128)(2,1)S(1)}, u32[]{:S(2)}, u32[]{:S(2)}) collective-permute-start(bf16[208,128]{1,0:T(8,128)(2,1)S(1)} %fusion.5), channel_id=1, source_target_pairs={{0,2},{1,3},{2,0},{3,1},{4,6},{5,7},{6,4},{7,5},{8,10},{9,11},{10,... | collective-permute-start | bytes 159752 | tf_op jit(solution)/shard_map/ppermute | solution.py:52
  158.5 4.1 %collective-permute-start.27 = (bf16[208,128]{1,0:T(8,128)(2,1)S(1)}, bf16[208,128]{1,0:T(8,128)(2,1)S(1)}, u32[]{:S(2)}, u32[]{:S(2)}) collective-permute-start(bf16[208,128]{1,0:T(8,128)(2,1)S(1)} %fusion.5), channel_id=1, source_target_pairs={{0,1},{1,0},{2,3},{3,2},{4,5},{5,4},{6,7},{7,6},{8,9},{9,8},{10,11... | collective-permute-start | bytes 159752 | tf_op jit(solution)/shard_map/ppermute | solution.py:52

commit v4 on v3

--- a/solution.py
+++ b/solution.py
@@ -70,9 +70,8 @@
     low_refs, k_refs, v_refs = take(shards), take(shards), take(shards)
     before = take(2) if earlier_count else None
     take(earlier_count)
-    att_ref, gq_ref, guq_ref, guv_ref = take(4)
+    att_ref, gq_ref, guq_ref, guv_ref, lgq_ref, lgv_ref = take(6)
     gv_refs = take(shards)
-    lgq_ref, lgv_ref = take(2)
 
     seqs, tokens = q_ref.shape[0], q_ref.shape[1]
     parts, part_rows = guq_ref.shape[1:3]
@@ -109,17 +108,21 @@
 
     cos4 = jnp.concatenate([cos] * GROUP, axis=0)
     sin4 = jnp.concatenate([sin] * GROUP, axis=0)
-    for s in range(seqs):
-        low = low_refs[0][s]
-        low_q = low[:, :RANK]
-        delta = heads(mm(low_q, upq, 1, 0))
+    every = range(seqs)
+    low_q = jnp.concatenate([low_refs[0][s][:, :RANK] for s in every], axis=0)
+    low_v = jnp.concatenate([r[s][:, RANK:] for s in every for r in low_refs], axis=0)
+    query_delta = mm(low_q, upq, 1, 0)
+    value_delta = mm(low_v, upv, 1, 0)
+    backs, gvs = [], []
+    for s in every:
+        delta = heads(query_delta[s * tokens : (s + 1) * tokens])
         delta = delta * cos4 + pltpu.roll(delta, HEAD_DIM // 2, 1) * sin4
         q = (heads(q_ref[s]).astype(f32) + delta).astype(bf16)
         g = heads(g_ref[s])
-        low_v = jnp.concatenate([r[s][:, RANK:] for r in low_refs], axis=0)
         keys = jnp.concatenate([r[s] for r in k_refs] + [pk_ref[s]], axis=0)
         base = jnp.concatenate([r[s] for r in v_refs], axis=0).astype(f32)
-        vals = jnp.concatenate([(base + mm(low_v, upv, 1, 0)).astype(bf16), pv_ref[s]], axis=0)
+        vals = (base + value_delta[s * span : (s + 1) * span]).astype(bf16)
+        vals = jnp.concatenate([vals, pv_ref[s]], axis=0)
 
         scores = mm(q, keys, 1, 1) * (scale * LOG2_E) + bias
         top = jnp.max(scores, axis=-1, keepdims=True)
@@ -136,16 +139,20 @@
         gq_ref[s] = lanes(gq)
         gq32 = gq.astype(f32)
         back = (gq32 * cos4 - pltpu.roll(gq32, HEAD_DIM // 2, 1) * sin4).astype(bf16)
-        back = lanes(back)
-        lgq_ref[s] += mm(back, upq, 1, 1)
+        backs.append(lanes(back))
         gv = mm(weights[:, :span], g, 0, 0).astype(bf16)
+        gvs.append(gv)
         for k in range(shards):
             gv_refs[k][s] = gv[k * tokens : (k + 1) * tokens]
-        lgv_ref[s] += mm(gv, upv, 1, 1)
-        up_q = mm(low_q, back, 0, 0)
-        up_v = mm(low_v, gv, 0, 0)
-        grad_up_q = up_q if s == 0 else grad_up_q + up_q
-        grad_up_v = up_v if s == 0 else grad_up_v + up_v
+    back = jnp.concatenate(backs, axis=0)
+    gv = jnp.concatenate(gvs, axis=0)
+    low_grad_q = mm(back, upq, 1, 1)
+    low_grad_v = mm(gv, upv, 1, 1)
+    for s in every:
+        lgq_ref[s] += low_grad_q[s * tokens : (s + 1) * tokens]
+        lgv_ref[s] += low_grad_v[s * span : (s + 1) * span]
+    grad_up_q = mm(low_q, back, 0, 0)
+    grad_up_v = mm(low_v, gv, 0, 0)
     grad_up_q, grad_up_v = grad_up_q.astype(bf16), grad_up_v.astype(bf16)
     for p in range(parts):
         rows = slice(p * part_rows, (p + 1) * part_rows)
@@ -168,7 +175,7 @@
 
     spec = pl.BlockSpec
     q_spec = spec((seqs, tokens, WIDE), lambda g: (0, 0, first + g))
-    gv_spec = spec((seqs, tokens, HEAD_DIM), lambda g: (0, 0, first + g))
+    gv_spec = spec((seqs, tokens, HEAD_DIM), lambda g: (0, 0, g))
     past_block = (seqs, past_len, HEAD_DIM)
     in_specs = [
         spec(memory_space=pltpu.SMEM),
@@ -194,30 +201,34 @@
         shape(query_base.shape, bf16),
         shape((HEADS, parts, RANK // parts, HEAD_DIM), bf16),
         shape((KV_HEADS, parts, RANK // parts, HEAD_DIM), bf16),
-    ] + [shape((seqs, tokens, KV), bf16)] * shards
+    ]
     placed_specs = [
         q_spec,
         q_spec,
         spec((GROUP, parts, RANK // parts, HEAD_DIM), lambda g: (first + g, 0, 0, 0)),
         spec((1, parts, RANK // parts, HEAD_DIM), lambda g: (first + g, 0, 0, 0)),
-    ] + [gv_spec] * shards
+    ]
     aliases = {}
     placed = len(placed_shapes)
     if earlier is not None:
         in_specs += [whole(low_q_shape), whole(low_v_shape)]
-        operands += list(earlier[placed:])
+        operands += list(earlier[placed : placed + 2])
         aliases = {len(operands) + i: i for i in range(placed)}
         in_specs += [spec(memory_space=pl.ANY)] * placed
         operands += list(earlier[:placed])
-    pairs = seqs * groups * GROUP * tokens * (shards * tokens + past_len)
+    scores = GROUP * tokens * (shards * tokens + past_len)
+    pairs = seqs * groups * scores
+    grant = min(12 * 2**20 + 96 * scores, 48 * 2**20)
     return pl.pallas_call(
         functools.partial(attention_kernel, shards, placed if earlier is not None else 0),
         grid=(groups,),
         in_specs=in_specs,
-        out_specs=placed_specs + [whole(low_q_shape), whole(low_v_shape)],
-        out_shape=placed_shapes + [low_q_shape, low_v_shape],
+        out_specs=placed_specs + [whole(low_q_shape), whole(low_v_shape)] + [gv_spec] * shards,
+        out_shape=placed_shapes
+        + [low_q_shape, low_v_shape]
+        + [shape((seqs, tokens, groups * HEAD_DIM), bf16)] * shards,
         input_output_aliases=aliases,
-        compiler_params=pltpu.CompilerParams(vmem_limit_bytes=48 * 1024 * 1024),
+        compiler_params=pltpu.CompilerParams(vmem_limit_bytes=grant),
         cost_estimate=pl.CostEstimate(
             flops=pairs * HEAD_DIM * 28, bytes_accessed=16 * 1024 * 1024, transcendentals=pairs
         ),
@@ -247,10 +258,9 @@
         low_ref[s] = low[s * low_ref.shape[1] : (s + 1) * low_ref.shape[1]]
 
 
-def adapters_packed(hidden, adapter_down, adapter_up, own_past, after):
-    sp, fs = lax.axis_size("sp"), lax.axis_size("fsdp")
-    z, x, r = (lax.axis_index(a) for a in ("sp", "fsdp", "rep"))
-    c = lax.rem(r, 2)
+def pack_adapters(adapter_down, adapter_up, own_past):
+    sp = lax.axis_size("sp")
+    c = lax.rem(lax.axis_index("rep"), 2)
     down_rows, up_rows = adapter_down.shape[0] // 2, RANK // 2
     blocks = adapter_up.shape[1] // HEAD_DIM
     down = lax.dynamic_slice_in_dim(adapter_down, c * down_rows, down_rows, 0)
@@ -261,17 +271,21 @@
     step = 1
     while step < sp:
         buf = jnp.concatenate([buf, partner(buf, "sp", step)], axis=0)
-        if step == 1:
-            buf = tie(buf, after[0])
         step *= 2
     seqs, each = own_past.shape[:2]
     past = buf[:, rows:].reshape(sp, seqs, each, -1).swapaxes(0, 1).reshape(seqs, sp * each, -1)
-    buf = buf[:, :rows]
+    return buf[:, :rows], past
+
+
+def adapters_packed(hidden, buf, before_swap):
+    fs = lax.axis_size("fsdp")
+    z, x, r = (lax.axis_index(a) for a in ("sp", "fsdp", "rep"))
+    c = lax.rem(r, 2)
     step = 1
     while step < fs:
         buf = jnp.concatenate([buf, partner(buf, "fsdp", step)], axis=0)
         step *= 2
-    other = partner(tie(buf, after[1]), "rep", 1)
+    other = partner(tie(buf, before_swap), "rep", 1)
     index = jnp.stack([z, x, c]).astype(jnp.int32)
     vmem = pl.BlockSpec(memory_space=pltpu.VMEM)
     seqs, tokens = hidden.shape[:2]
@@ -284,25 +298,23 @@
             jax.ShapeDtypeStruct((HEADS + KV_HEADS, RANK, HEAD_DIM), bf16),
             jax.ShapeDtypeStruct((seqs, tokens, 2 * RANK), bf16),
         ],
-        compiler_params=pltpu.CompilerParams(vmem_limit_bytes=32 * 1024 * 1024),
+        compiler_params=pltpu.CompilerParams(vmem_limit_bytes=16 * 1024 * 1024),
         cost_estimate=pl.CostEstimate(
             flops=2 * seqs * tokens * D * 2 * RANK, bytes_accessed=5 * 2**20, transcendentals=0
         ),
         name="low_rank",
     )(index, buf, other, hidden)
-    return down_full, up_blocks, low, past
-
-
-def adapters_plain(hidden, adapter_down, adapter_up, own_past, after):
-    sp = lax.axis_size("sp")
+    return down_full, up_blocks, low
+
+
+def adapters_plain(hidden, adapter_down, adapter_up):
     seqs, tokens = hidden.shape[:2]
-    past = jnp.concatenate([own_past] + [cyclic(own_past, "sp", k) for k in range(1, sp)], axis=1)
     down_full = lax.all_gather(adapter_down, ("sp", "fsdp"), axis=0, tiled=True)
     up_full = lax.all_gather(adapter_up, ("sp", "fsdp"), axis=1, tiled=True)
     rows = hidden.reshape(seqs * tokens, D)
     low = jnp.dot(rows, down_full, preferred_element_type=f32).astype(bf16)
     up_blocks = up_full.reshape(RANK, HEADS + KV_HEADS, HEAD_DIM).swapaxes(0, 1)
-    return down_full, up_blocks, low.reshape(seqs, tokens, 2 * RANK), past
+    return down_full, up_blocks, low.reshape(seqs, tokens, 2 * RANK)
 
 
 def grad_hidden_kernel(low_ref, down_ref, out_ref):
@@ -323,7 +335,7 @@
         ],
         out_specs=pl.BlockSpec((seqs, tokens, columns), lambda i: (0, 0, i)),
         out_shape=jax.ShapeDtypeStruct((seqs, tokens, D), bf16),
-        compiler_params=pltpu.CompilerParams(vmem_limit_bytes=32 * 1024 * 1024),
+        compiler_params=pltpu.CompilerParams(vmem_limit_bytes=16 * 1024 * 1024),
         cost_estimate=pl.CostEstimate(
             flops=2 * seqs * tokens * D * 2 * RANK, bytes_accessed=2**21, transcendentals=0
         ),
@@ -369,7 +381,7 @@
             out_specs=[vmem] * 2,
             out_shape=[packed] * 2,
             scratch_shapes=[pltpu.VMEM((rp, down_rows, 2 * RANK), bf16)],
-            compiler_params=pltpu.CompilerParams(vmem_limit_bytes=32 * 1024 * 1024),
+            compiler_params=pltpu.CompilerParams(vmem_limit_bytes=16 * 1024 * 1024),
             cost_estimate=pl.CostEstimate(
                 flops=2 * hidden.size * 2 * RANK, bytes_accessed=5 * 2**20, transcendentals=0
             ),
@@ -387,37 +399,43 @@
     return send, keep
 
 
-def finish_grads(send, keep, before):
+def finish_grads(send, keep, values):
     sp, fs, rp = (lax.axis_size(a) for a in ("sp", "fsdp", "rep"))
-    z, x, r = (lax.axis_index(a) for a in ("sp", "fsdp", "rep"))
+    z, r = lax.axis_index("sp"), lax.axis_index("rep")
     shards, _, rows, lanes = send.shape
     got = partner(send, "rep", 1)
-    for b in range(1, rp.bit_length() - 1):
-        shape = (shards, rp >> (b + 1), 2, rows, lanes)
-        mine = lax.rem(lax.div(r, 1 << b), 2)
-
-        def half(i):
-            return sum(
-                lax.dynamic_index_in_dim(a.reshape(shape), i, 2, keepdims=False).astype(f32)
-                for a in (keep, got)
-            ).astype(bf16)
-
-        send, keep = half(1 - mine), half(mine)
-        send = tie(send, before[0])
-        got = partner(send, "rep", 1 << b)
-    shape = (sp, fs, rows, lanes)
-
-    def over_fsdp(i):
-        return sum(
-            lax.dynamic_index_in_dim(a.reshape(shape), i, 1, keepdims=False).astype(f32)
-            for a in (keep, got)
-        ).astype(bf16)
-
-    total = over_fsdp(x).astype(f32)
-    for k in range(1, fs):
-        send = tie(over_fsdp(lax.rem(x + k, fs)), *before[:2])
-        total = total + cyclic(send, "fsdp", k).astype(f32)
-    over_sp = tie(total.astype(bf16), *before)
+    then = [along(tie(v, got), "sp", -k) for k, v in enumerate(values, 1)]
+    fs_bits, rep_bits = fs.bit_length() - 1, rp.bit_length() - 2
+    labels = [("fsdp", b) for b in reversed(range(fs_bits))]
+    labels += [("rep", b + 1) for b in reversed(range(rep_bits))]
+    shape = (sp,) + (2,) * len(labels) + (rows, lanes)
+    terms = [a.reshape(shape) for a in (keep, got)]
+
+    def halve(terms, order, before):
+        left = list(labels)
+        for step, label in enumerate(order):
+            axis, bit = label
+            dim = 1 + left.index(label)
+            left.remove(label)
+            mine = lax.rem(lax.div(lax.axis_index(axis), 1 << bit), 2)
+
+            def pick(i):
+                parts = [lax.dynamic_index_in_dim(a, i, dim, keepdims=False) for a in terms]
+                return sum(a.astype(f32) for a in parts).astype(bf16)
+
+            send = pick(1 - mine)
+            if step == 1:
+                send = tie(send, *before)
+            terms = [pick(mine), partner(send, axis, 1 << bit)]
+        return sum(a.astype(f32) for a in terms).astype(bf16)
+
+    cut = rows // 32 * 16
+    first_rep, first_fsdp = labels[::-1], labels
+    over_sp = halve([a[..., cut:, :] for a in terms], first_rep, then[:1])
+    if cut:
+        other = halve([a[..., :cut, :] for a in terms], first_fsdp, ())
+        over_sp = jnp.concatenate([other, over_sp], axis=1)
+    over_sp = tie(over_sp, *then)
     total = lax.dynamic_index_in_dim(over_sp, z, 0, keepdims=False).astype(f32)
     for k in range(1, sp):
         send = lax.dynamic_index_in_dim(over_sp, lax.rem(z + k, sp), 0, keepdims=False)
@@ -440,7 +458,7 @@
             up = [up[lo : lo + up_rows] for lo in range(0, up.shape[0], up_rows)]
             up = jnp.concatenate(up, axis=1)
         ups.append(up.reshape(up_rows, up_width))
-    return grad_down, jnp.concatenate(ups, axis=0)
+    return grad_down, jnp.concatenate(ups, axis=0), then, over_sp
 
 
 def body(
@@ -464,32 +482,43 @@
         cols = slice(first * HEAD_DIM, last * HEAD_DIM)
         own_kvs.append(jnp.concatenate([key_span[:, :, cols], value_base[:, :, cols]], axis=2))
     early = [own_kvs[0]]
-    for k in range(1, sp):
+    even = adapter_up.shape[1] % HEAD_DIM == 0
+    if even:
+        buf, past = pack_adapters(adapter_down, adapter_up, own_past)
+    else:
+        buf = own_past
+        past = [own_past] + [cyclic(own_past, "sp", k) for k in range(1, sp)]
+        past = jnp.concatenate(past, axis=1)
+    early.append(along(tie(early[0], buf), "sp", 1))
+    for k in range(2, sp):
         early.append(along(early[k - 1], "sp", 1))
-
-    even = adapter_up.shape[1] % HEAD_DIM == 0
-    adapters = adapters_packed if even else adapters_plain
-    down_full, up_blocks, low_own, past = adapters(
-        hidden, adapter_down, adapter_up, own_past, (early[1], early[min(2, sp - 1)])
-    )
-    low_own = tie(low_own, early[-1])
-    late = [own_kvs[1]] + [along(tie(own_kvs[1], low_own), "sp", k) for k in range(1, sp)]
-    lows = [low_own] + [along(low_own, "sp", k) for k in range(1, sp)]
+    if even:
+        down_full, up_blocks, low_own = adapters_packed(hidden, buf, early[1])
+    else:
+        down_full, up_blocks, low_own = adapters_plain(hidden, adapter_down, adapter_up)
+    low_sent = tie(low_own, early[min(2, sp - 1)])
+    lows = [low_own] + [along(low_sent, "sp", k) for k in range(1, sp)]
+    own_late = tie(own_kvs[1], low_own, early[-1])
+    late = [own_kvs[1]] + [along(own_late, "sp", k) for k in range(1, sp)]
     cos, sin = rotary_tables(tokens, past_len + z * tokens)
     place = z.astype(jnp.int32).reshape(1)
 
     made = None
+    value_own, value_got = [], []
     for (first, last), kvs in zip(CHUNKS, (early, late)):
         made = attention_chunk(
             first, last, place, query_base, grad_out, up_blocks, past, cos, sin, lows, kvs, made
         )
-    attended, grad_query, guq, guv = made[:4]
-    gvs = made[4 : 4 + sp]
-    low_grad_q, low_grad_v = made[4 + sp :]
+        gvs = made[6:]
+        value_own.append(gvs[0])
+        if last < KV_HEADS:
+            value_got.append([along(gvs[k], "sp", -k) for k in range(1, sp)])
+    attended, grad_query, guq, guv, low_grad_q, low_grad_v = made[:6]
 
     low_v_total = low_grad_v[:, :tokens]
     for k in range(1, sp):
         part = low_grad_v[:, k * tokens : (k + 1) * tokens].astype(bf16)
+        part = tie(part, *value_got[0])
         low_v_total = low_v_total + along(part, "sp", -k).astype(f32)
     low_grad = (
         jnp.concatenate([low_grad_q, low_v_total], axis=2)
@@ -497,17 +526,21 @@
         .reshape(seqs * tokens, 2 * RANK)
     )
     send, keep = packed_grads(hidden, low_grad, guq, guv, sp * fs)
-    value_parts = [along(gvs[k], "sp", -k) for k in range(1, sp)]
-    grad_down, grad_up = finish_grads(send, keep, value_parts)
-    grad_hidden = grad_hidden_of(low_grad, down_full, seqs, tokens)
-
-    grad_value = gvs[0].astype(f32)
-    for part in value_parts:
-        grad_value = grad_value + part.astype(f32)
+    grad_down, grad_up, got, mark = finish_grads(send, keep, gvs[1:])
+    value_got.append(got)
+    grad_hidden = grad_hidden_of(tie(low_grad, mark), down_full, seqs, tokens)
+
+    sums = []
+    for own, got in zip(value_own, value_got):
+        total = own.astype(f32)
+        for part in got:
+            total = total + part.astype(f32)
+        sums.append(total.astype(bf16))
+    grad_value = jnp.concatenate(sums, axis=2)
     return (
         attended,
         grad_query,
-        grad_value.astype(bf16),
+        grad_value,
         grad_hidden,
         grad_down,
         grad_up,

time: 165 us -> 148 us (0.90)
  waiting for transfers between devices: 70.3 us -> 53 us
  starting transfers between devices: 49.2 us -> 58 us
  Pallas kernels: 27.5 us -> 21.8 us
  local copies, waits for them, and re-layouts: 9.75 us -> 7.23 us
    ppermute x9 -> x12, waiting for transfers between devices: 36.1 us -> 28 us  [partner(): return lax.ppermute(x, axis, [(i, i ^ mask) for i in range(n)])]
    ppermute x15 -> x18, waiting for transfers between devices: 28.3 us -> 21.5 us  [along(): lax.ppermute(x, axis, [(i, i + shift) for i in range(n) if 0 <= i + shift...]
    pallas_call x2, Pallas kernels: 22.1 us -> 16.3 us  [attention_chunk(): pl.pallas_call(functools.partial(attention_kernel, shards, placed if earl...]
    ppermute x9 -> x12, starting transfers between devices: 9.28 us -> 14.5 us  [partner(): return lax.ppermute(x, axis, [(i, i ^ mask) for i in range(n)])]
    ppermute x15 -> x18, starting transfers between devices: 35.4 us -> 39.7 us  [along(): lax.ppermute(x, axis, [(i, i + shift) for i in range(n) if 0 <= i + shift...]
    convert_element_type x4 -> x10, other arithmetic: 4.04 us -> 1.47 us  [the longest x2 1.06 us: body(): sums.append(total.astype(bf16))]
    ppermute x4 -> x3, waiting for transfers between devices: 5.9 us -> 3.45 us  [cyclic(): return lax.ppermute(x, axis, [(i, (i + shift) % n) for i in range(n)])]
    slice x4, local copies, waits for them, and re-layouts: 1.77 us -> 0.01 us  [body(): key_span[:, :, cols]]
  transfers between devices with their start and end apart: 28 -> 33, of which waited for: 18 -> 19; matrix products, arithmetic and copies ran while one was open for 3% -> 2% of each run, Pallas kernels for 10% -> 14%
where the time goes in v4:
time: 148 us; the launch traced here: 147 us
  starting transfers between devices  58 us (39%)
  waiting for transfers between devices  53 us (36%)
  Pallas kernels  21.8 us (15%)
  local copies, waits for them, and re-layouts  7.23 us (5%)
  other arithmetic  5.21 us (4%)
  between operations  1.5 us (1%)
    ppermute x18, starting transfers between devices, along(): lax.ppermute(x, axis, [(i, i + shift) for i in range(n) if 0 <= i + shift...  39.7 us
    ppermute x12, waiting for transfers between devices, partner(): return lax.ppermute(x, axis, [(i, i ^ mask) for i in range(n)])  28 us
    ppermute x18, waiting for transfers between devices, along(): lax.ppermute(x, axis, [(i, i + shift) for i in range(n) if 0 <= i + shift...  21.5 us
    pallas_call x2, Pallas kernels, attention_chunk(): pl.pallas_call(functools.partial(attention_kernel, shards, placed if earl...  16.3 us
    ppermute x12, starting transfers between devices, partner(): return lax.ppermute(x, axis, [(i, i ^ mask) for i in range(n)])  14.5 us
    unnamed x62, local copies, waits for them, and re-layouts  6.7 us
    ppermute x3, starting transfers between devices, cyclic(): return lax.ppermute(x, axis, [(i, (i + shift) % n) for i in range(n)])  3.87 us
    ppermute x3, waiting for transfers between devices, cyclic(): return lax.ppermute(x, axis, [(i, (i + shift) % n) for i in range(n)])  3.45 us
  transfers between devices with their start and end apart: 33, of which 19 were waited for; matrix products, arithmetic and copies ran while one was open for 2% of the time, Pallas kernels for 14%

profile of v4, /device:TPU:0, one launch (start us, length us, event | category | flops | bytes accessed | tf_op | source)
XLA Modules:
  0.0 146.7 jit_solution(6251346825396759294)
XLA Ops:
  0.7 0.8 pad_maximum_fusion.10
  1.5 0.8 copy-done.19
  2.5 3.1 %collective-permute-start = (bf16[1,544,128]{2,1,0:T(8,128)(2,1)S(1)}, bf16[1,544,128]{2,1,0:T(8,128)(2,1)S(1)}, u32[]{:S(2)}, u32[]{:S(2)}) collective-permute-start(bf16[1,544,128]{2,1,0:T(8,128)(2,1)S(1)} %bitcast.52), channel_id=1, source_target_pairs={{0,8},{8,0},{16,24},{24,16},{1,9},{9,1},{17,25},{25,17},{2,10},{10... | collective-permute-start | bytes 417800 | tf_op jit(solution)/shard_map/ppermute | solution.py:52
  5.6 3.7 %collective-permute-done = bf16[1,544,128]{2,1,0:T(8,128)(2,1)S(1)} collective-permute-done((bf16[1,544,128]{2,1,0:T(8,128)(2,1)S(1)}, bf16[1,544,128]{2,1,0:T(8,128)(2,1)S(1)}, u32[]{:S(2)}, u32[]{:S(2)}) %collective-permute-start) | collective-permute-done | bytes 139296 | tf_op jit(solution)/shard_map/ppermute | solution.py:52
  9.3 2.8 %collective-permute-start.1 = (bf16[2,544,128]{2,1,0:T(8,128)(2,1)S(1)}, bf16[2,544,128]{2,1,0:T(8,128)(2,1)S(1)}, u32[]{:S(2)}, u32[]{:S(2)}) collective-permute-start(bf16[2,544,128]{2,1,0:T(8,128)(2,1)S(1)} %pad_maximum_fusion.3), channel_id=1, source_target_pairs={{0,16},{8,24},{16,0},{24,8},{1,17},{9,25},{17,1},{25,9},{2,18},{10... | collective-permute-start | bytes 835592 | tf_op jit(solution)/shard_map/ppermute | solution.py:52
  12.1 12.0 %collective-permute-done.1 = bf16[2,544,128]{2,1,0:T(8,128)(2,1)S(1)} collective-permute-done((bf16[2,544,128]{2,1,0:T(8,128)(2,1)S(1)}, bf16[2,544,128]{2,1,0:T(8,128)(2,1)S(1)}, u32[]{:S(2)}, u32[]{:S(2)}) %collective-permute-start.1) | collective-permute-done | bytes 278560 | tf_op jit(solution)/shard_map/ppermute | solution.py:52
  24.1 0.6 copy-done.11
  24.8 1.4 collective-permute-start.2
  26.2 2.7 %collective-permute-start.3 = (bf16[2,64,1280]{2,1,0:T(8,128)(2,1)S(1)}, bf16[2,64,1280]{2,1,0:T(8,128)(2,1)S(1)}, u32[]{:S(2)}, u32[]{:S(2)}) collective-permute-start(bf16[2,64,1280]{2,1,0:T(8,128)(2,1)S(1)} %pad_maximum_fusion.2.refs_12_.refs_16_), channel_id=1, source_target_pairs={{0,8},{8,16},{16,24},{1,9},{9,17},{17,25},{2,10},{10,18},{18,26},{... | collective-permute-start | bytes 983048 | tf_op jit(solution)/shard_map/ppermute | solution.py:47
  29.0 6.7 %collective-permute-done.2 = bf16[4,416,128]{2,1,0:T(8,128)(2,1)S(1)} collective-permute-done((bf16[4,416,128]{2,1,0:T(8,128)(2,1)S(1)}, bf16[4,416,128]{2,1,0:T(8,128)(2,1)S(1)}, u32[]{:S(2)}, u32[]{:S(2)}) %collective-permute-start.2) | collective-permute-done | bytes 426016 | tf_op jit(solution)/shard_map/ppermute | solution.py:52
  35.9 5.1 %collective-permute-start.5 = (bf16[2,64,1280]{2,1,0:T(8,128)(2,1)S(1)}, bf16[2,64,1280]{2,1,0:T(8,128)(2,1)}, u32[]{:S(2)}, u32[]{:S(2)}) collective-permute-start(bf16[2,64,1280]{2,1,0:T(8,128)(2,1)S(1)} %collective-permute-done.3.refs_13_.refs_17_), channel_id=1, source_target_pairs={{0,8},{8,16},{16,24},{1,9},{9,17},{17,25},{2,10},{10,18},{18,26},{... | collective-permute-start | bytes 983048 | tf_op jit(solution)/shard_map/ppermute | solution.py:47
  41.0 0.2 fusion.15
  41.3 6.5 %collective-permute-done.5.refs_14_.refs_18_ = bf16[2,64,1280]{2,1,0:T(8,128)(2,1)} collective-permute-done((bf16[2,64,1280]{2,1,0:T(8,128)(2,1)S(1)}, bf16[2,64,1280]{2,1,0:T(8,128)(2,1)}, u32[]{:S(2)}, u32[]{:S(2)}) %collective-permute-start.5) | collective-permute-done | bytes 327712 | tf_op jit(solution)/shard_map/ppermute | solution.py:47
  47.9 5.2 %collective-permute-start.9 = (bf16[2,64,1280]{2,1,0:T(8,128)(2,1)}, bf16[2,64,1280]{2,1,0:T(8,128)(2,1)}, u32[]{:S(2)}, u32[]{:S(2)}) collective-permute-start(bf16[2,64,1280]{2,1,0:T(8,128)(2,1)} %collective-permute-done.5.refs_14_.refs_18_), channel_id=1, source_target_pairs={{0,8},{8,16},{16,24},{1,9},{9,17},{17,25},{2,10},{10,18},{18,26},{... | collective-permute-start | bytes 983048 | tf_op jit(solution)/shard_map/ppermute | solution.py:47
  53.2 1.8 %low_rank.1 = (bf16[4096,128]{1,0:T(8,128)(2,1)S(1)}, bf16[40,64,128]{2,1,0:T(8,128)(2,1)S(1)}, bf16[2,64,128]{2,1,0:T(8,128)(2,1)S(1)}) custom-call(s32[3]{0:T(128)S(1)} %pad_add_fusion.index_ref, bf16[8,416,128]{2,1,0:T(8,128)(2,1)S(1)} %pad_maximum_fusion.own_ref, bf16[8,416,128]{2,1,0:T(8,128)(2,1)} %collective-permute-done.4.other_ref, ...), custom_call_target="tpu_custom_call" | custom-call | flops 134217728 | bytes 5242880 | tf_op jit(solution)/shard_map/low_rank/pallas_call | solution.py:292
  55.0 1.0 copy-done.3
  56.0 2.6 %collective-permute-start.6 = (bf16[2,64,128]{2,1,0:T(8,128)(2,1)S(1)}, bf16[2,64,128]{2,1,0:T(8,128)(2,1)S(1)}, u32[]{:S(2)}, u32[]{:S(2)}) collective-permute-start(bf16[2,64,128]{2,1,0:T(8,128)(2,1)S(1)} %get-tuple-element.48.refs_8_), channel_id=1, source_target_pairs={{0,8},{8,16},{16,24},{1,9},{9,17},{17,25},{2,10},{10,18},{18,26},{... | collective-permute-start | bytes 98312 | tf_op jit(solution)/shard_map/ppermute | solution.py:47
  58.6 3.8 %collective-permute-start.7 = (bf16[2,64,128]{2,1,0:T(8,128)(2,1)S(1)}, bf16[2,64,128]{2,1,0:T(8,128)(2,1)S(1)}, u32[]{:S(2)}, u32[]{:S(2)}) collective-permute-start(bf16[2,64,128]{2,1,0:T(8,128)(2,1)S(1)} %get-tuple-element.48.refs_8_), channel_id=1, source_target_pairs={{0,16},{8,24},{1,17},{9,25},{2,18},{10,26},{3,19},{11,27},{4,20},{... | collective-permute-start | bytes 98312 | tf_op jit(solution)/shard_map/ppermute | solution.py:47
  62.4 1.3 collective-permute-start.8
  63.9 1.3 collective-permute-start.10
  65.2 4.6 %collective-permute-start.11 = (bf16[2,64,768]{2,1,0:T(8,128)(2,1)S(1)}, bf16[2,64,768]{2,1,0:T(8,128)(2,1)S(1)}, u32[]{:S(2)}, u32[]{:S(2)}) collective-permute-start(bf16[2,64,768]{2,1,0:T(8,128)(2,1)S(1)} %pad_maximum_fusion.7.refs_12_.refs_16_), channel_id=1, source_target_pairs={{0,16},{8,24},{1,17},{9,25},{2,18},{10,26},{3,19},{11,27},{4,20},{... | collective-permute-start | bytes 589832 | tf_op jit(solution)/shard_map/ppermute | solution.py:47
  69.9 1.3 collective-permute-start.12
  71.2 1.2 copy-done.1
  72.5 1.2 copy-done.2
  73.7 1.0 copy-done.6
  74.7 10.2 %attention.2 = (bf16[2,64,4096]{2,1,0:T(8,128)(2,1)}, bf16[2,64,4096]{2,1,0:T(8,128)(2,1)}, bf16[32,4,16,128]{3,2,1,0:T(8,128)(2,1)S(1)}, bf16[8,4,16,128]{3,2,1...) custom-call(s32[1]{0:T(128)} %bitcast.place_ref, ...), custom_call_target="tpu_custom_call" | custom-call | flops 2495610880 | bytes 16777216 | tf_op jit(solution)/shard_map/attention/pallas_call | solution.py:222
  84.9 1.3 collective-permute-start.13
  86.2 1.3 collective-permute-start.14
  87.5 1.3 collective-permute-start.15
  88.8 6.1 %attention.3 = (bf16[2,64,4096]{2,1,0:T(8,128)(2,1)}, bf16[2,64,4096]{2,1,0:T(8,128)(2,1)}, bf16[32,4,16,128]{3,2,1,0:T(8,128)(2,1)S(1)}, bf16[8,4,16,128]{3,2,1...) custom-call(s32[1]{0:T(128)} %bitcast.place_ref, ...), custom_call_target="tpu_custom_call", output_to_operand_aliasing={{0}: (23, {}), {1}: (24, {}), {2}: (25, {}), {3}: (26, {})} | custom-call | flops 1497366528 | bytes 16777216 | tf_op jit(solution)/shard_map/attention/pallas_call | solution.py:222
  94.9 0.6 copy-done.7
  95.6 5.2 %collective-permute-done.14 = bf16[2,64,640]{2,1,0:T(8,128)(2,1)S(1)} collective-permute-done((bf16[2,64,640]{2,1,0:T(8,128)(2,1)S(1)}, bf16[2,64,640]{2,1,0:T(8,128)(2,1)S(1)}, u32[]{:S(2)}, u32[]{:S(2)}) %collective-permute-start.14) | collective-permute-done | bytes 163872 | tf_op jit(solution)/shard_map/ppermute | solution.py:47
  100.8 1.3 collective-permute-start.16
  102.1 1.3 collective-permute-start.17
  103.4 1.3 collective-permute-start.18
  104.7 2.2 %collective-permute-done.16 = bf16[2,64,64]{2,1,0:T(8,128)(2,1)S(1)} collective-permute-done((bf16[2,64,64]{2,1,0:T(8,128)(2,1)S(1)}, bf16[2,64,64]{2,1,0:T(8,128)(2,1)S(1)}, u32[]{:S(2)}, u32[]{:S(2)}) %collective-permute-start.16) | collective-permute-done | bytes 16416 | tf_op jit(solution)/shard_map/ppermute | solution.py:47
  107.0 1.9 %collective-permute-done.17 = bf16[2,64,64]{2,1,0:T(8,128)(2,1)S(1)} collective-permute-done((bf16[2,64,64]{2,1,0:T(8,128)(2,1)S(1)}, bf16[2,64,64]{2,1,0:T(8,128)(2,1)S(1)}, u32[]{:S(2)}, u32[]{:S(2)}) %collective-permute-start.17) | collective-permute-done | bytes 16416 | tf_op jit(solution)/shard_map/ppermute | solution.py:47
  108.9 3.3 %collective-permute-done.18 = bf16[2,64,64]{2,1,0:T(8,128)(2,1)S(1)} collective-permute-done((bf16[2,64,64]{2,1,0:T(8,128)(2,1)S(1)}, bf16[2,64,64]{2,1,0:T(8,128)(2,1)S(1)}, u32[]{:S(2)}, u32[]{:S(2)}) %collective-permute-start.18) | collective-permute-done | bytes 16416 | tf_op jit(solution)/shard_map/ppermute | solution.py:47
  112.3 1.6 %adapter_grads.1 = (bf16[8,2,208,128]{3,2,1,0:T(8,128)(2,1)}, bf16[8,2,208,128]{3,2,1,0:T(8,128)(2,1)S(1)}) custom-call(s32[1]{0:T(128)} %bitcast.2.core_ref, bf16[2,64,4096]{2,1,0:T(8,128)(2,1)S(1)} %copy-done, bf16[128,128]{1,0:T(8,128)(2,1)S(1)} %pad_maximum_fusion.13.low_ref, bf16[32,4,16,128]{3,2,1,0:T(8,128)(2,1)S(1)} %get-tuple-element.69.guq_ref, ...), custom_call_target="tpu_custom_call" | custom-call | flops 134217728 | bytes 5242880 | tf_op jit(solution)/shard_map/adapter_grads/pallas_call | solution.py:378
  114.0 1.0 add_convert_fusion.4
  115.1 1.4 collective-permute-done.19
  116.7 1.2 collective-permute-start.23
  118.1 1.6 %collective-permute-start.25 = (bf16[4,2,112,128]{3,2,0,1:T(8,128)(2,1)S(1)}, bf16[4,2,112,128]{3,2,0,1:T(8,128)(2,1)S(1)}, u32[]{:S(2)}, u32[]{:S(2)}) collective-permute-start(bf16[4,2,112,128]{3,2,0,1:T(8,128)(2,1)S(1)} %fusion), channel_id=1, source_target_pairs={{0,2},{1,3},{2,0},{3,1},{4,6},{5,7},{6,4},{7,5},{8,10},{9,11},{10,... | collective-permute-start | bytes 688136 | tf_op jit(solution)/shard_map/ppermute | solution.py:52
  119.7 1.3 collective-permute-start.20
  120.9 1.3 collective-permute-start.21
  122.2 1.3 collective-permute-start.22
  123.8 1.6 %collective-permute-start.24 = (bf16[4,96,128]{2,1,0:T(8,128)(2,1)S(1)}, bf16[4,96,128]{2,1,0:T(8,128)(2,1)S(1)}, u32[]{:S(2)}, u32[]{:S(2)}) collective-permute-start(bf16[4,96,128]{2,1,0:T(8,128)(2,1)S(1)} %fusion.14), channel_id=1, source_target_pairs={{0,2},{1,3},{2,0},{3,1},{4,6},{5,7},{6,4},{7,5},{8,10},{9,11},{10,... | collective-permute-start | bytes 294920 | tf_op jit(solution)/shard_map/ppermute | solution.py:52
  125.3 0.2 collective-permute-done.25
  125.5 1.7 %collective-permute-done.20 = bf16[2,64,384]{2,1,0:T(8,128)(2,1)S(1)} collective-permute-done((bf16[2,64,384]{2,1,0:T(8,128)(2,1)S(1)}, bf16[2,64,384]{2,1,0:T(8,128)(2,1)S(1)}, u32[]{:S(2)}, u32[]{:S(2)}) %collective-permute-start.20) | collective-permute-done | bytes 98336 | tf_op jit(solution)/shard_map/ppermute | solution.py:47
  127.2 0.9 collective-permute-start.26
  128.1 0.4 collective-permute-done.24
  128.5 3.5 %collective-permute-done.26 = bf16[4,112,128]{2,1,0:T(8,128)(2,1)S(1)} collective-permute-done((bf16[4,112,128]{2,1,0:T(8,128)(2,1)S(1)}, bf16[4,112,128]{2,1,0:T(8,128)(2,1)S(1)}, u32[]{:S(2)}, u32[]{:S(2)}) %collective-permute-start.26) | collective-permute-done | bytes 114720 | tf_op jit(solution)/shard_map/ppermute | solution.py:52
  132.1 0.5 collective-permute-done.21
  132.6 3.2 %collective-permute-start.28 = (bf16[208,128]{1,0:T(8,128)(2,1)S(1)}, bf16[208,128]{1,0:T(8,128)(2,1)S(1)}, u32[]{:S(2)}, u32[]{:S(2)}) collective-permute-start(bf16[208,128]{1,0:T(8,128)(2,1)S(1)} %get-tuple-element.96), channel_id=1, source_target_pairs={{0,16},{8,24},{16,0},{24,8},{1,17},{9,25},{17,1},{25,9},{2,18},{10... | collective-permute-start | bytes 159752 | tf_op jit(solution)/shard_map/ppermute | solution.py:42
  135.8 0.6 collective-permute-start.29
  136.5 2.0 %collective-permute-done.27 = bf16[208,128]{1,0:T(8,128)(2,1)S(1)} collective-permute-done((bf16[208,128]{1,0:T(8,128)(2,1)S(1)}, bf16[208,128]{1,0:T(8,128)(2,1)S(1)}, u32[]{:S(2)}, u32[]{:S(2)}) %collective-permute-start.27) | collective-permute-done | bytes 53280 | tf_op jit(solution)/shard_map/ppermute | solution.py:42
  138.6 1.4 collective-permute-done.29
  140.1 1.3 collective-permute-start.31
  141.4 0.5 collective-permute-start.32
  141.9 0.7 pad_maximum_fusion.4
  142.7 2.1 %grad_hidden.1 = bf16[2,64,4096]{2,1,0:T(8,128)(2,1)} custom-call(bf16[128,128]{1,0:T(8,128)(2,1)S(1)} %pad_maximum_fusion.13.low_ref, bf16[4096,128]{1,0:T(8,128)(2,1)S(1)} %copy-done.4), custom_call_target="tpu_custom_call" | custom-call | flops 134217728 | bytes 2097152 | tf_op jit(solution)/shard_map/grad_hidden/pallas_call | solution.py:329
  144.8 0.2 collective-permute-done.31
  145.3 0.7 pad_maximum_fusion.8
  146.0 0.7 pad_maximum_fusion.5
  (133 shorter events, 2.2 us)
Async XLA Ops:
  0.6 0.9 copy-start.18
  1.5 0.9 copy-start.19
  2.5 6.8 %collective-permute-start = (bf16[1,544,128]{2,1,0:T(8,128)(2,1)S(1)}, bf16[1,544,128]{2,1,0:T(8,128)(2,1)S(1)}, u32[]{:S(2)}, u32[]{:S(2)}) collective-permute-start(bf16[1,544,128]{2,1,0:T(8,128)(2,1)S(1)} %bitcast.52), channel_id=1, source_target_pairs={{0,8},{8,0},{16,24},{24,16},{1,9},{9,1},{17,25},{25,17},{2,10},{10... | collective-permute-start | bytes 417800 | tf_op jit(solution)/shard_map/ppermute | solution.py:52
  9.2 14.8 %copy-start.9 = (bf16[1,544,128]{2,1,0:T(8,128)(2,1)}, bf16[1,544,128]{2,1,0:T(8,128)(2,1)S(1)}, u32[]{:S(2)}) copy-start(bf16[1,544,128]{2,1,0:T(8,128)(2,1)S(1)} %collective-permute-done) | copy-start | bytes 417796
  9.3 14.8 %collective-permute-start.1 = (bf16[2,544,128]{2,1,0:T(8,128)(2,1)S(1)}, bf16[2,544,128]{2,1,0:T(8,128)(2,1)S(1)}, u32[]{:S(2)}, u32[]{:S(2)}) collective-permute-start(bf16[2,544,128]{2,1,0:T(8,128)(2,1)S(1)} %pad_maximum_fusion.3), channel_id=1, source_target_pairs={{0,16},{8,24},{16,0},{24,8},{1,17},{9,25},{17,1},{25,9},{2,18},{10... | collective-permute-start | bytes 835592 | tf_op jit(solution)/shard_map/ppermute | solution.py:52
  24.1 0.7 copy-start.11
  24.8 1.4 slice-start
  24.8 1.4 slice-start.2
  24.8 10.9 %collective-permute-start.2 = (bf16[4,416,128]{2,1,0:T(8,128)(2,1)S(1)}, bf16[4,416,128]{2,1,0:T(8,128)(2,1)S(1)}, u32[]{:S(2)}, u32[]{:S(2)}) collective-permute-start(bf16[4,416,128]{2,1,0:T(8,128)(2,1)S(1)} %slice.199), channel_id=1, source_target_pairs={{0,4},{4,0},{1,5},{5,1},{2,6},{6,2},{3,7},{7,3},{8,12},{12,8},{9,1... | collective-permute-start | bytes 1277960 | tf_op jit(solution)/shard_map/ppermute | solution.py:52
  26.2 27.0 %copy-start = (bf16[2,64,4096]{2,1,0:T(8,128)(2,1)S(1)}, bf16[2,64,4096]{2,1,0:T(8,128)(2,1)}, u32[]{:S(2)}) copy-start(bf16[2,64,4096]{2,1,0:T(8,128)(2,1)} %hidden_ref.3) | copy-start | bytes 3145732
  26.2 9.6 %collective-permute-start.3 = (bf16[2,64,1280]{2,1,0:T(8,128)(2,1)S(1)}, bf16[2,64,1280]{2,1,0:T(8,128)(2,1)S(1)}, u32[]{:S(2)}, u32[]{:S(2)}) collective-permute-start(bf16[2,64,1280]{2,1,0:T(8,128)(2,1)S(1)} %pad_maximum_fusion.2.refs_12_.refs_16_), channel_id=1, source_target_pairs={{0,8},{8,16},{16,24},{1,9},{9,17},{17,25},{2,10},{10,18},{18,26},{... | collective-permute-start | bytes 983048 | tf_op jit(solution)/shard_map/ppermute | solution.py:47
  35.8 5.5 %copy-start.5 = (bf16[2,64,1280]{2,1,0:T(8,128)(2,1)}, bf16[2,64,1280]{2,1,0:T(8,128)(2,1)S(1)}, u32[]{:S(2)}) copy-start(bf16[2,64,1280]{2,1,0:T(8,128)(2,1)S(1)} %collective-permute-done.3.refs_13_.refs_17_) | copy-start | bytes 983044
  35.8 17.4 %collective-permute-start.4 = (bf16[8,416,128]{2,1,0:T(8,128)(2,1)S(1)}, bf16[8,416,128]{2,1,0:T(8,128)(2,1)}, u32[]{:S(2)}, u32[]{:S(2)}) collective-permute-start(bf16[8,416,128]{2,1,0:T(8,128)(2,1)S(1)} %pad_maximum_fusion.own_ref), channel_id=1, source_target_pairs={{0,1},{1,0},{2,3},{3,2},{4,5},{5,4},{6,7},{7,6},{8,9},{9,8},{10,11... | collective-permute-start | bytes 2555912 | tf_op jit(solution)/shard_map/ppermute | solution.py:52
  35.9 12.0 %collective-permute-start.5 = (bf16[2,64,1280]{2,1,0:T(8,128)(2,1)S(1)}, bf16[2,64,1280]{2,1,0:T(8,128)(2,1)}, u32[]{:S(2)}, u32[]{:S(2)}) collective-permute-start(bf16[2,64,1280]{2,1,0:T(8,128)(2,1)S(1)} %collective-permute-done.3.refs_13_.refs_17_), channel_id=1, source_target_pairs={{0,8},{8,16},{16,24},{1,9},{9,17},{17,25},{2,10},{10,18},{18,26},{... | collective-permute-start | bytes 983048 | tf_op jit(solution)/shard_map/ppermute | solution.py:47
  41.0 12.1 %slice-start.3 = ((bf16[2,64,1024]{2,1,0:T(8,128)(2,1)}), bf16[2,64,384]{2,1,0:T(8,128)(2,1)S(1)}, s32[]{:S(2)}) async-start(bf16[2,64,1024]{2,1,0:T(8,128)(2,1)} %param.12), calls=%async_computation.3 | async-start | bytes 196608 | tf_op jit(solution)/shard_map/slice | solution.py:483
  41.2 12.0 %slice-start.1 = ((bf16[2,64,1024]{2,1,0:T(8,128)(2,1)}), bf16[2,64,384]{2,1,0:T(8,128)(2,1)S(1)}, s32[]{:S(2)}) async-start(bf16[2,64,1024]{2,1,0:T(8,128)(2,1)} %param.11), calls=%async_computation.1 | async-start | bytes 196608 | tf_op jit(solution)/shard_map/slice | solution.py:483
  47.9 16.1 %collective-permute-start.9 = (bf16[2,64,1280]{2,1,0:T(8,128)(2,1)}, bf16[2,64,1280]{2,1,0:T(8,128)(2,1)}, u32[]{:S(2)}, u32[]{:S(2)}) collective-permute-start(bf16[2,64,1280]{2,1,0:T(8,128)(2,1)} %collective-permute-done.5.refs_14_.refs_18_), channel_id=1, source_target_pairs={{0,8},{8,16},{16,24},{1,9},{9,17},{17,25},{2,10},{10,18},{18,26},{... | collective-permute-start | bytes 983048 | tf_op jit(solution)/shard_map/ppermute | solution.py:47
  53.2 10.6 %copy-start.10 = (bf16[1,544,128]{2,1,0:T(8,128)(2,1)S(1)}, bf16[1,544,128]{2,1,0:T(8,128)(2,1)}, u32[]{:S(2)}) copy-start(bf16[1,544,128]{2,1,0:T(8,128)(2,1)} %copy-done.9) | copy-start | bytes 417796
  53.2 10.6 %copy-start.12 = (bf16[2,544,128]{2,1,0:T(8,128)(2,1)S(1)}, bf16[2,544,128]{2,1,0:T(8,128)(2,1)}, u32[]{:S(2)}) copy-start(bf16[2,544,128]{2,1,0:T(8,128)(2,1)} %copy-done.11) | copy-start | bytes 835588
  55.0 1.0 copy-start.3
  56.0 13.9 %collective-permute-start.6 = (bf16[2,64,128]{2,1,0:T(8,128)(2,1)S(1)}, bf16[2,64,128]{2,1,0:T(8,128)(2,1)S(1)}, u32[]{:S(2)}, u32[]{:S(2)}) collective-permute-start(bf16[2,64,128]{2,1,0:T(8,128)(2,1)S(1)} %get-tuple-element.48.refs_8_), channel_id=1, source_target_pairs={{0,8},{8,16},{16,24},{1,9},{9,17},{17,25},{2,10},{10,18},{18,26},{... | collective-permute-start | bytes 98312 | tf_op jit(solution)/shard_map/ppermute | solution.py:47
  58.6 12.6 %collective-permute-start.7 = (bf16[2,64,128]{2,1,0:T(8,128)(2,1)S(1)}, bf16[2,64,128]{2,1,0:T(8,128)(2,1)S(1)}, u32[]{:S(2)}, u32[]{:S(2)}) collective-permute-start(bf16[2,64,128]{2,1,0:T(8,128)(2,1)S(1)} %get-tuple-element.48.refs_8_), channel_id=1, source_target_pairs={{0,16},{8,24},{1,17},{9,25},{2,18},{10,26},{3,19},{11,27},{4,20},{... | collective-permute-start | bytes 98312 | tf_op jit(solution)/shard_map/ppermute | solution.py:47
  62.4 8.8 %collective-permute-start.8 = (bf16[2,64,128]{2,1,0:T(8,128)(2,1)S(1)}, bf16[2,64,128]{2,1,0:T(8,128)(2,1)S(1)}, u32[]{:S(2)}, u32[]{:S(2)}) collective-permute-start(bf16[2,64,128]{2,1,0:T(8,128)(2,1)S(1)} %get-tuple-element.48.refs_8_), channel_id=1, source_target_pairs={{0,24},{1,25},{2,26},{3,27},{4,28},{5,29},{6,30},{7,31}} | collective-permute-start | bytes 98312 | tf_op jit(solution)/shard_map/ppermute | solution.py:47
  63.9 23.5 %collective-permute-start.10 = (bf16[2,64,768]{2,1,0:T(8,128)(2,1)S(1)}, bf16[2,64,768]{2,1,0:T(8,128)(2,1)S(1)}, u32[]{:S(2)}, u32[]{:S(2)}) collective-permute-start(bf16[2,64,768]{2,1,0:T(8,128)(2,1)S(1)} %pad_maximum_fusion.7.refs_12_.refs_16_), channel_id=1, source_target_pairs={{0,8},{8,16},{16,24},{1,9},{9,17},{17,25},{2,10},{10,18},{18,26},{... | collective-permute-start | bytes 589832 | tf_op jit(solution)/shard_map/ppermute | solution.py:47
  65.2 23.5 %collective-permute-start.11 = (bf16[2,64,768]{2,1,0:T(8,128)(2,1)S(1)}, bf16[2,64,768]{2,1,0:T(8,128)(2,1)S(1)}, u32[]{:S(2)}, u32[]{:S(2)}) collective-permute-start(bf16[2,64,768]{2,1,0:T(8,128)(2,1)S(1)} %pad_maximum_fusion.7.refs_12_.refs_16_), channel_id=1, source_target_pairs={{0,16},{8,24},{1,17},{9,25},{2,18},{10,26},{3,19},{11,27},{4,20},{... | collective-permute-start | bytes 589832 | tf_op jit(solution)/shard_map/ppermute | solution.py:47
  69.9 18.9 %collective-permute-start.12 = (bf16[2,64,768]{2,1,0:T(8,128)(2,1)S(1)}, bf16[2,64,768]{2,1,0:T(8,128)(2,1)S(1)}, u32[]{:S(2)}, u32[]{:S(2)}) collective-permute-start(bf16[2,64,768]{2,1,0:T(8,128)(2,1)S(1)} %pad_maximum_fusion.7.refs_12_.refs_16_), channel_id=1, source_target_pairs={{0,24},{1,25},{2,26},{3,27},{4,28},{5,29},{6,30},{7,31}} | collective-permute-start | bytes 589832 | tf_op jit(solution)/shard_map/ppermute | solution.py:47
  71.2 1.2 copy-start.1
  72.5 1.2 copy-start.2
  73.7 1.0 copy-start.6
  84.9 10.7 %collective-permute-start.13 = (bf16[2,64,640]{2,1,0:T(8,128)(2,1)S(1)}, bf16[2,64,640]{2,1,0:T(8,128)(2,1)S(1)}, u32[]{:S(2)}, u32[]{:S(2)}) collective-permute-start(bf16[2,64,640]{2,1,0:T(8,128)(2,1)S(1)} %get-tuple-element.59), channel_id=1, source_target_pairs={{8,0},{16,8},{24,16},{9,1},{17,9},{25,17},{10,2},{18,10},{26,18},{... | collective-permute-start | bytes 491528 | tf_op jit(solution)/shard_map/ppermute | solution.py:47
  86.2 14.6 %collective-permute-start.14 = (bf16[2,64,640]{2,1,0:T(8,128)(2,1)S(1)}, bf16[2,64,640]{2,1,0:T(8,128)(2,1)S(1)}, u32[]{:S(2)}, u32[]{:S(2)}) collective-permute-start(bf16[2,64,640]{2,1,0:T(8,128)(2,1)S(1)} %get-tuple-element.60), channel_id=1, source_target_pairs={{16,0},{24,8},{17,1},{25,9},{18,2},{26,10},{19,3},{27,11},{20,4},{... | collective-permute-start | bytes 491528 | tf_op jit(solution)/shard_map/ppermute | solution.py:47
  87.5 13.3 %collective-permute-start.15 = (bf16[2,64,640]{2,1,0:T(8,128)(2,1)S(1)}, bf16[2,64,640]{2,1,0:T(8,128)(2,1)S(1)}, u32[]{:S(2)}, u32[]{:S(2)}) collective-permute-start(bf16[2,64,640]{2,1,0:T(8,128)(2,1)S(1)} %get-tuple-element.61), channel_id=1, source_target_pairs={{24,0},{25,1},{26,2},{27,3},{28,4},{29,5},{30,6},{31,7}} | collective-permute-start | bytes 491528 | tf_op jit(solution)/shard_map/ppermute | solution.py:47
  94.9 0.6 copy-start.7
  95.6 16.8 %copy-start.13 = (bf16[2,64,640]{2,1,0:T(8,128)(2,1)}, bf16[2,64,640]{2,1,0:T(8,128)(2,1)S(1)}, u32[]{:S(2)}) copy-start(bf16[2,64,640]{2,1,0:T(8,128)(2,1)S(1)} %collective-permute-done.13) | copy-start | bytes 491524
  100.8 11.5 %copy-start.15 = (bf16[2,64,640]{2,1,0:T(8,128)(2,1)}, bf16[2,64,640]{2,1,0:T(8,128)(2,1)S(1)}, u32[]{:S(2)}) copy-start(bf16[2,64,640]{2,1,0:T(8,128)(2,1)S(1)} %collective-permute-done.14) | copy-start | bytes 491524
  100.8 13.1 %copy-start.17 = (bf16[2,64,640]{2,1,0:T(8,128)(2,1)}, bf16[2,64,640]{2,1,0:T(8,128)(2,1)S(1)}, u32[]{:S(2)}) copy-start(bf16[2,64,640]{2,1,0:T(8,128)(2,1)S(1)} %collective-permute-done.15) | copy-start | bytes 491524
  100.8 6.2 %collective-permute-start.16 = (bf16[2,64,64]{2,1,0:T(8,128)(2,1)S(1)}, bf16[2,64,64]{2,1,0:T(8,128)(2,1)S(1)}, u32[]{:S(2)}, u32[]{:S(2)}) collective-permute-start(bf16[2,64,64]{2,1,0:T(8,128)(2,1)S(1)} %get-tuple-element.66), channel_id=1, source_target_pairs={{8,0},{16,8},{24,16},{9,1},{17,9},{25,17},{10,2},{18,10},{26,18},{... | collective-permute-start | bytes 49160 | tf_op jit(solution)/shard_map/ppermute | solution.py:47
  102.1 6.8 %collective-permute-start.17 = (bf16[2,64,64]{2,1,0:T(8,128)(2,1)S(1)}, bf16[2,64,64]{2,1,0:T(8,128)(2,1)S(1)}, u32[]{:S(2)}, u32[]{:S(2)}) collective-permute-start(bf16[2,64,64]{2,1,0:T(8,128)(2,1)S(1)} %get-tuple-element.67), channel_id=1, source_target_pairs={{16,0},{24,8},{17,1},{25,9},{18,2},{26,10},{19,3},{27,11},{20,4},{... | collective-permute-start | bytes 49160 | tf_op jit(solution)/shard_map/ppermute | solution.py:47
  103.4 8.8 %collective-permute-start.18 = (bf16[2,64,64]{2,1,0:T(8,128)(2,1)S(1)}, bf16[2,64,64]{2,1,0:T(8,128)(2,1)S(1)}, u32[]{:S(2)}, u32[]{:S(2)}) collective-permute-start(bf16[2,64,64]{2,1,0:T(8,128)(2,1)S(1)} %get-tuple-element.68), channel_id=1, source_target_pairs={{24,0},{25,1},{26,2},{27,3},{28,4},{29,5},{30,6},{31,7}} | collective-permute-start | bytes 49160 | tf_op jit(solution)/shard_map/ppermute | solution.py:47
  112.3 1.6 %copy-start.14 = (bf16[2,64,640]{2,1,0:T(8,128)(2,1)S(1)}, bf16[2,64,640]{2,1,0:T(8,128)(2,1)}, u32[]{:S(2)}) copy-start(bf16[2,64,640]{2,1,0:T(8,128)(2,1)} %copy-done.13) | copy-start | bytes 491524
  112.3 1.6 %copy-start.16 = (bf16[2,64,640]{2,1,0:T(8,128)(2,1)S(1)}, bf16[2,64,640]{2,1,0:T(8,128)(2,1)}, u32[]{:S(2)}) copy-start(bf16[2,64,640]{2,1,0:T(8,128)(2,1)} %copy-done.15) | copy-start | bytes 491524
  114.0 2.6 %collective-permute-start.19 = (bf16[8,2,208,128]{3,2,1,0:T(8,128)(2,1)}, bf16[8,2,208,128]{3,2,1,0:T(8,128)(2,1)S(1)}, u32[]{:S(2)}, u32[]{:S(2)}) collective-permute-start(bf16[8,2,208,128]{3,2,1,0:T(8,128)(2,1)} %get-tuple-element.71), channel_id=1, source_target_pairs={{0,1},{1,0},{2,3},{3,2},{4,5},{5,4},{6,7},{7,6},{8,9},{9,8},{10,11... | collective-permute-start | bytes 2555912 | tf_op jit(solution)/shard_map/ppermute | solution.py:52
  116.7 7.0 %collective-permute-start.23 = (bf16[4,2,96,128]{3,2,0,1:T(8,128)(2,1)S(1)}, bf16[4,2,96,128]{3,2,0,1:T(8,128)(2,1)S(1)}, u32[]{:S(2)}, u32[]{:S(2)}) collective-permute-start(bf16[4,2,96,128]{3,2,0,1:T(8,128)(2,1)S(1)} %fusion.4), channel_id=1, source_target_pairs={{0,4},{4,0},{1,5},{5,1},{2,6},{6,2},{3,7},{7,3},{8,12},{12,8},{9,1... | collective-permute-start | bytes 589832 | tf_op jit(solution)/shard_map/ppermute | solution.py:52
  118.0 1.7 %copy-start.8 = (bf16[2,64,384]{2,1,0:T(8,128)(2,1)S(1)}, bf16[2,64,384]{2,1,0:T(8,128)(2,1)}, u32[]{:S(2)}) copy-start(bf16[2,64,384]{2,1,0:T(8,128)(2,1)} %copy-done.7) | copy-start | bytes 294916
  118.1 7.4 %collective-permute-start.25 = (bf16[4,2,112,128]{3,2,0,1:T(8,128)(2,1)S(1)}, bf16[4,2,112,128]{3,2,0,1:T(8,128)(2,1)S(1)}, u32[]{:S(2)}, u32[]{:S(2)}) collective-permute-start(bf16[4,2,112,128]{3,2,0,1:T(8,128)(2,1)S(1)} %fusion), channel_id=1, source_target_pairs={{0,2},{1,3},{2,0},{3,1},{4,6},{5,7},{6,4},{7,5},{8,10},{9,11},{10,... | collective-permute-start | bytes 688136 | tf_op jit(solution)/shard_map/ppermute | solution.py:52
  119.7 7.6 %collective-permute-start.20 = (bf16[2,64,384]{2,1,0:T(8,128)(2,1)S(1)}, bf16[2,64,384]{2,1,0:T(8,128)(2,1)S(1)}, u32[]{:S(2)}, u32[]{:S(2)}) collective-permute-start(bf16[2,64,384]{2,1,0:T(8,128)(2,1)S(1)} %copy-done.8), channel_id=1, source_target_pairs={{8,0},{16,8},{24,16},{9,1},{17,9},{25,17},{10,2},{18,10},{26,18},{... | collective-permute-start | bytes 294920 | tf_op jit(solution)/shard_map/ppermute | solution.py:47
  120.9 11.6 %collective-permute-start.21 = (bf16[2,64,384]{2,1,0:T(8,128)(2,1)S(1)}, bf16[2,64,384]{2,1,0:T(8,128)(2,1)S(1)}, u32[]{:S(2)}, u32[]{:S(2)}) collective-permute-start(bf16[2,64,384]{2,1,0:T(8,128)(2,1)S(1)} %get-tuple-element.74), channel_id=1, source_target_pairs={{16,0},{24,8},{17,1},{25,9},{18,2},{26,10},{19,3},{27,11},{20,4},{... | collective-permute-start | bytes 294920 | tf_op jit(solution)/shard_map/ppermute | solution.py:47
  122.2 10.3 %collective-permute-start.22 = (bf16[2,64,384]{2,1,0:T(8,128)(2,1)S(1)}, bf16[2,64,384]{2,1,0:T(8,128)(2,1)S(1)}, u32[]{:S(2)}, u32[]{:S(2)}) collective-permute-start(bf16[2,64,384]{2,1,0:T(8,128)(2,1)S(1)} %get-tuple-element.76), channel_id=1, source_target_pairs={{24,0},{25,1},{26,2},{27,3},{28,4},{29,5},{30,6},{31,7}} | collective-permute-start | bytes 294920 | tf_op jit(solution)/shard_map/ppermute | solution.py:47
  123.8 4.7 %collective-permute-start.24 = (bf16[4,96,128]{2,1,0:T(8,128)(2,1)S(1)}, bf16[4,96,128]{2,1,0:T(8,128)(2,1)S(1)}, u32[]{:S(2)}, u32[]{:S(2)}) collective-permute-start(bf16[4,96,128]{2,1,0:T(8,128)(2,1)S(1)} %fusion.14), channel_id=1, source_target_pairs={{0,2},{1,3},{2,0},{3,1},{4,6},{5,7},{6,4},{7,5},{8,10},{9,11},{10,... | collective-permute-start | bytes 294920 | tf_op jit(solution)/shard_map/ppermute | solution.py:52
  127.2 4.8 %collective-permute-start.26 = (bf16[4,112,128]{2,1,0:T(8,128)(2,1)S(1)}, bf16[4,112,128]{2,1,0:T(8,128)(2,1)S(1)}, u32[]{:S(2)}, u32[]{:S(2)}) collective-permute-start(bf16[4,112,128]{2,1,0:T(8,128)(2,1)S(1)} %fusion.9), channel_id=1, source_target_pairs={{0,4},{4,0},{1,5},{5,1},{2,6},{6,2},{3,7},{7,3},{8,12},{12,8},{9,1... | collective-permute-start | bytes 344072 | tf_op jit(solution)/shard_map/ppermute | solution.py:52
  132.1 10.6 %copy-start.4 = (bf16[4096,128]{1,0:T(8,128)(2,1)S(1)}, bf16[4096,128]{1,0:T(8,128)(2,1)}, u32[]{:S(2)}) copy-start(bf16[4096,128]{1,0:T(8,128)(2,1)} %copy-done.3) | copy-start | bytes 3145732
  132.6 6.0 %collective-permute-start.27 = (bf16[208,128]{1,0:T(8,128)(2,1)S(1)}, bf16[208,128]{1,0:T(8,128)(2,1)S(1)}, u32[]{:S(2)}, u32[]{:S(2)}) collective-permute-start(bf16[208,128]{1,0:T(8,128)(2,1)S(1)} %get-tuple-element.94), channel_id=1, source_target_pairs={{0,8},{8,16},{16,24},{24,0},{1,9},{9,17},{17,25},{25,1},{2,10},{10... | collective-permute-start | bytes 159752 | tf_op jit(solution)/shard_map/ppermute | solution.py:42
  132.6 5.9 %collective-permute-start.28 = (bf16[208,128]{1,0:T(8,128)(2,1)S(1)}, bf16[208,128]{1,0:T(8,128)(2,1)S(1)}, u32[]{:S(2)}, u32[]{:S(2)}) collective-permute-start(bf16[208,128]{1,0:T(8,128)(2,1)S(1)} %get-tuple-element.96), channel_id=1, source_target_pairs={{0,16},{8,24},{16,0},{24,8},{1,17},{9,25},{17,1},{25,9},{2,18},{10... | collective-permute-start | bytes 159752 | tf_op jit(solution)/shard_map/ppermute | solution.py:42
  135.8 4.1 %collective-permute-start.29 = (bf16[208,128]{1,0:T(8,128)(2,1)S(1)}, bf16[208,128]{1,0:T(8,128)(2,1)S(1)}, u32[]{:S(2)}, u32[]{:S(2)}) collective-permute-start(bf16[208,128]{1,0:T(8,128)(2,1)S(1)} %get-tuple-element.95), channel_id=1, source_target_pairs={{0,24},{8,0},{16,8},{24,16},{1,25},{9,1},{17,9},{25,17},{2,26},{10... | collective-permute-start | bytes 159752 | tf_op jit(solution)/shard_map/ppermute | solution.py:42
  140.0 4.8 %collective-permute-start.30 = (bf16[208,128]{1,0:T(8,128)(2,1)S(1)}, bf16[208,128]{1,0:T(8,128)(2,1)S(1)}, u32[]{:S(2)}, u32[]{:S(2)}) collective-permute-start(bf16[208,128]{1,0:T(8,128)(2,1)S(1)} %fusion.12), channel_id=1, source_target_pairs={{0,3},{1,2},{2,1},{3,0},{4,7},{5,6},{6,5},{7,4},{8,11},{9,10},{10,... | collective-permute-start | bytes 159752 | tf_op jit(solution)/shard_map/ppermute | solution.py:52
  140.1 4.9 %collective-permute-start.31 = (bf16[208,128]{1,0:T(8,128)(2,1)S(1)}, bf16[208,128]{1,0:T(8,128)(2,1)S(1)}, u32[]{:S(2)}, u32[]{:S(2)}) collective-permute-start(bf16[208,128]{1,0:T(8,128)(2,1)S(1)} %fusion.12), channel_id=1, source_target_pairs={{0,2},{1,3},{2,0},{3,1},{4,6},{5,7},{6,4},{7,5},{8,10},{9,11},{10,... | collective-permute-start | bytes 159752 | tf_op jit(solution)/shard_map/ppermute | solution.py:52
  141.4 3.6 %collective-permute-start.32 = (bf16[208,128]{1,0:T(8,128)(2,1)S(1)}, bf16[208,128]{1,0:T(8,128)(2,1)S(1)}, u32[]{:S(2)}, u32[]{:S(2)}) collective-permute-start(bf16[208,128]{1,0:T(8,128)(2,1)S(1)} %fusion.12), channel_id=1, source_target_pairs={{0,1},{1,0},{2,3},{3,2},{4,5},{5,4},{6,7},{7,6},{8,9},{9,8},{10,11... | collective-permute-start | bytes 159752 | tf_op jit(solution)/shard_map/ppermute | solution.py:52

commit v5 on v4

--- a/solution.py
+++ b/solution.py
@@ -42,9 +42,9 @@
     return lax.ppermute(x, axis, [(i, (i + shift) % n) for i in range(n)])
 
 
-def along(x, axis, shift):
+def along(x, axis, shift, start=0):
     n = lax.axis_size(axis)
-    return lax.ppermute(x, axis, [(i, i + shift) for i in range(n) if 0 <= i + shift < n])
+    return lax.ppermute(x, axis, [(i, i + shift) for i in range(start, n) if 0 <= i + shift < n])
 
 
 def partner(x, axis, mask):
@@ -60,20 +60,40 @@
     return lax.dot_general(a, b, (((ca,), (cb,)), ((), ())), preferred_element_type=f32)
 
 
-def attention_kernel(shards, earlier_count, place_ref, *refs):
+def attention_kernel(shards, earlier_count, first, place_ref, *refs):
     it = iter(refs)
 
     def take(n):
         return [next(it) for _ in range(n)]
 
-    q_ref, g_ref, upq_ref, upv_ref, pk_ref, pv_ref, cos_ref, sin_ref = take(8)
+    q_hbm, g_hbm, upq_ref, upv_ref, pk_ref, pv_ref, cos_ref, sin_ref = take(8)
     low_refs, k_refs, v_refs = take(shards), take(shards), take(shards)
     before = take(2) if earlier_count else None
     take(earlier_count)
     att_ref, gq_ref, guq_ref, guv_ref, lgq_ref, lgv_ref = take(6)
     gv_refs = take(shards)
-
-    seqs, tokens = q_ref.shape[0], q_ref.shape[1]
+    q_buf, g_buf, sems = take(3)
+
+    group, slot = pl.program_id(0), lax.rem(pl.program_id(0), 2)
+
+    def fetches(step, into):
+        at = pl.multiple_of((first + step) * WIDE, WIDE)
+        return [
+            pltpu.make_async_copy(hbm.at[:, :, pl.ds(at, WIDE)], buf.at[into], sems.at[i, into])
+            for i, (hbm, buf) in enumerate(((q_hbm, q_buf), (g_hbm, g_buf)))
+        ]
+
+    @pl.when(group == 0)
+    def _():
+        for copy in fetches(0, 0):
+            copy.start()
+
+    @pl.when(group + 1 < pl.num_programs(0))
+    def _():
+        for copy in fetches(group + 1, 1 - slot):
+            copy.start()
+
+    seqs, tokens = q_buf.shape[1:3]
     parts, part_rows = guq_ref.shape[1:3]
     span = shards * tokens
     past = pk_ref.shape[1]
@@ -113,12 +133,14 @@
     low_v = jnp.concatenate([r[s][:, RANK:] for s in every for r in low_refs], axis=0)
     query_delta = mm(low_q, upq, 1, 0)
     value_delta = mm(low_v, upv, 1, 0)
+    for copy in fetches(group, slot):
+        copy.wait()
     backs, gvs = [], []
     for s in every:
         delta = heads(query_delta[s * tokens : (s + 1) * tokens])
         delta = delta * cos4 + pltpu.roll(delta, HEAD_DIM // 2, 1) * sin4
-        q = (heads(q_ref[s]).astype(f32) + delta).astype(bf16)
-        g = heads(g_ref[s])
+        q = (heads(q_buf[slot, s]).astype(f32) + delta).astype(bf16)
+        g = heads(g_buf[slot, s])
         keys = jnp.concatenate([r[s] for r in k_refs] + [pk_ref[s]], axis=0)
         base = jnp.concatenate([r[s] for r in v_refs], axis=0).astype(f32)
         vals = (base + value_delta[s * span : (s + 1) * span]).astype(bf16)
@@ -179,8 +201,8 @@
     past_block = (seqs, past_len, HEAD_DIM)
     in_specs = [
         spec(memory_space=pltpu.SMEM),
-        q_spec,
-        q_spec,
+        spec(memory_space=pltpu.HBM),
+        spec(memory_space=pltpu.HBM),
         spec((GROUP, RANK, HEAD_DIM), lambda g: (first + g, 0, 0)),
         spec((1, RANK, HEAD_DIM), lambda g: (HEADS + first + g, 0, 0)),
         spec(past_block, lambda g: (0, 0, first + g)),
@@ -220,13 +242,18 @@
     pairs = seqs * groups * scores
     grant = min(12 * 2**20 + 96 * scores, 48 * 2**20)
     return pl.pallas_call(
-        functools.partial(attention_kernel, shards, placed if earlier is not None else 0),
+        functools.partial(attention_kernel, shards, placed if earlier else 0, first),
         grid=(groups,),
         in_specs=in_specs,
         out_specs=placed_specs + [whole(low_q_shape), whole(low_v_shape)] + [gv_spec] * shards,
         out_shape=placed_shapes
         + [low_q_shape, low_v_shape]
         + [shape((seqs, tokens, groups * HEAD_DIM), bf16)] * shards,
+        scratch_shapes=[
+            pltpu.VMEM((2, seqs, tokens, WIDE), bf16),
+            pltpu.VMEM((2, seqs, tokens, WIDE), bf16),
+            pltpu.SemaphoreType.DMA((2, 2)),
+        ],
         input_output_aliases=aliases,
         compiler_params=pltpu.CompilerParams(vmem_limit_bytes=grant),
         cost_estimate=pl.CostEstimate(
@@ -236,35 +263,38 @@
     )(*operands)
 
 
-def low_rank_kernel(fs, index_ref, own_ref, other_ref, hidden_ref, down_ref, up_ref, low_ref):
-    z, x, c = index_ref[0], index_ref[1], index_ref[2]
-    pieces = own_ref.shape[0]
-    sp = pieces // fs
-    down_rows = D // (2 * pieces)
-    blocks = up_ref.shape[0] // pieces
-    up_rows = RANK // 2
-    for r in range(pieces):
-        shard = (z ^ (r % sp)) * fs + (x ^ (r // sp))
-        for ref, half in ((own_ref, c), (other_ref, 1 - c)):
-            at = pl.multiple_of((shard * 2 + half) * down_rows, down_rows)
-            down_ref[pl.ds(at, down_rows), :] = ref[r, :down_rows]
-            at = pl.multiple_of(half * up_rows, up_rows)
+def low_rank_kernel(
+    sp, fs, rp, index_ref, own_ref, other_ref, hidden_ref, down_out, up_ref, low_ref, down_ref, sem
+):
+    z, x, r = index_ref[0], index_ref[1], index_ref[2]
+    shards = sp * fs
+    down_rows, up_rows = D // (shards * rp), RANK // rp
+    blocks = (HEADS + KV_HEADS) // shards
+    for piece in range(own_ref.shape[0]):
+        shard = (z ^ (piece % sp)) * fs + (x ^ (piece // sp % fs))
+        for swap, ref in enumerate((own_ref, other_ref)):
+            part = r ^ (piece // shards * 2 + swap)
+            at = pl.multiple_of((shard * rp + part) * down_rows, down_rows)
+            down_ref[pl.ds(at, down_rows), :] = ref[piece, :down_rows]
+            at = pl.multiple_of(part * up_rows, up_rows)
             for j in range(blocks):
                 lo = down_rows + j * up_rows
-                up_ref[shard * blocks + j, pl.ds(at, up_rows), :] = ref[r, lo : lo + up_rows]
+                up_ref[shard * blocks + j, pl.ds(at, up_rows), :] = ref[piece, lo : lo + up_rows]
+    copy = pltpu.make_async_copy(down_ref, down_out, sem)
+    copy.start()
     rows = jnp.concatenate([hidden_ref[s] for s in range(hidden_ref.shape[0])], axis=0)
     low = mm(rows, down_ref[...], 1, 0).astype(bf16)
     for s in range(low_ref.shape[0]):
         low_ref[s] = low[s * low_ref.shape[1] : (s + 1) * low_ref.shape[1]]
+    copy.wait()
 
 
 def pack_adapters(adapter_down, adapter_up, own_past):
-    sp = lax.axis_size("sp")
-    c = lax.rem(lax.axis_index("rep"), 2)
-    down_rows, up_rows = adapter_down.shape[0] // 2, RANK // 2
+    sp, rp, r = lax.axis_size("sp"), lax.axis_size("rep"), lax.axis_index("rep")
+    down_rows, up_rows = adapter_down.shape[0] // rp, RANK // rp
     blocks = adapter_up.shape[1] // HEAD_DIM
-    down = lax.dynamic_slice_in_dim(adapter_down, c * down_rows, down_rows, 0)
-    up = lax.dynamic_slice_in_dim(adapter_up, c * up_rows, up_rows, 0)
+    down = lax.dynamic_slice_in_dim(adapter_down, r * down_rows, down_rows, 0)
+    up = lax.dynamic_slice_in_dim(adapter_up, r * up_rows, up_rows, 0)
     up = [up[:, j * HEAD_DIM : (j + 1) * HEAD_DIM] for j in range(blocks)]
     rows = down_rows + blocks * up_rows
     buf = jnp.concatenate([down] + up + [own_past.reshape(-1, 2 * RANK)], axis=0)[None]
@@ -277,22 +307,27 @@
     return buf[:, :rows], past
 
 
-def adapters_packed(hidden, buf, before_swap):
-    fs = lax.axis_size("fsdp")
+def adapters_packed(hidden, buf, before_rep, before_swap):
+    sp, fs, rp = (lax.axis_size(a) for a in ("sp", "fsdp", "rep"))
     z, x, r = (lax.axis_index(a) for a in ("sp", "fsdp", "rep"))
-    c = lax.rem(r, 2)
     step = 1
     while step < fs:
         buf = jnp.concatenate([buf, partner(buf, "fsdp", step)], axis=0)
         step *= 2
+    step = 2
+    buf = tie(buf, before_rep)
+    while step < rp:
+        buf = jnp.concatenate([buf, partner(buf, "rep", step)], axis=0)
+        step *= 2
     other = partner(tie(buf, before_swap), "rep", 1)
-    index = jnp.stack([z, x, c]).astype(jnp.int32)
+    index = jnp.stack([z, x, r]).astype(jnp.int32)
     vmem = pl.BlockSpec(memory_space=pltpu.VMEM)
     seqs, tokens = hidden.shape[:2]
     down_full, up_blocks, low = pl.pallas_call(
-        functools.partial(low_rank_kernel, fs),
+        functools.partial(low_rank_kernel, sp, fs, rp),
         in_specs=[pl.BlockSpec(memory_space=pltpu.SMEM)] + [vmem] * 3,
-        out_specs=[vmem] * 3,
+        out_specs=[pl.BlockSpec(memory_space=pltpu.HBM), vmem, vmem],
+        scratch_shapes=[pltpu.VMEM((D, 2 * RANK), bf16), pltpu.SemaphoreType.DMA],
         out_shape=[
             jax.ShapeDtypeStruct((D, 2 * RANK), bf16),
             jax.ShapeDtypeStruct((HEADS + KV_HEADS, RANK, HEAD_DIM), bf16),
@@ -399,11 +434,11 @@
     return send, keep
 
 
-def finish_grads(send, keep, values):
+def finish_grads(send, keep, before, values, low_grad, hidden_of):
     sp, fs, rp = (lax.axis_size(a) for a in ("sp", "fsdp", "rep"))
     z, r = lax.axis_index("sp"), lax.axis_index("rep")
     shards, _, rows, lanes = send.shape
-    got = partner(send, "rep", 1)
+    got = partner(tie(send, *before), "rep", 1)
     then = [along(tie(v, got), "sp", -k) for k, v in enumerate(values, 1)]
     fs_bits, rep_bits = fs.bit_length() - 1, rp.bit_length() - 2
     labels = [("fsdp", b) for b in reversed(range(fs_bits))]
@@ -440,7 +475,8 @@
     for k in range(1, sp):
         send = lax.dynamic_index_in_dim(over_sp, lax.rem(z + k, sp), 0, keepdims=False)
         total = total + cyclic(send, "sp", k).astype(f32)
-    own = total.astype(bf16)
+    grad_hidden = hidden_of(tie(low_grad, over_sp))
+    own = tie(total.astype(bf16), grad_hidden)
     parts = [own] + [partner(own, "rep", m) for m in range(1, rp)]
     ordered = []
     for q in range(rp):
@@ -458,7 +494,7 @@
             up = [up[lo : lo + up_rows] for lo in range(0, up.shape[0], up_rows)]
             up = jnp.concatenate(up, axis=1)
         ups.append(up.reshape(up_rows, up_width))
-    return grad_down, jnp.concatenate(ups, axis=0), then, over_sp
+    return grad_down, jnp.concatenate(ups, axis=0), then, grad_hidden
 
 
 def body(
@@ -491,13 +527,12 @@
         past = jnp.concatenate(past, axis=1)
     early.append(along(tie(early[0], buf), "sp", 1))
     for k in range(2, sp):
-        early.append(along(early[k - 1], "sp", 1))
+        early.append(along(early[k - 1], "sp", 1, k - 1))
     if even:
-        down_full, up_blocks, low_own = adapters_packed(hidden, buf, early[1])
+        down_full, up_blocks, low_own = adapters_packed(hidden, buf, early[1], early[min(2, sp - 1)])
     else:
         down_full, up_blocks, low_own = adapters_plain(hidden, adapter_down, adapter_up)
-    low_sent = tie(low_own, early[min(2, sp - 1)])
-    lows = [low_own] + [along(low_sent, "sp", k) for k in range(1, sp)]
+    lows = [low_own] + [along(low_own, "sp", k) for k in range(1, sp)]
     own_late = tie(own_kvs[1], low_own, early[-1])
     late = [own_kvs[1]] + [along(own_late, "sp", k) for k in range(1, sp)]
     cos, sin = rotary_tables(tokens, past_len + z * tokens)
@@ -518,7 +553,7 @@
     low_v_total = low_grad_v[:, :tokens]
     for k in range(1, sp):
         part = low_grad_v[:, k * tokens : (k + 1) * tokens].astype(bf16)
-        part = tie(part, *value_got[0])
+        part = tie(part, value_got[0][0], value_got[0][-1])
         low_v_total = low_v_total + along(part, "sp", -k).astype(f32)
     low_grad = (
         jnp.concatenate([low_grad_q, low_v_total], axis=2)
@@ -526,9 +561,10 @@
         .reshape(seqs * tokens, 2 * RANK)
     )
     send, keep = packed_grads(hidden, low_grad, guq, guv, sp * fs)
-    grad_down, grad_up, got, mark = finish_grads(send, keep, gvs[1:])
+    grad_down, grad_up, got, grad_hidden = finish_grads(
+        send, keep, value_got[0], gvs[1:], low_grad, lambda x: grad_hidden_of(x, down_full, seqs, tokens)
+    )
     value_got.append(got)
-    grad_hidden = grad_hidden_of(tie(low_grad, mark), down_full, seqs, tokens)
 
     sums = []
     for own, got in zip(value_own, value_got):

time: 148 us -> 149 us (level)
  local copies, waits for them, and re-layouts: 7.23 us -> 17.2 us
  waiting for transfers between devices: 53 us -> 46.1 us
  starting transfers between devices: 58 us -> 54.9 us
  Pallas kernels: 21.8 us -> 23.3 us
    unnamed x62 -> x87, local copies, waits for them, and re-layouts: 6.7 us -> 16.6 us
    ppermute x18, waiting for transfers between devices: 21.5 us -> 14.9 us  [along(): lax.ppermute(x, axis, [(i, i + shift) for i in range(start, n) if 0 <= i...]
    ppermute x18, starting transfers between devices: 39.7 us -> 36.5 us  [along(): lax.ppermute(x, axis, [(i, i + shift) for i in range(start, n) if 0 <= i...]
    ppermute x3, waiting for transfers between devices: 3.45 us -> 1.86 us  [cyclic(): return lax.ppermute(x, axis, [(i, (i + shift) % n) for i in range(n)])]
    pallas_call x2, Pallas kernels: 16.3 us -> 17.8 us  [attention_chunk(): pl.pallas_call(functools.partial(attention_kernel, shards, placed if earl...]
    ppermute x12 -> x13, waiting for transfers between devices: 28 us -> 29.3 us  [partner(): return lax.ppermute(x, axis, [(i, i ^ mask) for i in range(n)])]
    ppermute x12 -> x13, starting transfers between devices: 14.5 us -> 14.6 us  [partner(): return lax.ppermute(x, axis, [(i, i ^ mask) for i in range(n)])]
  transfers between devices with their start and end apart: 33 -> 34, of which waited for: 19 -> 20; matrix products, arithmetic and copies ran while one was open for 2% -> 2% of each run, Pallas kernels for 14% -> 16%
where the time goes in v5:
time: 149 us; the launch traced here: 147 us
  starting transfers between devices  54.9 us (37%)
  waiting for transfers between devices  46.1 us (31%)
  Pallas kernels  23.3 us (16%)
  local copies, waits for them, and re-layouts  17.2 us (12%)
  other arithmetic  4.35 us (3%)
  between operations  1.62 us (1%)
    ppermute x18, starting transfers between devices, along(): lax.ppermute(x, axis, [(i, i + shift) for i in range(start, n) if 0 <= i...  36.5 us
    ppermute x13, waiting for transfers between devices, partner(): return lax.ppermute(x, axis, [(i, i ^ mask) for i in range(n)])  29.3 us
    pallas_call x2, Pallas kernels, attention_chunk(): pl.pallas_call(functools.partial(attention_kernel, shards, placed if earl...  17.8 us
    unnamed x87, local copies, waits for them, and re-layouts  16.6 us
    ppermute x18, waiting for transfers between devices, along(): lax.ppermute(x, axis, [(i, i + shift) for i in range(start, n) if 0 <= i...  14.9 us
    ppermute x13, starting transfers between devices, partner(): return lax.ppermute(x, axis, [(i, i ^ mask) for i in range(n)])  14.6 us
    ppermute x3, starting transfers between devices, cyclic(): return lax.ppermute(x, axis, [(i, (i + shift) % n) for i in range(n)])  3.87 us
  transfers between devices with their start and end apart: 34, of which 20 were waited for; matrix products, arithmetic and copies ran while one was open for 2% of the time, Pallas kernels for 16%

profile of v5, /device:TPU:0, one launch (start us, length us, event | category | flops | bytes accessed | tf_op | source)
XLA Modules:
  0.0 147.5 jit_solution(14574936987044672425)
XLA Ops:
  0.7 0.7 copy-done.31
  1.4 0.8 constant_dynamic-update-slice_fusion.6
  2.2 0.7 constant_dynamic-update-slice_fusion.5
  2.9 0.7 constant_dynamic-update-slice_fusion.4
  5.7 3.1 %collective-permute-start = (bf16[1,336,128]{2,1,0:T(8,128)(2,1)S(1)}, bf16[1,336,128]{2,1,0:T(8,128)(2,1)S(1)}, u32[]{:S(2)}, u32[]{:S(2)}) collective-permute-start(bf16[1,336,128]{2,1,0:T(8,128)(2,1)S(1)} %bitcast.53), channel_id=1, source_target_pairs={{0,8},{8,0},{16,24},{24,16},{1,9},{9,1},{17,25},{25,17},{2,10},{10... | collective-permute-start | bytes 258056 | tf_op jit(solution)/shard_map/ppermute | solution.py:52
  8.8 2.5 %collective-permute-done = bf16[1,336,128]{2,1,0:T(8,128)(2,1)S(1)} collective-permute-done((bf16[1,336,128]{2,1,0:T(8,128)(2,1)S(1)}, bf16[1,336,128]{2,1,0:T(8,128)(2,1)S(1)}, u32[]{:S(2)}, u32[]{:S(2)}) %collective-permute-start) | collective-permute-done | bytes 86048 | tf_op jit(solution)/shard_map/ppermute | solution.py:52
  11.3 3.0 %collective-permute-start.1 = (bf16[2,336,128]{2,1,0:T(8,128)(2,1)S(1)}, bf16[2,336,128]{2,1,0:T(8,128)(2,1)S(1)}, u32[]{:S(2)}, u32[]{:S(2)}) collective-permute-start(bf16[2,336,128]{2,1,0:T(8,128)(2,1)S(1)} %pad_maximum_fusion.7), channel_id=1, source_target_pairs={{0,16},{8,24},{16,0},{24,8},{1,17},{9,25},{17,1},{25,9},{2,18},{10... | collective-permute-start | bytes 516104 | tf_op jit(solution)/shard_map/ppermute | solution.py:52
  14.3 7.2 %collective-permute-done.1 = bf16[2,336,128]{2,1,0:T(8,128)(2,1)S(1)} collective-permute-done((bf16[2,336,128]{2,1,0:T(8,128)(2,1)S(1)}, bf16[2,336,128]{2,1,0:T(8,128)(2,1)S(1)}, u32[]{:S(2)}, u32[]{:S(2)}) %collective-permute-start.1) | collective-permute-done | bytes 172064 | tf_op jit(solution)/shard_map/ppermute | solution.py:52
  22.2 1.3 collective-permute-start.2
  23.6 2.6 %collective-permute-start.3 = (bf16[2,64,1280]{2,1,0:T(8,128)(2,1)S(1)}, bf16[2,64,1280]{2,1,0:T(8,128)(2,1)S(1)}, u32[]{:S(2)}, u32[]{:S(2)}) collective-permute-start(bf16[2,64,1280]{2,1,0:T(8,128)(2,1)S(1)} %pad_maximum_fusion.2.refs_12_.refs_16_), channel_id=1, source_target_pairs={{0,8},{8,16},{16,24},{1,9},{9,17},{17,25},{2,10},{10,18},{18,26},{... | collective-permute-start | bytes 983048 | tf_op jit(solution)/shard_map/ppermute | solution.py:47
  26.2 2.4 %collective-permute-done.2 = bf16[4,208,128]{2,1,0:T(8,128)(2,1)S(1)} collective-permute-done((bf16[4,208,128]{2,1,0:T(8,128)(2,1)S(1)}, bf16[4,208,128]{2,1,0:T(8,128)(2,1)S(1)}, u32[]{:S(2)}, u32[]{:S(2)}) %collective-permute-start.2) | collective-permute-done | bytes 213024 | tf_op jit(solution)/shard_map/ppermute | solution.py:52
  28.6 4.0 %collective-permute-done.3.refs_13_.refs_17_ = bf16[2,64,1280]{2,1,0:T(8,128)(2,1)S(1)} collective-permute-done((bf16[2,64,1280]{2,1,0:T(8,128)(2,1)S(1)}, bf16[2,64,1280]{2,1,0:T(8,128)(2,1)S(1)}, u32[]{:S(2)}, u32[]{:S(2)}) %collective-permute-start.3) | collective-permute-done | bytes 327712 | tf_op jit(solution)/shard_map/ppermute | solution.py:47
  32.6 1.5 %collective-permute-start.4 = (bf16[8,208,128]{2,1,0:T(8,128)(2,1)S(1)}, bf16[8,208,128]{2,1,0:T(8,128)(2,1)S(1)}, u32[]{:S(2)}, u32[]{:S(2)}) collective-permute-start(bf16[8,208,128]{2,1,0:T(8,128)(2,1)S(1)} %pad_maximum_fusion), channel_id=1, source_target_pairs={{0,2},{1,3},{2,0},{3,1},{4,6},{5,7},{6,4},{7,5},{8,10},{9,11},{10,... | collective-permute-start | bytes 1277960 | tf_op jit(solution)/shard_map/ppermute | solution.py:52
  34.1 1.4 collective-permute-start.5
  35.6 7.2 %collective-permute-done.4 = bf16[8,208,128]{2,1,0:T(8,128)(2,1)S(1)} collective-permute-done((bf16[8,208,128]{2,1,0:T(8,128)(2,1)S(1)}, bf16[8,208,128]{2,1,0:T(8,128)(2,1)S(1)}, u32[]{:S(2)}, u32[]{:S(2)}) %collective-permute-start.4) | collective-permute-done | bytes 426016 | tf_op jit(solution)/shard_map/ppermute | solution.py:52
  43.2 1.4 collective-permute-start.10
  45.4 1.8 %low_rank.1 = (bf16[4096,128]{1,0:T(8,128)(2,1)S(1)}, bf16[40,64,128]{2,1,0:T(8,128)(2,1)S(1)}, bf16[2,64,128]{2,1,0:T(8,128)(2,1)S(1)}) custom-call(s32[3]{0:T(128)S(1)} %pad_add_fusion.index_ref, bf16[16,208,128]{2,1,0:T(8,128)(2,1)S(1)} %constant_dynamic-update-slice_fusion.7.own_ref, bf16[16,208,128]{2,1,0:T(8,128)(2,1)} %collective-permute-done.6.other_ref, ...), custom_call_target="tpu_custom_call" | custom-call | flops 134217728 | bytes 5242880 | tf_op jit(solution)/shard_map/low_rank/pallas_call | solution.py:326
  47.2 1.0 copy-done.3
  48.2 4.4 %collective-permute-start.7 = (bf16[2,64,128]{2,1,0:T(8,128)(2,1)S(1)}, bf16[2,64,128]{2,1,0:T(8,128)(2,1)S(1)}, u32[]{:S(2)}, u32[]{:S(2)}) collective-permute-start(bf16[2,64,128]{2,1,0:T(8,128)(2,1)S(1)} %get-tuple-element.50.refs_8_), channel_id=1, source_target_pairs={{0,8},{8,16},{16,24},{1,9},{9,17},{17,25},{2,10},{10,18},{18,26},{... | collective-permute-start | bytes 98312 | tf_op jit(solution)/shard_map/ppermute | solution.py:47
  52.6 6.9 %collective-permute-start.8 = (bf16[2,64,128]{2,1,0:T(8,128)(2,1)S(1)}, bf16[2,64,128]{2,1,0:T(8,128)(2,1)S(1)}, u32[]{:S(2)}, u32[]{:S(2)}) collective-permute-start(bf16[2,64,128]{2,1,0:T(8,128)(2,1)S(1)} %get-tuple-element.50.refs_8_), channel_id=1, source_target_pairs={{0,16},{8,24},{1,17},{9,25},{2,18},{10,26},{3,19},{11,27},{4,20},{... | collective-permute-start | bytes 98312 | tf_op jit(solution)/shard_map/ppermute | solution.py:47
  59.5 1.3 collective-permute-start.9
  61.0 1.3 collective-permute-start.11
  62.3 4.3 %collective-permute-start.12 = (bf16[2,64,768]{2,1,0:T(8,128)(2,1)S(1)}, bf16[2,64,768]{2,1,0:T(8,128)(2,1)S(1)}, u32[]{:S(2)}, u32[]{:S(2)}) collective-permute-start(bf16[2,64,768]{2,1,0:T(8,128)(2,1)S(1)} %pad_maximum_fusion.6.refs_12_.refs_16_), channel_id=1, source_target_pairs={{0,16},{8,24},{1,17},{9,25},{2,18},{10,26},{3,19},{11,27},{4,20},{... | collective-permute-start | bytes 589832 | tf_op jit(solution)/shard_map/ppermute | solution.py:47
  66.6 1.3 collective-permute-start.13
  68.6 1.2 copy-done.1
  69.8 1.2 copy-done.2
  71.0 0.8 copy-done.12
  71.8 1.0 copy-done.14
  72.7 11.2 %attention.2 = (bf16[2,64,4096]{2,1,0:T(8,128)(2,1)}, bf16[2,64,4096]{2,1,0:T(8,128)(2,1)}, bf16[32,4,16,128]{3,2,1,0:T(8,128)(2,1)S(1)}, bf16[8,4,16,128]{3,2,1...) custom-call(s32[1]{0:T(128)} %bitcast.place_ref, ...), custom_call_target="tpu_custom_call" | custom-call | flops 2495610880 | bytes 16777216 | tf_op jit(solution)/shard_map/attention/pallas_call | solution.py:244
  84.0 1.3 collective-permute-start.14
  85.3 1.3 collective-permute-start.16
  86.6 0.7 copy-done.6
  87.4 0.8 copy-done.8
  88.1 0.8 copy-done.10
  88.9 6.7 %attention.3 = (bf16[2,64,4096]{2,1,0:T(8,128)(2,1)}, bf16[2,64,4096]{2,1,0:T(8,128)(2,1)}, bf16[32,4,16,128]{3,2,1,0:T(8,128)(2,1)S(1)}, bf16[8,4,16,128]{3,2,1...) custom-call(s32[1]{0:T(128)} %bitcast.place_ref, ...), custom_call_target="tpu_custom_call", output_to_operand_aliasing={{0}: (23, {}), {1}: (24, {}), {2}: (25, {}), {3}: (26, {})} | custom-call | flops 1497366528 | bytes 16777216 | tf_op jit(solution)/shard_map/attention/pallas_call | solution.py:244
  97.6 1.3 collective-permute-start.17
  98.9 1.3 collective-permute-start.18
  100.2 1.3 collective-permute-start.19
  101.5 1.3 collective-permute-start.15
  103.4 3.4 %collective-permute-done.18 = bf16[2,64,64]{2,1,0:T(8,128)(2,1)S(1)} collective-permute-done((bf16[2,64,64]{2,1,0:T(8,128)(2,1)S(1)}, bf16[2,64,64]{2,1,0:T(8,128)(2,1)S(1)}, u32[]{:S(2)}, u32[]{:S(2)}) %collective-permute-start.18) | collective-permute-done | bytes 16416 | tf_op jit(solution)/shard_map/ppermute | solution.py:47
  106.9 2.5 %collective-permute-done.19 = bf16[2,64,64]{2,1,0:T(8,128)(2,1)S(1)} collective-permute-done((bf16[2,64,64]{2,1,0:T(8,128)(2,1)S(1)}, bf16[2,64,64]{2,1,0:T(8,128)(2,1)S(1)}, u32[]{:S(2)}, u32[]{:S(2)}) %collective-permute-start.19) | collective-permute-done | bytes 16416 | tf_op jit(solution)/shard_map/ppermute | solution.py:47
  109.5 1.5 %adapter_grads.1 = (bf16[8,2,208,128]{3,2,1,0:T(8,128)(2,1)}, bf16[8,2,208,128]{3,2,1,0:T(8,128)(2,1)S(1)}) custom-call(s32[1]{0:T(128)} %bitcast.5.core_ref, bf16[2,64,4096]{2,1,0:T(8,128)(2,1)S(1)} %copy-done, bf16[128,128]{1,0:T(8,128)(2,1)S(1)} %pad_maximum_fusion.13.low_ref, bf16[32,4,16,128]{3,2,1,0:T(8,128)(2,1)S(1)} %get-tuple-element.71.guq_ref, ...), custom_call_target="tpu_custom_call" | custom-call | flops 134217728 | bytes 5242880 | tf_op jit(solution)/shard_map/adapter_grads/pallas_call | solution.py:413
  111.1 3.0 %collective-permute-done.15 = bf16[2,64,640]{2,1,0:T(8,128)(2,1)S(1)} collective-permute-done((bf16[2,64,640]{2,1,0:T(8,128)(2,1)S(1)}, bf16[2,64,640]{2,1,0:T(8,128)(2,1)S(1)}, u32[]{:S(2)}, u32[]{:S(2)}) %collective-permute-start.15) | collective-permute-done | bytes 163872 | tf_op jit(solution)/shard_map/ppermute | solution.py:47
  114.8 1.0 add_convert_fusion.4
  116.0 1.4 collective-permute-done.20
  117.6 1.5 %collective-permute-start.24 = (bf16[4,2,96,128]{3,2,0,1:T(8,128)(2,1)S(1)}, bf16[4,2,96,128]{3,2,0,1:T(8,128)(2,1)S(1)}, u32[]{:S(2)}, u32[]{:S(2)}) collective-permute-start(bf16[4,2,96,128]{3,2,0,1:T(8,128)(2,1)S(1)} %fusion.4), channel_id=1, source_target_pairs={{0,4},{4,0},{1,5},{5,1},{2,6},{6,2},{3,7},{7,3},{8,12},{12,8},{9,1... | collective-permute-start | bytes 589832 | tf_op jit(solution)/shard_map/ppermute | solution.py:52
  120.0 1.3 collective-permute-start.21
  121.3 1.3 collective-permute-start.22
  122.6 1.3 collective-permute-start.23
  124.6 0.9 collective-permute-start.25
  125.5 1.2 collective-permute-done.26
  127.3 1.9 %collective-permute-done.25 = bf16[4,96,128]{2,1,0:T(8,128)(2,1)S(1)} collective-permute-done((bf16[4,96,128]{2,1,0:T(8,128)(2,1)S(1)}, bf16[4,96,128]{2,1,0:T(8,128)(2,1)S(1)}, u32[]{:S(2)}, u32[]{:S(2)}) %collective-permute-start.25) | collective-permute-done | bytes 98336 | tf_op jit(solution)/shard_map/ppermute | solution.py:52
  129.3 2.3 %collective-permute-done.27 = bf16[4,112,128]{2,1,0:T(8,128)(2,1)S(1)} collective-permute-done((bf16[4,112,128]{2,1,0:T(8,128)(2,1)S(1)}, bf16[4,112,128]{2,1,0:T(8,128)(2,1)S(1)}, u32[]{:S(2)}, u32[]{:S(2)}) %collective-permute-start.27) | collective-permute-done | bytes 114720 | tf_op jit(solution)/shard_map/ppermute | solution.py:52
  131.7 1.3 collective-permute-done.22
  133.0 3.8 %collective-permute-start.29 = (bf16[208,128]{1,0:T(8,128)(2,1)S(1)}, bf16[208,128]{1,0:T(8,128)(2,1)S(1)}, u32[]{:S(2)}, u32[]{:S(2)}) collective-permute-start(bf16[208,128]{1,0:T(8,128)(2,1)S(1)} %get-tuple-element.100), channel_id=1, source_target_pairs={{0,16},{8,24},{16,0},{24,8},{1,17},{9,25},{17,1},{25,9},{2,18},{10... | collective-permute-start | bytes 159752 | tf_op jit(solution)/shard_map/ppermute | solution.py:42
  136.9 2.1 %grad_hidden.1 = bf16[2,64,4096]{2,1,0:T(8,128)(2,1)} custom-call(bf16[128,128]{1,0:T(8,128)(2,1)S(1)} %pad_maximum_fusion.13.low_ref, bf16[4096,128]{1,0:T(8,128)(2,1)S(1)} %copy-done.4), custom_call_target="tpu_custom_call" | custom-call | flops 134217728 | bytes 2097152 | tf_op jit(solution)/shard_map/grad_hidden/pallas_call | solution.py:364
  139.1 1.0 collective-permute-done.29
  140.0 0.9 collective-permute-done.30
  141.0 0.8 collective-permute-start.32
  141.8 1.1 collective-permute-start.33
  142.9 0.7 pad_maximum_fusion.3
  143.6 1.0 collective-permute-done.31
  144.6 1.1 collective-permute-done.32
  146.7 0.7 pad_maximum_fusion.4
  (161 shorter events, 12.0 us)
Async XLA Ops:
  0.6 0.7 copy-start.31
  0.6 0.7 copy-start.30
  5.7 5.6 %collective-permute-start = (bf16[1,336,128]{2,1,0:T(8,128)(2,1)S(1)}, bf16[1,336,128]{2,1,0:T(8,128)(2,1)S(1)}, u32[]{:S(2)}, u32[]{:S(2)}) collective-permute-start(bf16[1,336,128]{2,1,0:T(8,128)(2,1)S(1)} %bitcast.53), channel_id=1, source_target_pairs={{0,8},{8,0},{16,24},{24,16},{1,9},{9,1},{17,25},{25,17},{2,10},{10... | collective-permute-start | bytes 258056 | tf_op jit(solution)/shard_map/ppermute | solution.py:52
  11.3 10.2 %collective-permute-start.1 = (bf16[2,336,128]{2,1,0:T(8,128)(2,1)S(1)}, bf16[2,336,128]{2,1,0:T(8,128)(2,1)S(1)}, u32[]{:S(2)}, u32[]{:S(2)}) collective-permute-start(bf16[2,336,128]{2,1,0:T(8,128)(2,1)S(1)} %pad_maximum_fusion.7), channel_id=1, source_target_pairs={{0,16},{8,24},{16,0},{24,8},{1,17},{9,25},{17,1},{25,9},{2,18},{10... | collective-permute-start | bytes 516104 | tf_op jit(solution)/shard_map/ppermute | solution.py:52
  21.5 0.7 copy-start.23
  22.2 1.4 slice-start
  22.2 1.4 slice-start.2
  22.2 6.4 %collective-permute-start.2 = (bf16[4,208,128]{2,1,0:T(8,128)(2,1)S(1)}, bf16[4,208,128]{2,1,0:T(8,128)(2,1)S(1)}, u32[]{:S(2)}, u32[]{:S(2)}) collective-permute-start(bf16[4,208,128]{2,1,0:T(8,128)(2,1)S(1)} %slice.199), channel_id=1, source_target_pairs={{0,4},{4,0},{1,5},{5,1},{2,6},{6,2},{3,7},{7,3},{8,12},{12,8},{9,1... | collective-permute-start | bytes 638984 | tf_op jit(solution)/shard_map/ppermute | solution.py:52
  23.6 9.0 %collective-permute-start.3 = (bf16[2,64,1280]{2,1,0:T(8,128)(2,1)S(1)}, bf16[2,64,1280]{2,1,0:T(8,128)(2,1)S(1)}, u32[]{:S(2)}, u32[]{:S(2)}) collective-permute-start(bf16[2,64,1280]{2,1,0:T(8,128)(2,1)S(1)} %pad_maximum_fusion.2.refs_12_.refs_16_), channel_id=1, source_target_pairs={{0,8},{8,16},{16,24},{1,9},{9,17},{17,25},{2,10},{10,18},{18,26},{... | collective-permute-start | bytes 983048 | tf_op jit(solution)/shard_map/ppermute | solution.py:47
  32.6 2.9 %copy-start.13 = (bf16[2,64,1280]{2,1,0:T(8,128)(2,1)}, bf16[2,64,1280]{2,1,0:T(8,128)(2,1)S(1)}, u32[]{:S(2)}) copy-start(bf16[2,64,1280]{2,1,0:T(8,128)(2,1)S(1)} %collective-permute-done.3.refs_13_.refs_17_) | copy-start | bytes 983044
  32.6 10.1 %collective-permute-start.4 = (bf16[8,208,128]{2,1,0:T(8,128)(2,1)S(1)}, bf16[8,208,128]{2,1,0:T(8,128)(2,1)S(1)}, u32[]{:S(2)}, u32[]{:S(2)}) collective-permute-start(bf16[8,208,128]{2,1,0:T(8,128)(2,1)S(1)} %pad_maximum_fusion), channel_id=1, source_target_pairs={{0,2},{1,3},{2,0},{3,1},{4,6},{5,7},{6,4},{7,5},{8,10},{9,11},{10,... | collective-permute-start | bytes 1277960 | tf_op jit(solution)/shard_map/ppermute | solution.py:52
  34.1 8.7 %collective-permute-start.5 = (bf16[2,64,1280]{2,1,0:T(8,128)(2,1)S(1)}, bf16[2,64,1280]{2,1,0:T(8,128)(2,1)}, u32[]{:S(2)}, u32[]{:S(2)}) collective-permute-start(bf16[2,64,1280]{2,1,0:T(8,128)(2,1)S(1)} %collective-permute-done.3.refs_13_.refs_17_), channel_id=1, source_target_pairs={{8,16},{16,24},{9,17},{17,25},{10,18},{18,26},{11,19},{19,27},{12,... | collective-permute-start | bytes 983048 | tf_op jit(solution)/shard_map/ppermute | solution.py:47
  35.6 9.8 %copy-start = (bf16[2,64,4096]{2,1,0:T(8,128)(2,1)S(1)}, bf16[2,64,4096]{2,1,0:T(8,128)(2,1)}, u32[]{:S(2)}) copy-start(bf16[2,64,4096]{2,1,0:T(8,128)(2,1)} %hidden_ref.3) | copy-start | bytes 3145732
  42.8 2.6 %collective-permute-start.6 = (bf16[16,208,128]{2,1,0:T(8,128)(2,1)S(1)}, bf16[16,208,128]{2,1,0:T(8,128)(2,1)}, u32[]{:S(2)}, u32[]{:S(2)}) collective-permute-start(bf16[16,208,128]{2,1,0:T(8,128)(2,1)S(1)} %constant_dynamic-update-slice_fusion.7.own_ref), channel_id=1, source_target_pairs={{0,1},{1,0},{2,3},{3,2},{4,5},{5,4},{6,7},{7,6},{8,9},{9,8},{10,11... | collective-permute-start | bytes 2555912 | tf_op jit(solution)/shard_map/ppermute | solution.py:52
  42.9 1.8 %slice-start.3 = ((bf16[2,64,1024]{2,1,0:T(8,128)(2,1)}), bf16[2,64,384]{2,1,0:T(8,128)(2,1)S(1)}, s32[]{:S(2)}) async-start(bf16[2,64,1024]{2,1,0:T(8,128)(2,1)} %param.12), calls=%async_computation.3 | async-start | bytes 196608 | tf_op jit(solution)/shard_map/slice | solution.py:519
  43.1 1.6 %slice-start.1 = ((bf16[2,64,1024]{2,1,0:T(8,128)(2,1)}), bf16[2,64,384]{2,1,0:T(8,128)(2,1)S(1)}, s32[]{:S(2)}) async-start(bf16[2,64,1024]{2,1,0:T(8,128)(2,1)} %param.11), calls=%async_computation.1 | async-start | bytes 196608 | tf_op jit(solution)/shard_map/slice | solution.py:519
  43.2 17.7 %collective-permute-start.10 = (bf16[2,64,1280]{2,1,0:T(8,128)(2,1)}, bf16[2,64,1280]{2,1,0:T(8,128)(2,1)}, u32[]{:S(2)}, u32[]{:S(2)}) collective-permute-start(bf16[2,64,1280]{2,1,0:T(8,128)(2,1)} %collective-permute-done.5.refs_14_.refs_18_), channel_id=1, source_target_pairs={{16,24},{17,25},{18,26},{19,27},{20,28},{21,29},{22,30},{23,31}} | collective-permute-start | bytes 983048 | tf_op jit(solution)/shard_map/ppermute | solution.py:47
  44.7 16.1 %copy-start.24 = (bf16[2,336,128]{2,1,0:T(8,128)(2,1)S(1)}, bf16[2,336,128]{2,1,0:T(8,128)(2,1)}, u32[]{:S(2)}) copy-start(bf16[2,336,128]{2,1,0:T(8,128)(2,1)} %copy-done.23) | copy-start | bytes 516100
  47.2 1.0 copy-start.3
  48.2 20.4 %copy-start.5 = (bf16[2,64,128]{2,1,0:T(8,128)(2,1)}, bf16[2,64,128]{2,1,0:T(8,128)(2,1)S(1)}, u32[]{:S(2)}) copy-start(bf16[2,64,128]{2,1,0:T(8,128)(2,1)S(1)} %get-tuple-element.50.refs_8_) | copy-start | bytes 98308
  48.2 18.4 %collective-permute-start.7 = (bf16[2,64,128]{2,1,0:T(8,128)(2,1)S(1)}, bf16[2,64,128]{2,1,0:T(8,128)(2,1)S(1)}, u32[]{:S(2)}, u32[]{:S(2)}) collective-permute-start(bf16[2,64,128]{2,1,0:T(8,128)(2,1)S(1)} %get-tuple-element.50.refs_8_), channel_id=1, source_target_pairs={{0,8},{8,16},{16,24},{1,9},{9,17},{17,25},{2,10},{10,18},{18,26},{... | collective-permute-start | bytes 98312 | tf_op jit(solution)/shard_map/ppermute | solution.py:47
  52.6 15.3 %collective-permute-start.8 = (bf16[2,64,128]{2,1,0:T(8,128)(2,1)S(1)}, bf16[2,64,128]{2,1,0:T(8,128)(2,1)S(1)}, u32[]{:S(2)}, u32[]{:S(2)}) collective-permute-start(bf16[2,64,128]{2,1,0:T(8,128)(2,1)S(1)} %get-tuple-element.50.refs_8_), channel_id=1, source_target_pairs={{0,16},{8,24},{1,17},{9,25},{2,18},{10,26},{3,19},{11,27},{4,20},{... | collective-permute-start | bytes 98312 | tf_op jit(solution)/shard_map/ppermute | solution.py:47
  59.5 8.4 %collective-permute-start.9 = (bf16[2,64,128]{2,1,0:T(8,128)(2,1)S(1)}, bf16[2,64,128]{2,1,0:T(8,128)(2,1)S(1)}, u32[]{:S(2)}, u32[]{:S(2)}) collective-permute-start(bf16[2,64,128]{2,1,0:T(8,128)(2,1)S(1)} %get-tuple-element.50.refs_8_), channel_id=1, source_target_pairs={{0,24},{1,25},{2,26},{3,27},{4,28},{5,29},{6,30},{7,31}} | collective-permute-start | bytes 98312 | tf_op jit(solution)/shard_map/ppermute | solution.py:47
  61.0 25.6 %collective-permute-start.11 = (bf16[2,64,768]{2,1,0:T(8,128)(2,1)S(1)}, bf16[2,64,768]{2,1,0:T(8,128)(2,1)S(1)}, u32[]{:S(2)}, u32[]{:S(2)}) collective-permute-start(bf16[2,64,768]{2,1,0:T(8,128)(2,1)S(1)} %pad_maximum_fusion.6.refs_12_.refs_16_), channel_id=1, source_target_pairs={{0,8},{8,16},{16,24},{1,9},{9,17},{17,25},{2,10},{10,18},{18,26},{... | collective-permute-start | bytes 589832 | tf_op jit(solution)/shard_map/ppermute | solution.py:47
  62.3 24.3 %collective-permute-start.12 = (bf16[2,64,768]{2,1,0:T(8,128)(2,1)S(1)}, bf16[2,64,768]{2,1,0:T(8,128)(2,1)S(1)}, u32[]{:S(2)}, u32[]{:S(2)}) collective-permute-start(bf16[2,64,768]{2,1,0:T(8,128)(2,1)S(1)} %pad_maximum_fusion.6.refs_12_.refs_16_), channel_id=1, source_target_pairs={{0,16},{8,24},{1,17},{9,25},{2,18},{10,26},{3,19},{11,27},{4,20},{... | collective-permute-start | bytes 589832 | tf_op jit(solution)/shard_map/ppermute | solution.py:47
  66.6 17.4 %copy-start.7 = (bf16[2,64,128]{2,1,0:T(8,128)(2,1)}, bf16[2,64,128]{2,1,0:T(8,128)(2,1)S(1)}, u32[]{:S(2)}) copy-start(bf16[2,64,128]{2,1,0:T(8,128)(2,1)S(1)} %collective-permute-done.7.refs_9_) | copy-start | bytes 98308
  66.6 20.0 %collective-permute-start.13 = (bf16[2,64,768]{2,1,0:T(8,128)(2,1)S(1)}, bf16[2,64,768]{2,1,0:T(8,128)(2,1)S(1)}, u32[]{:S(2)}, u32[]{:S(2)}) collective-permute-start(bf16[2,64,768]{2,1,0:T(8,128)(2,1)S(1)} %pad_maximum_fusion.6.refs_12_.refs_16_), channel_id=1, source_target_pairs={{0,24},{1,25},{2,26},{3,27},{4,28},{5,29},{6,30},{7,31}} | collective-permute-start | bytes 589832 | tf_op jit(solution)/shard_map/ppermute | solution.py:47
  67.9 16.0 %copy-start.9 = (bf16[2,64,128]{2,1,0:T(8,128)(2,1)}, bf16[2,64,128]{2,1,0:T(8,128)(2,1)S(1)}, u32[]{:S(2)}) copy-start(bf16[2,64,128]{2,1,0:T(8,128)(2,1)S(1)} %collective-permute-done.8.refs_10_) | copy-start | bytes 98308
  68.6 1.2 copy-start.1
  69.8 1.2 copy-start.2
  71.0 0.8 copy-start.12
  71.8 1.0 copy-start.14
  83.9 11.6 %copy-start.15 = (bf16[2,64,640]{2,1,0:T(8,128)(2,1)}, bf16[2,64,640]{2,1,0:T(8,128)(2,1)S(1)}, u32[]{:S(2)}) copy-start(bf16[2,64,640]{2,1,0:T(8,128)(2,1)S(1)} %get-tuple-element.62) | copy-start | bytes 491524
  84.0 12.3 %collective-permute-start.14 = (bf16[2,64,640]{2,1,0:T(8,128)(2,1)S(1)}, bf16[2,64,640]{2,1,0:T(8,128)(2,1)S(1)}, u32[]{:S(2)}, u32[]{:S(2)}) collective-permute-start(bf16[2,64,640]{2,1,0:T(8,128)(2,1)S(1)} %get-tuple-element.61), channel_id=1, source_target_pairs={{8,0},{16,8},{24,16},{9,1},{17,9},{25,17},{10,2},{18,10},{26,18},{... | collective-permute-start | bytes 491528 | tf_op jit(solution)/shard_map/ppermute | solution.py:47
  85.3 11.0 %collective-permute-start.16 = (bf16[2,64,640]{2,1,0:T(8,128)(2,1)S(1)}, bf16[2,64,640]{2,1,0:T(8,128)(2,1)S(1)}, u32[]{:S(2)}, u32[]{:S(2)}) collective-permute-start(bf16[2,64,640]{2,1,0:T(8,128)(2,1)S(1)} %get-tuple-element.63), channel_id=1, source_target_pairs={{24,0},{25,1},{26,2},{27,3},{28,4},{29,5},{30,6},{31,7}} | collective-permute-start | bytes 491528 | tf_op jit(solution)/shard_map/ppermute | solution.py:47
  86.6 0.8 copy-start.6
  87.4 0.8 copy-start.8
  88.1 0.8 copy-start.10
  95.6 0.7 copy-start.21
  96.2 5.2 %copy-start.16 = (bf16[2,64,640]{2,1,0:T(8,128)(2,1)S(1)}, bf16[2,64,640]{2,1,0:T(8,128)(2,1)}, u32[]{:S(2)}) copy-start(bf16[2,64,640]{2,1,0:T(8,128)(2,1)} %copy-done.15) | copy-start | bytes 491524
  97.6 5.8 %collective-permute-start.17 = (bf16[2,64,64]{2,1,0:T(8,128)(2,1)S(1)}, bf16[2,64,64]{2,1,0:T(8,128)(2,1)S(1)}, u32[]{:S(2)}, u32[]{:S(2)}) collective-permute-start(bf16[2,64,64]{2,1,0:T(8,128)(2,1)S(1)} %get-tuple-element.68), channel_id=1, source_target_pairs={{8,0},{16,8},{24,16},{9,1},{17,9},{25,17},{10,2},{18,10},{26,18},{... | collective-permute-start | bytes 49160 | tf_op jit(solution)/shard_map/ppermute | solution.py:47
  98.9 8.0 %collective-permute-start.18 = (bf16[2,64,64]{2,1,0:T(8,128)(2,1)S(1)}, bf16[2,64,64]{2,1,0:T(8,128)(2,1)S(1)}, u32[]{:S(2)}, u32[]{:S(2)}) collective-permute-start(bf16[2,64,64]{2,1,0:T(8,128)(2,1)S(1)} %get-tuple-element.69), channel_id=1, source_target_pairs={{16,0},{24,8},{17,1},{25,9},{18,2},{26,10},{19,3},{27,11},{20,4},{... | collective-permute-start | bytes 49160 | tf_op jit(solution)/shard_map/ppermute | solution.py:47
  100.2 9.2 %collective-permute-start.19 = (bf16[2,64,64]{2,1,0:T(8,128)(2,1)S(1)}, bf16[2,64,64]{2,1,0:T(8,128)(2,1)S(1)}, u32[]{:S(2)}, u32[]{:S(2)}) collective-permute-start(bf16[2,64,64]{2,1,0:T(8,128)(2,1)S(1)} %get-tuple-element.70), channel_id=1, source_target_pairs={{24,0},{25,1},{26,2},{27,3},{28,4},{29,5},{30,6},{31,7}} | collective-permute-start | bytes 49160 | tf_op jit(solution)/shard_map/ppermute | solution.py:47
  101.5 12.6 %collective-permute-start.15 = (bf16[2,64,640]{2,1,0:T(8,128)(2,1)S(1)}, bf16[2,64,640]{2,1,0:T(8,128)(2,1)S(1)}, u32[]{:S(2)}, u32[]{:S(2)}) collective-permute-start(bf16[2,64,640]{2,1,0:T(8,128)(2,1)S(1)} %copy-done.16), channel_id=1, source_target_pairs={{16,0},{24,8},{17,1},{25,9},{18,2},{26,10},{19,3},{27,11},{20,4},{... | collective-permute-start | bytes 491528 | tf_op jit(solution)/shard_map/ppermute | solution.py:47
  109.5 5.3 %copy-start.26 = (bf16[2,64,640]{2,1,0:T(8,128)(2,1)S(1)}, bf16[2,64,640]{2,1,0:T(8,128)(2,1)}, u32[]{:S(2)}) copy-start(bf16[2,64,640]{2,1,0:T(8,128)(2,1)} %copy-done.25) | copy-start | bytes 491524
  109.5 5.3 %copy-start.28 = (bf16[2,64,640]{2,1,0:T(8,128)(2,1)S(1)}, bf16[2,64,640]{2,1,0:T(8,128)(2,1)}, u32[]{:S(2)}) copy-start(bf16[2,64,640]{2,1,0:T(8,128)(2,1)} %copy-done.27) | copy-start | bytes 491524
  114.8 2.6 %collective-permute-start.20 = (bf16[8,2,208,128]{3,2,1,0:T(8,128)(2,1)}, bf16[8,2,208,128]{3,2,1,0:T(8,128)(2,1)S(1)}, u32[]{:S(2)}, u32[]{:S(2)}) collective-permute-start(bf16[8,2,208,128]{3,2,1,0:T(8,128)(2,1)} %get-tuple-element.74), channel_id=1, source_target_pairs={{0,1},{1,0},{2,3},{3,2},{4,5},{5,4},{6,7},{7,6},{8,9},{9,8},{10,11... | collective-permute-start | bytes 2555912 | tf_op jit(solution)/shard_map/ppermute | solution.py:52
  117.6 7.0 %collective-permute-start.24 = (bf16[4,2,96,128]{3,2,0,1:T(8,128)(2,1)S(1)}, bf16[4,2,96,128]{3,2,0,1:T(8,128)(2,1)S(1)}, u32[]{:S(2)}, u32[]{:S(2)}) collective-permute-start(bf16[4,2,96,128]{3,2,0,1:T(8,128)(2,1)S(1)} %fusion.4), channel_id=1, source_target_pairs={{0,4},{4,0},{1,5},{5,1},{2,6},{6,2},{3,7},{7,3},{8,12},{12,8},{9,1... | collective-permute-start | bytes 589832 | tf_op jit(solution)/shard_map/ppermute | solution.py:52
  119.1 0.9 copy-start.22
  119.2 2.2 %copy-start.20 = (bf16[2,64,384]{2,1,0:T(8,128)(2,1)S(1)}, bf16[2,64,384]{2,1,0:T(8,128)(2,1)}, u32[]{:S(2)}) copy-start(bf16[2,64,384]{2,1,0:T(8,128)(2,1)} %copy-done.19) | copy-start | bytes 294916
  119.2 3.5 %copy-start.18 = (bf16[2,64,384]{2,1,0:T(8,128)(2,1)S(1)}, bf16[2,64,384]{2,1,0:T(8,128)(2,1)}, u32[]{:S(2)}) copy-start(bf16[2,64,384]{2,1,0:T(8,128)(2,1)} %copy-done.17) | copy-start | bytes 294916
  119.2 7.4 %collective-permute-start.26 = (bf16[4,2,112,128]{3,2,0,1:T(8,128)(2,1)S(1)}, bf16[4,2,112,128]{3,2,0,1:T(8,128)(2,1)S(1)}, u32[]{:S(2)}, u32[]{:S(2)}) collective-permute-start(bf16[4,2,112,128]{3,2,0,1:T(8,128)(2,1)S(1)} %fusion), channel_id=1, source_target_pairs={{0,2},{1,3},{2,0},{3,1},{4,6},{5,7},{6,4},{7,5},{8,10},{9,11},{10,... | collective-permute-start | bytes 688136 | tf_op jit(solution)/shard_map/ppermute | solution.py:52
  120.0 6.7 %collective-permute-start.21 = (bf16[2,64,384]{2,1,0:T(8,128)(2,1)S(1)}, bf16[2,64,384]{2,1,0:T(8,128)(2,1)S(1)}, u32[]{:S(2)}, u32[]{:S(2)}) collective-permute-start(bf16[2,64,384]{2,1,0:T(8,128)(2,1)S(1)} %copy-done.22), channel_id=1, source_target_pairs={{8,0},{16,8},{24,16},{9,1},{17,9},{25,17},{10,2},{18,10},{26,18},{... | collective-permute-start | bytes 294920 | tf_op jit(solution)/shard_map/ppermute | solution.py:47
  121.3 11.6 %collective-permute-start.22 = (bf16[2,64,384]{2,1,0:T(8,128)(2,1)S(1)}, bf16[2,64,384]{2,1,0:T(8,128)(2,1)S(1)}, u32[]{:S(2)}, u32[]{:S(2)}) collective-permute-start(bf16[2,64,384]{2,1,0:T(8,128)(2,1)S(1)} %copy-done.20), channel_id=1, source_target_pairs={{16,0},{24,8},{17,1},{25,9},{18,2},{26,10},{19,3},{27,11},{20,4},{... | collective-permute-start | bytes 294920 | tf_op jit(solution)/shard_map/ppermute | solution.py:47
  122.6 10.3 %collective-permute-start.23 = (bf16[2,64,384]{2,1,0:T(8,128)(2,1)S(1)}, bf16[2,64,384]{2,1,0:T(8,128)(2,1)S(1)}, u32[]{:S(2)}, u32[]{:S(2)}) collective-permute-start(bf16[2,64,384]{2,1,0:T(8,128)(2,1)S(1)} %copy-done.18), channel_id=1, source_target_pairs={{24,0},{25,1},{26,2},{27,3},{28,4},{29,5},{30,6},{31,7}} | collective-permute-start | bytes 294920 | tf_op jit(solution)/shard_map/ppermute | solution.py:47
  124.6 4.7 %collective-permute-start.25 = (bf16[4,96,128]{2,1,0:T(8,128)(2,1)S(1)}, bf16[4,96,128]{2,1,0:T(8,128)(2,1)S(1)}, u32[]{:S(2)}, u32[]{:S(2)}) collective-permute-start(bf16[4,96,128]{2,1,0:T(8,128)(2,1)S(1)} %fusion.14), channel_id=1, source_target_pairs={{0,2},{1,3},{2,0},{3,1},{4,6},{5,7},{6,4},{7,5},{8,10},{9,11},{10,... | collective-permute-start | bytes 294920 | tf_op jit(solution)/shard_map/ppermute | solution.py:52
  126.7 10.2 %copy-start.4 = (bf16[4096,128]{1,0:T(8,128)(2,1)S(1)}, bf16[4096,128]{1,0:T(8,128)(2,1)}, u32[]{:S(2)}) copy-start(bf16[4096,128]{1,0:T(8,128)(2,1)} %copy-done.3) | copy-start | bytes 3145732
  126.7 4.9 %collective-permute-start.27 = (bf16[4,112,128]{2,1,0:T(8,128)(2,1)S(1)}, bf16[4,112,128]{2,1,0:T(8,128)(2,1)S(1)}, u32[]{:S(2)}, u32[]{:S(2)}) collective-permute-start(bf16[4,112,128]{2,1,0:T(8,128)(2,1)S(1)} %fusion.9), channel_id=1, source_target_pairs={{0,4},{4,0},{1,5},{5,1},{2,6},{6,2},{3,7},{7,3},{8,12},{12,8},{9,1... | collective-permute-start | bytes 344072 | tf_op jit(solution)/shard_map/ppermute | solution.py:52
  133.0 6.1 %collective-permute-start.28 = (bf16[208,128]{1,0:T(8,128)(2,1)S(1)}, bf16[208,128]{1,0:T(8,128)(2,1)S(1)}, u32[]{:S(2)}, u32[]{:S(2)}) collective-permute-start(bf16[208,128]{1,0:T(8,128)(2,1)S(1)} %get-tuple-element.98), channel_id=1, source_target_pairs={{0,8},{8,16},{16,24},{24,0},{1,9},{9,17},{17,25},{25,1},{2,10},{10... | collective-permute-start | bytes 159752 | tf_op jit(solution)/shard_map/ppermute | solution.py:42
  133.0 7.0 %collective-permute-start.29 = (bf16[208,128]{1,0:T(8,128)(2,1)S(1)}, bf16[208,128]{1,0:T(8,128)(2,1)S(1)}, u32[]{:S(2)}, u32[]{:S(2)}) collective-permute-start(bf16[208,128]{1,0:T(8,128)(2,1)S(1)} %get-tuple-element.100), channel_id=1, source_target_pairs={{0,16},{8,24},{16,0},{24,8},{1,17},{9,25},{17,1},{25,9},{2,18},{10... | collective-permute-start | bytes 159752 | tf_op jit(solution)/shard_map/ppermute | solution.py:42
  136.8 4.1 %collective-permute-start.30 = (bf16[208,128]{1,0:T(8,128)(2,1)S(1)}, bf16[208,128]{1,0:T(8,128)(2,1)S(1)}, u32[]{:S(2)}, u32[]{:S(2)}) collective-permute-start(bf16[208,128]{1,0:T(8,128)(2,1)S(1)} %get-tuple-element.99), channel_id=1, source_target_pairs={{0,24},{8,0},{16,8},{24,16},{1,25},{9,1},{17,9},{25,17},{2,26},{10... | collective-permute-start | bytes 159752 | tf_op jit(solution)/shard_map/ppermute | solution.py:42
  141.0 3.6 %collective-permute-start.31 = (bf16[208,128]{1,0:T(8,128)(2,1)S(1)}, bf16[208,128]{1,0:T(8,128)(2,1)S(1)}, u32[]{:S(2)}, u32[]{:S(2)}) collective-permute-start(bf16[208,128]{1,0:T(8,128)(2,1)S(1)} %fusion.12), channel_id=1, source_target_pairs={{0,3},{1,2},{2,1},{3,0},{4,7},{5,6},{6,5},{7,4},{8,11},{9,10},{10,... | collective-permute-start | bytes 159752 | tf_op jit(solution)/shard_map/ppermute | solution.py:52
  141.0 4.7 %collective-permute-start.32 = (bf16[208,128]{1,0:T(8,128)(2,1)S(1)}, bf16[208,128]{1,0:T(8,128)(2,1)S(1)}, u32[]{:S(2)}, u32[]{:S(2)}) collective-permute-start(bf16[208,128]{1,0:T(8,128)(2,1)S(1)} %fusion.12), channel_id=1, source_target_pairs={{0,2},{1,3},{2,0},{3,1},{4,6},{5,7},{6,4},{7,5},{8,10},{9,11},{10,... | collective-permute-start | bytes 159752 | tf_op jit(solution)/shard_map/ppermute | solution.py:52
  141.8 3.9 %collective-permute-start.33 = (bf16[208,128]{1,0:T(8,128)(2,1)S(1)}, bf16[208,128]{1,0:T(8,128)(2,1)S(1)}, u32[]{:S(2)}, u32[]{:S(2)}) collective-permute-start(bf16[208,128]{1,0:T(8,128)(2,1)S(1)} %fusion.12), channel_id=1, source_target_pairs={{0,1},{1,0},{2,3},{3,2},{4,5},{5,4},{6,7},{7,6},{8,9},{9,8},{10,11... | collective-permute-start | bytes 159752 | tf_op jit(solution)/shard_map/ppermute | solution.py:52
  (6 other events, 3.9 us)

commit v6 on v5

--- a/solution.py
+++ b/solution.py
@@ -18,7 +18,6 @@
 WIDE = GROUP * HEAD_DIM
 ROPE_BASE = 500000.0
 HIDDEN_MASK = -1e30
-CHUNKS = ((0, 5), (5, 8))
 LOG2_E = 1.4426950408889634
 
 f32 = jnp.float32
@@ -60,7 +59,7 @@
     return lax.dot_general(a, b, (((ca,), (cb,)), ((), ())), preferred_element_type=f32)
 
 
-def attention_kernel(shards, earlier_count, first, place_ref, *refs):
+def attention_kernel(shards, place_ref, *refs):
     it = iter(refs)
 
     def take(n):
@@ -68,8 +67,6 @@
 
     q_hbm, g_hbm, upq_ref, upv_ref, pk_ref, pv_ref, cos_ref, sin_ref = take(8)
     low_refs, k_refs, v_refs = take(shards), take(shards), take(shards)
-    before = take(2) if earlier_count else None
-    take(earlier_count)
     att_ref, gq_ref, guq_ref, guv_ref, lgq_ref, lgv_ref = take(6)
     gv_refs = take(shards)
     q_buf, g_buf, sems = take(3)
@@ -77,7 +74,7 @@
     group, slot = pl.program_id(0), lax.rem(pl.program_id(0), 2)
 
     def fetches(step, into):
-        at = pl.multiple_of((first + step) * WIDE, WIDE)
+        at = pl.multiple_of(step * WIDE, WIDE)
         return [
             pltpu.make_async_copy(hbm.at[:, :, pl.ds(at, WIDE)], buf.at[into], sems.at[i, into])
             for i, (hbm, buf) in enumerate(((q_hbm, q_buf), (g_hbm, g_buf)))
@@ -105,12 +102,8 @@
 
     @pl.when(pl.program_id(0) == 0)
     def _():
-        if before is None:
-            lgq_ref[...] = jnp.zeros_like(lgq_ref)
-            lgv_ref[...] = jnp.zeros_like(lgv_ref)
-        else:
-            lgq_ref[...] = before[0][...]
-            lgv_ref[...] = before[1][...]
+        lgq_ref[...] = jnp.zeros_like(lgq_ref)
+        lgv_ref[...] = jnp.zeros_like(lgv_ref)
 
     col = lax.broadcasted_iota(jnp.int32, (tokens, span + past), 1)
     row = lax.broadcasted_iota(jnp.int32, (tokens, span + past), 0)
@@ -183,84 +176,74 @@
         guv_ref[0, p] = grad_up_v[rows]
 
 
-def attention_chunk(
-    first, last, place, query_base, grad_out, up_blocks, past, cos, sin, lows, kvs, earlier
-):
+def attention(place, query_base, grad_out, up_blocks, past, cos, sin, lows, kvs):
     shards = len(kvs)
     parts = lax.axis_size("rep")
     seqs, tokens = query_base.shape[:2]
     past_len = past.shape[1]
-    groups = last - first
 
     def whole(x):
         return pl.BlockSpec(x.shape, lambda g: (0,) * len(x.shape))
 
     spec = pl.BlockSpec
-    q_spec = spec((seqs, tokens, WIDE), lambda g: (0, 0, first + g))
+    q_spec = spec((seqs, tokens, WIDE), lambda g: (0, 0, g))
     gv_spec = spec((seqs, tokens, HEAD_DIM), lambda g: (0, 0, g))
     past_block = (seqs, past_len, HEAD_DIM)
     in_specs = [
         spec(memory_space=pltpu.SMEM),
         spec(memory_space=pltpu.HBM),
         spec(memory_space=pltpu.HBM),
-        spec((GROUP, RANK, HEAD_DIM), lambda g: (first + g, 0, 0)),
-        spec((1, RANK, HEAD_DIM), lambda g: (HEADS + first + g, 0, 0)),
-        spec(past_block, lambda g: (0, 0, first + g)),
-        spec(past_block, lambda g: (0, 0, KV_HEADS + first + g)),
+        spec((GROUP, RANK, HEAD_DIM), lambda g: (g, 0, 0)),
+        spec((1, RANK, HEAD_DIM), lambda g: (HEADS + g, 0, 0)),
+        spec(past_block, lambda g: (0, 0, g)),
+        spec(past_block, lambda g: (0, 0, KV_HEADS + g)),
         whole(cos),
         whole(sin),
     ]
     in_specs += [whole(x) for x in lows]
-    in_specs += [spec((seqs, tokens, HEAD_DIM), lambda g: (0, 0, g))] * shards
-    in_specs += [spec((seqs, tokens, HEAD_DIM), lambda g: (0, 0, groups + g))] * shards
-    operands = [place, query_base, grad_out, up_blocks, up_blocks, past, past, cos, sin]
-    operands += list(lows) + list(kvs) + list(kvs)
+    in_specs += [gv_spec] * shards
+    in_specs += [spec((seqs, tokens, HEAD_DIM), lambda g: (0, 0, KV_HEADS + g))] * shards
     shape = jax.ShapeDtypeStruct
     low_q_shape = shape((seqs, tokens, RANK), f32)
     low_v_shape = shape((seqs, shards * tokens, RANK), f32)
-    placed_shapes = [
-        shape(query_base.shape, bf16),
-        shape(query_base.shape, bf16),
-        shape((HEADS, parts, RANK // parts, HEAD_DIM), bf16),
-        shape((KV_HEADS, parts, RANK // parts, HEAD_DIM), bf16),
-    ]
-    placed_specs = [
-        q_spec,
-        q_spec,
-        spec((GROUP, parts, RANK // parts, HEAD_DIM), lambda g: (first + g, 0, 0, 0)),
-        spec((1, parts, RANK // parts, HEAD_DIM), lambda g: (first + g, 0, 0, 0)),
-    ]
-    aliases = {}
-    placed = len(placed_shapes)
-    if earlier is not None:
-        in_specs += [whole(low_q_shape), whole(low_v_shape)]
-        operands += list(earlier[placed : placed + 2])
-        aliases = {len(operands) + i: i for i in range(placed)}
-        in_specs += [spec(memory_space=pl.ANY)] * placed
-        operands += list(earlier[:placed])
+    part_rows = RANK // parts
     scores = GROUP * tokens * (shards * tokens + past_len)
-    pairs = seqs * groups * scores
-    grant = min(12 * 2**20 + 96 * scores, 48 * 2**20)
+    pairs = seqs * KV_HEADS * scores
     return pl.pallas_call(
-        functools.partial(attention_kernel, shards, placed if earlier else 0, first),
-        grid=(groups,),
+        functools.partial(attention_kernel, shards),
+        grid=(KV_HEADS,),
         in_specs=in_specs,
-        out_specs=placed_specs + [whole(low_q_shape), whole(low_v_shape)] + [gv_spec] * shards,
-        out_shape=placed_shapes
-        + [low_q_shape, low_v_shape]
-        + [shape((seqs, tokens, groups * HEAD_DIM), bf16)] * shards,
+        out_specs=[
+            q_spec,
+            q_spec,
+            spec((GROUP, parts, part_rows, HEAD_DIM), lambda g: (g, 0, 0, 0)),
+            spec((1, parts, part_rows, HEAD_DIM), lambda g: (g, 0, 0, 0)),
+            whole(low_q_shape),
+            whole(low_v_shape),
+        ]
+        + [gv_spec] * shards,
+        out_shape=[
+            shape(query_base.shape, bf16),
+            shape(query_base.shape, bf16),
+            shape((HEADS, parts, part_rows, HEAD_DIM), bf16),
+            shape((KV_HEADS, parts, part_rows, HEAD_DIM), bf16),
+            low_q_shape,
+            low_v_shape,
+        ]
+        + [shape((seqs, tokens, KV), bf16)] * shards,
         scratch_shapes=[
             pltpu.VMEM((2, seqs, tokens, WIDE), bf16),
             pltpu.VMEM((2, seqs, tokens, WIDE), bf16),
             pltpu.SemaphoreType.DMA((2, 2)),
         ],
-        input_output_aliases=aliases,
-        compiler_params=pltpu.CompilerParams(vmem_limit_bytes=grant),
+        compiler_params=pltpu.CompilerParams(
+            vmem_limit_bytes=min(8 * 2**20 + 96 * scores, 48 * 2**20)
+        ),
         cost_estimate=pl.CostEstimate(
-            flops=pairs * HEAD_DIM * 28, bytes_accessed=16 * 1024 * 1024, transcendentals=pairs
+            flops=pairs * HEAD_DIM * 120, bytes_accessed=2**16, transcendentals=pairs
         ),
         name="attention",
-    )(*operands)
+    )(place, query_base, grad_out, up_blocks, up_blocks, past, past, cos, sin, *lows, *kvs, *kvs)
 
 
 def low_rank_kernel(
@@ -289,15 +272,35 @@
     copy.wait()
 
 
+def pack_kernel(rp, part_ref, down_ref, up_ref, past_ref, out_ref):
+    r = part_ref[0]
+    down_rows, up_rows = down_ref.shape[0] // rp, RANK // rp
+    out_ref[0, :down_rows] = down_ref[pl.ds(pl.multiple_of(r * down_rows, down_rows), down_rows)]
+    at = pl.multiple_of(r * up_rows, up_rows)
+    lo = down_rows
+    for j in range(up_ref.shape[1] // HEAD_DIM):
+        cols = slice(j * HEAD_DIM, (j + 1) * HEAD_DIM)
+        out_ref[0, lo : lo + up_rows] = up_ref[pl.ds(at, up_rows), cols]
+        lo += up_rows
+    out_ref[0, lo:] = past_ref[...]
+
+
 def pack_adapters(adapter_down, adapter_up, own_past):
     sp, rp, r = lax.axis_size("sp"), lax.axis_size("rep"), lax.axis_index("rep")
     down_rows, up_rows = adapter_down.shape[0] // rp, RANK // rp
     blocks = adapter_up.shape[1] // HEAD_DIM
-    down = lax.dynamic_slice_in_dim(adapter_down, r * down_rows, down_rows, 0)
-    up = lax.dynamic_slice_in_dim(adapter_up, r * up_rows, up_rows, 0)
-    up = [up[:, j * HEAD_DIM : (j + 1) * HEAD_DIM] for j in range(blocks)]
-    rows = down_rows + blocks * up_rows
-    buf = jnp.concatenate([down] + up + [own_past.reshape(-1, 2 * RANK)], axis=0)[None]
+    rows = down_rows + adapter_up.shape[1] // HEAD_DIM * up_rows
+    packed_past = own_past.reshape(-1, 2 * RANK)
+    vmem = pl.BlockSpec(memory_space=pltpu.VMEM)
+    buf = pl.pallas_call(
+        functools.partial(pack_kernel, rp),
+        in_specs=[pl.BlockSpec(memory_space=pltpu.SMEM)] + [vmem] * 3,
+        out_specs=vmem,
+        out_shape=jax.ShapeDtypeStruct((1, rows + packed_past.shape[0], 2 * RANK), bf16),
+        compiler_params=pltpu.CompilerParams(vmem_limit_bytes=8 * 1024 * 1024),
+        cost_estimate=pl.CostEstimate(flops=0, bytes_accessed=2**19, transcendentals=0),
+        name="pack",
+    )(r.astype(jnp.int32).reshape(1), adapter_down, adapter_up, packed_past)
     step = 1
     while step < sp:
         buf = jnp.concatenate([buf, partner(buf, "sp", step)], axis=0)
@@ -333,9 +336,9 @@
             jax.ShapeDtypeStruct((HEADS + KV_HEADS, RANK, HEAD_DIM), bf16),
             jax.ShapeDtypeStruct((seqs, tokens, 2 * RANK), bf16),
         ],
-        compiler_params=pltpu.CompilerParams(vmem_limit_bytes=16 * 1024 * 1024),
+        compiler_params=pltpu.CompilerParams(vmem_limit_bytes=12 * 1024 * 1024),
         cost_estimate=pl.CostEstimate(
-            flops=2 * seqs * tokens * D * 2 * RANK, bytes_accessed=5 * 2**20, transcendentals=0
+            flops=2 * seqs * tokens * D * 2 * RANK, bytes_accessed=2**16, transcendentals=0
         ),
         name="low_rank",
     )(index, buf, other, hidden)
@@ -370,9 +373,9 @@
         ],
         out_specs=pl.BlockSpec((seqs, tokens, columns), lambda i: (0, 0, i)),
         out_shape=jax.ShapeDtypeStruct((seqs, tokens, D), bf16),
-        compiler_params=pltpu.CompilerParams(vmem_limit_bytes=16 * 1024 * 1024),
+        compiler_params=pltpu.CompilerParams(vmem_limit_bytes=12 * 1024 * 1024),
         cost_estimate=pl.CostEstimate(
-            flops=2 * seqs * tokens * D * 2 * RANK, bytes_accessed=2**21, transcendentals=0
+            flops=16 * seqs * tokens * D * 2 * RANK, bytes_accessed=2**16, transcendentals=0
         ),
         name="grad_hidden",
     )(low_grad, down_full)
@@ -416,7 +419,7 @@
             out_specs=[vmem] * 2,
             out_shape=[packed] * 2,
             scratch_shapes=[pltpu.VMEM((rp, down_rows, 2 * RANK), bf16)],
-            compiler_params=pltpu.CompilerParams(vmem_limit_bytes=16 * 1024 * 1024),
+            compiler_params=pltpu.CompilerParams(vmem_limit_bytes=12 * 1024 * 1024),
             cost_estimate=pl.CostEstimate(
                 flops=2 * hidden.size * 2 * RANK, bytes_accessed=5 * 2**20, transcendentals=0
             ),
@@ -434,19 +437,18 @@
     return send, keep
 
 
-def finish_grads(send, keep, before, values, low_grad, hidden_of):
+def finish_grads(send, keep, values, low_grad, hidden_of):
     sp, fs, rp = (lax.axis_size(a) for a in ("sp", "fsdp", "rep"))
     z, r = lax.axis_index("sp"), lax.axis_index("rep")
     shards, _, rows, lanes = send.shape
-    got = partner(tie(send, *before), "rep", 1)
-    then = [along(tie(v, got), "sp", -k) for k, v in enumerate(values, 1)]
+    got = partner(tie(send, values[0]), "rep", 1)
     fs_bits, rep_bits = fs.bit_length() - 1, rp.bit_length() - 2
     labels = [("fsdp", b) for b in reversed(range(fs_bits))]
     labels += [("rep", b + 1) for b in reversed(range(rep_bits))]
     shape = (sp,) + (2,) * len(labels) + (rows, lanes)
     terms = [a.reshape(shape) for a in (keep, got)]
 
-    def halve(terms, order, before):
+    def halve(terms, order):
         left = list(labels)
         for step, label in enumerate(order):
             axis, bit = label
@@ -459,18 +461,18 @@
                 return sum(a.astype(f32) for a in parts).astype(bf16)
 
             send = pick(1 - mine)
-            if step == 1:
-                send = tie(send, *before)
+            if step == 0:
+                send = tie(send, *values[2:])
             terms = [pick(mine), partner(send, axis, 1 << bit)]
         return sum(a.astype(f32) for a in terms).astype(bf16)
 
     cut = rows // 32 * 16
     first_rep, first_fsdp = labels[::-1], labels
-    over_sp = halve([a[..., cut:, :] for a in terms], first_rep, then[:1])
+    over_sp = halve([a[..., cut:, :] for a in terms], first_rep)
     if cut:
-        other = halve([a[..., :cut, :] for a in terms], first_fsdp, ())
+        other = halve([a[..., :cut, :] for a in terms], first_fsdp)
         over_sp = jnp.concatenate([other, over_sp], axis=1)
-    over_sp = tie(over_sp, *then)
+    over_sp = tie(over_sp, *values)
     total = lax.dynamic_index_in_dim(over_sp, z, 0, keepdims=False).astype(f32)
     for k in range(1, sp):
         send = lax.dynamic_index_in_dim(over_sp, lax.rem(z + k, sp), 0, keepdims=False)
@@ -494,7 +496,7 @@
             up = [up[lo : lo + up_rows] for lo in range(0, up.shape[0], up_rows)]
             up = jnp.concatenate(up, axis=1)
         ups.append(up.reshape(up_rows, up_width))
-    return grad_down, jnp.concatenate(ups, axis=0), then, grad_hidden
+    return grad_down, jnp.concatenate(ups, axis=0), grad_hidden
 
 
 def body(
@@ -513,11 +515,7 @@
     seqs, tokens = hidden.shape[:2]
     past_len = past_keys.shape[1] * sp
     own_past = jnp.concatenate([past_keys, past_values], axis=2)
-    own_kvs = []
-    for first, last in CHUNKS:
-        cols = slice(first * HEAD_DIM, last * HEAD_DIM)
-        own_kvs.append(jnp.concatenate([key_span[:, :, cols], value_base[:, :, cols]], axis=2))
-    early = [own_kvs[0]]
+    kvs = [jnp.concatenate([key_span, value_base], axis=2)]
     even = adapter_up.shape[1] % HEAD_DIM == 0
     if even:
         buf, past = pack_adapters(adapter_down, adapter_up, own_past)
@@ -525,35 +523,24 @@
         buf = own_past
         past = [own_past] + [cyclic(own_past, "sp", k) for k in range(1, sp)]
         past = jnp.concatenate(past, axis=1)
-    early.append(along(tie(early[0], buf), "sp", 1))
+    kvs.append(along(tie(kvs[0], buf), "sp", 1))
     for k in range(2, sp):
-        early.append(along(early[k - 1], "sp", 1, k - 1))
+        kvs.append(along(kvs[k - 1], "sp", 1, k - 1))
     if even:
-        down_full, up_blocks, low_own = adapters_packed(hidden, buf, early[1], early[min(2, sp - 1)])
+        down_full, up_blocks, low_own = adapters_packed(hidden, buf, kvs[1], kvs[min(2, sp - 1)])
     else:
         down_full, up_blocks, low_own = adapters_plain(hidden, adapter_down, adapter_up)
     lows = [low_own] + [along(low_own, "sp", k) for k in range(1, sp)]
-    own_late = tie(own_kvs[1], low_own, early[-1])
-    late = [own_kvs[1]] + [along(own_late, "sp", k) for k in range(1, sp)]
     cos, sin = rotary_tables(tokens, past_len + z * tokens)
     place = z.astype(jnp.int32).reshape(1)
 
-    made = None
-    value_own, value_got = [], []
-    for (first, last), kvs in zip(CHUNKS, (early, late)):
-        made = attention_chunk(
-            first, last, place, query_base, grad_out, up_blocks, past, cos, sin, lows, kvs, made
-        )
-        gvs = made[6:]
-        value_own.append(gvs[0])
-        if last < KV_HEADS:
-            value_got.append([along(gvs[k], "sp", -k) for k in range(1, sp)])
+    made = attention(place, query_base, grad_out, up_blocks, past, cos, sin, lows, kvs)
     attended, grad_query, guq, guv, low_grad_q, low_grad_v = made[:6]
+    value_own, value_got = made[6], [along(made[6 + k], "sp", -k) for k in range(1, sp)]
 
     low_v_total = low_grad_v[:, :tokens]
     for k in range(1, sp):
         part = low_grad_v[:, k * tokens : (k + 1) * tokens].astype(bf16)
-        part = tie(part, value_got[0][0], value_got[0][-1])
         low_v_total = low_v_total + along(part, "sp", -k).astype(f32)
     low_grad = (
         jnp.concatenate([low_grad_q, low_v_total], axis=2)
@@ -561,22 +548,16 @@
         .reshape(seqs * tokens, 2 * RANK)
     )
     send, keep = packed_grads(hidden, low_grad, guq, guv, sp * fs)
-    grad_down, grad_up, got, grad_hidden = finish_grads(
-        send, keep, value_got[0], gvs[1:], low_grad, lambda x: grad_hidden_of(x, down_full, seqs, tokens)
+    grad_down, grad_up, grad_hidden = finish_grads(
+        send, keep, value_got, low_grad, lambda x: grad_hidden_of(x, down_full, seqs, tokens)
     )
-    value_got.append(got)
-
-    sums = []
-    for own, got in zip(value_own, value_got):
-        total = own.astype(f32)
-        for part in got:
-            total = total + part.astype(f32)
-        sums.append(total.astype(bf16))
-    grad_value = jnp.concatenate(sums, axis=2)
+    grad_value = value_own.astype(f32)
+    for part in value_got:
+        grad_value = grad_value + part.astype(f32)
     return (
         attended,
         grad_query,
-        grad_value,
+        grad_value.astype(bf16),
         grad_hidden,
         grad_down,
         grad_up,

time: 149 us -> 146 us (0.980)
  waiting for transfers between devices: 46.1 us -> 59.3 us
  starting transfers between devices: 54.9 us -> 47.7 us
  local copies, waits for them, and re-layouts: 17.2 us -> 10.2 us
    ppermute x18 -> x12, waiting for transfers between devices: 14.9 us -> 23.4 us  [along(): lax.ppermute(x, axis, [(i, i + shift) for i in range(start, n) if 0 <= i...]
    unnamed x87 -> x62, local copies, waits for them, and re-layouts: 16.6 us -> 9.64 us
    ppermute x18 -> x12, starting transfers between devices: 36.5 us -> 30 us  [along(): lax.ppermute(x, axis, [(i, i + shift) for i in range(start, n) if 0 <= i...]
    ppermute x13, waiting for transfers between devices: 29.3 us -> 35.4 us  [partner(): return lax.ppermute(x, axis, [(i, i ^ mask) for i in range(n)])]
  transfers between devices with their start and end apart: 34 -> 28, of which waited for: 20 -> 20; matrix products, arithmetic and copies ran while one was open for 2% -> 2% of each run, Pallas kernels for 16% -> 3%
where the time goes in v6:
time: 146 us; the launch traced here: 145 us
  waiting for transfers between devices  59.3 us (41%)
  starting transfers between devices  47.7 us (33%)
  Pallas kernels  22.2 us (15%)
  local copies, waits for them, and re-layouts  10.2 us (7%)
  other arithmetic  4.17 us (3%)
    ppermute x13, waiting for transfers between devices, partner(): return lax.ppermute(x, axis, [(i, i ^ mask) for i in range(n)])  35.4 us
    ppermute x12, starting transfers between devices, along(): lax.ppermute(x, axis, [(i, i + shift) for i in range(start, n) if 0 <= i...  30 us
    ppermute x12, waiting for transfers between devices, along(): lax.ppermute(x, axis, [(i, i + shift) for i in range(start, n) if 0 <= i...  23.4 us
    pallas_call x1, Pallas kernels, attention(): pl.pallas_call(functools.partial(attention_kernel, shards), grid=(KV_HEAD...  17.3 us
    ppermute x13, starting transfers between devices, partner(): return lax.ppermute(x, axis, [(i, i ^ mask) for i in range(n)])  13.9 us
    unnamed x62, local copies, waits for them, and re-layouts  9.64 us
    ppermute x3, starting transfers between devices, cyclic(): return lax.ppermute(x, axis, [(i, (i + shift) % n) for i in range(n)])  3.86 us
  transfers between devices with their start and end apart: 28, of which 20 were waited for; matrix products, arithmetic and copies ran while one was open for 2% of the time, Pallas kernels for 3%

profile of v6, /device:TPU:0, one launch (start us, length us, event | category | flops | bytes accessed | tf_op | source)
XLA Modules:
  0.0 145.0 jit_solution(15823224802063308856)
XLA Ops:
  0.6 0.8 pad_maximum_fusion.7
  1.5 0.1 copy-done.1
  1.6 0.9 copy-done.2
  2.5 3.1 %collective-permute-start = (bf16[1,336,128]{2,1,0:T(8,128)(2,1)S(1)}, bf16[1,336,128]{2,1,0:T(8,128)(2,1)S(1)}, u32[]{:S(2)}, u32[]{:S(2)}) collective-permute-start(bf16[1,336,128]{2,1,0:T(8,128)(2,1)S(1)} %pack.1), channel_id=1, source_target_pairs={{0,8},{8,0},{16,24},{24,16},{1,9},{9,1},{17,25},{25,17},{2,10},{10... | collective-permute-start | bytes 258056 | tf_op jit(solution)/shard_map/ppermute | solution.py:51
  5.6 2.5 %collective-permute-done = bf16[1,336,128]{2,1,0:T(8,128)(2,1)S(1)} collective-permute-done((bf16[1,336,128]{2,1,0:T(8,128)(2,1)S(1)}, bf16[1,336,128]{2,1,0:T(8,128)(2,1)S(1)}, u32[]{:S(2)}, u32[]{:S(2)}) %collective-permute-start) | collective-permute-done | bytes 86048 | tf_op jit(solution)/shard_map/ppermute | solution.py:51
  8.1 3.0 %collective-permute-start.1 = (bf16[2,336,128]{2,1,0:T(8,128)(2,1)S(1)}, bf16[2,336,128]{2,1,0:T(8,128)(2,1)S(1)}, u32[]{:S(2)}, u32[]{:S(2)}) collective-permute-start(bf16[2,336,128]{2,1,0:T(8,128)(2,1)S(1)} %pad_maximum_fusion.4), channel_id=1, source_target_pairs={{0,16},{8,24},{16,0},{24,8},{1,17},{9,25},{17,1},{25,9},{2,18},{10... | collective-permute-start | bytes 516104 | tf_op jit(solution)/shard_map/ppermute | solution.py:51
  11.2 7.1 %collective-permute-done.1 = bf16[2,336,128]{2,1,0:T(8,128)(2,1)S(1)} collective-permute-done((bf16[2,336,128]{2,1,0:T(8,128)(2,1)S(1)}, bf16[2,336,128]{2,1,0:T(8,128)(2,1)S(1)}, u32[]{:S(2)}, u32[]{:S(2)}) %collective-permute-start.1) | collective-permute-done | bytes 172064 | tf_op jit(solution)/shard_map/ppermute | solution.py:51
  18.4 0.6 copy-done.16
  19.0 2.4 %collective-permute-start.3 = (bf16[2,64,2048]{2,1,0:T(8,128)(2,1)S(1)}, bf16[2,64,2048]{2,1,0:T(8,128)(2,1)S(1)}, u32[]{:S(2)}, u32[]{:S(2)}) collective-permute-start(bf16[2,64,2048]{2,1,0:T(8,128)(2,1)S(1)} %constant_dynamic-update-slice_fusion.refs_12_.refs_16_), channel_id=1, source_target_pairs={{0,8},{8,16},{16,24},{1,9},{9,17},{17,25},{2,10},{10,18},{18,26},{... | collective-permute-start | bytes 1572872 | tf_op jit(solution)/shard_map/ppermute | solution.py:46
  21.4 1.6 %collective-permute-start.2 = (bf16[4,208,128]{2,1,0:T(8,128)(2,1)S(1)}, bf16[4,208,128]{2,1,0:T(8,128)(2,1)S(1)}, u32[]{:S(2)}, u32[]{:S(2)}) collective-permute-start(bf16[4,208,128]{2,1,0:T(8,128)(2,1)S(1)} %slice.163), channel_id=1, source_target_pairs={{0,4},{4,0},{1,5},{5,1},{2,6},{6,2},{3,7},{7,3},{8,12},{12,8},{9,1... | collective-permute-start | bytes 638984 | tf_op jit(solution)/shard_map/ppermute | solution.py:51
  23.0 5.0 %collective-permute-done.2 = bf16[4,208,128]{2,1,0:T(8,128)(2,1)S(1)} collective-permute-done((bf16[4,208,128]{2,1,0:T(8,128)(2,1)S(1)}, bf16[4,208,128]{2,1,0:T(8,128)(2,1)S(1)}, u32[]{:S(2)}, u32[]{:S(2)}) %collective-permute-start.2) | collective-permute-done | bytes 213024 | tf_op jit(solution)/shard_map/ppermute | solution.py:51
  28.0 4.3 %collective-permute-done.3.refs_13_.refs_17_ = bf16[2,64,2048]{2,1,0:T(8,128)(2,1)S(1)} collective-permute-done((bf16[2,64,2048]{2,1,0:T(8,128)(2,1)S(1)}, bf16[2,64,2048]{2,1,0:T(8,128)(2,1)S(1)}, u32[]{:S(2)}, u32[]{:S(2)}) %collective-permute-start.3) | collective-permute-done | bytes 524320 | tf_op jit(solution)/shard_map/ppermute | solution.py:46
  32.3 1.5 %collective-permute-start.4 = (bf16[8,208,128]{2,1,0:T(8,128)(2,1)S(1)}, bf16[8,208,128]{2,1,0:T(8,128)(2,1)S(1)}, u32[]{:S(2)}, u32[]{:S(2)}) collective-permute-start(bf16[8,208,128]{2,1,0:T(8,128)(2,1)S(1)} %pad_maximum_fusion), channel_id=1, source_target_pairs={{0,2},{1,3},{2,0},{3,1},{4,6},{5,7},{6,4},{7,5},{8,10},{9,11},{10,... | collective-permute-start | bytes 1277960 | tf_op jit(solution)/shard_map/ppermute | solution.py:51
  33.8 1.5 %collective-permute-start.5 = (bf16[2,64,2048]{2,1,0:T(8,128)(2,1)S(1)}, bf16[2,64,2048]{2,1,0:T(8,128)(2,1)}, u32[]{:S(2)}, u32[]{:S(2)}) collective-permute-start(bf16[2,64,2048]{2,1,0:T(8,128)(2,1)S(1)} %collective-permute-done.3.refs_13_.refs_17_), channel_id=1, source_target_pairs={{8,16},{16,24},{9,17},{17,25},{10,18},{18,26},{11,19},{19,27},{12,... | collective-permute-start | bytes 1572872 | tf_op jit(solution)/shard_map/ppermute | solution.py:46
  35.4 7.4 %collective-permute-done.4 = bf16[8,208,128]{2,1,0:T(8,128)(2,1)S(1)} collective-permute-done((bf16[8,208,128]{2,1,0:T(8,128)(2,1)S(1)}, bf16[8,208,128]{2,1,0:T(8,128)(2,1)S(1)}, u32[]{:S(2)}, u32[]{:S(2)}) %collective-permute-start.4) | collective-permute-done | bytes 426016 | tf_op jit(solution)/shard_map/ppermute | solution.py:51
  42.9 1.5 %collective-permute-start.10 = (bf16[2,64,2048]{2,1,0:T(8,128)(2,1)}, bf16[2,64,2048]{2,1,0:T(8,128)(2,1)}, u32[]{:S(2)}, u32[]{:S(2)}) collective-permute-start(bf16[2,64,2048]{2,1,0:T(8,128)(2,1)} %collective-permute-done.5.refs_14_.refs_18_), channel_id=1, source_target_pairs={{16,24},{17,25},{18,26},{19,27},{20,28},{21,29},{22,30},{23,31}} | collective-permute-start | bytes 1572872 | tf_op jit(solution)/shard_map/ppermute | solution.py:46
  44.5 0.2 fusion.15
  44.8 0.5 collective-permute-done.6.other_ref
  45.3 1.2 low_rank.1
  46.5 1.0 copy-done.5
  47.5 0.8 copy-done.7
  48.3 8.4 %collective-permute-start.7 = (bf16[2,64,128]{2,1,0:T(8,128)(2,1)S(1)}, bf16[2,64,128]{2,1,0:T(8,128)(2,1)S(1)}, u32[]{:S(2)}, u32[]{:S(2)}) collective-permute-start(bf16[2,64,128]{2,1,0:T(8,128)(2,1)S(1)} %get-tuple-element.34.refs_8_), channel_id=1, source_target_pairs={{0,8},{8,16},{16,24},{1,9},{9,17},{17,25},{2,10},{10,18},{18,26},{... | collective-permute-start | bytes 98312 | tf_op jit(solution)/shard_map/ppermute | solution.py:46
  56.7 7.2 %collective-permute-start.8 = (bf16[2,64,128]{2,1,0:T(8,128)(2,1)S(1)}, bf16[2,64,128]{2,1,0:T(8,128)(2,1)S(1)}, u32[]{:S(2)}, u32[]{:S(2)}) collective-permute-start(bf16[2,64,128]{2,1,0:T(8,128)(2,1)S(1)} %get-tuple-element.34.refs_8_), channel_id=1, source_target_pairs={{0,16},{8,24},{1,17},{9,25},{2,18},{10,26},{3,19},{11,27},{4,20},{... | collective-permute-start | bytes 98312 | tf_op jit(solution)/shard_map/ppermute | solution.py:46
  63.9 1.3 collective-permute-start.9
  65.4 0.1 collective-permute-done.8.refs_10_
  65.5 1.3 collective-permute-done.9.refs_11_
  66.8 1.2 copy-done.3
  68.0 1.2 copy-done.4
  69.3 1.1 copy-done.8
  70.3 1.0 copy-done.10
  71.4 17.3 %attention.1 = (bf16[2,64,4096]{2,1,0:T(8,128)(2,1)}, bf16[2,64,4096]{2,1,0:T(8,128)(2,1)}, bf16[32,4,16,128]{3,2,1,0:T(8,128)(2,1)S(1)}, bf16[8,4,16,128]{3,2,1...) custom-call(s32[1]{0:T(128)} %bitcast.place_ref, ...), custom_call_target="tpu_custom_call" | custom-call | flops 17112760320 | bytes 65536 | tf_op jit(solution)/shard_map/attention/pallas_call | solution.py:212
  88.7 0.6 copy-done.11
  89.4 0.1 copy-done.13
  89.5 1.3 collective-permute-start.14
  90.8 1.3 collective-permute-start.15
  92.1 1.3 collective-permute-start.16
  93.4 1.3 collective-permute-start.11
  94.7 0.6 collective-permute-done.14
  95.3 2.6 %collective-permute-done.15 = bf16[2,64,64]{2,1,0:T(8,128)(2,1)S(1)} collective-permute-done((bf16[2,64,64]{2,1,0:T(8,128)(2,1)S(1)}, bf16[2,64,64]{2,1,0:T(8,128)(2,1)S(1)}, u32[]{:S(2)}, u32[]{:S(2)}) %collective-permute-start.15) | collective-permute-done | bytes 16416 | tf_op jit(solution)/shard_map/ppermute | solution.py:46
  97.9 3.2 %collective-permute-done.16 = bf16[2,64,64]{2,1,0:T(8,128)(2,1)S(1)} collective-permute-done((bf16[2,64,64]{2,1,0:T(8,128)(2,1)S(1)}, bf16[2,64,64]{2,1,0:T(8,128)(2,1)S(1)}, u32[]{:S(2)}, u32[]{:S(2)}) %collective-permute-start.16) | collective-permute-done | bytes 16416 | tf_op jit(solution)/shard_map/ppermute | solution.py:46
  101.1 0.1 pad_maximum_fusion.10.low_ref
  101.2 1.6 %adapter_grads.1 = (bf16[8,2,208,128]{3,2,1,0:T(8,128)(2,1)}, bf16[8,2,208,128]{3,2,1,0:T(8,128)(2,1)S(1)}) custom-call(s32[1]{0:T(128)} %bitcast.6.core_ref, bf16[2,64,4096]{2,1,0:T(8,128)(2,1)S(1)} %copy-done, bf16[128,128]{1,0:T(8,128)(2,1)S(1)} %pad_maximum_fusion.10.low_ref, bf16[32,4,16,128]{3,2,1,0:T(8,128)(2,1)S(1)} %get-tuple-element.43.guq_ref, ...), custom_call_target="tpu_custom_call" | custom-call | flops 134217728 | bytes 5242880 | tf_op jit(solution)/shard_map/adapter_grads/pallas_call | solution.py:416
  102.8 1.4 collective-permute-done.11
  104.2 0.7 copy-done.18
  104.9 1.3 collective-permute-start.13
  106.2 1.3 collective-permute-start.12
  107.8 9.9 %collective-permute-done.13 = bf16[2,64,1024]{2,1,0:T(8,128)(2,1)S(1)} collective-permute-done((bf16[2,64,1024]{2,1,0:T(8,128)(2,1)S(1)}, bf16[2,64,1024]{2,1,0:T(8,128)(2,1)S(1)}, u32[]{:S(2)}, u32[]{:S(2)}) %collective-permute-start.13) | collective-permute-done | bytes 262176 | tf_op jit(solution)/shard_map/ppermute | solution.py:46
  117.8 1.5 %collective-permute-start.18 = (bf16[4,2,96,128]{3,2,0,1:T(8,128)(2,1)S(1)}, bf16[4,2,96,128]{3,2,0,1:T(8,128)(2,1)S(1)}, u32[]{:S(2)}, u32[]{:S(2)}) collective-permute-start(bf16[4,2,96,128]{3,2,0,1:T(8,128)(2,1)S(1)} %fusion.4), channel_id=1, source_target_pairs={{0,4},{4,0},{1,5},{5,1},{2,6},{6,2},{3,7},{7,3},{8,12},{12,8},{9,1... | collective-permute-start | bytes 589832 | tf_op jit(solution)/shard_map/ppermute | solution.py:51
  119.4 0.6 collective-permute-start.20
  120.1 3.8 %collective-permute-done.18 = bf16[4,2,96,128]{3,2,0,1:T(8,128)(2,1)S(1)} collective-permute-done((bf16[4,2,96,128]{3,2,0,1:T(8,128)(2,1)S(1)}, bf16[4,2,96,128]{3,2,0,1:T(8,128)(2,1)S(1)}, u32[]{:S(2)}, u32[]{:S(2)}) %collective-permute-start.18) | collective-permute-done | bytes 196640 | tf_op jit(solution)/shard_map/ppermute | solution.py:51
  123.9 0.6 collective-permute-start.19
  124.5 2.4 %collective-permute-done.20 = bf16[4,2,112,128]{3,2,0,1:T(8,128)(2,1)S(1)} collective-permute-done((bf16[4,2,112,128]{3,2,0,1:T(8,128)(2,1)S(1)}, bf16[4,2,112,128]{3,2,0,1:T(8,128)(2,1)S(1)}, u32[]{:S(2)}, u32[]{:S(2)}) %collective-permute-start.20) | collective-permute-done | bytes 229408 | tf_op jit(solution)/shard_map/ppermute | solution.py:51
  127.0 1.6 %collective-permute-done.19 = bf16[4,96,128]{2,1,0:T(8,128)(2,1)S(1)} collective-permute-done((bf16[4,96,128]{2,1,0:T(8,128)(2,1)S(1)}, bf16[4,96,128]{2,1,0:T(8,128)(2,1)S(1)}, u32[]{:S(2)}, u32[]{:S(2)}) %collective-permute-start.19) | collective-permute-done | bytes 98336 | tf_op jit(solution)/shard_map/ppermute | solution.py:51
  128.6 3.2 %collective-permute-done.21 = bf16[4,112,128]{2,1,0:T(8,128)(2,1)S(1)} collective-permute-done((bf16[4,112,128]{2,1,0:T(8,128)(2,1)S(1)}, bf16[4,112,128]{2,1,0:T(8,128)(2,1)S(1)}, u32[]{:S(2)}, u32[]{:S(2)}) %collective-permute-start.21) | collective-permute-done | bytes 114720 | tf_op jit(solution)/shard_map/ppermute | solution.py:51
  132.1 3.7 %collective-permute-start.24 = (bf16[208,128]{1,0:T(8,128)(2,1)S(1)}, bf16[208,128]{1,0:T(8,128)(2,1)S(1)}, u32[]{:S(2)}, u32[]{:S(2)}) collective-permute-start(bf16[208,128]{1,0:T(8,128)(2,1)S(1)} %get-tuple-element.67), channel_id=1, source_target_pairs={{0,24},{8,0},{16,8},{24,16},{1,25},{9,1},{17,9},{25,17},{2,26},{10... | collective-permute-start | bytes 159752 | tf_op jit(solution)/shard_map/ppermute | solution.py:41
  135.8 2.1 %grad_hidden.1 = bf16[2,64,4096]{2,1,0:T(8,128)(2,1)} custom-call(bf16[128,128]{1,0:T(8,128)(2,1)S(1)} %pad_maximum_fusion.10.low_ref, bf16[4096,128]{1,0:T(8,128)(2,1)S(1)} %copy-done.6), custom_call_target="tpu_custom_call" | custom-call | flops 1073741824 | bytes 65536 | tf_op jit(solution)/shard_map/grad_hidden/pallas_call | solution.py:367
  137.9 0.5 collective-permute-done.24
  138.6 0.6 collective-permute-start.26
  139.2 1.3 collective-permute-start.27
  140.4 0.9 add_convert_fusion
  141.3 0.8 collective-permute-done.25
  142.1 1.1 collective-permute-done.26
  143.6 0.7 pad_maximum_fusion.5
  144.3 0.7 pad_maximum_fusion.2
  (112 shorter events, 2.0 us)
Async XLA Ops:
  0.6 0.9 copy-start.1
  1.6 0.9 copy-start.2
  2.5 8.7 %copy-start.20 = (bf16[2,64,1024]{2,1,0:T(8,128)(2,1)S(1)}, bf16[2,64,1024]{2,1,0:T(8,128)(2,1)}, u32[]{:S(2)}) copy-start(bf16[2,64,1024]{2,1,0:T(8,128)(2,1)} %param.11) | copy-start | bytes 786436
  2.5 5.6 %collective-permute-start = (bf16[1,336,128]{2,1,0:T(8,128)(2,1)S(1)}, bf16[1,336,128]{2,1,0:T(8,128)(2,1)S(1)}, u32[]{:S(2)}, u32[]{:S(2)}) collective-permute-start(bf16[1,336,128]{2,1,0:T(8,128)(2,1)S(1)} %pack.1), channel_id=1, source_target_pairs={{0,8},{8,0},{16,24},{24,16},{1,9},{9,1},{17,25},{25,17},{2,10},{10... | collective-permute-start | bytes 258056 | tf_op jit(solution)/shard_map/ppermute | solution.py:51
  8.1 3.1 %copy-start.21 = (bf16[2,64,1024]{2,1,0:T(8,128)(2,1)S(1)}, bf16[2,64,1024]{2,1,0:T(8,128)(2,1)}, u32[]{:S(2)}) copy-start(bf16[2,64,1024]{2,1,0:T(8,128)(2,1)} %param.12) | copy-start | bytes 786436
  8.1 10.2 %collective-permute-start.1 = (bf16[2,336,128]{2,1,0:T(8,128)(2,1)S(1)}, bf16[2,336,128]{2,1,0:T(8,128)(2,1)S(1)}, u32[]{:S(2)}, u32[]{:S(2)}) collective-permute-start(bf16[2,336,128]{2,1,0:T(8,128)(2,1)S(1)} %pad_maximum_fusion.4), channel_id=1, source_target_pairs={{0,16},{8,24},{16,0},{24,8},{1,17},{9,25},{17,1},{25,9},{2,18},{10... | collective-permute-start | bytes 516104 | tf_op jit(solution)/shard_map/ppermute | solution.py:51
  18.3 0.7 copy-start.16
  19.0 13.3 %collective-permute-start.3 = (bf16[2,64,2048]{2,1,0:T(8,128)(2,1)S(1)}, bf16[2,64,2048]{2,1,0:T(8,128)(2,1)S(1)}, u32[]{:S(2)}, u32[]{:S(2)}) collective-permute-start(bf16[2,64,2048]{2,1,0:T(8,128)(2,1)S(1)} %constant_dynamic-update-slice_fusion.refs_12_.refs_16_), channel_id=1, source_target_pairs={{0,8},{8,16},{16,24},{1,9},{9,17},{17,25},{2,10},{10,18},{18,26},{... | collective-permute-start | bytes 1572872 | tf_op jit(solution)/shard_map/ppermute | solution.py:46
  21.4 6.5 %collective-permute-start.2 = (bf16[4,208,128]{2,1,0:T(8,128)(2,1)S(1)}, bf16[4,208,128]{2,1,0:T(8,128)(2,1)S(1)}, u32[]{:S(2)}, u32[]{:S(2)}) collective-permute-start(bf16[4,208,128]{2,1,0:T(8,128)(2,1)S(1)} %slice.163), channel_id=1, source_target_pairs={{0,4},{4,0},{1,5},{5,1},{2,6},{6,2},{3,7},{7,3},{8,12},{12,8},{9,1... | collective-permute-start | bytes 638984 | tf_op jit(solution)/shard_map/ppermute | solution.py:51
  28.0 17.3 %copy-start = (bf16[2,64,4096]{2,1,0:T(8,128)(2,1)S(1)}, bf16[2,64,4096]{2,1,0:T(8,128)(2,1)}, u32[]{:S(2)}) copy-start(bf16[2,64,4096]{2,1,0:T(8,128)(2,1)} %hidden_ref.3) | copy-start | bytes 3145732
  32.3 10.5 %copy-start.9 = (bf16[2,64,2048]{2,1,0:T(8,128)(2,1)}, bf16[2,64,2048]{2,1,0:T(8,128)(2,1)S(1)}, u32[]{:S(2)}) copy-start(bf16[2,64,2048]{2,1,0:T(8,128)(2,1)S(1)} %collective-permute-done.3.refs_13_.refs_17_) | copy-start | bytes 1572868
  32.3 10.4 %collective-permute-start.4 = (bf16[8,208,128]{2,1,0:T(8,128)(2,1)S(1)}, bf16[8,208,128]{2,1,0:T(8,128)(2,1)S(1)}, u32[]{:S(2)}, u32[]{:S(2)}) collective-permute-start(bf16[8,208,128]{2,1,0:T(8,128)(2,1)S(1)} %pad_maximum_fusion), channel_id=1, source_target_pairs={{0,2},{1,3},{2,0},{3,1},{4,6},{5,7},{6,4},{7,5},{8,10},{9,11},{10,... | collective-permute-start | bytes 1277960 | tf_op jit(solution)/shard_map/ppermute | solution.py:51
  33.8 9.0 %collective-permute-start.5 = (bf16[2,64,2048]{2,1,0:T(8,128)(2,1)S(1)}, bf16[2,64,2048]{2,1,0:T(8,128)(2,1)}, u32[]{:S(2)}, u32[]{:S(2)}) collective-permute-start(bf16[2,64,2048]{2,1,0:T(8,128)(2,1)S(1)} %collective-permute-done.3.refs_13_.refs_17_), channel_id=1, source_target_pairs={{8,16},{16,24},{9,17},{17,25},{10,18},{18,26},{11,19},{19,27},{12,... | collective-permute-start | bytes 1572872 | tf_op jit(solution)/shard_map/ppermute | solution.py:46
  42.8 2.4 %collective-permute-start.6 = (bf16[16,208,128]{2,1,0:T(8,128)(2,1)S(1)}, bf16[16,208,128]{2,1,0:T(8,128)(2,1)S(1)}, u32[]{:S(2)}, u32[]{:S(2)}) collective-permute-start(bf16[16,208,128]{2,1,0:T(8,128)(2,1)S(1)} %constant_dynamic-update-slice_fusion.2.own_ref), channel_id=1, source_target_pairs={{0,1},{1,0},{2,3},{3,2},{4,5},{5,4},{6,7},{7,6},{8,9},{9,8},{10,11... | collective-permute-start | bytes 2555912 | tf_op jit(solution)/shard_map/ppermute | solution.py:51
  42.9 22.4 %collective-permute-start.10 = (bf16[2,64,2048]{2,1,0:T(8,128)(2,1)}, bf16[2,64,2048]{2,1,0:T(8,128)(2,1)}, u32[]{:S(2)}, u32[]{:S(2)}) collective-permute-start(bf16[2,64,2048]{2,1,0:T(8,128)(2,1)} %collective-permute-done.5.refs_14_.refs_18_), channel_id=1, source_target_pairs={{16,24},{17,25},{18,26},{19,27},{20,28},{21,29},{22,30},{23,31}} | collective-permute-start | bytes 1572872 | tf_op jit(solution)/shard_map/ppermute | solution.py:46
  44.8 20.4 %copy-start.17 = (bf16[2,336,128]{2,1,0:T(8,128)(2,1)S(1)}, bf16[2,336,128]{2,1,0:T(8,128)(2,1)}, u32[]{:S(2)}) copy-start(bf16[2,336,128]{2,1,0:T(8,128)(2,1)} %copy-done.16) | copy-start | bytes 516100
  46.5 1.0 copy-start.5
  47.5 0.8 copy-start.7
  48.3 17.1 %collective-permute-start.7 = (bf16[2,64,128]{2,1,0:T(8,128)(2,1)S(1)}, bf16[2,64,128]{2,1,0:T(8,128)(2,1)S(1)}, u32[]{:S(2)}, u32[]{:S(2)}) collective-permute-start(bf16[2,64,128]{2,1,0:T(8,128)(2,1)S(1)} %get-tuple-element.34.refs_8_), channel_id=1, source_target_pairs={{0,8},{8,16},{16,24},{1,9},{9,17},{17,25},{2,10},{10,18},{18,26},{... | collective-permute-start | bytes 98312 | tf_op jit(solution)/shard_map/ppermute | solution.py:46
  56.7 8.8 %collective-permute-start.8 = (bf16[2,64,128]{2,1,0:T(8,128)(2,1)S(1)}, bf16[2,64,128]{2,1,0:T(8,128)(2,1)S(1)}, u32[]{:S(2)}, u32[]{:S(2)}) collective-permute-start(bf16[2,64,128]{2,1,0:T(8,128)(2,1)S(1)} %get-tuple-element.34.refs_8_), channel_id=1, source_target_pairs={{0,16},{8,24},{1,17},{9,25},{2,18},{10,26},{3,19},{11,27},{4,20},{... | collective-permute-start | bytes 98312 | tf_op jit(solution)/shard_map/ppermute | solution.py:46
  63.9 2.9 %collective-permute-start.9 = (bf16[2,64,128]{2,1,0:T(8,128)(2,1)S(1)}, bf16[2,64,128]{2,1,0:T(8,128)(2,1)S(1)}, u32[]{:S(2)}, u32[]{:S(2)}) collective-permute-start(bf16[2,64,128]{2,1,0:T(8,128)(2,1)S(1)} %get-tuple-element.34.refs_8_), channel_id=1, source_target_pairs={{0,24},{1,25},{2,26},{3,27},{4,28},{5,29},{6,30},{7,31}} | collective-permute-start | bytes 98312 | tf_op jit(solution)/shard_map/ppermute | solution.py:46
  66.8 1.2 copy-start.3
  68.0 1.2 copy-start.4
  69.3 1.1 copy-start.8
  70.3 1.0 copy-start.10
  88.7 0.7 copy-start.11
  88.7 0.8 copy-start.13
  88.7 0.9 copy-start.15
  89.5 5.8 %collective-permute-start.14 = (bf16[2,64,64]{2,1,0:T(8,128)(2,1)S(1)}, bf16[2,64,64]{2,1,0:T(8,128)(2,1)S(1)}, u32[]{:S(2)}, u32[]{:S(2)}) collective-permute-start(bf16[2,64,64]{2,1,0:T(8,128)(2,1)S(1)} %get-tuple-element.69), channel_id=1, source_target_pairs={{8,0},{16,8},{24,16},{9,1},{17,9},{25,17},{10,2},{18,10},{26,18},{... | collective-permute-start | bytes 49160 | tf_op jit(solution)/shard_map/ppermute | solution.py:46
  90.8 7.1 %collective-permute-start.15 = (bf16[2,64,64]{2,1,0:T(8,128)(2,1)S(1)}, bf16[2,64,64]{2,1,0:T(8,128)(2,1)S(1)}, u32[]{:S(2)}, u32[]{:S(2)}) collective-permute-start(bf16[2,64,64]{2,1,0:T(8,128)(2,1)S(1)} %get-tuple-element.71), channel_id=1, source_target_pairs={{16,0},{24,8},{17,1},{25,9},{18,2},{26,10},{19,3},{27,11},{20,4},{... | collective-permute-start | bytes 49160 | tf_op jit(solution)/shard_map/ppermute | solution.py:46
  92.1 8.9 %collective-permute-start.16 = (bf16[2,64,64]{2,1,0:T(8,128)(2,1)S(1)}, bf16[2,64,64]{2,1,0:T(8,128)(2,1)S(1)}, u32[]{:S(2)}, u32[]{:S(2)}) collective-permute-start(bf16[2,64,64]{2,1,0:T(8,128)(2,1)S(1)} %get-tuple-element.70), channel_id=1, source_target_pairs={{24,0},{25,1},{26,2},{27,3},{28,4},{29,5},{30,6},{31,7}} | collective-permute-start | bytes 49160 | tf_op jit(solution)/shard_map/ppermute | solution.py:46
  93.4 10.7 %collective-permute-start.11 = (bf16[2,64,1024]{2,1,0:T(8,128)(2,1)}, bf16[2,64,1024]{2,1,0:T(8,128)(2,1)S(1)}, u32[]{:S(2)}, u32[]{:S(2)}) collective-permute-start(bf16[2,64,1024]{2,1,0:T(8,128)(2,1)} %copy-done.15), channel_id=1, source_target_pairs={{8,0},{16,8},{24,16},{9,1},{17,9},{25,17},{10,2},{18,10},{26,18},{... | collective-permute-start | bytes 786440 | tf_op jit(solution)/shard_map/ppermute | solution.py:46
  101.2 3.7 %copy-start.14 = (bf16[2,64,1024]{2,1,0:T(8,128)(2,1)S(1)}, bf16[2,64,1024]{2,1,0:T(8,128)(2,1)}, u32[]{:S(2)}) copy-start(bf16[2,64,1024]{2,1,0:T(8,128)(2,1)} %copy-done.13) | copy-start | bytes 786436
  101.2 5.0 %copy-start.12 = (bf16[2,64,1024]{2,1,0:T(8,128)(2,1)S(1)}, bf16[2,64,1024]{2,1,0:T(8,128)(2,1)}, u32[]{:S(2)}) copy-start(bf16[2,64,1024]{2,1,0:T(8,128)(2,1)} %copy-done.11) | copy-start | bytes 786436
  104.2 0.7 copy-start.18
  104.9 2.8 %collective-permute-start.17 = (bf16[8,2,208,128]{3,2,1,0:T(8,128)(2,1)}, bf16[8,2,208,128]{3,2,1,0:T(8,128)(2,1)S(1)}, u32[]{:S(2)}, u32[]{:S(2)}) collective-permute-start(bf16[8,2,208,128]{3,2,1,0:T(8,128)(2,1)} %get-tuple-element.47), channel_id=1, source_target_pairs={{0,1},{1,0},{2,3},{3,2},{4,5},{5,4},{6,7},{7,6},{8,9},{9,8},{10,11... | collective-permute-start | bytes 2555912 | tf_op jit(solution)/shard_map/ppermute | solution.py:51
  104.9 12.9 %collective-permute-start.13 = (bf16[2,64,1024]{2,1,0:T(8,128)(2,1)S(1)}, bf16[2,64,1024]{2,1,0:T(8,128)(2,1)S(1)}, u32[]{:S(2)}, u32[]{:S(2)}) collective-permute-start(bf16[2,64,1024]{2,1,0:T(8,128)(2,1)S(1)} %copy-done.14), channel_id=1, source_target_pairs={{24,0},{25,1},{26,2},{27,3},{28,4},{29,5},{30,6},{31,7}} | collective-permute-start | bytes 786440 | tf_op jit(solution)/shard_map/ppermute | solution.py:46
  106.2 25.7 %collective-permute-start.12 = (bf16[2,64,1024]{2,1,0:T(8,128)(2,1)S(1)}, bf16[2,64,1024]{2,1,0:T(8,128)(2,1)S(1)}, u32[]{:S(2)}, u32[]{:S(2)}) collective-permute-start(bf16[2,64,1024]{2,1,0:T(8,128)(2,1)S(1)} %copy-done.12), channel_id=1, source_target_pairs={{16,0},{24,8},{17,1},{25,9},{18,2},{26,10},{19,3},{27,11},{20,4},{... | collective-permute-start | bytes 786440 | tf_op jit(solution)/shard_map/ppermute | solution.py:46
  117.8 6.1 %collective-permute-start.18 = (bf16[4,2,96,128]{3,2,0,1:T(8,128)(2,1)S(1)}, bf16[4,2,96,128]{3,2,0,1:T(8,128)(2,1)S(1)}, u32[]{:S(2)}, u32[]{:S(2)}) collective-permute-start(bf16[4,2,96,128]{3,2,0,1:T(8,128)(2,1)S(1)} %fusion.4), channel_id=1, source_target_pairs={{0,4},{4,0},{1,5},{5,1},{2,6},{6,2},{3,7},{7,3},{8,12},{12,8},{9,1... | collective-permute-start | bytes 589832 | tf_op jit(solution)/shard_map/ppermute | solution.py:51
  119.4 7.5 %collective-permute-start.20 = (bf16[4,2,112,128]{3,2,0,1:T(8,128)(2,1)S(1)}, bf16[4,2,112,128]{3,2,0,1:T(8,128)(2,1)S(1)}, u32[]{:S(2)}, u32[]{:S(2)}) collective-permute-start(bf16[4,2,112,128]{3,2,0,1:T(8,128)(2,1)S(1)} %fusion), channel_id=1, source_target_pairs={{0,2},{1,3},{2,0},{3,1},{4,6},{5,7},{6,4},{7,5},{8,10},{9,11},{10,... | collective-permute-start | bytes 688136 | tf_op jit(solution)/shard_map/ppermute | solution.py:51
  123.9 11.9 %copy-start.6 = (bf16[4096,128]{1,0:T(8,128)(2,1)S(1)}, bf16[4096,128]{1,0:T(8,128)(2,1)}, u32[]{:S(2)}) copy-start(bf16[4096,128]{1,0:T(8,128)(2,1)} %copy-done.5) | copy-start | bytes 3145732
  123.9 4.7 %collective-permute-start.19 = (bf16[4,96,128]{2,1,0:T(8,128)(2,1)S(1)}, bf16[4,96,128]{2,1,0:T(8,128)(2,1)S(1)}, u32[]{:S(2)}, u32[]{:S(2)}) collective-permute-start(bf16[4,96,128]{2,1,0:T(8,128)(2,1)S(1)} %fusion.14), channel_id=1, source_target_pairs={{0,2},{1,3},{2,0},{3,1},{4,6},{5,7},{6,4},{7,5},{8,10},{9,11},{10,... | collective-permute-start | bytes 294920 | tf_op jit(solution)/shard_map/ppermute | solution.py:51
  126.9 4.9 %collective-permute-start.21 = (bf16[4,112,128]{2,1,0:T(8,128)(2,1)S(1)}, bf16[4,112,128]{2,1,0:T(8,128)(2,1)S(1)}, u32[]{:S(2)}, u32[]{:S(2)}) collective-permute-start(bf16[4,112,128]{2,1,0:T(8,128)(2,1)S(1)} %fusion.9), channel_id=1, source_target_pairs={{0,4},{4,0},{1,5},{5,1},{2,6},{6,2},{3,7},{7,3},{8,12},{12,8},{9,1... | collective-permute-start | bytes 344072 | tf_op jit(solution)/shard_map/ppermute | solution.py:51
  131.9 6.0 %collective-permute-start.22 = (bf16[208,128]{1,0:T(8,128)(2,1)S(1)}, bf16[208,128]{1,0:T(8,128)(2,1)S(1)}, u32[]{:S(2)}, u32[]{:S(2)}) collective-permute-start(bf16[208,128]{1,0:T(8,128)(2,1)S(1)} %get-tuple-element.66), channel_id=1, source_target_pairs={{0,8},{8,16},{16,24},{24,0},{1,9},{9,17},{17,25},{25,1},{2,10},{10... | collective-permute-start | bytes 159752 | tf_op jit(solution)/shard_map/ppermute | solution.py:41
  132.0 5.9 %collective-permute-start.23 = (bf16[208,128]{1,0:T(8,128)(2,1)S(1)}, bf16[208,128]{1,0:T(8,128)(2,1)S(1)}, u32[]{:S(2)}, u32[]{:S(2)}) collective-permute-start(bf16[208,128]{1,0:T(8,128)(2,1)S(1)} %get-tuple-element.68), channel_id=1, source_target_pairs={{0,16},{8,24},{16,0},{24,8},{1,17},{9,25},{17,1},{25,9},{2,18},{10... | collective-permute-start | bytes 159752 | tf_op jit(solution)/shard_map/ppermute | solution.py:41
  132.1 6.4 %collective-permute-start.24 = (bf16[208,128]{1,0:T(8,128)(2,1)S(1)}, bf16[208,128]{1,0:T(8,128)(2,1)S(1)}, u32[]{:S(2)}, u32[]{:S(2)}) collective-permute-start(bf16[208,128]{1,0:T(8,128)(2,1)S(1)} %get-tuple-element.67), channel_id=1, source_target_pairs={{0,24},{8,0},{16,8},{24,16},{1,25},{9,1},{17,9},{25,17},{2,26},{10... | collective-permute-start | bytes 159752 | tf_op jit(solution)/shard_map/ppermute | solution.py:41
  137.9 2.5 %copy-start.19 = (bf16[2,64,1024]{2,1,0:T(8,128)(2,1)S(1)}, bf16[2,64,1024]{2,1,0:T(8,128)(2,1)}, u32[]{:S(2)}) copy-start(bf16[2,64,1024]{2,1,0:T(8,128)(2,1)} %copy-done.18) | copy-start | bytes 786436
  138.5 3.6 %collective-permute-start.25 = (bf16[208,128]{1,0:T(8,128)(2,1)S(1)}, bf16[208,128]{1,0:T(8,128)(2,1)S(1)}, u32[]{:S(2)}, u32[]{:S(2)}) collective-permute-start(bf16[208,128]{1,0:T(8,128)(2,1)S(1)} %fusion.12), channel_id=1, source_target_pairs={{0,3},{1,2},{2,1},{3,0},{4,7},{5,6},{6,5},{7,4},{8,11},{9,10},{10,... | collective-permute-start | bytes 159752 | tf_op jit(solution)/shard_map/ppermute | solution.py:51
  138.6 4.7 %collective-permute-start.26 = (bf16[208,128]{1,0:T(8,128)(2,1)S(1)}, bf16[208,128]{1,0:T(8,128)(2,1)S(1)}, u32[]{:S(2)}, u32[]{:S(2)}) collective-permute-start(bf16[208,128]{1,0:T(8,128)(2,1)S(1)} %fusion.12), channel_id=1, source_target_pairs={{0,2},{1,3},{2,0},{3,1},{4,6},{5,7},{6,4},{7,5},{8,10},{9,11},{10,... | collective-permute-start | bytes 159752 | tf_op jit(solution)/shard_map/ppermute | solution.py:51
  139.2 4.1 %collective-permute-start.27 = (bf16[208,128]{1,0:T(8,128)(2,1)S(1)}, bf16[208,128]{1,0:T(8,128)(2,1)S(1)}, u32[]{:S(2)}, u32[]{:S(2)}) collective-permute-start(bf16[208,128]{1,0:T(8,128)(2,1)S(1)} %fusion.12), channel_id=1, source_target_pairs={{0,1},{1,0},{2,3},{3,2},{4,5},{5,4},{6,7},{7,6},{8,9},{9,8},{10,11... | collective-permute-start | bytes 159752 | tf_op jit(solution)/shard_map/ppermute | solution.py:51

commit v7 on v6

--- a/solution.py
+++ b/solution.py
@@ -176,8 +176,8 @@
         guv_ref[0, p] = grad_up_v[rows]
 
 
-def attention(place, query_base, grad_out, up_blocks, past, cos, sin, lows, kvs):
-    shards = len(kvs)
+def attention(place, query_base, grad_out, up_blocks, past, cos, sin, lows, keys, bases):
+    shards = len(keys)
     parts = lax.axis_size("rep")
     seqs, tokens = query_base.shape[:2]
     past_len = past.shape[1]
@@ -201,8 +201,7 @@
         whole(sin),
     ]
     in_specs += [whole(x) for x in lows]
-    in_specs += [gv_spec] * shards
-    in_specs += [spec((seqs, tokens, HEAD_DIM), lambda g: (0, 0, KV_HEADS + g))] * shards
+    in_specs += [gv_spec] * (2 * shards)
     shape = jax.ShapeDtypeStruct
     low_q_shape = shape((seqs, tokens, RANK), f32)
     low_v_shape = shape((seqs, shards * tokens, RANK), f32)
@@ -243,7 +242,7 @@
             flops=pairs * HEAD_DIM * 120, bytes_accessed=2**16, transcendentals=pairs
         ),
         name="attention",
-    )(place, query_base, grad_out, up_blocks, up_blocks, past, past, cos, sin, *lows, *kvs, *kvs)
+    )(place, query_base, grad_out, up_blocks, up_blocks, past, past, cos, sin, *lows, *keys, *bases)
 
 
 def low_rank_kernel(
@@ -318,11 +317,11 @@
         buf = jnp.concatenate([buf, partner(buf, "fsdp", step)], axis=0)
         step *= 2
     step = 2
-    buf = tie(buf, before_rep)
+    buf = tie(buf, *before_rep)
     while step < rp:
         buf = jnp.concatenate([buf, partner(buf, "rep", step)], axis=0)
         step *= 2
-    other = partner(tie(buf, before_swap), "rep", 1)
+    other = partner(tie(buf, *before_swap), "rep", 1)
     index = jnp.stack([z, x, r]).astype(jnp.int32)
     vmem = pl.BlockSpec(memory_space=pltpu.VMEM)
     seqs, tokens = hidden.shape[:2]
@@ -441,7 +440,9 @@
     sp, fs, rp = (lax.axis_size(a) for a in ("sp", "fsdp", "rep"))
     z, r = lax.axis_index("sp"), lax.axis_index("rep")
     shards, _, rows, lanes = send.shape
-    got = partner(tie(send, values[0]), "rep", 1)
+    far = [along(values[k - 1], "sp", -k) for k in range(3, sp)]
+    got = partner(tie(send, *far), "rep", 1)
+    values = [along(tie(values[1], got), "sp", -2)] + far
     fs_bits, rep_bits = fs.bit_length() - 1, rp.bit_length() - 2
     labels = [("fsdp", b) for b in reversed(range(fs_bits))]
     labels += [("rep", b + 1) for b in reversed(range(rep_bits))]
@@ -450,7 +451,7 @@
 
     def halve(terms, order):
         left = list(labels)
-        for step, label in enumerate(order):
+        for label in order:
             axis, bit = label
             dim = 1 + left.index(label)
             left.remove(label)
@@ -461,8 +462,6 @@
                 return sum(a.astype(f32) for a in parts).astype(bf16)
 
             send = pick(1 - mine)
-            if step == 0:
-                send = tie(send, *values[2:])
             terms = [pick(mine), partner(send, axis, 1 << bit)]
         return sum(a.astype(f32) for a in terms).astype(bf16)
 
@@ -496,7 +495,7 @@
             up = [up[lo : lo + up_rows] for lo in range(0, up.shape[0], up_rows)]
             up = jnp.concatenate(up, axis=1)
         ups.append(up.reshape(up_rows, up_width))
-    return grad_down, jnp.concatenate(ups, axis=0), grad_hidden
+    return grad_down, jnp.concatenate(ups, axis=0), grad_hidden, values
 
 
 def body(
@@ -515,7 +514,6 @@
     seqs, tokens = hidden.shape[:2]
     past_len = past_keys.shape[1] * sp
     own_past = jnp.concatenate([past_keys, past_values], axis=2)
-    kvs = [jnp.concatenate([key_span, value_base], axis=2)]
     even = adapter_up.shape[1] % HEAD_DIM == 0
     if even:
         buf, past = pack_adapters(adapter_down, adapter_up, own_past)
@@ -523,20 +521,25 @@
         buf = own_past
         past = [own_past] + [cyclic(own_past, "sp", k) for k in range(1, sp)]
         past = jnp.concatenate(past, axis=1)
-    kvs.append(along(tie(kvs[0], buf), "sp", 1))
-    for k in range(2, sp):
-        kvs.append(along(kvs[k - 1], "sp", 1, k - 1))
+    keys, bases = [key_span], [value_base]
+    for line in (keys, bases):
+        line.append(along(tie(line[0], buf), "sp", 1))
+        for k in range(2, sp):
+            line.append(along(line[k - 1], "sp", 1, k - 1))
+    second = min(2, sp - 1)
     if even:
-        down_full, up_blocks, low_own = adapters_packed(hidden, buf, kvs[1], kvs[min(2, sp - 1)])
+        down_full, up_blocks, low_own = adapters_packed(
+            hidden, buf, (keys[1], bases[1]), (keys[second], bases[second])
+        )
     else:
         down_full, up_blocks, low_own = adapters_plain(hidden, adapter_down, adapter_up)
     lows = [low_own] + [along(low_own, "sp", k) for k in range(1, sp)]
     cos, sin = rotary_tables(tokens, past_len + z * tokens)
     place = z.astype(jnp.int32).reshape(1)
 
-    made = attention(place, query_base, grad_out, up_blocks, past, cos, sin, lows, kvs)
+    made = attention(place, query_base, grad_out, up_blocks, past, cos, sin, lows, keys, bases)
     attended, grad_query, guq, guv, low_grad_q, low_grad_v = made[:6]
-    value_own, value_got = made[6], [along(made[6 + k], "sp", -k) for k in range(1, sp)]
+    value_own, values = made[6], made[7:]
 
     low_v_total = low_grad_v[:, :tokens]
     for k in range(1, sp):
@@ -547,12 +550,13 @@
         .astype(bf16)
         .reshape(seqs * tokens, 2 * RANK)
     )
-    send, keep = packed_grads(hidden, low_grad, guq, guv, sp * fs)
-    grad_down, grad_up, grad_hidden = finish_grads(
-        send, keep, value_got, low_grad, lambda x: grad_hidden_of(x, down_full, seqs, tokens)
+    first_got = along(values[0], "sp", -1)
+    send, keep = packed_grads(hidden, tie(low_grad, first_got), guq, guv, sp * fs)
+    grad_down, grad_up, grad_hidden, got = finish_grads(
+        send, keep, values, low_grad, lambda x: grad_hidden_of(x, down_full, seqs, tokens)
     )
     grad_value = value_own.astype(f32)
-    for part in value_got:
+    for part in (first_got, *got):
         grad_value = grad_value + part.astype(f32)
     return (
         attended,

time: 146 us -> 148 us (1.014)
  starting transfers between devices: 47.7 us -> 53.2 us
  waiting for transfers between devices: 59.3 us -> 55.9 us
    ppermute x13, waiting for transfers between devices: 35.4 us -> 29.2 us  [partner(): return lax.ppermute(x, axis, [(i, i ^ mask) for i in range(n)])]
    ppermute x12 -> x15, starting transfers between devices: 30 us -> 35.1 us  [along(): lax.ppermute(x, axis, [(i, i + shift) for i in range(start, n) if 0 <= i...]
    ppermute x12 -> x15, waiting for transfers between devices: 23.4 us -> 25 us  [along(): lax.ppermute(x, axis, [(i, i + shift) for i in range(start, n) if 0 <= i...]
    unnamed x62 -> x61, local copies, waits for them, and re-layouts: 9.64 us -> 9.77 us
  transfers between devices with their start and end apart: 28 -> 31, of which waited for: 20 -> 22; matrix products, arithmetic and copies ran while one was open for 2% -> 1% of each run, Pallas kernels for 3% -> 3%
where the time goes in v7:
time: 148 us; the launch traced here: 147 us
  waiting for transfers between devices  55.9 us (38%)
  starting transfers between devices  53.2 us (36%)
  Pallas kernels  22.1 us (15%)
  local copies, waits for them, and re-layouts  10.3 us (7%)
  other arithmetic  4.16 us (3%)
    ppermute x15, starting transfers between devices, along(): lax.ppermute(x, axis, [(i, i + shift) for i in range(start, n) if 0 <= i...  35.1 us
    ppermute x13, waiting for transfers between devices, partner(): return lax.ppermute(x, axis, [(i, i ^ mask) for i in range(n)])  29.2 us
    ppermute x15, waiting for transfers between devices, along(): lax.ppermute(x, axis, [(i, i + shift) for i in range(start, n) if 0 <= i...  25 us
    pallas_call x1, Pallas kernels, attention(): pl.pallas_call(functools.partial(attention_kernel, shards), grid=(KV_HEAD...  17.2 us
    ppermute x13, starting transfers between devices, partner(): return lax.ppermute(x, axis, [(i, i ^ mask) for i in range(n)])  14.3 us
    unnamed x61, local copies, waits for them, and re-layouts  9.77 us
    ppermute x3, starting transfers between devices, cyclic(): return lax.ppermute(x, axis, [(i, (i + shift) % n) for i in range(n)])  3.86 us
  transfers between devices with their start and end apart: 31, of which 22 were waited for; matrix products, arithmetic and copies ran while one was open for 1% of the time, Pallas kernels for 3%

profile of v7, /device:TPU:0, one launch (start us, length us, event | category | flops | bytes accessed | tf_op | source)
XLA Modules:
  0.0 147.1 jit_solution(3307858490035046559)
XLA Ops:
  0.6 0.8 pad_maximum_fusion.7
  1.6 0.9 copy-done.2
  2.5 3.1 %collective-permute-start = (bf16[1,336,128]{2,1,0:T(8,128)(2,1)S(1)}, bf16[1,336,128]{2,1,0:T(8,128)(2,1)S(1)}, u32[]{:S(2)}, u32[]{:S(2)}) collective-permute-start(bf16[1,336,128]{2,1,0:T(8,128)(2,1)S(1)} %pack.1), channel_id=1, source_target_pairs={{0,8},{8,0},{16,24},{24,16},{1,9},{9,1},{17,25},{25,17},{2,10},{10... | collective-permute-start | bytes 258056 | tf_op jit(solution)/shard_map/ppermute | solution.py:51
  5.6 2.5 %collective-permute-done = bf16[1,336,128]{2,1,0:T(8,128)(2,1)S(1)} collective-permute-done((bf16[1,336,128]{2,1,0:T(8,128)(2,1)S(1)}, bf16[1,336,128]{2,1,0:T(8,128)(2,1)S(1)}, u32[]{:S(2)}, u32[]{:S(2)}) %collective-permute-start) | collective-permute-done | bytes 86048 | tf_op jit(solution)/shard_map/ppermute | solution.py:51
  8.1 3.0 %collective-permute-start.1 = (bf16[2,336,128]{2,1,0:T(8,128)(2,1)S(1)}, bf16[2,336,128]{2,1,0:T(8,128)(2,1)S(1)}, u32[]{:S(2)}, u32[]{:S(2)}) collective-permute-start(bf16[2,336,128]{2,1,0:T(8,128)(2,1)S(1)} %pad_maximum_fusion.4), channel_id=1, source_target_pairs={{0,16},{8,24},{16,0},{24,8},{1,17},{9,25},{17,1},{25,9},{2,18},{10... | collective-permute-start | bytes 516104 | tf_op jit(solution)/shard_map/ppermute | solution.py:51
  11.1 7.2 %collective-permute-done.1 = bf16[2,336,128]{2,1,0:T(8,128)(2,1)S(1)} collective-permute-done((bf16[2,336,128]{2,1,0:T(8,128)(2,1)S(1)}, bf16[2,336,128]{2,1,0:T(8,128)(2,1)S(1)}, u32[]{:S(2)}, u32[]{:S(2)}) %collective-permute-start.1) | collective-permute-done | bytes 172064 | tf_op jit(solution)/shard_map/ppermute | solution.py:51
  18.4 0.6 copy-done.20
  19.0 1.3 collective-permute-start.2
  20.4 2.6 %collective-permute-start.3 = (bf16[2,64,1024]{2,1,0:T(8,128)(2,1)S(1)}, bf16[2,64,1024]{2,1,0:T(8,128)(2,1)S(1)}, u32[]{:S(2)}, u32[]{:S(2)}) collective-permute-start(bf16[2,64,1024]{2,1,0:T(8,128)(2,1)S(1)} %copy-done.9), channel_id=1, source_target_pairs={{0,8},{8,16},{16,24},{1,9},{9,17},{17,25},{2,10},{10,18},{18,26},{... | collective-permute-start | bytes 786440 | tf_op jit(solution)/shard_map/ppermute | solution.py:46
  23.0 1.9 %collective-permute-start.4 = (bf16[2,64,1024]{2,1,0:T(8,128)(2,1)S(1)}, bf16[2,64,1024]{2,1,0:T(8,128)(2,1)S(1)}, u32[]{:S(2)}, u32[]{:S(2)}) collective-permute-start(bf16[2,64,1024]{2,1,0:T(8,128)(2,1)S(1)} %copy-done.10), channel_id=1, source_target_pairs={{0,8},{8,16},{16,24},{1,9},{9,17},{17,25},{2,10},{10,18},{18,26},{... | collective-permute-start | bytes 786440 | tf_op jit(solution)/shard_map/ppermute | solution.py:46
  25.4 4.2 %collective-permute-done.3.refs_13_ = bf16[2,64,1024]{2,1,0:T(8,128)(2,1)S(1)} collective-permute-done((bf16[2,64,1024]{2,1,0:T(8,128)(2,1)S(1)}, bf16[2,64,1024]{2,1,0:T(8,128)(2,1)S(1)}, u32[]{:S(2)}, u32[]{:S(2)}) %collective-permute-start.3) | collective-permute-done | bytes 262176 | tf_op jit(solution)/shard_map/ppermute | solution.py:46
  29.7 3.9 %collective-permute-done.4.refs_17_ = bf16[2,64,1024]{2,1,0:T(8,128)(2,1)S(1)} collective-permute-done((bf16[2,64,1024]{2,1,0:T(8,128)(2,1)S(1)}, bf16[2,64,1024]{2,1,0:T(8,128)(2,1)S(1)}, u32[]{:S(2)}, u32[]{:S(2)}) %collective-permute-start.4) | collective-permute-done | bytes 262176 | tf_op jit(solution)/shard_map/ppermute | solution.py:46
  33.6 1.5 %collective-permute-start.5 = (bf16[8,208,128]{2,1,0:T(8,128)(2,1)S(1)}, bf16[8,208,128]{2,1,0:T(8,128)(2,1)S(1)}, u32[]{:S(2)}, u32[]{:S(2)}) collective-permute-start(bf16[8,208,128]{2,1,0:T(8,128)(2,1)S(1)} %pad_maximum_fusion), channel_id=1, source_target_pairs={{0,2},{1,3},{2,0},{3,1},{4,6},{5,7},{6,4},{7,5},{8,10},{9,11},{10,... | collective-permute-start | bytes 1277960 | tf_op jit(solution)/shard_map/ppermute | solution.py:51
  35.1 1.4 collective-permute-start.6
  36.5 1.4 collective-permute-start.7
  37.9 5.8 %collective-permute-done.5 = bf16[8,208,128]{2,1,0:T(8,128)(2,1)S(1)} collective-permute-done((bf16[8,208,128]{2,1,0:T(8,128)(2,1)S(1)}, bf16[8,208,128]{2,1,0:T(8,128)(2,1)S(1)}, u32[]{:S(2)}, u32[]{:S(2)}) %collective-permute-start.5) | collective-permute-done | bytes 426016 | tf_op jit(solution)/shard_map/ppermute | solution.py:51
  44.1 1.4 collective-permute-start.12
  45.5 1.4 collective-permute-start.13
  47.0 1.2 low_rank.1
  48.3 1.0 copy-done.5
  49.2 0.8 copy-done.7
  50.1 14.8 %collective-permute-start.10 = (bf16[2,64,128]{2,1,0:T(8,128)(2,1)S(1)}, bf16[2,64,128]{2,1,0:T(8,128)(2,1)S(1)}, u32[]{:S(2)}, u32[]{:S(2)}) collective-permute-start(bf16[2,64,128]{2,1,0:T(8,128)(2,1)S(1)} %get-tuple-element.36.refs_8_), channel_id=1, source_target_pairs={{0,16},{8,24},{1,17},{9,25},{2,18},{10,26},{3,19},{11,27},{4,20},{... | collective-permute-start | bytes 98312 | tf_op jit(solution)/shard_map/ppermute | solution.py:46
  64.9 1.3 collective-permute-start.11
  66.2 1.3 collective-permute-start.9
  67.7 1.3 collective-permute-done.9.refs_9_
  69.0 1.2 copy-done.3
  70.3 1.2 copy-done.4
  71.5 1.1 copy-done.8
  72.6 0.9 copy-done.16
  73.5 17.2 %attention.1 = (bf16[2,64,4096]{2,1,0:T(8,128)(2,1)}, bf16[2,64,4096]{2,1,0:T(8,128)(2,1)}, bf16[32,4,16,128]{3,2,1,0:T(8,128)(2,1)S(1)}, bf16[8,4,16,128]{3,2,1...) custom-call(s32[1]{0:T(128)} %bitcast.place_ref, ...), custom_call_target="tpu_custom_call" | custom-call | flops 17112760320 | bytes 65536 | tf_op jit(solution)/shard_map/attention/pallas_call | solution.py:211
  90.8 0.7 copy-done.18
  91.5 0.7 copy-done.11
  92.3 1.3 collective-permute-start.15
  93.6 1.3 collective-permute-start.16
  94.9 1.3 collective-permute-start.17
  96.2 1.3 collective-permute-start.14
  97.5 1.3 collective-permute-start.18
  98.8 2.4 %collective-permute-done.16 = bf16[2,64,64]{2,1,0:T(8,128)(2,1)S(1)} collective-permute-done((bf16[2,64,64]{2,1,0:T(8,128)(2,1)S(1)}, bf16[2,64,64]{2,1,0:T(8,128)(2,1)S(1)}, u32[]{:S(2)}, u32[]{:S(2)}) %collective-permute-start.16) | collective-permute-done | bytes 16416 | tf_op jit(solution)/shard_map/ppermute | solution.py:46
  101.2 3.0 %collective-permute-done.17 = bf16[2,64,64]{2,1,0:T(8,128)(2,1)S(1)} collective-permute-done((bf16[2,64,64]{2,1,0:T(8,128)(2,1)S(1)}, bf16[2,64,64]{2,1,0:T(8,128)(2,1)S(1)}, u32[]{:S(2)}, u32[]{:S(2)}) %collective-permute-start.17) | collective-permute-done | bytes 16416 | tf_op jit(solution)/shard_map/ppermute | solution.py:46
  104.4 2.6 %collective-permute-done.14 = bf16[2,64,1024]{2,1,0:T(8,128)(2,1)S(1)} collective-permute-done((bf16[2,64,1024]{2,1,0:T(8,128)(2,1)S(1)}, bf16[2,64,1024]{2,1,0:T(8,128)(2,1)S(1)}, u32[]{:S(2)}, u32[]{:S(2)}) %collective-permute-start.14) | collective-permute-done | bytes 262176 | tf_op jit(solution)/shard_map/ppermute | solution.py:46
  107.0 1.6 %adapter_grads.1 = (bf16[8,2,208,128]{3,2,1,0:T(8,128)(2,1)}, bf16[8,2,208,128]{3,2,1,0:T(8,128)(2,1)S(1)}) custom-call(s32[1]{0:T(128)} %bitcast.4.core_ref, bf16[2,64,4096]{2,1,0:T(8,128)(2,1)S(1)} %copy-done, bf16[128,128]{1,0:T(8,128)(2,1)S(1)} %pad_maximum_fusion.10.low_ref, bf16[32,4,16,128]{3,2,1,0:T(8,128)(2,1)S(1)} %get-tuple-element.45.guq_ref, ...), custom_call_target="tpu_custom_call" | custom-call | flops 134217728 | bytes 5242880 | tf_op jit(solution)/shard_map/adapter_grads/pallas_call | solution.py:415
  108.6 6.0 %collective-permute-done.18 = bf16[2,64,1024]{2,1,0:T(8,128)(2,1)S(1)} collective-permute-done((bf16[2,64,1024]{2,1,0:T(8,128)(2,1)}, bf16[2,64,1024]{2,1,0:T(8,128)(2,1)S(1)}, u32[]{:S(2)}, u32[]{:S(2)}) %collective-permute-start.18) | collective-permute-done | bytes 262176 | tf_op jit(solution)/shard_map/ppermute | solution.py:46
  114.8 2.4 %collective-permute-done.19 = bf16[8,2,208,128]{3,2,1,0:T(8,128)(2,1)S(1)} collective-permute-done((bf16[8,2,208,128]{3,2,1,0:T(8,128)(2,1)}, bf16[8,2,208,128]{3,2,1,0:T(8,128)(2,1)S(1)}, u32[]{:S(2)}, u32[]{:S(2)}) %collective-permute-start.19) | collective-permute-done | bytes 852000 | tf_op jit(solution)/shard_map/ppermute | solution.py:51
  117.4 1.5 %collective-permute-start.21 = (bf16[4,2,96,128]{3,2,0,1:T(8,128)(2,1)S(1)}, bf16[4,2,96,128]{3,2,0,1:T(8,128)(2,1)S(1)}, u32[]{:S(2)}, u32[]{:S(2)}) collective-permute-start(bf16[4,2,96,128]{3,2,0,1:T(8,128)(2,1)S(1)} %fusion.4), channel_id=1, source_target_pairs={{0,4},{4,0},{1,5},{5,1},{2,6},{6,2},{3,7},{7,3},{8,12},{12,8},{9,1... | collective-permute-start | bytes 589832 | tf_op jit(solution)/shard_map/ppermute | solution.py:51
  119.0 0.6 collective-permute-start.23
  119.9 1.3 collective-permute-start.20
  121.3 3.1 %collective-permute-done.21 = bf16[4,2,96,128]{3,2,0,1:T(8,128)(2,1)S(1)} collective-permute-done((bf16[4,2,96,128]{3,2,0,1:T(8,128)(2,1)S(1)}, bf16[4,2,96,128]{3,2,0,1:T(8,128)(2,1)S(1)}, u32[]{:S(2)}, u32[]{:S(2)}) %collective-permute-start.21) | collective-permute-done | bytes 196640 | tf_op jit(solution)/shard_map/ppermute | solution.py:51
  124.4 0.6 collective-permute-start.22
  125.0 1.4 collective-permute-done.23
  126.5 0.7 collective-permute-start.24
  127.1 2.0 %collective-permute-done.22 = bf16[4,96,128]{2,1,0:T(8,128)(2,1)S(1)} collective-permute-done((bf16[4,96,128]{2,1,0:T(8,128)(2,1)S(1)}, bf16[4,96,128]{2,1,0:T(8,128)(2,1)S(1)}, u32[]{:S(2)}, u32[]{:S(2)}) %collective-permute-start.22) | collective-permute-done | bytes 98336 | tf_op jit(solution)/shard_map/ppermute | solution.py:51
  129.2 2.2 %collective-permute-done.24 = bf16[4,112,128]{2,1,0:T(8,128)(2,1)S(1)} collective-permute-done((bf16[4,112,128]{2,1,0:T(8,128)(2,1)S(1)}, bf16[4,112,128]{2,1,0:T(8,128)(2,1)S(1)}, u32[]{:S(2)}, u32[]{:S(2)}) %collective-permute-start.24) | collective-permute-done | bytes 114720 | tf_op jit(solution)/shard_map/ppermute | solution.py:51
  131.4 1.3 collective-permute-done.20
  132.9 3.7 %collective-permute-start.27 = (bf16[208,128]{1,0:T(8,128)(2,1)S(1)}, bf16[208,128]{1,0:T(8,128)(2,1)S(1)}, u32[]{:S(2)}, u32[]{:S(2)}) collective-permute-start(bf16[208,128]{1,0:T(8,128)(2,1)S(1)} %get-tuple-element.69), channel_id=1, source_target_pairs={{0,24},{8,0},{16,8},{24,16},{1,25},{9,1},{17,9},{25,17},{2,26},{10... | collective-permute-start | bytes 159752 | tf_op jit(solution)/shard_map/ppermute | solution.py:41
  136.6 2.1 %grad_hidden.1 = bf16[2,64,4096]{2,1,0:T(8,128)(2,1)} custom-call(bf16[128,128]{1,0:T(8,128)(2,1)S(1)} %pad_maximum_fusion.10.low_ref, bf16[4096,128]{1,0:T(8,128)(2,1)S(1)} %copy-done.6), custom_call_target="tpu_custom_call" | custom-call | flops 1073741824 | bytes 65536 | tf_op jit(solution)/shard_map/grad_hidden/pallas_call | solution.py:366
  138.7 0.5 collective-permute-done.25
  139.3 1.2 collective-permute-done.26
  140.7 1.0 collective-permute-start.29
  141.7 0.8 collective-permute-start.30
  142.5 0.9 add_convert_fusion
  143.4 0.9 collective-permute-done.28
  144.3 1.1 collective-permute-done.29
  145.7 0.7 pad_maximum_fusion.5
  146.4 0.7 pad_maximum_fusion.2
  (116 shorter events, 3.2 us)
Async XLA Ops:
  0.6 0.9 copy-start.1
  1.6 0.9 copy-start.2
  2.5 5.6 %collective-permute-start = (bf16[1,336,128]{2,1,0:T(8,128)(2,1)S(1)}, bf16[1,336,128]{2,1,0:T(8,128)(2,1)S(1)}, u32[]{:S(2)}, u32[]{:S(2)}) collective-permute-start(bf16[1,336,128]{2,1,0:T(8,128)(2,1)S(1)} %pack.1), channel_id=1, source_target_pairs={{0,8},{8,0},{16,24},{24,16},{1,9},{9,1},{17,25},{25,17},{2,10},{10... | collective-permute-start | bytes 258056 | tf_op jit(solution)/shard_map/ppermute | solution.py:51
  8.1 10.2 %collective-permute-start.1 = (bf16[2,336,128]{2,1,0:T(8,128)(2,1)S(1)}, bf16[2,336,128]{2,1,0:T(8,128)(2,1)S(1)}, u32[]{:S(2)}, u32[]{:S(2)}) collective-permute-start(bf16[2,336,128]{2,1,0:T(8,128)(2,1)S(1)} %pad_maximum_fusion.4), channel_id=1, source_target_pairs={{0,16},{8,24},{16,0},{24,8},{1,17},{9,25},{17,1},{25,9},{2,18},{10... | collective-permute-start | bytes 516104 | tf_op jit(solution)/shard_map/ppermute | solution.py:51
  18.3 0.7 copy-start.20
  18.3 4.6 %copy-start.10 = (bf16[2,64,1024]{2,1,0:T(8,128)(2,1)S(1)}, bf16[2,64,1024]{2,1,0:T(8,128)(2,1)}, u32[]{:S(2)}) copy-start(bf16[2,64,1024]{2,1,0:T(8,128)(2,1)} %refs_16_.1) | copy-start | bytes 786436
  19.0 1.4 copy-start.9
  19.0 6.4 %collective-permute-start.2 = (bf16[4,208,128]{2,1,0:T(8,128)(2,1)S(1)}, bf16[4,208,128]{2,1,0:T(8,128)(2,1)S(1)}, u32[]{:S(2)}, u32[]{:S(2)}) collective-permute-start(bf16[4,208,128]{2,1,0:T(8,128)(2,1)S(1)} %slice.163), channel_id=1, source_target_pairs={{0,4},{4,0},{1,5},{5,1},{2,6},{6,2},{3,7},{7,3},{8,12},{12,8},{9,1... | collective-permute-start | bytes 638984 | tf_op jit(solution)/shard_map/ppermute | solution.py:51
  20.4 9.3 %collective-permute-start.3 = (bf16[2,64,1024]{2,1,0:T(8,128)(2,1)S(1)}, bf16[2,64,1024]{2,1,0:T(8,128)(2,1)S(1)}, u32[]{:S(2)}, u32[]{:S(2)}) collective-permute-start(bf16[2,64,1024]{2,1,0:T(8,128)(2,1)S(1)} %copy-done.9), channel_id=1, source_target_pairs={{0,8},{8,16},{16,24},{1,9},{9,17},{17,25},{2,10},{10,18},{18,26},{... | collective-permute-start | bytes 786440 | tf_op jit(solution)/shard_map/ppermute | solution.py:46
  23.0 10.6 %collective-permute-start.4 = (bf16[2,64,1024]{2,1,0:T(8,128)(2,1)S(1)}, bf16[2,64,1024]{2,1,0:T(8,128)(2,1)S(1)}, u32[]{:S(2)}, u32[]{:S(2)}) collective-permute-start(bf16[2,64,1024]{2,1,0:T(8,128)(2,1)S(1)} %copy-done.10), channel_id=1, source_target_pairs={{0,8},{8,16},{16,24},{1,9},{9,17},{17,25},{2,10},{10,18},{18,26},{... | collective-permute-start | bytes 786440 | tf_op jit(solution)/shard_map/ppermute | solution.py:46
  25.4 21.6 %copy-start = (bf16[2,64,4096]{2,1,0:T(8,128)(2,1)S(1)}, bf16[2,64,4096]{2,1,0:T(8,128)(2,1)}, u32[]{:S(2)}) copy-start(bf16[2,64,4096]{2,1,0:T(8,128)(2,1)} %hidden_ref.3) | copy-start | bytes 3145732
  29.7 8.2 %copy-start.13 = (bf16[2,64,1024]{2,1,0:T(8,128)(2,1)}, bf16[2,64,1024]{2,1,0:T(8,128)(2,1)S(1)}, u32[]{:S(2)}) copy-start(bf16[2,64,1024]{2,1,0:T(8,128)(2,1)S(1)} %collective-permute-done.3.refs_13_) | copy-start | bytes 786436
  33.6 4.3 %copy-start.15 = (bf16[2,64,1024]{2,1,0:T(8,128)(2,1)}, bf16[2,64,1024]{2,1,0:T(8,128)(2,1)S(1)}, u32[]{:S(2)}) copy-start(bf16[2,64,1024]{2,1,0:T(8,128)(2,1)S(1)} %collective-permute-done.4.refs_17_) | copy-start | bytes 786436
  33.6 10.1 %collective-permute-start.5 = (bf16[8,208,128]{2,1,0:T(8,128)(2,1)S(1)}, bf16[8,208,128]{2,1,0:T(8,128)(2,1)S(1)}, u32[]{:S(2)}, u32[]{:S(2)}) collective-permute-start(bf16[8,208,128]{2,1,0:T(8,128)(2,1)S(1)} %pad_maximum_fusion), channel_id=1, source_target_pairs={{0,2},{1,3},{2,0},{3,1},{4,6},{5,7},{6,4},{7,5},{8,10},{9,11},{10,... | collective-permute-start | bytes 1277960 | tf_op jit(solution)/shard_map/ppermute | solution.py:51
  35.1 8.7 %collective-permute-start.6 = (bf16[2,64,1024]{2,1,0:T(8,128)(2,1)S(1)}, bf16[2,64,1024]{2,1,0:T(8,128)(2,1)}, u32[]{:S(2)}, u32[]{:S(2)}) collective-permute-start(bf16[2,64,1024]{2,1,0:T(8,128)(2,1)S(1)} %collective-permute-done.3.refs_13_), channel_id=1, source_target_pairs={{8,16},{16,24},{9,17},{17,25},{10,18},{18,26},{11,19},{19,27},{12,... | collective-permute-start | bytes 786440 | tf_op jit(solution)/shard_map/ppermute | solution.py:46
  36.5 7.3 %collective-permute-start.7 = (bf16[2,64,1024]{2,1,0:T(8,128)(2,1)S(1)}, bf16[2,64,1024]{2,1,0:T(8,128)(2,1)}, u32[]{:S(2)}, u32[]{:S(2)}) collective-permute-start(bf16[2,64,1024]{2,1,0:T(8,128)(2,1)S(1)} %collective-permute-done.4.refs_17_), channel_id=1, source_target_pairs={{8,16},{16,24},{9,17},{17,25},{10,18},{18,26},{11,19},{19,27},{12,... | collective-permute-start | bytes 786440 | tf_op jit(solution)/shard_map/ppermute | solution.py:46
  43.8 3.2 %collective-permute-start.8 = (bf16[16,208,128]{2,1,0:T(8,128)(2,1)S(1)}, bf16[16,208,128]{2,1,0:T(8,128)(2,1)S(1)}, u32[]{:S(2)}, u32[]{:S(2)}) collective-permute-start(bf16[16,208,128]{2,1,0:T(8,128)(2,1)S(1)} %constant_dynamic-update-slice_fusion.own_ref), channel_id=1, source_target_pairs={{0,1},{1,0},{2,3},{3,2},{4,5},{5,4},{6,7},{7,6},{8,9},{9,8},{10,11... | collective-permute-start | bytes 2555912 | tf_op jit(solution)/shard_map/ppermute | solution.py:51
  44.1 23.5 %collective-permute-start.12 = (bf16[2,64,1024]{2,1,0:T(8,128)(2,1)}, bf16[2,64,1024]{2,1,0:T(8,128)(2,1)}, u32[]{:S(2)}, u32[]{:S(2)}) collective-permute-start(bf16[2,64,1024]{2,1,0:T(8,128)(2,1)} %collective-permute-done.6.refs_14_), channel_id=1, source_target_pairs={{16,24},{17,25},{18,26},{19,27},{20,28},{21,29},{22,30},{23,31}} | collective-permute-start | bytes 786440 | tf_op jit(solution)/shard_map/ppermute | solution.py:46
  45.5 22.2 %collective-permute-start.13 = (bf16[2,64,1024]{2,1,0:T(8,128)(2,1)}, bf16[2,64,1024]{2,1,0:T(8,128)(2,1)}, u32[]{:S(2)}, u32[]{:S(2)}) collective-permute-start(bf16[2,64,1024]{2,1,0:T(8,128)(2,1)} %collective-permute-done.7.refs_18_), channel_id=1, source_target_pairs={{16,24},{17,25},{18,26},{19,27},{20,28},{21,29},{22,30},{23,31}} | collective-permute-start | bytes 786440 | tf_op jit(solution)/shard_map/ppermute | solution.py:46
  47.0 20.4 %copy-start.21 = (bf16[2,336,128]{2,1,0:T(8,128)(2,1)S(1)}, bf16[2,336,128]{2,1,0:T(8,128)(2,1)}, u32[]{:S(2)}) copy-start(bf16[2,336,128]{2,1,0:T(8,128)(2,1)} %copy-done.20) | copy-start | bytes 516100
  48.2 1.0 copy-start.5
  49.2 0.8 copy-start.7
  50.1 17.6 %collective-permute-start.10 = (bf16[2,64,128]{2,1,0:T(8,128)(2,1)S(1)}, bf16[2,64,128]{2,1,0:T(8,128)(2,1)S(1)}, u32[]{:S(2)}, u32[]{:S(2)}) collective-permute-start(bf16[2,64,128]{2,1,0:T(8,128)(2,1)S(1)} %get-tuple-element.36.refs_8_), channel_id=1, source_target_pairs={{0,16},{8,24},{1,17},{9,25},{2,18},{10,26},{3,19},{11,27},{4,20},{... | collective-permute-start | bytes 98312 | tf_op jit(solution)/shard_map/ppermute | solution.py:46
  64.9 2.9 %collective-permute-start.11 = (bf16[2,64,128]{2,1,0:T(8,128)(2,1)S(1)}, bf16[2,64,128]{2,1,0:T(8,128)(2,1)S(1)}, u32[]{:S(2)}, u32[]{:S(2)}) collective-permute-start(bf16[2,64,128]{2,1,0:T(8,128)(2,1)S(1)} %get-tuple-element.36.refs_8_), channel_id=1, source_target_pairs={{0,24},{1,25},{2,26},{3,27},{4,28},{5,29},{6,30},{7,31}} | collective-permute-start | bytes 98312 | tf_op jit(solution)/shard_map/ppermute | solution.py:46
  66.2 2.9 %collective-permute-start.9 = (bf16[2,64,128]{2,1,0:T(8,128)(2,1)S(1)}, bf16[2,64,128]{2,1,0:T(8,128)(2,1)S(1)}, u32[]{:S(2)}, u32[]{:S(2)}) collective-permute-start(bf16[2,64,128]{2,1,0:T(8,128)(2,1)S(1)} %get-tuple-element.36.refs_8_), channel_id=1, source_target_pairs={{0,8},{8,16},{16,24},{1,9},{9,17},{17,25},{2,10},{10,18},{18,26},{... | collective-permute-start | bytes 98312 | tf_op jit(solution)/shard_map/ppermute | solution.py:46
  67.5 1.5 %copy-start.14 = (bf16[2,64,1024]{2,1,0:T(8,128)(2,1)S(1)}, bf16[2,64,1024]{2,1,0:T(8,128)(2,1)}, u32[]{:S(2)}) copy-start(bf16[2,64,1024]{2,1,0:T(8,128)(2,1)} %copy-done.13) | copy-start | bytes 786436
  69.0 1.2 copy-start.3
  70.3 1.2 copy-start.4
  71.5 1.1 copy-start.8
  72.6 0.9 copy-start.16
  90.8 0.7 copy-start.18
  91.5 0.7 copy-start.11
  91.5 0.8 copy-start.17
  91.5 4.7 %copy-start.19 = (bf16[2,64,1024]{2,1,0:T(8,128)(2,1)S(1)}, bf16[2,64,1024]{2,1,0:T(8,128)(2,1)}, u32[]{:S(2)}) copy-start(bf16[2,64,1024]{2,1,0:T(8,128)(2,1)} %copy-done.18) | copy-start | bytes 786436
  92.3 6.5 %collective-permute-start.15 = (bf16[2,64,64]{2,1,0:T(8,128)(2,1)S(1)}, bf16[2,64,64]{2,1,0:T(8,128)(2,1)S(1)}, u32[]{:S(2)}, u32[]{:S(2)}) collective-permute-start(bf16[2,64,64]{2,1,0:T(8,128)(2,1)S(1)} %get-tuple-element.71), channel_id=1, source_target_pairs={{8,0},{16,8},{24,16},{9,1},{17,9},{25,17},{10,2},{18,10},{26,18},{... | collective-permute-start | bytes 49160 | tf_op jit(solution)/shard_map/ppermute | solution.py:46
  93.6 7.7 %collective-permute-start.16 = (bf16[2,64,64]{2,1,0:T(8,128)(2,1)S(1)}, bf16[2,64,64]{2,1,0:T(8,128)(2,1)S(1)}, u32[]{:S(2)}, u32[]{:S(2)}) collective-permute-start(bf16[2,64,64]{2,1,0:T(8,128)(2,1)S(1)} %get-tuple-element.73), channel_id=1, source_target_pairs={{16,0},{24,8},{17,1},{25,9},{18,2},{26,10},{19,3},{27,11},{20,4},{... | collective-permute-start | bytes 49160 | tf_op jit(solution)/shard_map/ppermute | solution.py:46
  94.9 9.4 %collective-permute-start.17 = (bf16[2,64,64]{2,1,0:T(8,128)(2,1)S(1)}, bf16[2,64,64]{2,1,0:T(8,128)(2,1)S(1)}, u32[]{:S(2)}, u32[]{:S(2)}) collective-permute-start(bf16[2,64,64]{2,1,0:T(8,128)(2,1)S(1)} %get-tuple-element.72), channel_id=1, source_target_pairs={{24,0},{25,1},{26,2},{27,3},{28,4},{29,5},{30,6},{31,7}} | collective-permute-start | bytes 49160 | tf_op jit(solution)/shard_map/ppermute | solution.py:46
  96.2 10.8 %collective-permute-start.14 = (bf16[2,64,1024]{2,1,0:T(8,128)(2,1)S(1)}, bf16[2,64,1024]{2,1,0:T(8,128)(2,1)S(1)}, u32[]{:S(2)}, u32[]{:S(2)}) collective-permute-start(bf16[2,64,1024]{2,1,0:T(8,128)(2,1)S(1)} %copy-done.19), channel_id=1, source_target_pairs={{8,0},{16,8},{24,16},{9,1},{17,9},{25,17},{10,2},{18,10},{26,18},{... | collective-permute-start | bytes 786440 | tf_op jit(solution)/shard_map/ppermute | solution.py:46
  97.5 17.1 %collective-permute-start.18 = (bf16[2,64,1024]{2,1,0:T(8,128)(2,1)}, bf16[2,64,1024]{2,1,0:T(8,128)(2,1)S(1)}, u32[]{:S(2)}, u32[]{:S(2)}) collective-permute-start(bf16[2,64,1024]{2,1,0:T(8,128)(2,1)} %copy-done.17), channel_id=1, source_target_pairs={{24,0},{25,1},{26,2},{27,3},{28,4},{29,5},{30,6},{31,7}} | collective-permute-start | bytes 786440 | tf_op jit(solution)/shard_map/ppermute | solution.py:46
  114.6 2.6 %collective-permute-start.19 = (bf16[8,2,208,128]{3,2,1,0:T(8,128)(2,1)}, bf16[8,2,208,128]{3,2,1,0:T(8,128)(2,1)S(1)}, u32[]{:S(2)}, u32[]{:S(2)}) collective-permute-start(bf16[8,2,208,128]{3,2,1,0:T(8,128)(2,1)} %get-tuple-element.49), channel_id=1, source_target_pairs={{0,1},{1,0},{2,3},{3,2},{4,5},{5,4},{6,7},{7,6},{8,9},{9,8},{10,11... | collective-permute-start | bytes 2555912 | tf_op jit(solution)/shard_map/ppermute | solution.py:51
  117.4 7.0 %collective-permute-start.21 = (bf16[4,2,96,128]{3,2,0,1:T(8,128)(2,1)S(1)}, bf16[4,2,96,128]{3,2,0,1:T(8,128)(2,1)S(1)}, u32[]{:S(2)}, u32[]{:S(2)}) collective-permute-start(bf16[4,2,96,128]{3,2,0,1:T(8,128)(2,1)S(1)} %fusion.4), channel_id=1, source_target_pairs={{0,4},{4,0},{1,5},{5,1},{2,6},{6,2},{3,7},{7,3},{8,12},{12,8},{9,1... | collective-permute-start | bytes 589832 | tf_op jit(solution)/shard_map/ppermute | solution.py:51
  118.9 1.0 copy-start.12
  119.0 7.4 %collective-permute-start.23 = (bf16[4,2,112,128]{3,2,0,1:T(8,128)(2,1)S(1)}, bf16[4,2,112,128]{3,2,0,1:T(8,128)(2,1)S(1)}, u32[]{:S(2)}, u32[]{:S(2)}) collective-permute-start(bf16[4,2,112,128]{3,2,0,1:T(8,128)(2,1)S(1)} %fusion), channel_id=1, source_target_pairs={{0,2},{1,3},{2,0},{3,1},{4,6},{5,7},{6,4},{7,5},{8,10},{9,11},{10,... | collective-permute-start | bytes 688136 | tf_op jit(solution)/shard_map/ppermute | solution.py:51
  119.9 12.9 %collective-permute-start.20 = (bf16[2,64,1024]{2,1,0:T(8,128)(2,1)S(1)}, bf16[2,64,1024]{2,1,0:T(8,128)(2,1)S(1)}, u32[]{:S(2)}, u32[]{:S(2)}) collective-permute-start(bf16[2,64,1024]{2,1,0:T(8,128)(2,1)S(1)} %copy-done.12), channel_id=1, source_target_pairs={{16,0},{24,8},{17,1},{25,9},{18,2},{26,10},{19,3},{27,11},{20,4},{... | collective-permute-start | bytes 786440 | tf_op jit(solution)/shard_map/ppermute | solution.py:46
  124.4 12.2 %copy-start.6 = (bf16[4096,128]{1,0:T(8,128)(2,1)S(1)}, bf16[4096,128]{1,0:T(8,128)(2,1)}, u32[]{:S(2)}) copy-start(bf16[4096,128]{1,0:T(8,128)(2,1)} %copy-done.5) | copy-start | bytes 3145732
  124.4 4.7 %collective-permute-start.22 = (bf16[4,96,128]{2,1,0:T(8,128)(2,1)S(1)}, bf16[4,96,128]{2,1,0:T(8,128)(2,1)S(1)}, u32[]{:S(2)}, u32[]{:S(2)}) collective-permute-start(bf16[4,96,128]{2,1,0:T(8,128)(2,1)S(1)} %fusion.14), channel_id=1, source_target_pairs={{0,2},{1,3},{2,0},{3,1},{4,6},{5,7},{6,4},{7,5},{8,10},{9,11},{10,... | collective-permute-start | bytes 294920 | tf_op jit(solution)/shard_map/ppermute | solution.py:51
  126.5 4.9 %collective-permute-start.24 = (bf16[4,112,128]{2,1,0:T(8,128)(2,1)S(1)}, bf16[4,112,128]{2,1,0:T(8,128)(2,1)S(1)}, u32[]{:S(2)}, u32[]{:S(2)}) collective-permute-start(bf16[4,112,128]{2,1,0:T(8,128)(2,1)S(1)} %fusion.9), channel_id=1, source_target_pairs={{0,4},{4,0},{1,5},{5,1},{2,6},{6,2},{3,7},{7,3},{8,12},{12,8},{9,1... | collective-permute-start | bytes 344072 | tf_op jit(solution)/shard_map/ppermute | solution.py:51
  132.7 6.5 %collective-permute-start.25 = (bf16[208,128]{1,0:T(8,128)(2,1)S(1)}, bf16[208,128]{1,0:T(8,128)(2,1)S(1)}, u32[]{:S(2)}, u32[]{:S(2)}) collective-permute-start(bf16[208,128]{1,0:T(8,128)(2,1)S(1)} %get-tuple-element.68), channel_id=1, source_target_pairs={{0,8},{8,16},{16,24},{24,0},{1,9},{9,17},{17,25},{25,1},{2,10},{10... | collective-permute-start | bytes 159752 | tf_op jit(solution)/shard_map/ppermute | solution.py:41
  132.8 7.7 %collective-permute-start.26 = (bf16[208,128]{1,0:T(8,128)(2,1)S(1)}, bf16[208,128]{1,0:T(8,128)(2,1)S(1)}, u32[]{:S(2)}, u32[]{:S(2)}) collective-permute-start(bf16[208,128]{1,0:T(8,128)(2,1)S(1)} %get-tuple-element.70), channel_id=1, source_target_pairs={{0,16},{8,24},{16,0},{24,8},{1,17},{9,25},{17,1},{25,9},{2,18},{10... | collective-permute-start | bytes 159752 | tf_op jit(solution)/shard_map/ppermute | solution.py:41
  132.9 7.6 %collective-permute-start.27 = (bf16[208,128]{1,0:T(8,128)(2,1)S(1)}, bf16[208,128]{1,0:T(8,128)(2,1)S(1)}, u32[]{:S(2)}, u32[]{:S(2)}) collective-permute-start(bf16[208,128]{1,0:T(8,128)(2,1)S(1)} %get-tuple-element.69), channel_id=1, source_target_pairs={{0,24},{8,0},{16,8},{24,16},{1,25},{9,1},{17,9},{25,17},{2,26},{10... | collective-permute-start | bytes 159752 | tf_op jit(solution)/shard_map/ppermute | solution.py:41
  140.6 3.7 %collective-permute-start.28 = (bf16[208,128]{1,0:T(8,128)(2,1)S(1)}, bf16[208,128]{1,0:T(8,128)(2,1)S(1)}, u32[]{:S(2)}, u32[]{:S(2)}) collective-permute-start(bf16[208,128]{1,0:T(8,128)(2,1)S(1)} %fusion.12), channel_id=1, source_target_pairs={{0,3},{1,2},{2,1},{3,0},{4,7},{5,6},{6,5},{7,4},{8,11},{9,10},{10,... | collective-permute-start | bytes 159752 | tf_op jit(solution)/shard_map/ppermute | solution.py:51
  140.7 4.8 %collective-permute-start.29 = (bf16[208,128]{1,0:T(8,128)(2,1)S(1)}, bf16[208,128]{1,0:T(8,128)(2,1)S(1)}, u32[]{:S(2)}, u32[]{:S(2)}) collective-permute-start(bf16[208,128]{1,0:T(8,128)(2,1)S(1)} %fusion.12), channel_id=1, source_target_pairs={{0,2},{1,3},{2,0},{3,1},{4,6},{5,7},{6,4},{7,5},{8,10},{9,11},{10,... | collective-permute-start | bytes 159752 | tf_op jit(solution)/shard_map/ppermute | solution.py:51
  141.7 3.7 %collective-permute-start.30 = (bf16[208,128]{1,0:T(8,128)(2,1)S(1)}, bf16[208,128]{1,0:T(8,128)(2,1)S(1)}, u32[]{:S(2)}, u32[]{:S(2)}) collective-permute-start(bf16[208,128]{1,0:T(8,128)(2,1)S(1)} %fusion.12), channel_id=1, source_target_pairs={{0,1},{1,0},{2,3},{3,2},{4,5},{5,4},{6,7},{7,6},{8,9},{9,8},{10,11... | collective-permute-start | bytes 159752 | tf_op jit(solution)/shard_map/ppermute | solution.py:51

commit v8 on v7

--- a/solution.py
+++ b/solution.py
@@ -284,7 +284,7 @@
     out_ref[0, lo:] = past_ref[...]
 
 
-def pack_adapters(adapter_down, adapter_up, own_past):
+def pack_adapters(adapter_down, adapter_up, own_past, before):
     sp, rp, r = lax.axis_size("sp"), lax.axis_size("rep"), lax.axis_index("rep")
     down_rows, up_rows = adapter_down.shape[0] // rp, RANK // rp
     blocks = adapter_up.shape[1] // HEAD_DIM
@@ -303,21 +303,24 @@
     step = 1
     while step < sp:
         buf = jnp.concatenate([buf, partner(buf, "sp", step)], axis=0)
+        if step == 1:
+            buf = tie(buf, before)
         step *= 2
     seqs, each = own_past.shape[:2]
     past = buf[:, rows:].reshape(sp, seqs, each, -1).swapaxes(0, 1).reshape(seqs, sp * each, -1)
     return buf[:, :rows], past
 
 
-def adapters_packed(hidden, buf, before_rep, before_swap):
+def adapters_packed(hidden, buf, before_fsdp, before_rep, before_swap):
     sp, fs, rp = (lax.axis_size(a) for a in ("sp", "fsdp", "rep"))
     z, x, r = (lax.axis_index(a) for a in ("sp", "fsdp", "rep"))
+    buf = tie(buf, before_fsdp)
     step = 1
     while step < fs:
         buf = jnp.concatenate([buf, partner(buf, "fsdp", step)], axis=0)
         step *= 2
     step = 2
-    buf = tie(buf, *before_rep)
+    buf = tie(buf, before_rep)
     while step < rp:
         buf = jnp.concatenate([buf, partner(buf, "rep", step)], axis=0)
         step *= 2
@@ -441,7 +444,7 @@
     z, r = lax.axis_index("sp"), lax.axis_index("rep")
     shards, _, rows, lanes = send.shape
     far = [along(values[k - 1], "sp", -k) for k in range(3, sp)]
-    got = partner(tie(send, *far), "rep", 1)
+    got = partner(send, "rep", 1)
     values = [along(tie(values[1], got), "sp", -2)] + far
     fs_bits, rep_bits = fs.bit_length() - 1, rp.bit_length() - 2
     labels = [("fsdp", b) for b in reversed(range(fs_bits))]
@@ -461,7 +464,7 @@
                 parts = [lax.dynamic_index_in_dim(a, i, dim, keepdims=False) for a in terms]
                 return sum(a.astype(f32) for a in parts).astype(bf16)
 
-            send = pick(1 - mine)
+            send = tie(pick(1 - mine), *far)
             terms = [pick(mine), partner(send, axis, 1 << bit)]
         return sum(a.astype(f32) for a in terms).astype(bf16)
 
@@ -514,22 +517,20 @@
     seqs, tokens = hidden.shape[:2]
     past_len = past_keys.shape[1] * sp
     own_past = jnp.concatenate([past_keys, past_values], axis=2)
+    keys, bases = [key_span], [value_base]
+    for line in (keys, bases):
+        for k in range(1, sp):
+            line.append(along(line[k - 1], "sp", 1, k - 1))
     even = adapter_up.shape[1] % HEAD_DIM == 0
     if even:
-        buf, past = pack_adapters(adapter_down, adapter_up, own_past)
+        buf, past = pack_adapters(adapter_down, adapter_up, own_past, keys[1])
     else:
-        buf = own_past
         past = [own_past] + [cyclic(own_past, "sp", k) for k in range(1, sp)]
         past = jnp.concatenate(past, axis=1)
-    keys, bases = [key_span], [value_base]
-    for line in (keys, bases):
-        line.append(along(tie(line[0], buf), "sp", 1))
-        for k in range(2, sp):
-            line.append(along(line[k - 1], "sp", 1, k - 1))
     second = min(2, sp - 1)
     if even:
         down_full, up_blocks, low_own = adapters_packed(
-            hidden, buf, (keys[1], bases[1]), (keys[second], bases[second])
+            hidden, buf, bases[1], keys[second], (bases[second], keys[min(3, sp - 1)])
         )
     else:
         down_full, up_blocks, low_own = adapters_plain(hidden, adapter_down, adapter_up)
@@ -551,7 +552,8 @@
         .reshape(seqs * tokens, 2 * RANK)
     )
     first_got = along(values[0], "sp", -1)
-    send, keep = packed_grads(hidden, tie(low_grad, first_got), guq, guv, sp * fs)
+    send, keep = packed_grads(hidden, low_grad, guq, guv, sp * fs)
+    send = tie(send, first_got)
     grad_down, grad_up, grad_hidden, got = finish_grads(
         send, keep, values, low_grad, lambda x: grad_hidden_of(x, down_full, seqs, tokens)
     )

time: 148 us -> 156 us (1.054)
  starting transfers between devices: 53.2 us -> 64.3 us
  waiting for transfers between devices: 55.9 us -> 47.8 us
  local copies, waits for them, and re-layouts: 10.3 us -> 14.3 us
    ppermute x15, starting transfers between devices: 35.1 us -> 47.4 us  [along(): lax.ppermute(x, axis, [(i, i + shift) for i in range(start, n) if 0 <= i...]
    ppermute x15, waiting for transfers between devices: 25 us -> 20.4 us  [along(): lax.ppermute(x, axis, [(i, i + shift) for i in range(start, n) if 0 <= i...]
    ppermute x13, waiting for transfers between devices: 29.2 us -> 25.7 us  [partner(): return lax.ppermute(x, axis, [(i, i ^ mask) for i in range(n)])]
    unnamed x61 -> x74, local copies, waits for them, and re-layouts: 9.77 us -> 12.8 us
  transfers between devices with their start and end apart: 31 -> 31, of which waited for: 22 -> 22; matrix products, arithmetic and copies ran while one was open for 1% -> 3% of each run, Pallas kernels for 3% -> 3%
where the time goes in v8:
time: 156 us; the launch traced here: 155 us
  starting transfers between devices  64.3 us (41%)
  waiting for transfers between devices  47.8 us (31%)
  Pallas kernels  22.3 us (14%)
  local copies, waits for them, and re-layouts  14.3 us (9%)
  other arithmetic  4.71 us (3%)
    ppermute x15, starting transfers between devices, along(): lax.ppermute(x, axis, [(i, i + shift) for i in range(start, n) if 0 <= i...  47.4 us
    ppermute x13, waiting for transfers between devices, partner(): return lax.ppermute(x, axis, [(i, i ^ mask) for i in range(n)])  25.7 us
    ppermute x15, waiting for transfers between devices, along(): lax.ppermute(x, axis, [(i, i + shift) for i in range(start, n) if 0 <= i...  20.4 us
    pallas_call x1, Pallas kernels, attention(): pl.pallas_call(functools.partial(attention_kernel, shards), grid=(KV_HEAD...  17.4 us
    ppermute x13, starting transfers between devices, partner(): return lax.ppermute(x, axis, [(i, i ^ mask) for i in range(n)])  13 us
    unnamed x74, local copies, waits for them, and re-layouts  12.8 us
    ppermute x3, starting transfers between devices, cyclic(): return lax.ppermute(x, axis, [(i, (i + shift) % n) for i in range(n)])  3.86 us
  transfers between devices with their start and end apart: 31, of which 22 were waited for; matrix products, arithmetic and copies ran while one was open for 3% of the time, Pallas kernels for 3%

profile of v8, /device:TPU:0, one launch (start us, length us, event | category | flops | bytes accessed | tf_op | source)
XLA Modules:
  0.0 154.8 jit_solution(5944585591015219909)
XLA Ops:
  0.6 5.1 %collective-permute-start.1 = (bf16[2,64,1024]{2,1,0:T(8,128)(2,1)}, bf16[2,64,1024]{2,1,0:T(8,128)(2,1)S(1)}, u32[]{:S(2)}, u32[]{:S(2)}) collective-permute-start(bf16[2,64,1024]{2,1,0:T(8,128)(2,1)} %refs_12_.1), channel_id=1, source_target_pairs={{0,8},{8,16},{16,24},{1,9},{9,17},{17,25},{2,10},{10,18},{18,26},{... | collective-permute-start | bytes 786440 | tf_op jit(solution)/shard_map/ppermute | solution.py:46
  5.7 0.8 pad_maximum_fusion.5
  6.5 0.9 copy-done.2
  7.4 1.6 %collective-permute-start = (bf16[1,336,128]{2,1,0:T(8,128)(2,1)S(1)}, bf16[1,336,128]{2,1,0:T(8,128)(2,1)S(1)}, u32[]{:S(2)}, u32[]{:S(2)}) collective-permute-start(bf16[1,336,128]{2,1,0:T(8,128)(2,1)S(1)} %pack.1), channel_id=1, source_target_pairs={{0,8},{8,0},{16,24},{24,16},{1,9},{9,1},{17,25},{25,17},{2,10},{10... | collective-permute-start | bytes 258056 | tf_op jit(solution)/shard_map/ppermute | solution.py:51
  9.1 4.2 %collective-permute-done = bf16[1,336,128]{2,1,0:T(8,128)(2,1)S(1)} collective-permute-done((bf16[1,336,128]{2,1,0:T(8,128)(2,1)S(1)}, bf16[1,336,128]{2,1,0:T(8,128)(2,1)S(1)}, u32[]{:S(2)}, u32[]{:S(2)}) %collective-permute-start) | collective-permute-done | bytes 86048 | tf_op jit(solution)/shard_map/ppermute | solution.py:51
  13.4 2.7 %collective-permute-start.2 = (bf16[2,336,128]{2,1,0:T(8,128)(2,1)S(1)}, bf16[2,336,128]{2,1,0:T(8,128)(2,1)S(1)}, u32[]{:S(2)}, u32[]{:S(2)}) collective-permute-start(bf16[2,336,128]{2,1,0:T(8,128)(2,1)S(1)} %pad_maximum_fusion.3), channel_id=1, source_target_pairs={{0,16},{8,24},{16,0},{24,8},{1,17},{9,25},{17,1},{25,9},{2,18},{10... | collective-permute-start | bytes 516104 | tf_op jit(solution)/shard_map/ppermute | solution.py:51
  16.0 4.4 %collective-permute-start.3 = (bf16[2,64,1024]{2,1,0:T(8,128)(2,1)S(1)}, bf16[2,64,1024]{2,1,0:T(8,128)(2,1)S(1)}, u32[]{:S(2)}, u32[]{:S(2)}) collective-permute-start(bf16[2,64,1024]{2,1,0:T(8,128)(2,1)S(1)} %copy-done.8), channel_id=1, source_target_pairs={{0,8},{8,16},{16,24},{1,9},{9,17},{17,25},{2,10},{10,18},{18,26},{... | collective-permute-start | bytes 786440 | tf_op jit(solution)/shard_map/ppermute | solution.py:46
  20.4 2.9 %collective-permute-done.2 = bf16[2,336,128]{2,1,0:T(8,128)(2,1)S(1)} collective-permute-done((bf16[2,336,128]{2,1,0:T(8,128)(2,1)S(1)}, bf16[2,336,128]{2,1,0:T(8,128)(2,1)S(1)}, u32[]{:S(2)}, u32[]{:S(2)}) %collective-permute-start.2) | collective-permute-done | bytes 172064 | tf_op jit(solution)/shard_map/ppermute | solution.py:51
  23.4 1.4 collective-permute-done.3.refs_17_
  24.8 1.5 collective-permute-start.4
  26.3 0.7 collective-permute-start.5
  27.0 3.7 %collective-permute-done.4 = bf16[4,208,128]{2,1,0:T(8,128)(2,1)S(1)} collective-permute-done((bf16[4,208,128]{2,1,0:T(8,128)(2,1)S(1)}, bf16[4,208,128]{2,1,0:T(8,128)(2,1)S(1)}, u32[]{:S(2)}, u32[]{:S(2)}) %collective-permute-start.4) | collective-permute-done | bytes 213024 | tf_op jit(solution)/shard_map/ppermute | solution.py:51
  30.7 1.6 %collective-permute-start.6 = (bf16[8,208,128]{2,1,0:T(8,128)(2,1)S(1)}, bf16[8,208,128]{2,1,0:T(8,128)(2,1)S(1)}, u32[]{:S(2)}, u32[]{:S(2)}) collective-permute-start(bf16[8,208,128]{2,1,0:T(8,128)(2,1)S(1)} %pad_maximum_fusion), channel_id=1, source_target_pairs={{0,2},{1,3},{2,0},{3,1},{4,6},{5,7},{6,4},{7,5},{8,10},{9,11},{10,... | collective-permute-start | bytes 1277960 | tf_op jit(solution)/shard_map/ppermute | solution.py:51
  32.3 1.4 collective-permute-start.7
  33.7 0.7 collective-permute-start.8
  34.4 4.7 %collective-permute-done.6 = bf16[8,208,128]{2,1,0:T(8,128)(2,1)S(1)} collective-permute-done((bf16[8,208,128]{2,1,0:T(8,128)(2,1)S(1)}, bf16[8,208,128]{2,1,0:T(8,128)(2,1)S(1)}, u32[]{:S(2)}, u32[]{:S(2)}) %collective-permute-start.6) | collective-permute-done | bytes 426016 | tf_op jit(solution)/shard_map/ppermute | solution.py:51
  39.2 0.7 copy-done.20
  39.9 1.4 collective-permute-start.13
  41.3 0.8 fusion.15
  42.3 1.2 low_rank.1
  43.5 1.0 copy-done.5
  44.5 14.1 %collective-permute-start.10 = (bf16[2,64,128]{2,1,0:T(8,128)(2,1)S(1)}, bf16[2,64,128]{2,1,0:T(8,128)(2,1)S(1)}, u32[]{:S(2)}, u32[]{:S(2)}) collective-permute-start(bf16[2,64,128]{2,1,0:T(8,128)(2,1)S(1)} %get-tuple-element.39.refs_8_), channel_id=1, source_target_pairs={{0,8},{8,16},{16,24},{1,9},{9,17},{17,25},{2,10},{10,18},{18,26},{... | collective-permute-start | bytes 98312 | tf_op jit(solution)/shard_map/ppermute | solution.py:46
  58.6 10.7 %collective-permute-start.11 = (bf16[2,64,128]{2,1,0:T(8,128)(2,1)S(1)}, bf16[2,64,128]{2,1,0:T(8,128)(2,1)S(1)}, u32[]{:S(2)}, u32[]{:S(2)}) collective-permute-start(bf16[2,64,128]{2,1,0:T(8,128)(2,1)S(1)} %get-tuple-element.39.refs_8_), channel_id=1, source_target_pairs={{0,16},{8,24},{1,17},{9,25},{2,18},{10,26},{3,19},{11,27},{4,20},{... | collective-permute-start | bytes 98312 | tf_op jit(solution)/shard_map/ppermute | solution.py:46
  69.3 1.3 collective-permute-start.12
  70.7 0.9 slice.164
  72.7 1.2 copy-done.3
  73.9 1.2 copy-done.4
  75.1 0.9 copy-done.9
  76.1 0.9 copy-done.15
  77.0 0.9 copy-done.17
  78.0 0.9 copy-done.19
  78.9 0.9 copy-done.21
  79.9 17.4 %attention.1 = (bf16[2,64,4096]{2,1,0:T(8,128)(2,1)}, bf16[2,64,4096]{2,1,0:T(8,128)(2,1)}, bf16[32,4,16,128]{3,2,1,0:T(8,128)(2,1)S(1)}, bf16[8,4,16,128]{3,2,1...) custom-call(s32[1]{0:T(128)} %bitcast.place_ref, ...), custom_call_target="tpu_custom_call" | custom-call | flops 17112760320 | bytes 65536 | tf_op jit(solution)/shard_map/attention/pallas_call | solution.py:211
  97.2 0.7 copy-done.22
  98.0 0.7 copy-done.10
  98.7 1.3 collective-permute-start.15
  100.0 1.3 collective-permute-start.16
  101.3 1.3 collective-permute-start.17
  102.6 1.3 collective-permute-start.14
  103.9 0.6 collective-permute-done.15
  104.5 2.2 %collective-permute-done.16 = bf16[2,64,64]{2,1,0:T(8,128)(2,1)S(1)} collective-permute-done((bf16[2,64,64]{2,1,0:T(8,128)(2,1)S(1)}, bf16[2,64,64]{2,1,0:T(8,128)(2,1)S(1)}, u32[]{:S(2)}, u32[]{:S(2)}) %collective-permute-start.16) | collective-permute-done | bytes 16416 | tf_op jit(solution)/shard_map/ppermute | solution.py:46
  106.7 3.7 %collective-permute-done.17 = bf16[2,64,64]{2,1,0:T(8,128)(2,1)S(1)} collective-permute-done((bf16[2,64,64]{2,1,0:T(8,128)(2,1)S(1)}, bf16[2,64,64]{2,1,0:T(8,128)(2,1)S(1)}, u32[]{:S(2)}, u32[]{:S(2)}) %collective-permute-start.17) | collective-permute-done | bytes 16416 | tf_op jit(solution)/shard_map/ppermute | solution.py:46
  110.6 1.6 %adapter_grads.1 = (bf16[8,2,208,128]{3,2,1,0:T(8,128)(2,1)}, bf16[8,2,208,128]{3,2,1,0:T(8,128)(2,1)S(1)}) custom-call(s32[1]{0:T(128)} %bitcast.4.core_ref, bf16[2,64,4096]{2,1,0:T(8,128)(2,1)S(1)} %copy-done, bf16[128,128]{1,0:T(8,128)(2,1)S(1)} %pad_maximum_fusion.8.low_ref, bf16[32,4,16,128]{3,2,1,0:T(8,128)(2,1)S(1)} %get-tuple-element.47.guq_ref, ...), custom_call_target="tpu_custom_call" | custom-call | flops 134217728 | bytes 5242880 | tf_op jit(solution)/shard_map/adapter_grads/pallas_call | solution.py:418
  112.2 1.2 collective-permute-done.14
  113.4 0.7 copy-done.25
  114.1 1.3 collective-permute-start.20
  115.6 1.1 collective-permute-done.18
  116.9 9.6 %collective-permute-done.20 = bf16[2,64,1024]{2,1,0:T(8,128)(2,1)S(1)} collective-permute-done((bf16[2,64,1024]{2,1,0:T(8,128)(2,1)S(1)}, bf16[2,64,1024]{2,1,0:T(8,128)(2,1)S(1)}, u32[]{:S(2)}, u32[]{:S(2)}) %collective-permute-start.20) | collective-permute-done | bytes 262176 | tf_op jit(solution)/shard_map/ppermute | solution.py:46
  128.0 1.3 collective-permute-start.19
  129.5 3.6 %collective-permute-done.21 = bf16[4,2,96,128]{3,2,0,1:T(8,128)(2,1)S(1)} collective-permute-done((bf16[4,2,96,128]{3,2,0,1:T(8,128)(2,1)S(1)}, bf16[4,2,96,128]{3,2,0,1:T(8,128)(2,1)S(1)}, u32[]{:S(2)}, u32[]{:S(2)}) %collective-permute-start.21) | collective-permute-done | bytes 196640 | tf_op jit(solution)/shard_map/ppermute | solution.py:51
  134.2 2.1 %collective-permute-start.24 = (bf16[4,112,128]{2,1,0:T(8,128)(2,1)S(1)}, bf16[4,112,128]{2,1,0:T(8,128)(2,1)S(1)}, u32[]{:S(2)}, u32[]{:S(2)}) collective-permute-start(bf16[4,112,128]{2,1,0:T(8,128)(2,1)S(1)} %fusion.9), channel_id=1, source_target_pairs={{0,4},{4,0},{1,5},{5,1},{2,6},{6,2},{3,7},{7,3},{8,12},{12,8},{9,1... | collective-permute-start | bytes 344072 | tf_op jit(solution)/shard_map/ppermute | solution.py:51
  136.3 1.5 collective-permute-done.22
  137.8 1.3 collective-permute-done.24
  139.2 1.2 collective-permute-done.19
  140.5 3.7 %collective-permute-start.27 = (bf16[208,128]{1,0:T(8,128)(2,1)S(1)}, bf16[208,128]{1,0:T(8,128)(2,1)S(1)}, u32[]{:S(2)}, u32[]{:S(2)}) collective-permute-start(bf16[208,128]{1,0:T(8,128)(2,1)S(1)} %get-tuple-element.75), channel_id=1, source_target_pairs={{0,24},{8,0},{16,8},{24,16},{1,25},{9,1},{17,9},{25,17},{2,26},{10... | collective-permute-start | bytes 159752 | tf_op jit(solution)/shard_map/ppermute | solution.py:41
  144.3 2.1 %grad_hidden.1 = bf16[2,64,4096]{2,1,0:T(8,128)(2,1)} custom-call(bf16[128,128]{1,0:T(8,128)(2,1)S(1)} %pad_maximum_fusion.8.low_ref, bf16[4096,128]{1,0:T(8,128)(2,1)S(1)} %copy-done.6), custom_call_target="tpu_custom_call" | custom-call | flops 1073741824 | bytes 65536 | tf_op jit(solution)/shard_map/grad_hidden/pallas_call | solution.py:369
  146.9 1.2 collective-permute-done.26
  148.3 1.0 collective-permute-start.29
  149.3 0.8 collective-permute-start.30
  150.2 0.9 add_convert_fusion
  151.0 0.9 collective-permute-done.28
  151.9 1.1 collective-permute-done.29
  153.4 0.7 pad_maximum_fusion.4
  154.1 0.7 pad_maximum_fusion.1
  (129 shorter events, 5.9 us)
Async XLA Ops:
  0.6 5.9 %copy-start.1 = (bf16[512,128]{1,0:T(8,128)(2,1)S(1)}, bf16[512,128]{1,0:T(8,128)(2,1)}, u32[]{:S(2)}) copy-start(bf16[512,128]{1,0:T(8,128)(2,1)} %down_ref.1) | copy-start | bytes 393220
  0.6 12.7 %collective-permute-start.1 = (bf16[2,64,1024]{2,1,0:T(8,128)(2,1)}, bf16[2,64,1024]{2,1,0:T(8,128)(2,1)S(1)}, u32[]{:S(2)}, u32[]{:S(2)}) collective-permute-start(bf16[2,64,1024]{2,1,0:T(8,128)(2,1)} %refs_12_.1), channel_id=1, source_target_pairs={{0,8},{8,16},{16,24},{1,9},{9,17},{17,25},{2,10},{10,18},{18,26},{... | collective-permute-start | bytes 786440 | tf_op jit(solution)/shard_map/ppermute | solution.py:46
  6.5 0.9 copy-start.2
  7.4 8.6 %copy-start.8 = (bf16[2,64,1024]{2,1,0:T(8,128)(2,1)S(1)}, bf16[2,64,1024]{2,1,0:T(8,128)(2,1)}, u32[]{:S(2)}) copy-start(bf16[2,64,1024]{2,1,0:T(8,128)(2,1)} %refs_16_.1) | copy-start | bytes 786436
  7.4 5.9 %collective-permute-start = (bf16[1,336,128]{2,1,0:T(8,128)(2,1)S(1)}, bf16[1,336,128]{2,1,0:T(8,128)(2,1)S(1)}, u32[]{:S(2)}, u32[]{:S(2)}) collective-permute-start(bf16[1,336,128]{2,1,0:T(8,128)(2,1)S(1)} %pack.1), channel_id=1, source_target_pairs={{0,8},{8,0},{16,24},{24,16},{1,9},{9,1},{17,25},{25,17},{2,10},{10... | collective-permute-start | bytes 258056 | tf_op jit(solution)/shard_map/ppermute | solution.py:51
  13.3 12.9 %copy-start.14 = (bf16[2,64,1024]{2,1,0:T(8,128)(2,1)}, bf16[2,64,1024]{2,1,0:T(8,128)(2,1)S(1)}, u32[]{:S(2)}) copy-start(bf16[2,64,1024]{2,1,0:T(8,128)(2,1)S(1)} %collective-permute-done.1.refs_13_) | copy-start | bytes 786436
  13.4 10.0 %collective-permute-start.2 = (bf16[2,336,128]{2,1,0:T(8,128)(2,1)S(1)}, bf16[2,336,128]{2,1,0:T(8,128)(2,1)S(1)}, u32[]{:S(2)}, u32[]{:S(2)}) collective-permute-start(bf16[2,336,128]{2,1,0:T(8,128)(2,1)S(1)} %pad_maximum_fusion.3), channel_id=1, source_target_pairs={{0,16},{8,24},{16,0},{24,8},{1,17},{9,25},{17,1},{25,9},{2,18},{10... | collective-permute-start | bytes 516104 | tf_op jit(solution)/shard_map/ppermute | solution.py:51
  16.0 8.8 %collective-permute-start.3 = (bf16[2,64,1024]{2,1,0:T(8,128)(2,1)S(1)}, bf16[2,64,1024]{2,1,0:T(8,128)(2,1)S(1)}, u32[]{:S(2)}, u32[]{:S(2)}) collective-permute-start(bf16[2,64,1024]{2,1,0:T(8,128)(2,1)S(1)} %copy-done.8), channel_id=1, source_target_pairs={{0,8},{8,16},{16,24},{1,9},{9,17},{17,25},{2,10},{10,18},{18,26},{... | collective-permute-start | bytes 786440 | tf_op jit(solution)/shard_map/ppermute | solution.py:46
  23.4 3.6 %copy-start.24 = (bf16[4,336,128]{2,1,0:T(8,128)(2,1)}, bf16[4,336,128]{2,1,0:T(8,128)(2,1)S(1)}, u32[]{:S(2)}) copy-start(bf16[4,336,128]{2,1,0:T(8,128)(2,1)S(1)} %constant_dynamic-update-slice_fusion) | copy-start | bytes 1032196
  24.8 7.5 %copy-start.16 = (bf16[2,64,1024]{2,1,0:T(8,128)(2,1)}, bf16[2,64,1024]{2,1,0:T(8,128)(2,1)S(1)}, u32[]{:S(2)}) copy-start(bf16[2,64,1024]{2,1,0:T(8,128)(2,1)S(1)} %collective-permute-done.3.refs_17_) | copy-start | bytes 786436
  24.8 5.8 %collective-permute-start.4 = (bf16[4,208,128]{2,1,0:T(8,128)(2,1)S(1)}, bf16[4,208,128]{2,1,0:T(8,128)(2,1)S(1)}, u32[]{:S(2)}, u32[]{:S(2)}) collective-permute-start(bf16[4,208,128]{2,1,0:T(8,128)(2,1)S(1)} %slice.163), channel_id=1, source_target_pairs={{0,4},{4,0},{1,5},{5,1},{2,6},{6,2},{3,7},{7,3},{8,12},{12,8},{9,1... | collective-permute-start | bytes 638984 | tf_op jit(solution)/shard_map/ppermute | solution.py:51
  26.3 4.4 %collective-permute-start.5 = (bf16[2,64,1024]{2,1,0:T(8,128)(2,1)S(1)}, bf16[2,64,1024]{2,1,0:T(8,128)(2,1)S(1)}, u32[]{:S(2)}, u32[]{:S(2)}) collective-permute-start(bf16[2,64,1024]{2,1,0:T(8,128)(2,1)S(1)} %collective-permute-done.1.refs_13_), channel_id=1, source_target_pairs={{8,16},{16,24},{9,17},{17,25},{10,18},{18,26},{11,19},{19,27},{12,... | collective-permute-start | bytes 786440 | tf_op jit(solution)/shard_map/ppermute | solution.py:46
  30.7 11.6 %copy-start = (bf16[2,64,4096]{2,1,0:T(8,128)(2,1)S(1)}, bf16[2,64,4096]{2,1,0:T(8,128)(2,1)}, u32[]{:S(2)}) copy-start(bf16[2,64,4096]{2,1,0:T(8,128)(2,1)} %hidden_ref.3) | copy-start | bytes 3145732
  30.7 3.7 %copy-start.18 = (bf16[2,64,1024]{2,1,0:T(8,128)(2,1)}, bf16[2,64,1024]{2,1,0:T(8,128)(2,1)S(1)}, u32[]{:S(2)}) copy-start(bf16[2,64,1024]{2,1,0:T(8,128)(2,1)S(1)} %collective-permute-done.5.refs_14_) | copy-start | bytes 786436
  30.7 8.4 %collective-permute-start.6 = (bf16[8,208,128]{2,1,0:T(8,128)(2,1)S(1)}, bf16[8,208,128]{2,1,0:T(8,128)(2,1)S(1)}, u32[]{:S(2)}, u32[]{:S(2)}) collective-permute-start(bf16[8,208,128]{2,1,0:T(8,128)(2,1)S(1)} %pad_maximum_fusion), channel_id=1, source_target_pairs={{0,2},{1,3},{2,0},{3,1},{4,6},{5,7},{6,4},{7,5},{8,10},{9,11},{10,... | collective-permute-start | bytes 1277960 | tf_op jit(solution)/shard_map/ppermute | solution.py:51
  32.3 6.9 %collective-permute-start.7 = (bf16[2,64,1024]{2,1,0:T(8,128)(2,1)S(1)}, bf16[2,64,1024]{2,1,0:T(8,128)(2,1)}, u32[]{:S(2)}, u32[]{:S(2)}) collective-permute-start(bf16[2,64,1024]{2,1,0:T(8,128)(2,1)S(1)} %collective-permute-done.3.refs_17_), channel_id=1, source_target_pairs={{8,16},{16,24},{9,17},{17,25},{10,18},{18,26},{11,19},{19,27},{12,... | collective-permute-start | bytes 786440 | tf_op jit(solution)/shard_map/ppermute | solution.py:46
  33.7 5.5 %collective-permute-start.8 = (bf16[2,64,1024]{2,1,0:T(8,128)(2,1)S(1)}, bf16[2,64,1024]{2,1,0:T(8,128)(2,1)S(1)}, u32[]{:S(2)}, u32[]{:S(2)}) collective-permute-start(bf16[2,64,1024]{2,1,0:T(8,128)(2,1)S(1)} %collective-permute-done.5.refs_14_), channel_id=1, source_target_pairs={{16,24},{17,25},{18,26},{19,27},{20,28},{21,29},{22,30},{23,31}} | collective-permute-start | bytes 786440 | tf_op jit(solution)/shard_map/ppermute | solution.py:46
  39.2 0.7 copy-start.20
  39.9 2.4 %collective-permute-start.9 = (bf16[16,208,128]{2,1,0:T(8,128)(2,1)S(1)}, bf16[16,208,128]{2,1,0:T(8,128)(2,1)S(1)}, u32[]{:S(2)}, u32[]{:S(2)}) collective-permute-start(bf16[16,208,128]{2,1,0:T(8,128)(2,1)S(1)} %constant_dynamic-update-slice_fusion.2.own_ref), channel_id=1, source_target_pairs={{0,1},{1,0},{2,3},{3,2},{4,5},{5,4},{6,7},{7,6},{8,9},{9,8},{10,11... | collective-permute-start | bytes 2555912 | tf_op jit(solution)/shard_map/ppermute | solution.py:51
  39.9 31.9 %collective-permute-start.13 = (bf16[2,64,1024]{2,1,0:T(8,128)(2,1)}, bf16[2,64,1024]{2,1,0:T(8,128)(2,1)}, u32[]{:S(2)}, u32[]{:S(2)}) collective-permute-start(bf16[2,64,1024]{2,1,0:T(8,128)(2,1)} %collective-permute-done.7.refs_18_), channel_id=1, source_target_pairs={{16,24},{17,25},{18,26},{19,27},{20,28},{21,29},{22,30},{23,31}} | collective-permute-start | bytes 786440 | tf_op jit(solution)/shard_map/ppermute | solution.py:46
  42.2 28.5 %copy-start.27 = (f32[64,64]{1,0:T(8,128)S(1)}, f32[64,64]{1,0:T(8,128)}, u32[]{:S(2)}) copy-start(f32[64,64]{1,0:T(8,128)} %get-tuple-element.82) | copy-start | bytes 49156
  43.5 1.0 copy-start.5
  44.5 27.4 %collective-permute-start.10 = (bf16[2,64,128]{2,1,0:T(8,128)(2,1)S(1)}, bf16[2,64,128]{2,1,0:T(8,128)(2,1)S(1)}, u32[]{:S(2)}, u32[]{:S(2)}) collective-permute-start(bf16[2,64,128]{2,1,0:T(8,128)(2,1)S(1)} %get-tuple-element.39.refs_8_), channel_id=1, source_target_pairs={{0,8},{8,16},{16,24},{1,9},{9,17},{17,25},{2,10},{10,18},{18,26},{... | collective-permute-start | bytes 98312 | tf_op jit(solution)/shard_map/ppermute | solution.py:46
  58.6 13.2 %collective-permute-start.11 = (bf16[2,64,128]{2,1,0:T(8,128)(2,1)S(1)}, bf16[2,64,128]{2,1,0:T(8,128)(2,1)S(1)}, u32[]{:S(2)}, u32[]{:S(2)}) collective-permute-start(bf16[2,64,128]{2,1,0:T(8,128)(2,1)S(1)} %get-tuple-element.39.refs_8_), channel_id=1, source_target_pairs={{0,16},{8,24},{1,17},{9,25},{2,18},{10,26},{3,19},{11,27},{4,20},{... | collective-permute-start | bytes 98312 | tf_op jit(solution)/shard_map/ppermute | solution.py:46
  69.3 2.9 %collective-permute-start.12 = (bf16[2,64,128]{2,1,0:T(8,128)(2,1)S(1)}, bf16[2,64,128]{2,1,0:T(8,128)(2,1)S(1)}, u32[]{:S(2)}, u32[]{:S(2)}) collective-permute-start(bf16[2,64,128]{2,1,0:T(8,128)(2,1)S(1)} %get-tuple-element.39.refs_8_), channel_id=1, source_target_pairs={{0,24},{1,25},{2,26},{3,27},{4,28},{5,29},{6,30},{7,31}} | collective-permute-start | bytes 98312 | tf_op jit(solution)/shard_map/ppermute | solution.py:46
  71.7 1.0 copy-start.7
  72.7 1.2 copy-start.3
  73.9 1.2 copy-start.4
  75.1 0.9 copy-start.9
  76.1 0.9 copy-start.15
  77.0 0.9 copy-start.17
  78.0 0.9 copy-start.19
  78.9 0.9 copy-start.21
  97.2 0.7 copy-start.22
  97.9 0.7 copy-start.10
  97.9 0.8 copy-start.12
  97.9 4.7 %copy-start.23 = (bf16[2,64,1024]{2,1,0:T(8,128)(2,1)S(1)}, bf16[2,64,1024]{2,1,0:T(8,128)(2,1)}, u32[]{:S(2)}) copy-start(bf16[2,64,1024]{2,1,0:T(8,128)(2,1)} %copy-done.22) | copy-start | bytes 786436
  98.7 5.8 %collective-permute-start.15 = (bf16[2,64,64]{2,1,0:T(8,128)(2,1)S(1)}, bf16[2,64,64]{2,1,0:T(8,128)(2,1)S(1)}, u32[]{:S(2)}, u32[]{:S(2)}) collective-permute-start(bf16[2,64,64]{2,1,0:T(8,128)(2,1)S(1)} %get-tuple-element.77), channel_id=1, source_target_pairs={{8,0},{16,8},{24,16},{9,1},{17,9},{25,17},{10,2},{18,10},{26,18},{... | collective-permute-start | bytes 49160 | tf_op jit(solution)/shard_map/ppermute | solution.py:46
  100.0 6.7 %collective-permute-start.16 = (bf16[2,64,64]{2,1,0:T(8,128)(2,1)S(1)}, bf16[2,64,64]{2,1,0:T(8,128)(2,1)S(1)}, u32[]{:S(2)}, u32[]{:S(2)}) collective-permute-start(bf16[2,64,64]{2,1,0:T(8,128)(2,1)S(1)} %get-tuple-element.79), channel_id=1, source_target_pairs={{16,0},{24,8},{17,1},{25,9},{18,2},{26,10},{19,3},{27,11},{20,4},{... | collective-permute-start | bytes 49160 | tf_op jit(solution)/shard_map/ppermute | solution.py:46
  101.3 9.1 %collective-permute-start.17 = (bf16[2,64,64]{2,1,0:T(8,128)(2,1)S(1)}, bf16[2,64,64]{2,1,0:T(8,128)(2,1)S(1)}, u32[]{:S(2)}, u32[]{:S(2)}) collective-permute-start(bf16[2,64,64]{2,1,0:T(8,128)(2,1)S(1)} %get-tuple-element.78), channel_id=1, source_target_pairs={{24,0},{25,1},{26,2},{27,3},{28,4},{29,5},{30,6},{31,7}} | collective-permute-start | bytes 49160 | tf_op jit(solution)/shard_map/ppermute | solution.py:46
  102.6 10.8 %collective-permute-start.14 = (bf16[2,64,1024]{2,1,0:T(8,128)(2,1)S(1)}, bf16[2,64,1024]{2,1,0:T(8,128)(2,1)S(1)}, u32[]{:S(2)}, u32[]{:S(2)}) collective-permute-start(bf16[2,64,1024]{2,1,0:T(8,128)(2,1)S(1)} %copy-done.23), channel_id=1, source_target_pairs={{8,0},{16,8},{24,16},{9,1},{17,9},{25,17},{10,2},{18,10},{26,18},{... | collective-permute-start | bytes 786440 | tf_op jit(solution)/shard_map/ppermute | solution.py:46
  110.6 3.6 %copy-start.13 = (bf16[2,64,1024]{2,1,0:T(8,128)(2,1)S(1)}, bf16[2,64,1024]{2,1,0:T(8,128)(2,1)}, u32[]{:S(2)}) copy-start(bf16[2,64,1024]{2,1,0:T(8,128)(2,1)} %copy-done.12) | copy-start | bytes 786436
  113.4 0.7 copy-start.25
  114.1 2.6 %collective-permute-start.18 = (bf16[8,2,208,128]{3,2,1,0:T(8,128)(2,1)}, bf16[8,2,208,128]{3,2,1,0:T(8,128)(2,1)S(1)}, u32[]{:S(2)}, u32[]{:S(2)}) collective-permute-start(bf16[8,2,208,128]{3,2,1,0:T(8,128)(2,1)} %get-tuple-element.50), channel_id=1, source_target_pairs={{0,1},{1,0},{2,3},{3,2},{4,5},{5,4},{6,7},{7,6},{8,9},{9,8},{10,11... | collective-permute-start | bytes 2555912 | tf_op jit(solution)/shard_map/ppermute | solution.py:51
  114.1 12.4 %collective-permute-start.20 = (bf16[2,64,1024]{2,1,0:T(8,128)(2,1)S(1)}, bf16[2,64,1024]{2,1,0:T(8,128)(2,1)S(1)}, u32[]{:S(2)}, u32[]{:S(2)}) collective-permute-start(bf16[2,64,1024]{2,1,0:T(8,128)(2,1)S(1)} %copy-done.13), channel_id=1, source_target_pairs={{24,0},{25,1},{26,2},{27,3},{28,4},{29,5},{30,6},{31,7}} | collective-permute-start | bytes 786440 | tf_op jit(solution)/shard_map/ppermute | solution.py:46
  126.5 6.5 %collective-permute-start.21 = (bf16[4,2,96,128]{3,2,0,1:T(8,128)(2,1)S(1)}, bf16[4,2,96,128]{3,2,0,1:T(8,128)(2,1)S(1)}, u32[]{:S(2)}, u32[]{:S(2)}) collective-permute-start(bf16[4,2,96,128]{3,2,0,1:T(8,128)(2,1)S(1)} %fusion.4), channel_id=1, source_target_pairs={{0,4},{4,0},{1,5},{5,1},{2,6},{6,2},{3,7},{7,3},{8,12},{12,8},{9,1... | collective-permute-start | bytes 589832 | tf_op jit(solution)/shard_map/ppermute | solution.py:51
  127.1 1.0 copy-start.11
  127.2 7.0 %collective-permute-start.23 = (bf16[4,2,112,128]{3,2,0,1:T(8,128)(2,1)S(1)}, bf16[4,2,112,128]{3,2,0,1:T(8,128)(2,1)S(1)}, u32[]{:S(2)}, u32[]{:S(2)}) collective-permute-start(bf16[4,2,112,128]{3,2,0,1:T(8,128)(2,1)S(1)} %fusion), channel_id=1, source_target_pairs={{0,2},{1,3},{2,0},{3,1},{4,6},{5,7},{6,4},{7,5},{8,10},{9,11},{10,... | collective-permute-start | bytes 688136 | tf_op jit(solution)/shard_map/ppermute | solution.py:51
  128.0 12.3 %collective-permute-start.19 = (bf16[2,64,1024]{2,1,0:T(8,128)(2,1)S(1)}, bf16[2,64,1024]{2,1,0:T(8,128)(2,1)S(1)}, u32[]{:S(2)}, u32[]{:S(2)}) collective-permute-start(bf16[2,64,1024]{2,1,0:T(8,128)(2,1)S(1)} %copy-done.11), channel_id=1, source_target_pairs={{16,0},{24,8},{17,1},{25,9},{18,2},{26,10},{19,3},{27,11},{20,4},{... | collective-permute-start | bytes 786440 | tf_op jit(solution)/shard_map/ppermute | solution.py:46
  133.1 11.2 %copy-start.6 = (bf16[4096,128]{1,0:T(8,128)(2,1)S(1)}, bf16[4096,128]{1,0:T(8,128)(2,1)}, u32[]{:S(2)}) copy-start(bf16[4096,128]{1,0:T(8,128)(2,1)} %copy-done.5) | copy-start | bytes 3145732
  133.1 4.7 %collective-permute-start.22 = (bf16[4,96,128]{2,1,0:T(8,128)(2,1)S(1)}, bf16[4,96,128]{2,1,0:T(8,128)(2,1)S(1)}, u32[]{:S(2)}, u32[]{:S(2)}) collective-permute-start(bf16[4,96,128]{2,1,0:T(8,128)(2,1)S(1)} %fusion.14), channel_id=1, source_target_pairs={{0,2},{1,3},{2,0},{3,1},{4,6},{5,7},{6,4},{7,5},{8,10},{9,11},{10,... | collective-permute-start | bytes 294920 | tf_op jit(solution)/shard_map/ppermute | solution.py:51
  134.2 4.9 %collective-permute-start.24 = (bf16[4,112,128]{2,1,0:T(8,128)(2,1)S(1)}, bf16[4,112,128]{2,1,0:T(8,128)(2,1)S(1)}, u32[]{:S(2)}, u32[]{:S(2)}) collective-permute-start(bf16[4,112,128]{2,1,0:T(8,128)(2,1)S(1)} %fusion.9), channel_id=1, source_target_pairs={{0,4},{4,0},{1,5},{5,1},{2,6},{6,2},{3,7},{7,3},{8,12},{12,8},{9,1... | collective-permute-start | bytes 344072 | tf_op jit(solution)/shard_map/ppermute | solution.py:51
  140.4 6.5 %collective-permute-start.25 = (bf16[208,128]{1,0:T(8,128)(2,1)S(1)}, bf16[208,128]{1,0:T(8,128)(2,1)S(1)}, u32[]{:S(2)}, u32[]{:S(2)}) collective-permute-start(bf16[208,128]{1,0:T(8,128)(2,1)S(1)} %get-tuple-element.74), channel_id=1, source_target_pairs={{0,8},{8,16},{16,24},{24,0},{1,9},{9,17},{17,25},{25,1},{2,10},{10... | collective-permute-start | bytes 159752 | tf_op jit(solution)/shard_map/ppermute | solution.py:41
  140.5 7.7 %collective-permute-start.26 = (bf16[208,128]{1,0:T(8,128)(2,1)S(1)}, bf16[208,128]{1,0:T(8,128)(2,1)S(1)}, u32[]{:S(2)}, u32[]{:S(2)}) collective-permute-start(bf16[208,128]{1,0:T(8,128)(2,1)S(1)} %get-tuple-element.76), channel_id=1, source_target_pairs={{0,16},{8,24},{16,0},{24,8},{1,17},{9,25},{17,1},{25,9},{2,18},{10... | collective-permute-start | bytes 159752 | tf_op jit(solution)/shard_map/ppermute | solution.py:41
  140.5 7.6 %collective-permute-start.27 = (bf16[208,128]{1,0:T(8,128)(2,1)S(1)}, bf16[208,128]{1,0:T(8,128)(2,1)S(1)}, u32[]{:S(2)}, u32[]{:S(2)}) collective-permute-start(bf16[208,128]{1,0:T(8,128)(2,1)S(1)} %get-tuple-element.75), channel_id=1, source_target_pairs={{0,24},{8,0},{16,8},{24,16},{1,25},{9,1},{17,9},{25,17},{2,26},{10... | collective-permute-start | bytes 159752 | tf_op jit(solution)/shard_map/ppermute | solution.py:41
  146.4 3.8 %copy-start.26 = (bf16[2,64,1024]{2,1,0:T(8,128)(2,1)S(1)}, bf16[2,64,1024]{2,1,0:T(8,128)(2,1)}, u32[]{:S(2)}) copy-start(bf16[2,64,1024]{2,1,0:T(8,128)(2,1)} %copy-done.25) | copy-start | bytes 786436
  148.2 3.7 %collective-permute-start.28 = (bf16[208,128]{1,0:T(8,128)(2,1)S(1)}, bf16[208,128]{1,0:T(8,128)(2,1)S(1)}, u32[]{:S(2)}, u32[]{:S(2)}) collective-permute-start(bf16[208,128]{1,0:T(8,128)(2,1)S(1)} %fusion.12), channel_id=1, source_target_pairs={{0,3},{1,2},{2,1},{3,0},{4,7},{5,6},{6,5},{7,4},{8,11},{9,10},{10,... | collective-permute-start | bytes 159752 | tf_op jit(solution)/shard_map/ppermute | solution.py:51
  148.3 4.8 %collective-permute-start.29 = (bf16[208,128]{1,0:T(8,128)(2,1)S(1)}, bf16[208,128]{1,0:T(8,128)(2,1)S(1)}, u32[]{:S(2)}, u32[]{:S(2)}) collective-permute-start(bf16[208,128]{1,0:T(8,128)(2,1)S(1)} %fusion.12), channel_id=1, source_target_pairs={{0,2},{1,3},{2,0},{3,1},{4,6},{5,7},{6,4},{7,5},{8,10},{9,11},{10,... | collective-permute-start | bytes 159752 | tf_op jit(solution)/shard_map/ppermute | solution.py:51
  149.3 3.7 %collective-permute-start.30 = (bf16[208,128]{1,0:T(8,128)(2,1)S(1)}, bf16[208,128]{1,0:T(8,128)(2,1)S(1)}, u32[]{:S(2)}, u32[]{:S(2)}) collective-permute-start(bf16[208,128]{1,0:T(8,128)(2,1)S(1)} %fusion.12), channel_id=1, source_target_pairs={{0,1},{1,0},{2,3},{3,2},{4,5},{5,4},{6,7},{7,6},{8,9},{9,8},{10,11... | collective-permute-start | bytes 159752 | tf_op jit(solution)/shard_map/ppermute | solution.py:51

commit v9 on v6

--- a/solution.py
+++ b/solution.py
@@ -247,8 +247,9 @@
 
 
 def low_rank_kernel(
-    sp, fs, rp, index_ref, own_ref, other_ref, hidden_ref, down_out, up_ref, low_ref, down_ref, sem
+    sp, fs, rp, index_ref, own_ref, other_ref, hidden_ref, *refs
 ):
+    down_out, up_ref, low_ref, down_ref, sem = refs[-5:]
     z, x, r = index_ref[0], index_ref[1], index_ref[2]
     shards = sp * fs
     down_rows, up_rows = D // (shards * rp), RANK // rp
@@ -310,7 +311,7 @@
     return buf[:, :rows], past
 
 
-def adapters_packed(hidden, buf, before_rep, before_swap):
+def adapters_packed(hidden, buf, before_rep, before_swap, staged):
     sp, fs, rp = (lax.axis_size(a) for a in ("sp", "fsdp", "rep"))
     z, x, r = (lax.axis_index(a) for a in ("sp", "fsdp", "rep"))
     step = 1
@@ -328,7 +329,9 @@
     seqs, tokens = hidden.shape[:2]
     down_full, up_blocks, low = pl.pallas_call(
         functools.partial(low_rank_kernel, sp, fs, rp),
-        in_specs=[pl.BlockSpec(memory_space=pltpu.SMEM)] + [vmem] * 3,
+        in_specs=[pl.BlockSpec(memory_space=pltpu.SMEM)]
+        + [vmem] * 3
+        + [pl.BlockSpec(memory_space=pl.ANY)] * len(staged),
         out_specs=[pl.BlockSpec(memory_space=pltpu.HBM), vmem, vmem],
         scratch_shapes=[pltpu.VMEM((D, 2 * RANK), bf16), pltpu.SemaphoreType.DMA],
         out_shape=[
@@ -341,7 +344,7 @@
             flops=2 * seqs * tokens * D * 2 * RANK, bytes_accessed=2**16, transcendentals=0
         ),
         name="low_rank",
-    )(index, buf, other, hidden)
+    )(index, buf, other, hidden, *staged)
     return down_full, up_blocks, low
 
 
@@ -441,7 +444,13 @@
     sp, fs, rp = (lax.axis_size(a) for a in ("sp", "fsdp", "rep"))
     z, r = lax.axis_index("sp"), lax.axis_index("rep")
     shards, _, rows, lanes = send.shape
-    got = partner(tie(send, values[0]), "rep", 1)
+    part, hops = values[-1], []
+    for k in range(sp - 1, 1, -1):
+        if hops:
+            part = (values[k].astype(f32) + hops[-1].astype(f32)).astype(bf16)
+        hops.append(along(part, "sp", -1, k))
+    got = partner(tie(send, *hops[:1]), "rep", 1)
+    marks = []
     fs_bits, rep_bits = fs.bit_length() - 1, rp.bit_length() - 2
     labels = [("fsdp", b) for b in reversed(range(fs_bits))]
     labels += [("rep", b + 1) for b in reversed(range(rep_bits))]
@@ -461,9 +470,11 @@
                 return sum(a.astype(f32) for a in parts).astype(bf16)
 
             send = pick(1 - mine)
+            if step == 1:
+                send = tie(send, *hops[1:])
+            terms = [pick(mine), partner(send, axis, 1 << bit)]
             if step == 0:
-                send = tie(send, *values[2:])
-            terms = [pick(mine), partner(send, axis, 1 << bit)]
+                marks.append(terms[1])
         return sum(a.astype(f32) for a in terms).astype(bf16)
 
     cut = rows // 32 * 16
@@ -472,7 +483,12 @@
     if cut:
         other = halve([a[..., :cut, :] for a in terms], first_fsdp)
         over_sp = jnp.concatenate([other, over_sp], axis=1)
-    over_sp = tie(over_sp, *values)
+    part = values[1]
+    if hops:
+        part = (part.astype(f32) + tie(hops[-1], *marks).astype(f32)).astype(bf16)
+    last = along(part, "sp", -1, 1)
+    grad_value = (values[0].astype(f32) + last.astype(f32)).astype(bf16)
+    over_sp = tie(over_sp, last)
     total = lax.dynamic_index_in_dim(over_sp, z, 0, keepdims=False).astype(f32)
     for k in range(1, sp):
         send = lax.dynamic_index_in_dim(over_sp, lax.rem(z + k, sp), 0, keepdims=False)
@@ -496,7 +512,7 @@
             up = [up[lo : lo + up_rows] for lo in range(0, up.shape[0], up_rows)]
             up = jnp.concatenate(up, axis=1)
         ups.append(up.reshape(up_rows, up_width))
-    return grad_down, jnp.concatenate(ups, axis=0), grad_hidden
+    return grad_down, jnp.concatenate(ups, axis=0), grad_hidden, grad_value
 
 
 def body(
@@ -527,7 +543,9 @@
     for k in range(2, sp):
         kvs.append(along(kvs[k - 1], "sp", 1, k - 1))
     if even:
-        down_full, up_blocks, low_own = adapters_packed(hidden, buf, kvs[1], kvs[min(2, sp - 1)])
+        down_full, up_blocks, low_own = adapters_packed(
+            hidden, buf, kvs[1], kvs[min(2, sp - 1)], (query_base, grad_out, *kvs[:3])
+        )
     else:
         down_full, up_blocks, low_own = adapters_plain(hidden, adapter_down, adapter_up)
     lows = [low_own] + [along(low_own, "sp", k) for k in range(1, sp)]
@@ -536,7 +554,7 @@
 
     made = attention(place, query_base, grad_out, up_blocks, past, cos, sin, lows, kvs)
     attended, grad_query, guq, guv, low_grad_q, low_grad_v = made[:6]
-    value_own, value_got = made[6], [along(made[6 + k], "sp", -k) for k in range(1, sp)]
+    values = made[6:]
 
     low_v_total = low_grad_v[:, :tokens]
     for k in range(1, sp):
@@ -548,16 +566,13 @@
         .reshape(seqs * tokens, 2 * RANK)
     )
     send, keep = packed_grads(hidden, low_grad, guq, guv, sp * fs)
-    grad_down, grad_up, grad_hidden = finish_grads(
-        send, keep, value_got, low_grad, lambda x: grad_hidden_of(x, down_full, seqs, tokens)
+    grad_down, grad_up, grad_hidden, grad_value = finish_grads(
+        send, keep, values, low_grad, lambda x: grad_hidden_of(x, down_full, seqs, tokens)
     )
-    grad_value = value_own.astype(f32)
-    for part in value_got:
-        grad_value = grad_value + part.astype(f32)
     return (
         attended,
         grad_query,
-        grad_value.astype(bf16),
+        grad_value,
         grad_hidden,
         grad_down,
         grad_up,

time: 146 us -> 151 us (1.034)
  local copies, waits for them, and re-layouts: 10.2 us -> 19.8 us
  waiting for transfers between devices: 59.3 us -> 52.2 us
  starting transfers between devices: 47.7 us -> 49.5 us
    unnamed x62 -> x92, local copies, waits for them, and re-layouts: 9.64 us -> 19.2 us
    ppermute x12, waiting for transfers between devices: 23.4 us -> 18.7 us  [along(): lax.ppermute(x, axis, [(i, i + shift) for i in range(start, n) if 0 <= i...]
    ppermute x13, waiting for transfers between devices: 35.4 us -> 33.4 us  [partner(): return lax.ppermute(x, axis, [(i, i ^ mask) for i in range(n)])]
    ppermute x3, starting transfers between devices: 3.86 us -> 5.56 us  [cyclic(): return lax.ppermute(x, axis, [(i, (i + shift) % n) for i in range(n)])]
  transfers between devices with their start and end apart: 28 -> 28, of which waited for: 20 -> 16; matrix products, arithmetic and copies ran while one was open for 2% -> 2% of each run, Pallas kernels for 3% -> 3%
where the time goes in v9:
time: 151 us; the launch traced here: 150 us
  waiting for transfers between devices  52.2 us (35%)
  starting transfers between devices  49.5 us (33%)
  Pallas kernels  22.2 us (15%)
  local copies, waits for them, and re-layouts  19.8 us (13%)
  other arithmetic  4.82 us (3%)
    ppermute x13, waiting for transfers between devices, partner(): return lax.ppermute(x, axis, [(i, i ^ mask) for i in range(n)])  33.4 us
    ppermute x12, starting transfers between devices, along(): lax.ppermute(x, axis, [(i, i + shift) for i in range(start, n) if 0 <= i...  29.5 us
    unnamed x92, local copies, waits for them, and re-layouts  19.2 us
    ppermute x12, waiting for transfers between devices, along(): lax.ppermute(x, axis, [(i, i + shift) for i in range(start, n) if 0 <= i...  18.7 us
    pallas_call x1, Pallas kernels, attention(): pl.pallas_call(functools.partial(attention_kernel, shards), grid=(KV_HEAD...  17.3 us
    ppermute x13, starting transfers between devices, partner(): return lax.ppermute(x, axis, [(i, i ^ mask) for i in range(n)])  14.5 us
    ppermute x3, starting transfers between devices, cyclic(): return lax.ppermute(x, axis, [(i, (i + shift) % n) for i in range(n)])  5.56 us
  transfers between devices with their start and end apart: 28, of which 16 were waited for; matrix products, arithmetic and copies ran while one was open for 2% of the time, Pallas kernels for 3%

profile of v9, /device:TPU:0, one launch (start us, length us, event | category | flops | bytes accessed | tf_op | source)
XLA Modules:
  0.0 149.9 jit_solution(14807002991156219813)
XLA Ops:
  0.6 0.8 pad_maximum_fusion.7
  1.6 0.9 copy-done.13
  2.5 3.1 %collective-permute-start = (bf16[1,336,128]{2,1,0:T(8,128)(2,1)S(1)}, bf16[1,336,128]{2,1,0:T(8,128)(2,1)S(1)}, u32[]{:S(2)}, u32[]{:S(2)}) collective-permute-start(bf16[1,336,128]{2,1,0:T(8,128)(2,1)S(1)} %pack.1), channel_id=1, source_target_pairs={{0,8},{8,0},{16,24},{24,16},{1,9},{9,1},{17,25},{25,17},{2,10},{10... | collective-permute-start | bytes 258056 | tf_op jit(solution)/shard_map/ppermute | solution.py:51
  5.6 2.5 %collective-permute-done = bf16[1,336,128]{2,1,0:T(8,128)(2,1)S(1)} collective-permute-done((bf16[1,336,128]{2,1,0:T(8,128)(2,1)S(1)}, bf16[1,336,128]{2,1,0:T(8,128)(2,1)S(1)}, u32[]{:S(2)}, u32[]{:S(2)}) %collective-permute-start) | collective-permute-done | bytes 86048 | tf_op jit(solution)/shard_map/ppermute | solution.py:51
  8.1 3.0 %collective-permute-start.1 = (bf16[2,336,128]{2,1,0:T(8,128)(2,1)S(1)}, bf16[2,336,128]{2,1,0:T(8,128)(2,1)S(1)}, u32[]{:S(2)}, u32[]{:S(2)}) collective-permute-start(bf16[2,336,128]{2,1,0:T(8,128)(2,1)S(1)} %pad_maximum_fusion.4), channel_id=1, source_target_pairs={{0,16},{8,24},{16,0},{24,8},{1,17},{9,25},{17,1},{25,9},{2,18},{10... | collective-permute-start | bytes 516104 | tf_op jit(solution)/shard_map/ppermute | solution.py:51
  11.2 7.1 %collective-permute-done.1 = bf16[2,336,128]{2,1,0:T(8,128)(2,1)S(1)} collective-permute-done((bf16[2,336,128]{2,1,0:T(8,128)(2,1)S(1)}, bf16[2,336,128]{2,1,0:T(8,128)(2,1)S(1)}, u32[]{:S(2)}, u32[]{:S(2)}) %collective-permute-start.1) | collective-permute-done | bytes 172064 | tf_op jit(solution)/shard_map/ppermute | solution.py:51
  18.4 0.6 copy-done.31
  19.0 2.4 %collective-permute-start.3 = (bf16[2,64,2048]{2,1,0:T(8,128)(2,1)S(1)}, bf16[2,64,2048]{2,1,0:T(8,128)(2,1)S(1)}, u32[]{:S(2)}, u32[]{:S(2)}) collective-permute-start(bf16[2,64,2048]{2,1,0:T(8,128)(2,1)S(1)} %constant_dynamic-update-slice_fusion.refs_2_.refs_12_.refs_16_), channel_id=1, source_target_pairs={{0,8},{8,16},{16,24},{1,9},{9,17},{17,25},{2,10},{10,18},{18,26},{... | collective-permute-start | bytes 1572872 | tf_op jit(solution)/shard_map/ppermute | solution.py:46
  21.4 1.6 %collective-permute-start.2 = (bf16[4,208,128]{2,1,0:T(8,128)(2,1)S(1)}, bf16[4,208,128]{2,1,0:T(8,128)(2,1)S(1)}, u32[]{:S(2)}, u32[]{:S(2)}) collective-permute-start(bf16[4,208,128]{2,1,0:T(8,128)(2,1)S(1)} %slice.163), channel_id=1, source_target_pairs={{0,4},{4,0},{1,5},{5,1},{2,6},{6,2},{3,7},{7,3},{8,12},{12,8},{9,1... | collective-permute-start | bytes 638984 | tf_op jit(solution)/shard_map/ppermute | solution.py:51
  23.0 5.0 %collective-permute-done.2 = bf16[4,208,128]{2,1,0:T(8,128)(2,1)S(1)} collective-permute-done((bf16[4,208,128]{2,1,0:T(8,128)(2,1)S(1)}, bf16[4,208,128]{2,1,0:T(8,128)(2,1)S(1)}, u32[]{:S(2)}, u32[]{:S(2)}) %collective-permute-start.2) | collective-permute-done | bytes 213024 | tf_op jit(solution)/shard_map/ppermute | solution.py:51
  28.0 4.3 %collective-permute-done.3.refs_3_.refs_13_.refs_17_ = bf16[2,64,2048]{2,1,0:T(8,128)(2,1)S(1)} collective-permute-done((bf16[2,64,2048]{2,1,0:T(8,128)(2,1)S(1)}, bf16[2,64,2048]{2,1,0:T(8,128)(2,1)S(1)}, u32[]{:S(2)}, u32[]{:S(2)}) %collective-permute-start.3) | collective-permute-done | bytes 524320 | tf_op jit(solution)/shard_map/ppermute | solution.py:46
  32.3 1.5 %collective-permute-start.4 = (bf16[8,208,128]{2,1,0:T(8,128)(2,1)S(1)}, bf16[8,208,128]{2,1,0:T(8,128)(2,1)S(1)}, u32[]{:S(2)}, u32[]{:S(2)}) collective-permute-start(bf16[8,208,128]{2,1,0:T(8,128)(2,1)S(1)} %pad_maximum_fusion), channel_id=1, source_target_pairs={{0,2},{1,3},{2,0},{3,1},{4,6},{5,7},{6,4},{7,5},{8,10},{9,11},{10,... | collective-permute-start | bytes 1277960 | tf_op jit(solution)/shard_map/ppermute | solution.py:51
  33.9 1.5 collective-permute-start.5
  35.4 7.4 %collective-permute-done.4 = bf16[8,208,128]{2,1,0:T(8,128)(2,1)S(1)} collective-permute-done((bf16[8,208,128]{2,1,0:T(8,128)(2,1)S(1)}, bf16[8,208,128]{2,1,0:T(8,128)(2,1)S(1)}, u32[]{:S(2)}, u32[]{:S(2)}) %collective-permute-start.4) | collective-permute-done | bytes 426016 | tf_op jit(solution)/shard_map/ppermute | solution.py:51
  43.0 1.5 collective-permute-start.10
  44.7 0.7 pad_maximum_fusion.8
  45.4 1.2 copy-done.1
  46.6 1.2 copy-done.3
  47.9 1.0 copy-done.6
  48.9 1.2 low_rank.1
  50.1 1.0 copy-done.15
  51.1 0.8 copy-done.17
  51.9 8.5 %collective-permute-start.7 = (bf16[2,64,128]{2,1,0:T(8,128)(2,1)S(1)}, bf16[2,64,128]{2,1,0:T(8,128)(2,1)S(1)}, u32[]{:S(2)}, u32[]{:S(2)}) collective-permute-start(bf16[2,64,128]{2,1,0:T(8,128)(2,1)S(1)} %get-tuple-element.35.refs_8_), channel_id=1, source_target_pairs={{0,8},{8,16},{16,24},{1,9},{9,17},{17,25},{2,10},{10,18},{18,26},{... | collective-permute-start | bytes 98312 | tf_op jit(solution)/shard_map/ppermute | solution.py:46
  60.5 7.7 %collective-permute-start.8 = (bf16[2,64,128]{2,1,0:T(8,128)(2,1)S(1)}, bf16[2,64,128]{2,1,0:T(8,128)(2,1)S(1)}, u32[]{:S(2)}, u32[]{:S(2)}) collective-permute-start(bf16[2,64,128]{2,1,0:T(8,128)(2,1)S(1)} %get-tuple-element.35.refs_8_), channel_id=1, source_target_pairs={{0,16},{8,24},{1,17},{9,25},{2,18},{10,26},{3,19},{11,27},{4,20},{... | collective-permute-start | bytes 98312 | tf_op jit(solution)/shard_map/ppermute | solution.py:46
  68.1 1.3 collective-permute-start.9
  70.3 0.6 copy-done.25
  71.6 1.2 copy-done.2
  72.9 1.2 copy-done.4
  74.1 0.8 copy-done.14
  74.9 1.1 copy-done.18
  75.9 0.8 copy-done.22
  76.7 0.8 copy-done.24
  77.5 0.8 copy-done.26
  78.2 0.8 copy-done.28
  79.0 17.3 %attention.1 = (bf16[2,64,4096]{2,1,0:T(8,128)(2,1)}, bf16[2,64,4096]{2,1,0:T(8,128)(2,1)}, bf16[32,4,16,128]{3,2,1,0:T(8,128)(2,1)S(1)}, bf16[8,4,16,128]{3,2,1...) custom-call(s32[1]{0:T(128)} %bitcast.place_ref, ...), custom_call_target="tpu_custom_call" | custom-call | flops 17112760320 | bytes 65536 | tf_op jit(solution)/shard_map/attention/pallas_call | solution.py:212
  96.3 0.7 copy-done.19
  97.0 0.7 copy-done.8
  97.8 1.3 collective-permute-start.13
  99.0 1.3 collective-permute-start.14
  100.3 1.3 collective-permute-start.15
  101.7 0.7 collective-permute-start.11
  102.3 1.2 collective-permute-done.13
  103.5 2.2 %collective-permute-done.14 = bf16[2,64,64]{2,1,0:T(8,128)(2,1)S(1)} collective-permute-done((bf16[2,64,64]{2,1,0:T(8,128)(2,1)S(1)}, bf16[2,64,64]{2,1,0:T(8,128)(2,1)S(1)}, u32[]{:S(2)}, u32[]{:S(2)}) %collective-permute-start.14) | collective-permute-done | bytes 16416 | tf_op jit(solution)/shard_map/ppermute | solution.py:46
  105.7 3.7 %collective-permute-done.15 = bf16[2,64,64]{2,1,0:T(8,128)(2,1)S(1)} collective-permute-done((bf16[2,64,64]{2,1,0:T(8,128)(2,1)S(1)}, bf16[2,64,64]{2,1,0:T(8,128)(2,1)S(1)}, u32[]{:S(2)}, u32[]{:S(2)}) %collective-permute-start.15) | collective-permute-done | bytes 16416 | tf_op jit(solution)/shard_map/ppermute | solution.py:46
  109.6 1.6 %adapter_grads.1 = (bf16[8,2,208,128]{3,2,1,0:T(8,128)(2,1)}, bf16[8,2,208,128]{3,2,1,0:T(8,128)(2,1)S(1)}) custom-call(s32[1]{0:T(128)} %bitcast.4.core_ref, bf16[2,64,4096]{2,1,0:T(8,128)(2,1)S(1)} %copy-done, bf16[128,128]{1,0:T(8,128)(2,1)S(1)} %pad_maximum_fusion.10.low_ref, bf16[32,4,16,128]{3,2,1,0:T(8,128)(2,1)S(1)} %get-tuple-element.44.guq_ref, ...), custom_call_target="tpu_custom_call" | custom-call | flops 134217728 | bytes 5242880 | tf_op jit(solution)/shard_map/adapter_grads/pallas_call | solution.py:419
  111.3 0.6 copy-done.33
  112.1 0.9 copy-done.11
  113.1 0.7 collective-permute-start.12
  114.0 1.6 %collective-permute-start.18 = (bf16[4,2,96,128]{3,2,0,1:T(8,128)(2,1)S(1)}, bf16[4,2,96,128]{3,2,0,1:T(8,128)(2,1)S(1)}, u32[]{:S(2)}, u32[]{:S(2)}) collective-permute-start(bf16[4,2,96,128]{3,2,0,1:T(8,128)(2,1)S(1)} %fusion.4), channel_id=1, source_target_pairs={{0,4},{4,0},{1,5},{5,1},{2,6},{6,2},{3,7},{7,3},{8,12},{12,8},{9,1... | collective-permute-start | bytes 589832 | tf_op jit(solution)/shard_map/ppermute | solution.py:51
  116.4 4.6 %collective-permute-done.18 = bf16[4,2,96,128]{3,2,0,1:T(8,128)(2,1)S(1)} collective-permute-done((bf16[4,2,96,128]{3,2,0,1:T(8,128)(2,1)S(1)}, bf16[4,2,96,128]{3,2,0,1:T(8,128)(2,1)S(1)}, u32[]{:S(2)}, u32[]{:S(2)}) %collective-permute-start.18) | collective-permute-done | bytes 196640 | tf_op jit(solution)/shard_map/ppermute | solution.py:51
  121.6 1.5 %collective-permute-done.17 = bf16[4,2,112,128]{3,2,0,1:T(8,128)(2,1)S(1)} collective-permute-done((bf16[4,2,112,128]{3,2,0,1:T(8,128)(2,1)S(1)}, bf16[4,2,112,128]{3,2,0,1:T(8,128)(2,1)S(1)}, u32[]{:S(2)}, u32[]{:S(2)}) %collective-permute-start.17) | collective-permute-done | bytes 229408 | tf_op jit(solution)/shard_map/ppermute | solution.py:51
  123.8 1.4 collective-permute-start.19
  125.7 2.3 %collective-permute-done.21 = bf16[4,112,128]{2,1,0:T(8,128)(2,1)S(1)} collective-permute-done((bf16[4,112,128]{2,1,0:T(8,128)(2,1)S(1)}, bf16[4,112,128]{2,1,0:T(8,128)(2,1)S(1)}, u32[]{:S(2)}, u32[]{:S(2)}) %collective-permute-start.21) | collective-permute-done | bytes 114720 | tf_op jit(solution)/shard_map/ppermute | solution.py:51
  128.1 7.2 %collective-permute-done.19 = bf16[2,64,1024]{2,1,0:T(8,128)(2,1)S(1)} collective-permute-done((bf16[2,64,1024]{2,1,0:T(8,128)(2,1)S(1)}, bf16[2,64,1024]{2,1,0:T(8,128)(2,1)S(1)}, u32[]{:S(2)}, u32[]{:S(2)}) %collective-permute-start.19) | collective-permute-done | bytes 262176 | tf_op jit(solution)/shard_map/ppermute | solution.py:46
  135.3 1.8 %collective-permute-start.22 = (bf16[208,128]{1,0:T(8,128)(2,1)S(1)}, bf16[208,128]{1,0:T(8,128)(2,1)S(1)}, u32[]{:S(2)}, u32[]{:S(2)}) collective-permute-start(bf16[208,128]{1,0:T(8,128)(2,1)S(1)} %get-tuple-element.68), channel_id=1, source_target_pairs={{0,8},{8,16},{16,24},{24,0},{1,9},{9,17},{17,25},{25,1},{2,10},{10... | collective-permute-start | bytes 159752 | tf_op jit(solution)/shard_map/ppermute | solution.py:41
  137.0 0.9 collective-permute-start.23
  138.0 2.8 %collective-permute-start.24 = (bf16[208,128]{1,0:T(8,128)(2,1)S(1)}, bf16[208,128]{1,0:T(8,128)(2,1)S(1)}, u32[]{:S(2)}, u32[]{:S(2)}) collective-permute-start(bf16[208,128]{1,0:T(8,128)(2,1)S(1)} %get-tuple-element.69), channel_id=1, source_target_pairs={{0,24},{8,0},{16,8},{24,16},{1,25},{9,1},{17,9},{25,17},{2,26},{10... | collective-permute-start | bytes 159752 | tf_op jit(solution)/shard_map/ppermute | solution.py:41
  140.8 2.1 %grad_hidden.1 = bf16[2,64,4096]{2,1,0:T(8,128)(2,1)} custom-call(bf16[128,128]{1,0:T(8,128)(2,1)S(1)} %pad_maximum_fusion.10.low_ref, bf16[4096,128]{1,0:T(8,128)(2,1)S(1)} %copy-done.16), custom_call_target="tpu_custom_call" | custom-call | flops 1073741824 | bytes 65536 | tf_op jit(solution)/shard_map/grad_hidden/pallas_call | solution.py:370
  143.1 1.6 %collective-permute-start.26 = (bf16[208,128]{1,0:T(8,128)(2,1)S(1)}, bf16[208,128]{1,0:T(8,128)(2,1)S(1)}, u32[]{:S(2)}, u32[]{:S(2)}) collective-permute-start(bf16[208,128]{1,0:T(8,128)(2,1)S(1)} %fusion.12), channel_id=1, source_target_pairs={{0,2},{1,3},{2,0},{3,1},{4,6},{5,7},{6,4},{7,5},{8,10},{9,11},{10,... | collective-permute-start | bytes 159752 | tf_op jit(solution)/shard_map/ppermute | solution.py:51
  144.9 0.8 add_convert_fusion
  145.7 1.4 collective-permute-done.25
  147.1 1.1 collective-permute-done.26
  148.5 0.7 pad_maximum_fusion.5
  149.2 0.7 pad_maximum_fusion.2
  (144 shorter events, 6.2 us)
Async XLA Ops:
  0.6 0.9 copy-start.12
  1.6 0.9 copy-start.13
  2.5 8.7 %copy-start.35 = (bf16[2,64,1024]{2,1,0:T(8,128)(2,1)S(1)}, bf16[2,64,1024]{2,1,0:T(8,128)(2,1)}, u32[]{:S(2)}) copy-start(bf16[2,64,1024]{2,1,0:T(8,128)(2,1)} %param.11) | copy-start | bytes 786436
  2.5 5.6 %collective-permute-start = (bf16[1,336,128]{2,1,0:T(8,128)(2,1)S(1)}, bf16[1,336,128]{2,1,0:T(8,128)(2,1)S(1)}, u32[]{:S(2)}, u32[]{:S(2)}) collective-permute-start(bf16[1,336,128]{2,1,0:T(8,128)(2,1)S(1)} %pack.1), channel_id=1, source_target_pairs={{0,8},{8,0},{16,24},{24,16},{1,9},{9,1},{17,25},{25,17},{2,10},{10... | collective-permute-start | bytes 258056 | tf_op jit(solution)/shard_map/ppermute | solution.py:51
  8.1 10.2 %copy-start.29 = (bf16[1,336,128]{2,1,0:T(8,128)(2,1)}, bf16[1,336,128]{2,1,0:T(8,128)(2,1)S(1)}, u32[]{:S(2)}) copy-start(bf16[1,336,128]{2,1,0:T(8,128)(2,1)S(1)} %collective-permute-done) | copy-start | bytes 258052
  8.1 3.1 %copy-start.36 = (bf16[2,64,1024]{2,1,0:T(8,128)(2,1)S(1)}, bf16[2,64,1024]{2,1,0:T(8,128)(2,1)}, u32[]{:S(2)}) copy-start(bf16[2,64,1024]{2,1,0:T(8,128)(2,1)} %param.12) | copy-start | bytes 786436
  8.1 10.2 %collective-permute-start.1 = (bf16[2,336,128]{2,1,0:T(8,128)(2,1)S(1)}, bf16[2,336,128]{2,1,0:T(8,128)(2,1)S(1)}, u32[]{:S(2)}, u32[]{:S(2)}) collective-permute-start(bf16[2,336,128]{2,1,0:T(8,128)(2,1)S(1)} %pad_maximum_fusion.4), channel_id=1, source_target_pairs={{0,16},{8,24},{16,0},{24,8},{1,17},{9,25},{17,1},{25,9},{2,18},{10... | collective-permute-start | bytes 516104 | tf_op jit(solution)/shard_map/ppermute | solution.py:51
  18.3 0.7 copy-start.31
  19.0 13.3 %collective-permute-start.3 = (bf16[2,64,2048]{2,1,0:T(8,128)(2,1)S(1)}, bf16[2,64,2048]{2,1,0:T(8,128)(2,1)S(1)}, u32[]{:S(2)}, u32[]{:S(2)}) collective-permute-start(bf16[2,64,2048]{2,1,0:T(8,128)(2,1)S(1)} %constant_dynamic-update-slice_fusion.refs_2_.refs_12_.refs_16_), channel_id=1, source_target_pairs={{0,8},{8,16},{16,24},{1,9},{9,17},{17,25},{2,10},{10,18},{18,26},{... | collective-permute-start | bytes 1572872 | tf_op jit(solution)/shard_map/ppermute | solution.py:46
  21.4 6.5 %collective-permute-start.2 = (bf16[4,208,128]{2,1,0:T(8,128)(2,1)S(1)}, bf16[4,208,128]{2,1,0:T(8,128)(2,1)S(1)}, u32[]{:S(2)}, u32[]{:S(2)}) collective-permute-start(bf16[4,208,128]{2,1,0:T(8,128)(2,1)S(1)} %slice.163), channel_id=1, source_target_pairs={{0,4},{4,0},{1,5},{5,1},{2,6},{6,2},{3,7},{7,3},{8,12},{12,8},{9,1... | collective-permute-start | bytes 638984 | tf_op jit(solution)/shard_map/ppermute | solution.py:51
  28.0 17.4 %copy-start = (bf16[2,64,4096]{2,1,0:T(8,128)(2,1)S(1)}, bf16[2,64,4096]{2,1,0:T(8,128)(2,1)}, u32[]{:S(2)}) copy-start(bf16[2,64,4096]{2,1,0:T(8,128)(2,1)} %hidden_ref.3) | copy-start | bytes 3145732
  32.3 10.5 %copy-start.5 = (bf16[2,64,2048]{2,1,0:T(8,128)(2,1)}, bf16[2,64,2048]{2,1,0:T(8,128)(2,1)S(1)}, u32[]{:S(2)}) copy-start(bf16[2,64,2048]{2,1,0:T(8,128)(2,1)S(1)} %collective-permute-done.3.refs_3_.refs_13_.refs_17_) | copy-start | bytes 1572868
  32.3 10.4 %collective-permute-start.4 = (bf16[8,208,128]{2,1,0:T(8,128)(2,1)S(1)}, bf16[8,208,128]{2,1,0:T(8,128)(2,1)S(1)}, u32[]{:S(2)}, u32[]{:S(2)}) collective-permute-start(bf16[8,208,128]{2,1,0:T(8,128)(2,1)S(1)} %pad_maximum_fusion), channel_id=1, source_target_pairs={{0,2},{1,3},{2,0},{3,1},{4,6},{5,7},{6,4},{7,5},{8,10},{9,11},{10,... | collective-permute-start | bytes 1277960 | tf_op jit(solution)/shard_map/ppermute | solution.py:51
  33.9 9.0 %collective-permute-start.5 = (bf16[2,64,2048]{2,1,0:T(8,128)(2,1)S(1)}, bf16[2,64,2048]{2,1,0:T(8,128)(2,1)}, u32[]{:S(2)}, u32[]{:S(2)}) collective-permute-start(bf16[2,64,2048]{2,1,0:T(8,128)(2,1)S(1)} %collective-permute-done.3.refs_3_.refs_13_.refs_17_), channel_id=1, source_target_pairs={{8,16},{16,24},{9,17},{17,25},{10,18},{18,26},{11,19},{19,27},{12,... | collective-permute-start | bytes 1572872 | tf_op jit(solution)/shard_map/ppermute | solution.py:46
  42.8 2.6 %collective-permute-start.6 = (bf16[16,208,128]{2,1,0:T(8,128)(2,1)S(1)}, bf16[16,208,128]{2,1,0:T(8,128)(2,1)S(1)}, u32[]{:S(2)}, u32[]{:S(2)}) collective-permute-start(bf16[16,208,128]{2,1,0:T(8,128)(2,1)S(1)} %constant_dynamic-update-slice_fusion.2.own_ref), channel_id=1, source_target_pairs={{0,1},{1,0},{2,3},{3,2},{4,5},{5,4},{6,7},{7,6},{8,9},{9,8},{10,11... | collective-permute-start | bytes 2555912 | tf_op jit(solution)/shard_map/ppermute | solution.py:51
  43.0 26.7 %collective-permute-start.10 = (bf16[2,64,2048]{2,1,0:T(8,128)(2,1)}, bf16[2,64,2048]{2,1,0:T(8,128)(2,1)}, u32[]{:S(2)}, u32[]{:S(2)}) collective-permute-start(bf16[2,64,2048]{2,1,0:T(8,128)(2,1)} %collective-permute-done.5.refs_4_.refs_14_.refs_18_), channel_id=1, source_target_pairs={{16,24},{17,25},{18,26},{19,27},{20,28},{21,29},{22,30},{23,31}} | collective-permute-start | bytes 1572872 | tf_op jit(solution)/shard_map/ppermute | solution.py:46
  45.4 1.2 copy-start.1
  46.6 1.2 copy-start.3
  47.9 1.0 copy-start.6
  48.9 20.5 %copy-start.30 = (bf16[1,336,128]{2,1,0:T(8,128)(2,1)S(1)}, bf16[1,336,128]{2,1,0:T(8,128)(2,1)}, u32[]{:S(2)}) copy-start(bf16[1,336,128]{2,1,0:T(8,128)(2,1)} %copy-done.29) | copy-start | bytes 258052
  48.9 20.6 %copy-start.32 = (bf16[2,336,128]{2,1,0:T(8,128)(2,1)S(1)}, bf16[2,336,128]{2,1,0:T(8,128)(2,1)}, u32[]{:S(2)}) copy-start(bf16[2,336,128]{2,1,0:T(8,128)(2,1)} %copy-done.31) | copy-start | bytes 516100
  50.1 1.0 copy-start.15
  51.1 0.8 copy-start.17
  51.9 17.6 %copy-start.21 = (bf16[2,64,128]{2,1,0:T(8,128)(2,1)}, bf16[2,64,128]{2,1,0:T(8,128)(2,1)S(1)}, u32[]{:S(2)}) copy-start(bf16[2,64,128]{2,1,0:T(8,128)(2,1)S(1)} %get-tuple-element.35.refs_8_) | copy-start | bytes 98308
  51.9 19.7 %copy-start.7 = (bf16[2,64,2048]{2,1,0:T(8,128)(2,1)S(1)}, bf16[2,64,2048]{2,1,0:T(8,128)(2,1)}, u32[]{:S(2)}) copy-start(bf16[2,64,2048]{2,1,0:T(8,128)(2,1)} %copy-done.5) | copy-start | bytes 1572868
  51.9 17.7 %collective-permute-start.7 = (bf16[2,64,128]{2,1,0:T(8,128)(2,1)S(1)}, bf16[2,64,128]{2,1,0:T(8,128)(2,1)S(1)}, u32[]{:S(2)}, u32[]{:S(2)}) collective-permute-start(bf16[2,64,128]{2,1,0:T(8,128)(2,1)S(1)} %get-tuple-element.35.refs_8_), channel_id=1, source_target_pairs={{0,8},{8,16},{16,24},{1,9},{9,17},{17,25},{2,10},{10,18},{18,26},{... | collective-permute-start | bytes 98312 | tf_op jit(solution)/shard_map/ppermute | solution.py:46
  60.5 9.8 %collective-permute-start.8 = (bf16[2,64,128]{2,1,0:T(8,128)(2,1)S(1)}, bf16[2,64,128]{2,1,0:T(8,128)(2,1)S(1)}, u32[]{:S(2)}, u32[]{:S(2)}) collective-permute-start(bf16[2,64,128]{2,1,0:T(8,128)(2,1)S(1)} %get-tuple-element.35.refs_8_), channel_id=1, source_target_pairs={{0,16},{8,24},{1,17},{9,25},{2,18},{10,26},{3,19},{11,27},{4,20},{... | collective-permute-start | bytes 98312 | tf_op jit(solution)/shard_map/ppermute | solution.py:46
  68.1 2.9 %collective-permute-start.9 = (bf16[2,64,128]{2,1,0:T(8,128)(2,1)S(1)}, bf16[2,64,128]{2,1,0:T(8,128)(2,1)S(1)}, u32[]{:S(2)}, u32[]{:S(2)}) collective-permute-start(bf16[2,64,128]{2,1,0:T(8,128)(2,1)S(1)} %get-tuple-element.35.refs_8_), channel_id=1, source_target_pairs={{0,24},{1,25},{2,26},{3,27},{4,28},{5,29},{6,30},{7,31}} | collective-permute-start | bytes 98312 | tf_op jit(solution)/shard_map/ppermute | solution.py:46
  69.6 0.6 copy-start.23
  70.3 0.6 copy-start.25
  71.6 1.2 copy-start.2
  72.9 1.2 copy-start.4
  74.1 0.8 copy-start.14
  74.9 1.1 copy-start.18
  75.9 0.8 copy-start.22
  76.7 0.8 copy-start.24
  77.5 0.8 copy-start.26
  78.2 0.8 copy-start.28
  96.3 0.7 copy-start.19
  97.0 0.7 copy-start.8
  97.0 0.8 copy-start.10
  97.0 4.7 %copy-start.20 = (bf16[2,64,1024]{2,1,0:T(8,128)(2,1)S(1)}, bf16[2,64,1024]{2,1,0:T(8,128)(2,1)}, u32[]{:S(2)}) copy-start(bf16[2,64,1024]{2,1,0:T(8,128)(2,1)} %copy-done.19) | copy-start | bytes 786436
  97.8 5.8 %collective-permute-start.13 = (bf16[2,64,64]{2,1,0:T(8,128)(2,1)S(1)}, bf16[2,64,64]{2,1,0:T(8,128)(2,1)S(1)}, u32[]{:S(2)}, u32[]{:S(2)}) collective-permute-start(bf16[2,64,64]{2,1,0:T(8,128)(2,1)S(1)} %get-tuple-element.71), channel_id=1, source_target_pairs={{8,0},{16,8},{24,16},{9,1},{17,9},{25,17},{10,2},{18,10},{26,18},{... | collective-permute-start | bytes 49160 | tf_op jit(solution)/shard_map/ppermute | solution.py:46
  99.0 6.7 %collective-permute-start.14 = (bf16[2,64,64]{2,1,0:T(8,128)(2,1)S(1)}, bf16[2,64,64]{2,1,0:T(8,128)(2,1)S(1)}, u32[]{:S(2)}, u32[]{:S(2)}) collective-permute-start(bf16[2,64,64]{2,1,0:T(8,128)(2,1)S(1)} %get-tuple-element.73), channel_id=1, source_target_pairs={{16,0},{24,8},{17,1},{25,9},{18,2},{26,10},{19,3},{27,11},{20,4},{... | collective-permute-start | bytes 49160 | tf_op jit(solution)/shard_map/ppermute | solution.py:46
  100.3 9.1 %collective-permute-start.15 = (bf16[2,64,64]{2,1,0:T(8,128)(2,1)S(1)}, bf16[2,64,64]{2,1,0:T(8,128)(2,1)S(1)}, u32[]{:S(2)}, u32[]{:S(2)}) collective-permute-start(bf16[2,64,64]{2,1,0:T(8,128)(2,1)S(1)} %get-tuple-element.72), channel_id=1, source_target_pairs={{24,0},{25,1},{26,2},{27,3},{28,4},{29,5},{30,6},{31,7}} | collective-permute-start | bytes 49160 | tf_op jit(solution)/shard_map/ppermute | solution.py:46
  101.7 9.5 %collective-permute-start.11 = (bf16[2,64,1024]{2,1,0:T(8,128)(2,1)S(1)}, bf16[2,64,1024]{2,1,0:T(8,128)(2,1)S(1)}, u32[]{:S(2)}, u32[]{:S(2)}) collective-permute-start(bf16[2,64,1024]{2,1,0:T(8,128)(2,1)S(1)} %copy-done.20), channel_id=1, source_target_pairs={{24,16},{25,17},{26,18},{27,19},{28,20},{29,21},{30,22},{31,23}} | collective-permute-start | bytes 786440 | tf_op jit(solution)/shard_map/ppermute | solution.py:46
  111.2 0.7 copy-start.33
  111.2 2.6 %collective-permute-start.16 = (bf16[8,2,208,128]{3,2,1,0:T(8,128)(2,1)}, bf16[8,2,208,128]{3,2,1,0:T(8,128)(2,1)S(1)}, u32[]{:S(2)}, u32[]{:S(2)}) collective-permute-start(bf16[8,2,208,128]{3,2,1,0:T(8,128)(2,1)} %get-tuple-element.48), channel_id=1, source_target_pairs={{0,1},{1,0},{2,3},{3,2},{4,5},{5,4},{6,7},{7,6},{8,9},{9,8},{10,11... | collective-permute-start | bytes 2555912 | tf_op jit(solution)/shard_map/ppermute | solution.py:51
  112.0 1.0 copy-start.11
  112.0 1.0 copy-start.34
  113.1 7.9 %collective-permute-start.12 = (bf16[2,64,1024]{2,1,0:T(8,128)(2,1)S(1)}, bf16[2,64,1024]{2,1,0:T(8,128)(2,1)S(1)}, u32[]{:S(2)}, u32[]{:S(2)}) collective-permute-start(bf16[2,64,1024]{2,1,0:T(8,128)(2,1)S(1)} %add_convert_fusion.2), channel_id=1, source_target_pairs={{16,8},{24,16},{17,9},{25,17},{18,10},{26,18},{19,11},{27,19},{20,... | collective-permute-start | bytes 786440 | tf_op jit(solution)/shard_map/ppermute | solution.py:46
  114.0 7.0 %collective-permute-start.18 = (bf16[4,2,96,128]{3,2,0,1:T(8,128)(2,1)S(1)}, bf16[4,2,96,128]{3,2,0,1:T(8,128)(2,1)S(1)}, u32[]{:S(2)}, u32[]{:S(2)}) collective-permute-start(bf16[4,2,96,128]{3,2,0,1:T(8,128)(2,1)S(1)} %fusion.4), channel_id=1, source_target_pairs={{0,4},{4,0},{1,5},{5,1},{2,6},{6,2},{3,7},{7,3},{8,12},{12,8},{9,1... | collective-permute-start | bytes 589832 | tf_op jit(solution)/shard_map/ppermute | solution.py:51
  115.7 7.4 %collective-permute-start.17 = (bf16[4,2,112,128]{3,2,0,1:T(8,128)(2,1)S(1)}, bf16[4,2,112,128]{3,2,0,1:T(8,128)(2,1)S(1)}, u32[]{:S(2)}, u32[]{:S(2)}) collective-permute-start(bf16[4,2,112,128]{3,2,0,1:T(8,128)(2,1)S(1)} %fusion), channel_id=1, source_target_pairs={{0,2},{1,3},{2,0},{3,1},{4,6},{5,7},{6,4},{7,5},{8,10},{9,11},{10,... | collective-permute-start | bytes 688136 | tf_op jit(solution)/shard_map/ppermute | solution.py:51
  116.4 7.3 %copy-start.9 = (bf16[2,64,1024]{2,1,0:T(8,128)(2,1)S(1)}, bf16[2,64,1024]{2,1,0:T(8,128)(2,1)}, u32[]{:S(2)}) copy-start(bf16[2,64,1024]{2,1,0:T(8,128)(2,1)} %copy-done.8) | copy-start | bytes 786436
  121.0 4.7 %collective-permute-start.20 = (bf16[4,96,128]{2,1,0:T(8,128)(2,1)S(1)}, bf16[4,96,128]{2,1,0:T(8,128)(2,1)S(1)}, u32[]{:S(2)}, u32[]{:S(2)}) collective-permute-start(bf16[4,96,128]{2,1,0:T(8,128)(2,1)S(1)} %fusion.14), channel_id=1, source_target_pairs={{0,2},{1,3},{2,0},{3,1},{4,6},{5,7},{6,4},{7,5},{8,10},{9,11},{10,... | collective-permute-start | bytes 294920 | tf_op jit(solution)/shard_map/ppermute | solution.py:51
  123.1 4.9 %collective-permute-start.21 = (bf16[4,112,128]{2,1,0:T(8,128)(2,1)S(1)}, bf16[4,112,128]{2,1,0:T(8,128)(2,1)S(1)}, u32[]{:S(2)}, u32[]{:S(2)}) collective-permute-start(bf16[4,112,128]{2,1,0:T(8,128)(2,1)S(1)} %fusion.9), channel_id=1, source_target_pairs={{0,4},{4,0},{1,5},{5,1},{2,6},{6,2},{3,7},{7,3},{8,12},{12,8},{9,1... | collective-permute-start | bytes 344072 | tf_op jit(solution)/shard_map/ppermute | solution.py:51
  123.7 17.1 %copy-start.16 = (bf16[4096,128]{1,0:T(8,128)(2,1)S(1)}, bf16[4096,128]{1,0:T(8,128)(2,1)}, u32[]{:S(2)}) copy-start(bf16[4096,128]{1,0:T(8,128)(2,1)} %copy-done.15) | copy-start | bytes 3145732
  123.8 11.5 %collective-permute-start.19 = (bf16[2,64,1024]{2,1,0:T(8,128)(2,1)S(1)}, bf16[2,64,1024]{2,1,0:T(8,128)(2,1)S(1)}, u32[]{:S(2)}, u32[]{:S(2)}) collective-permute-start(bf16[2,64,1024]{2,1,0:T(8,128)(2,1)S(1)} %add_convert_fusion.1), channel_id=1, source_target_pairs={{8,0},{16,8},{24,16},{9,1},{17,9},{25,17},{10,2},{18,10},{26,18},{... | collective-permute-start | bytes 786440 | tf_op jit(solution)/shard_map/ppermute | solution.py:46
  135.3 7.7 %collective-permute-start.22 = (bf16[208,128]{1,0:T(8,128)(2,1)S(1)}, bf16[208,128]{1,0:T(8,128)(2,1)S(1)}, u32[]{:S(2)}, u32[]{:S(2)}) collective-permute-start(bf16[208,128]{1,0:T(8,128)(2,1)S(1)} %get-tuple-element.68), channel_id=1, source_target_pairs={{0,8},{8,16},{16,24},{24,0},{1,9},{9,17},{17,25},{25,1},{2,10},{10... | collective-permute-start | bytes 159752 | tf_op jit(solution)/shard_map/ppermute | solution.py:41
  137.0 5.9 %collective-permute-start.23 = (bf16[208,128]{1,0:T(8,128)(2,1)S(1)}, bf16[208,128]{1,0:T(8,128)(2,1)S(1)}, u32[]{:S(2)}, u32[]{:S(2)}) collective-permute-start(bf16[208,128]{1,0:T(8,128)(2,1)S(1)} %get-tuple-element.70), channel_id=1, source_target_pairs={{0,16},{8,24},{16,0},{24,8},{1,17},{9,25},{17,1},{25,9},{2,18},{10... | collective-permute-start | bytes 159752 | tf_op jit(solution)/shard_map/ppermute | solution.py:41
  138.0 5.0 %collective-permute-start.24 = (bf16[208,128]{1,0:T(8,128)(2,1)S(1)}, bf16[208,128]{1,0:T(8,128)(2,1)S(1)}, u32[]{:S(2)}, u32[]{:S(2)}) collective-permute-start(bf16[208,128]{1,0:T(8,128)(2,1)S(1)} %get-tuple-element.69), channel_id=1, source_target_pairs={{0,24},{8,0},{16,8},{24,16},{1,25},{9,1},{17,9},{25,17},{2,26},{10... | collective-permute-start | bytes 159752 | tf_op jit(solution)/shard_map/ppermute | solution.py:41
  143.0 4.1 %collective-permute-start.25 = (bf16[208,128]{1,0:T(8,128)(2,1)S(1)}, bf16[208,128]{1,0:T(8,128)(2,1)S(1)}, u32[]{:S(2)}, u32[]{:S(2)}) collective-permute-start(bf16[208,128]{1,0:T(8,128)(2,1)S(1)} %fusion.12), channel_id=1, source_target_pairs={{0,3},{1,2},{2,1},{3,0},{4,7},{5,6},{6,5},{7,4},{8,11},{9,10},{10,... | collective-permute-start | bytes 159752 | tf_op jit(solution)/shard_map/ppermute | solution.py:51
  143.1 5.1 %collective-permute-start.26 = (bf16[208,128]{1,0:T(8,128)(2,1)S(1)}, bf16[208,128]{1,0:T(8,128)(2,1)S(1)}, u32[]{:S(2)}, u32[]{:S(2)}) collective-permute-start(bf16[208,128]{1,0:T(8,128)(2,1)S(1)} %fusion.12), channel_id=1, source_target_pairs={{0,2},{1,3},{2,0},{3,1},{4,6},{5,7},{6,4},{7,5},{8,10},{9,11},{10,... | collective-permute-start | bytes 159752 | tf_op jit(solution)/shard_map/ppermute | solution.py:51
  144.7 3.6 %collective-permute-start.27 = (bf16[208,128]{1,0:T(8,128)(2,1)S(1)}, bf16[208,128]{1,0:T(8,128)(2,1)S(1)}, u32[]{:S(2)}, u32[]{:S(2)}) collective-permute-start(bf16[208,128]{1,0:T(8,128)(2,1)S(1)} %fusion.12), channel_id=1, source_target_pairs={{0,1},{1,0},{2,3},{3,2},{4,5},{5,4},{6,7},{7,6},{8,9},{9,8},{10,11... | collective-permute-start | bytes 159752 | tf_op jit(solution)/shard_map/ppermute | solution.py:51
  (1 other events, 0.6 us)

commit v10 on v9

--- a/solution.py
+++ b/solution.py
@@ -311,7 +311,7 @@
     return buf[:, :rows], past
 
 
-def adapters_packed(hidden, buf, before_rep, before_swap, staged):
+def adapters_packed(hidden, buf, before_rep, before_swap):
     sp, fs, rp = (lax.axis_size(a) for a in ("sp", "fsdp", "rep"))
     z, x, r = (lax.axis_index(a) for a in ("sp", "fsdp", "rep"))
     step = 1
@@ -329,9 +329,7 @@
     seqs, tokens = hidden.shape[:2]
     down_full, up_blocks, low = pl.pallas_call(
         functools.partial(low_rank_kernel, sp, fs, rp),
-        in_specs=[pl.BlockSpec(memory_space=pltpu.SMEM)]
-        + [vmem] * 3
-        + [pl.BlockSpec(memory_space=pl.ANY)] * len(staged),
+        in_specs=[pl.BlockSpec(memory_space=pltpu.SMEM)] + [vmem] * 3,
         out_specs=[pl.BlockSpec(memory_space=pltpu.HBM), vmem, vmem],
         scratch_shapes=[pltpu.VMEM((D, 2 * RANK), bf16), pltpu.SemaphoreType.DMA],
         out_shape=[
@@ -344,7 +342,7 @@
             flops=2 * seqs * tokens * D * 2 * RANK, bytes_accessed=2**16, transcendentals=0
         ),
         name="low_rank",
-    )(index, buf, other, hidden, *staged)
+    )(index, buf, other, hidden)
     return down_full, up_blocks, low
 
 
@@ -488,13 +486,12 @@
         part = (part.astype(f32) + tie(hops[-1], *marks).astype(f32)).astype(bf16)
     last = along(part, "sp", -1, 1)
     grad_value = (values[0].astype(f32) + last.astype(f32)).astype(bf16)
-    over_sp = tie(over_sp, last)
     total = lax.dynamic_index_in_dim(over_sp, z, 0, keepdims=False).astype(f32)
     for k in range(1, sp):
         send = lax.dynamic_index_in_dim(over_sp, lax.rem(z + k, sp), 0, keepdims=False)
         total = total + cyclic(send, "sp", k).astype(f32)
     grad_hidden = hidden_of(tie(low_grad, over_sp))
-    own = tie(total.astype(bf16), grad_hidden)
+    own = tie(total.astype(bf16), grad_hidden, last)
     parts = [own] + [partner(own, "rep", m) for m in range(1, rp)]
     ordered = []
     for q in range(rp):
@@ -543,9 +540,7 @@
     for k in range(2, sp):
         kvs.append(along(kvs[k - 1], "sp", 1, k - 1))
     if even:
-        down_full, up_blocks, low_own = adapters_packed(
-            hidden, buf, kvs[1], kvs[min(2, sp - 1)], (query_base, grad_out, *kvs[:3])
-        )
+        down_full, up_blocks, low_own = adapters_packed(hidden, buf, kvs[1], kvs[min(2, sp - 1)])
     else:
         down_full, up_blocks, low_own = adapters_plain(hidden, adapter_down, adapter_up)
     lows = [low_own] + [along(low_own, "sp", k) for k in range(1, sp)]

time: 151 us -> 145 us (0.960)
  local copies, waits for them, and re-layouts: 19.8 us -> 15.2 us
  waiting for transfers between devices: 52.2 us -> 49.7 us
  starting transfers between devices: 49.5 us -> 51.8 us
    ppermute x12, waiting for transfers between devices: 18.7 us -> 12.1 us  [along(): lax.ppermute(x, axis, [(i, i + shift) for i in range(start, n) if 0 <= i...]
    unnamed x92 -> x70, local copies, waits for them, and re-layouts: 19.2 us -> 14.6 us
    ppermute x3, starting transfers between devices: 5.56 us -> 8.47 us  [cyclic(): return lax.ppermute(x, axis, [(i, (i + shift) % n) for i in range(n)])]
    ppermute x3, waiting for transfers between devices: 0.01 us -> 2.86 us  [cyclic(): return lax.ppermute(x, axis, [(i, (i + shift) % n) for i in range(n)])]
  transfers between devices with their start and end apart: 28 -> 28, of which waited for: 16 -> 19; matrix products, arithmetic and copies ran while one was open for 2% -> 2% of each run, Pallas kernels for 3% -> 3%
where the time goes in v10:
time: 145 us; the launch traced here: 144 us
  starting transfers between devices  51.8 us (36%)
  waiting for transfers between devices  49.7 us (34%)
  Pallas kernels  22.2 us (15%)
  local copies, waits for them, and re-layouts  15.2 us (10%)
  other arithmetic  4.22 us (3%)
    ppermute x13, waiting for transfers between devices, partner(): return lax.ppermute(x, axis, [(i, i ^ mask) for i in range(n)])  34.8 us
    ppermute x12, starting transfers between devices, along(): lax.ppermute(x, axis, [(i, i + shift) for i in range(start, n) if 0 <= i...  28.9 us
    pallas_call x1, Pallas kernels, attention(): pl.pallas_call(functools.partial(attention_kernel, shards), grid=(KV_HEAD...  17.3 us
    unnamed x70, local copies, waits for them, and re-layouts  14.6 us
    ppermute x13, starting transfers between devices, partner(): return lax.ppermute(x, axis, [(i, i ^ mask) for i in range(n)])  14.5 us
    ppermute x12, waiting for transfers between devices, along(): lax.ppermute(x, axis, [(i, i + shift) for i in range(start, n) if 0 <= i...  12.1 us
    ppermute x3, starting transfers between devices, cyclic(): return lax.ppermute(x, axis, [(i, (i + shift) % n) for i in range(n)])  8.47 us
  transfers between devices with their start and end apart: 28, of which 19 were waited for; matrix products, arithmetic and copies ran while one was open for 2% of the time, Pallas kernels for 3%

profile of v10, /device:TPU:0, one launch (start us, length us, event | category | flops | bytes accessed | tf_op | source)
XLA Modules:
  0.0 144.4 jit_solution(15567852026715119572)
XLA Ops:
  0.6 0.8 pad_maximum_fusion.7
  1.6 0.9 copy-done.4
  2.5 3.1 %collective-permute-start = (bf16[1,336,128]{2,1,0:T(8,128)(2,1)S(1)}, bf16[1,336,128]{2,1,0:T(8,128)(2,1)S(1)}, u32[]{:S(2)}, u32[]{:S(2)}) collective-permute-start(bf16[1,336,128]{2,1,0:T(8,128)(2,1)S(1)} %pack.1), channel_id=1, source_target_pairs={{0,8},{8,0},{16,24},{24,16},{1,9},{9,1},{17,25},{25,17},{2,10},{10... | collective-permute-start | bytes 258056 | tf_op jit(solution)/shard_map/ppermute | solution.py:51
  5.6 2.5 %collective-permute-done = bf16[1,336,128]{2,1,0:T(8,128)(2,1)S(1)} collective-permute-done((bf16[1,336,128]{2,1,0:T(8,128)(2,1)S(1)}, bf16[1,336,128]{2,1,0:T(8,128)(2,1)S(1)}, u32[]{:S(2)}, u32[]{:S(2)}) %collective-permute-start) | collective-permute-done | bytes 86048 | tf_op jit(solution)/shard_map/ppermute | solution.py:51
  8.1 3.0 %collective-permute-start.1 = (bf16[2,336,128]{2,1,0:T(8,128)(2,1)S(1)}, bf16[2,336,128]{2,1,0:T(8,128)(2,1)S(1)}, u32[]{:S(2)}, u32[]{:S(2)}) collective-permute-start(bf16[2,336,128]{2,1,0:T(8,128)(2,1)S(1)} %pad_maximum_fusion.4), channel_id=1, source_target_pairs={{0,16},{8,24},{16,0},{24,8},{1,17},{9,25},{17,1},{25,9},{2,18},{10... | collective-permute-start | bytes 516104 | tf_op jit(solution)/shard_map/ppermute | solution.py:51
  11.2 7.1 %collective-permute-done.1 = bf16[2,336,128]{2,1,0:T(8,128)(2,1)S(1)} collective-permute-done((bf16[2,336,128]{2,1,0:T(8,128)(2,1)S(1)}, bf16[2,336,128]{2,1,0:T(8,128)(2,1)S(1)}, u32[]{:S(2)}, u32[]{:S(2)}) %collective-permute-start.1) | collective-permute-done | bytes 172064 | tf_op jit(solution)/shard_map/ppermute | solution.py:51
  18.4 2.4 %collective-permute-start.3 = (bf16[2,64,2048]{2,1,0:T(8,128)(2,1)S(1)}, bf16[2,64,2048]{2,1,0:T(8,128)(2,1)S(1)}, u32[]{:S(2)}, u32[]{:S(2)}) collective-permute-start(bf16[2,64,2048]{2,1,0:T(8,128)(2,1)S(1)} %constant_dynamic-update-slice_fusion.refs_12_.refs_16_), channel_id=1, source_target_pairs={{0,8},{8,16},{16,24},{1,9},{9,17},{17,25},{2,10},{10,18},{18,26},{... | collective-permute-start | bytes 1572872 | tf_op jit(solution)/shard_map/ppermute | solution.py:46
  20.8 1.6 %collective-permute-start.2 = (bf16[4,208,128]{2,1,0:T(8,128)(2,1)S(1)}, bf16[4,208,128]{2,1,0:T(8,128)(2,1)S(1)}, u32[]{:S(2)}, u32[]{:S(2)}) collective-permute-start(bf16[4,208,128]{2,1,0:T(8,128)(2,1)S(1)} %slice.163), channel_id=1, source_target_pairs={{0,4},{4,0},{1,5},{5,1},{2,6},{6,2},{3,7},{7,3},{8,12},{12,8},{9,1... | collective-permute-start | bytes 638984 | tf_op jit(solution)/shard_map/ppermute | solution.py:51
  22.4 5.0 %collective-permute-done.2 = bf16[4,208,128]{2,1,0:T(8,128)(2,1)S(1)} collective-permute-done((bf16[4,208,128]{2,1,0:T(8,128)(2,1)S(1)}, bf16[4,208,128]{2,1,0:T(8,128)(2,1)S(1)}, u32[]{:S(2)}, u32[]{:S(2)}) %collective-permute-start.2) | collective-permute-done | bytes 213024 | tf_op jit(solution)/shard_map/ppermute | solution.py:51
  27.4 4.3 %collective-permute-done.3.refs_13_.refs_17_ = bf16[2,64,2048]{2,1,0:T(8,128)(2,1)S(1)} collective-permute-done((bf16[2,64,2048]{2,1,0:T(8,128)(2,1)S(1)}, bf16[2,64,2048]{2,1,0:T(8,128)(2,1)S(1)}, u32[]{:S(2)}, u32[]{:S(2)}) %collective-permute-start.3) | collective-permute-done | bytes 524320 | tf_op jit(solution)/shard_map/ppermute | solution.py:46
  31.7 1.5 %collective-permute-start.4 = (bf16[8,208,128]{2,1,0:T(8,128)(2,1)S(1)}, bf16[8,208,128]{2,1,0:T(8,128)(2,1)S(1)}, u32[]{:S(2)}, u32[]{:S(2)}) collective-permute-start(bf16[8,208,128]{2,1,0:T(8,128)(2,1)S(1)} %pad_maximum_fusion), channel_id=1, source_target_pairs={{0,2},{1,3},{2,0},{3,1},{4,6},{5,7},{6,4},{7,5},{8,10},{9,11},{10,... | collective-permute-start | bytes 1277960 | tf_op jit(solution)/shard_map/ppermute | solution.py:51
  33.2 1.5 %collective-permute-start.5 = (bf16[2,64,2048]{2,1,0:T(8,128)(2,1)S(1)}, bf16[2,64,2048]{2,1,0:T(8,128)(2,1)}, u32[]{:S(2)}, u32[]{:S(2)}) collective-permute-start(bf16[2,64,2048]{2,1,0:T(8,128)(2,1)S(1)} %collective-permute-done.3.refs_13_.refs_17_), channel_id=1, source_target_pairs={{8,16},{16,24},{9,17},{17,25},{10,18},{18,26},{11,19},{19,27},{12,... | collective-permute-start | bytes 1572872 | tf_op jit(solution)/shard_map/ppermute | solution.py:46
  34.7 7.4 %collective-permute-done.4 = bf16[8,208,128]{2,1,0:T(8,128)(2,1)S(1)} collective-permute-done((bf16[8,208,128]{2,1,0:T(8,128)(2,1)S(1)}, bf16[8,208,128]{2,1,0:T(8,128)(2,1)S(1)}, u32[]{:S(2)}, u32[]{:S(2)}) %collective-permute-start.4) | collective-permute-done | bytes 426016 | tf_op jit(solution)/shard_map/ppermute | solution.py:51
  42.3 1.5 %collective-permute-start.10 = (bf16[2,64,2048]{2,1,0:T(8,128)(2,1)}, bf16[2,64,2048]{2,1,0:T(8,128)(2,1)}, u32[]{:S(2)}, u32[]{:S(2)}) collective-permute-start(bf16[2,64,2048]{2,1,0:T(8,128)(2,1)} %collective-permute-done.5.refs_14_.refs_18_), channel_id=1, source_target_pairs={{16,24},{17,25},{18,26},{19,27},{20,28},{21,29},{22,30},{23,31}} | collective-permute-start | bytes 1572872 | tf_op jit(solution)/shard_map/ppermute | solution.py:46
  44.7 1.2 low_rank.1
  45.9 1.0 copy-done.7
  46.8 0.8 copy-done.9
  47.7 8.6 %collective-permute-start.7 = (bf16[2,64,128]{2,1,0:T(8,128)(2,1)S(1)}, bf16[2,64,128]{2,1,0:T(8,128)(2,1)S(1)}, u32[]{:S(2)}, u32[]{:S(2)}) collective-permute-start(bf16[2,64,128]{2,1,0:T(8,128)(2,1)S(1)} %get-tuple-element.34.refs_8_), channel_id=1, source_target_pairs={{0,8},{8,16},{16,24},{1,9},{9,17},{17,25},{2,10},{10,18},{18,26},{... | collective-permute-start | bytes 98312 | tf_op jit(solution)/shard_map/ppermute | solution.py:46
  56.3 7.2 %collective-permute-start.8 = (bf16[2,64,128]{2,1,0:T(8,128)(2,1)S(1)}, bf16[2,64,128]{2,1,0:T(8,128)(2,1)S(1)}, u32[]{:S(2)}, u32[]{:S(2)}) collective-permute-start(bf16[2,64,128]{2,1,0:T(8,128)(2,1)S(1)} %get-tuple-element.34.refs_8_), channel_id=1, source_target_pairs={{0,16},{8,24},{1,17},{9,25},{2,18},{10,26},{3,19},{11,27},{4,20},{... | collective-permute-start | bytes 98312 | tf_op jit(solution)/shard_map/ppermute | solution.py:46
  63.4 1.3 collective-permute-start.9
  64.9 0.6 copy-done.16
  65.5 0.6 copy-done.18
  66.3 0.6 copy-done.20
  66.9 1.2 copy-done.5
  68.1 1.2 copy-done.6
  69.4 1.1 copy-done.10
  70.5 1.0 copy-done.12
  71.5 0.8 copy-done.15
  72.3 0.8 copy-done.17
  73.0 0.8 copy-done.19
  73.8 0.8 copy-done.21
  74.5 17.3 %attention.1 = (bf16[2,64,4096]{2,1,0:T(8,128)(2,1)}, bf16[2,64,4096]{2,1,0:T(8,128)(2,1)}, bf16[32,4,16,128]{3,2,1,0:T(8,128)(2,1)S(1)}, bf16[8,4,16,128]{3,2,1...) custom-call(s32[1]{0:T(128)} %bitcast.place_ref, ...), custom_call_target="tpu_custom_call" | custom-call | flops 17112760320 | bytes 65536 | tf_op jit(solution)/shard_map/attention/pallas_call | solution.py:212
  91.9 0.6 copy-done.13
  92.5 1.3 collective-permute-start.13
  93.8 1.3 collective-permute-start.14
  95.1 1.3 collective-permute-start.15
  96.4 0.7 collective-permute-start.11
  97.1 1.2 collective-permute-done.13
  98.3 3.6 %collective-permute-done.14 = bf16[2,64,64]{2,1,0:T(8,128)(2,1)S(1)} collective-permute-done((bf16[2,64,64]{2,1,0:T(8,128)(2,1)S(1)}, bf16[2,64,64]{2,1,0:T(8,128)(2,1)S(1)}, u32[]{:S(2)}, u32[]{:S(2)}) %collective-permute-start.14) | collective-permute-done | bytes 16416 | tf_op jit(solution)/shard_map/ppermute | solution.py:46
  101.9 2.7 %collective-permute-done.15 = bf16[2,64,64]{2,1,0:T(8,128)(2,1)S(1)} collective-permute-done((bf16[2,64,64]{2,1,0:T(8,128)(2,1)S(1)}, bf16[2,64,64]{2,1,0:T(8,128)(2,1)S(1)}, u32[]{:S(2)}, u32[]{:S(2)}) %collective-permute-start.15) | collective-permute-done | bytes 16416 | tf_op jit(solution)/shard_map/ppermute | solution.py:46
  104.8 1.6 %adapter_grads.1 = (bf16[8,2,208,128]{3,2,1,0:T(8,128)(2,1)}, bf16[8,2,208,128]{3,2,1,0:T(8,128)(2,1)S(1)}) custom-call(s32[1]{0:T(128)} %bitcast.4.core_ref, bf16[2,64,4096]{2,1,0:T(8,128)(2,1)S(1)} %copy-done, bf16[128,128]{1,0:T(8,128)(2,1)S(1)} %pad_maximum_fusion.10.low_ref, bf16[32,4,16,128]{3,2,1,0:T(8,128)(2,1)S(1)} %get-tuple-element.43.guq_ref, ...), custom_call_target="tpu_custom_call" | custom-call | flops 134217728 | bytes 5242880 | tf_op jit(solution)/shard_map/adapter_grads/pallas_call | solution.py:417
  106.4 0.7 copy-done.22
  107.3 0.9 copy-done.23
  108.2 0.7 collective-permute-start.12
  108.9 0.8 collective-permute-done.16
  109.8 1.6 %collective-permute-start.18 = (bf16[4,2,96,128]{3,2,0,1:T(8,128)(2,1)S(1)}, bf16[4,2,96,128]{3,2,0,1:T(8,128)(2,1)S(1)}, u32[]{:S(2)}, u32[]{:S(2)}) collective-permute-start(bf16[4,2,96,128]{3,2,0,1:T(8,128)(2,1)S(1)} %fusion.4), channel_id=1, source_target_pairs={{0,4},{4,0},{1,5},{5,1},{2,6},{6,2},{3,7},{7,3},{8,12},{12,8},{9,1... | collective-permute-start | bytes 589832 | tf_op jit(solution)/shard_map/ppermute | solution.py:51
  112.2 4.6 %collective-permute-done.18 = bf16[4,2,96,128]{3,2,0,1:T(8,128)(2,1)S(1)} collective-permute-done((bf16[4,2,96,128]{3,2,0,1:T(8,128)(2,1)S(1)}, bf16[4,2,96,128]{3,2,0,1:T(8,128)(2,1)S(1)}, u32[]{:S(2)}, u32[]{:S(2)}) %collective-permute-start.18) | collective-permute-done | bytes 196640 | tf_op jit(solution)/shard_map/ppermute | solution.py:51
  117.5 1.5 %collective-permute-done.17 = bf16[4,2,112,128]{3,2,0,1:T(8,128)(2,1)S(1)} collective-permute-done((bf16[4,2,112,128]{3,2,0,1:T(8,128)(2,1)S(1)}, bf16[4,2,112,128]{3,2,0,1:T(8,128)(2,1)S(1)}, u32[]{:S(2)}, u32[]{:S(2)}) %collective-permute-start.17) | collective-permute-done | bytes 229408 | tf_op jit(solution)/shard_map/ppermute | solution.py:51
  119.0 0.6 collective-permute-start.21
  119.7 1.3 collective-permute-start.19
  121.0 0.6 collective-permute-done.20
  121.6 2.2 %collective-permute-done.21 = bf16[4,112,128]{2,1,0:T(8,128)(2,1)S(1)} collective-permute-done((bf16[4,112,128]{2,1,0:T(8,128)(2,1)S(1)}, bf16[4,112,128]{2,1,0:T(8,128)(2,1)S(1)}, u32[]{:S(2)}, u32[]{:S(2)}) %collective-permute-start.21) | collective-permute-done | bytes 114720 | tf_op jit(solution)/shard_map/ppermute | solution.py:51
  124.0 3.9 %collective-permute-start.22 = (bf16[208,128]{1,0:T(8,128)(2,1)S(1)}, bf16[208,128]{1,0:T(8,128)(2,1)S(1)}, u32[]{:S(2)}, u32[]{:S(2)}) collective-permute-start(bf16[208,128]{1,0:T(8,128)(2,1)S(1)} %get-tuple-element.66), channel_id=1, source_target_pairs={{0,8},{8,16},{16,24},{24,0},{1,9},{9,17},{17,25},{25,1},{2,10},{10... | collective-permute-start | bytes 159752 | tf_op jit(solution)/shard_map/ppermute | solution.py:41
  127.9 3.4 %collective-permute-start.23 = (bf16[208,128]{1,0:T(8,128)(2,1)S(1)}, bf16[208,128]{1,0:T(8,128)(2,1)S(1)}, u32[]{:S(2)}, u32[]{:S(2)}) collective-permute-start(bf16[208,128]{1,0:T(8,128)(2,1)S(1)} %get-tuple-element.67), channel_id=1, source_target_pairs={{0,16},{8,24},{16,0},{24,8},{1,17},{9,25},{17,1},{25,9},{2,18},{10... | collective-permute-start | bytes 159752 | tf_op jit(solution)/shard_map/ppermute | solution.py:41
  131.3 1.2 collective-permute-start.24
  132.4 2.1 %grad_hidden.1 = bf16[2,64,4096]{2,1,0:T(8,128)(2,1)} custom-call(bf16[128,128]{1,0:T(8,128)(2,1)S(1)} %pad_maximum_fusion.10.low_ref, bf16[4096,128]{1,0:T(8,128)(2,1)S(1)} %copy-done.8), custom_call_target="tpu_custom_call" | custom-call | flops 1073741824 | bytes 65536 | tf_op jit(solution)/shard_map/grad_hidden/pallas_call | solution.py:368
  134.6 2.2 %collective-permute-done.22 = bf16[208,128]{1,0:T(8,128)(2,1)S(1)} collective-permute-done((bf16[208,128]{1,0:T(8,128)(2,1)S(1)}, bf16[208,128]{1,0:T(8,128)(2,1)S(1)}, u32[]{:S(2)}, u32[]{:S(2)}) %collective-permute-start.22) | collective-permute-done | bytes 53280 | tf_op jit(solution)/shard_map/ppermute | solution.py:41
  136.8 0.6 collective-permute-done.23
  137.5 1.6 %collective-permute-start.26 = (bf16[208,128]{1,0:T(8,128)(2,1)S(1)}, bf16[208,128]{1,0:T(8,128)(2,1)S(1)}, u32[]{:S(2)}, u32[]{:S(2)}) collective-permute-start(bf16[208,128]{1,0:T(8,128)(2,1)S(1)} %fusion.12), channel_id=1, source_target_pairs={{0,2},{1,3},{2,0},{3,1},{4,6},{5,7},{6,4},{7,5},{8,10},{9,11},{10,... | collective-permute-start | bytes 159752 | tf_op jit(solution)/shard_map/ppermute | solution.py:51
  139.4 0.8 add_convert_fusion
  140.2 1.4 collective-permute-done.25
  141.6 1.1 collective-permute-done.26
  143.0 0.7 pad_maximum_fusion.5
  143.7 0.7 pad_maximum_fusion.3
  (121 shorter events, 4.3 us)
Async XLA Ops:
  0.6 0.9 copy-start.3
  1.6 0.9 copy-start.4
  2.5 8.7 %copy-start.24 = (bf16[2,64,1024]{2,1,0:T(8,128)(2,1)S(1)}, bf16[2,64,1024]{2,1,0:T(8,128)(2,1)}, u32[]{:S(2)}) copy-start(bf16[2,64,1024]{2,1,0:T(8,128)(2,1)} %param.11) | copy-start | bytes 786436
  2.5 5.6 %collective-permute-start = (bf16[1,336,128]{2,1,0:T(8,128)(2,1)S(1)}, bf16[1,336,128]{2,1,0:T(8,128)(2,1)S(1)}, u32[]{:S(2)}, u32[]{:S(2)}) collective-permute-start(bf16[1,336,128]{2,1,0:T(8,128)(2,1)S(1)} %pack.1), channel_id=1, source_target_pairs={{0,8},{8,0},{16,24},{24,16},{1,9},{9,1},{17,25},{25,17},{2,10},{10... | collective-permute-start | bytes 258056 | tf_op jit(solution)/shard_map/ppermute | solution.py:51
  8.1 3.1 %copy-start.25 = (bf16[2,64,1024]{2,1,0:T(8,128)(2,1)S(1)}, bf16[2,64,1024]{2,1,0:T(8,128)(2,1)}, u32[]{:S(2)}) copy-start(bf16[2,64,1024]{2,1,0:T(8,128)(2,1)} %param.12) | copy-start | bytes 786436
  8.1 10.2 %collective-permute-start.1 = (bf16[2,336,128]{2,1,0:T(8,128)(2,1)S(1)}, bf16[2,336,128]{2,1,0:T(8,128)(2,1)S(1)}, u32[]{:S(2)}, u32[]{:S(2)}) collective-permute-start(bf16[2,336,128]{2,1,0:T(8,128)(2,1)S(1)} %pad_maximum_fusion.4), channel_id=1, source_target_pairs={{0,16},{8,24},{16,0},{24,8},{1,17},{9,25},{17,1},{25,9},{2,18},{10... | collective-permute-start | bytes 516104 | tf_op jit(solution)/shard_map/ppermute | solution.py:51
  11.2 7.2 %copy-start.1 = (bf16[2,64,2048]{2,1,0:T(8,128)(2,1)}, bf16[2,64,2048]{2,1,0:T(8,128)(2,1)S(1)}, u32[]{:S(2)}) copy-start(bf16[2,64,2048]{2,1,0:T(8,128)(2,1)S(1)} %constant_dynamic-update-slice_fusion.refs_12_.refs_16_) | copy-start | bytes 1572868
  18.4 13.3 %collective-permute-start.3 = (bf16[2,64,2048]{2,1,0:T(8,128)(2,1)S(1)}, bf16[2,64,2048]{2,1,0:T(8,128)(2,1)S(1)}, u32[]{:S(2)}, u32[]{:S(2)}) collective-permute-start(bf16[2,64,2048]{2,1,0:T(8,128)(2,1)S(1)} %constant_dynamic-update-slice_fusion.refs_12_.refs_16_), channel_id=1, source_target_pairs={{0,8},{8,16},{16,24},{1,9},{9,17},{17,25},{2,10},{10,18},{18,26},{... | collective-permute-start | bytes 1572872 | tf_op jit(solution)/shard_map/ppermute | solution.py:46
  20.8 6.5 %collective-permute-start.2 = (bf16[4,208,128]{2,1,0:T(8,128)(2,1)S(1)}, bf16[4,208,128]{2,1,0:T(8,128)(2,1)S(1)}, u32[]{:S(2)}, u32[]{:S(2)}) collective-permute-start(bf16[4,208,128]{2,1,0:T(8,128)(2,1)S(1)} %slice.163), channel_id=1, source_target_pairs={{0,4},{4,0},{1,5},{5,1},{2,6},{6,2},{3,7},{7,3},{8,12},{12,8},{9,1... | collective-permute-start | bytes 638984 | tf_op jit(solution)/shard_map/ppermute | solution.py:51
  27.4 17.3 %copy-start = (bf16[2,64,4096]{2,1,0:T(8,128)(2,1)S(1)}, bf16[2,64,4096]{2,1,0:T(8,128)(2,1)}, u32[]{:S(2)}) copy-start(bf16[2,64,4096]{2,1,0:T(8,128)(2,1)} %hidden_ref.3) | copy-start | bytes 3145732
  31.7 10.5 %copy-start.11 = (bf16[2,64,2048]{2,1,0:T(8,128)(2,1)}, bf16[2,64,2048]{2,1,0:T(8,128)(2,1)S(1)}, u32[]{:S(2)}) copy-start(bf16[2,64,2048]{2,1,0:T(8,128)(2,1)S(1)} %collective-permute-done.3.refs_13_.refs_17_) | copy-start | bytes 1572868
  31.7 10.4 %collective-permute-start.4 = (bf16[8,208,128]{2,1,0:T(8,128)(2,1)S(1)}, bf16[8,208,128]{2,1,0:T(8,128)(2,1)S(1)}, u32[]{:S(2)}, u32[]{:S(2)}) collective-permute-start(bf16[8,208,128]{2,1,0:T(8,128)(2,1)S(1)} %pad_maximum_fusion), channel_id=1, source_target_pairs={{0,2},{1,3},{2,0},{3,1},{4,6},{5,7},{6,4},{7,5},{8,10},{9,11},{10,... | collective-permute-start | bytes 1277960 | tf_op jit(solution)/shard_map/ppermute | solution.py:51
  33.2 9.0 %collective-permute-start.5 = (bf16[2,64,2048]{2,1,0:T(8,128)(2,1)S(1)}, bf16[2,64,2048]{2,1,0:T(8,128)(2,1)}, u32[]{:S(2)}, u32[]{:S(2)}) collective-permute-start(bf16[2,64,2048]{2,1,0:T(8,128)(2,1)S(1)} %collective-permute-done.3.refs_13_.refs_17_), channel_id=1, source_target_pairs={{8,16},{16,24},{9,17},{17,25},{10,18},{18,26},{11,19},{19,27},{12,... | collective-permute-start | bytes 1572872 | tf_op jit(solution)/shard_map/ppermute | solution.py:46
  42.2 2.4 %collective-permute-start.6 = (bf16[16,208,128]{2,1,0:T(8,128)(2,1)S(1)}, bf16[16,208,128]{2,1,0:T(8,128)(2,1)S(1)}, u32[]{:S(2)}, u32[]{:S(2)}) collective-permute-start(bf16[16,208,128]{2,1,0:T(8,128)(2,1)S(1)} %constant_dynamic-update-slice_fusion.2.own_ref), channel_id=1, source_target_pairs={{0,1},{1,0},{2,3},{3,2},{4,5},{5,4},{6,7},{7,6},{8,9},{9,8},{10,11... | collective-permute-start | bytes 2555912 | tf_op jit(solution)/shard_map/ppermute | solution.py:51
  42.3 22.6 %collective-permute-start.10 = (bf16[2,64,2048]{2,1,0:T(8,128)(2,1)}, bf16[2,64,2048]{2,1,0:T(8,128)(2,1)}, u32[]{:S(2)}, u32[]{:S(2)}) collective-permute-start(bf16[2,64,2048]{2,1,0:T(8,128)(2,1)} %collective-permute-done.5.refs_14_.refs_18_), channel_id=1, source_target_pairs={{16,24},{17,25},{18,26},{19,27},{20,28},{21,29},{22,30},{23,31}} | collective-permute-start | bytes 1572872 | tf_op jit(solution)/shard_map/ppermute | solution.py:46
  45.9 1.0 copy-start.7
  46.8 0.8 copy-start.9
  47.7 17.1 %copy-start.14 = (bf16[2,64,128]{2,1,0:T(8,128)(2,1)}, bf16[2,64,128]{2,1,0:T(8,128)(2,1)S(1)}, u32[]{:S(2)}) copy-start(bf16[2,64,128]{2,1,0:T(8,128)(2,1)S(1)} %get-tuple-element.34.refs_8_) | copy-start | bytes 98308
  47.7 19.2 %copy-start.2 = (bf16[2,64,2048]{2,1,0:T(8,128)(2,1)S(1)}, bf16[2,64,2048]{2,1,0:T(8,128)(2,1)}, u32[]{:S(2)}) copy-start(bf16[2,64,2048]{2,1,0:T(8,128)(2,1)} %copy-done.1) | copy-start | bytes 1572868
  47.7 17.2 %collective-permute-start.7 = (bf16[2,64,128]{2,1,0:T(8,128)(2,1)S(1)}, bf16[2,64,128]{2,1,0:T(8,128)(2,1)S(1)}, u32[]{:S(2)}, u32[]{:S(2)}) collective-permute-start(bf16[2,64,128]{2,1,0:T(8,128)(2,1)S(1)} %get-tuple-element.34.refs_8_), channel_id=1, source_target_pairs={{0,8},{8,16},{16,24},{1,9},{9,17},{17,25},{2,10},{10,18},{18,26},{... | collective-permute-start | bytes 98312 | tf_op jit(solution)/shard_map/ppermute | solution.py:46
  56.3 9.3 %collective-permute-start.8 = (bf16[2,64,128]{2,1,0:T(8,128)(2,1)S(1)}, bf16[2,64,128]{2,1,0:T(8,128)(2,1)S(1)}, u32[]{:S(2)}, u32[]{:S(2)}) collective-permute-start(bf16[2,64,128]{2,1,0:T(8,128)(2,1)S(1)} %get-tuple-element.34.refs_8_), channel_id=1, source_target_pairs={{0,16},{8,24},{1,17},{9,25},{2,18},{10,26},{3,19},{11,27},{4,20},{... | collective-permute-start | bytes 98312 | tf_op jit(solution)/shard_map/ppermute | solution.py:46
  63.4 2.9 %collective-permute-start.9 = (bf16[2,64,128]{2,1,0:T(8,128)(2,1)S(1)}, bf16[2,64,128]{2,1,0:T(8,128)(2,1)S(1)}, u32[]{:S(2)}, u32[]{:S(2)}) collective-permute-start(bf16[2,64,128]{2,1,0:T(8,128)(2,1)S(1)} %get-tuple-element.34.refs_8_), channel_id=1, source_target_pairs={{0,24},{1,25},{2,26},{3,27},{4,28},{5,29},{6,30},{7,31}} | collective-permute-start | bytes 98312 | tf_op jit(solution)/shard_map/ppermute | solution.py:46
  64.9 0.6 copy-start.16
  65.5 0.6 copy-start.18
  66.3 0.6 copy-start.20
  66.9 1.2 copy-start.5
  68.1 1.2 copy-start.6
  69.4 1.1 copy-start.10
  70.5 1.0 copy-start.12
  71.5 0.8 copy-start.15
  72.3 0.8 copy-start.17
  73.0 0.8 copy-start.19
  73.8 0.8 copy-start.21
  91.8 0.7 copy-start.13
  92.5 5.8 %collective-permute-start.13 = (bf16[2,64,64]{2,1,0:T(8,128)(2,1)S(1)}, bf16[2,64,64]{2,1,0:T(8,128)(2,1)S(1)}, u32[]{:S(2)}, u32[]{:S(2)}) collective-permute-start(bf16[2,64,64]{2,1,0:T(8,128)(2,1)S(1)} %get-tuple-element.69), channel_id=1, source_target_pairs={{8,0},{16,8},{24,16},{9,1},{17,9},{25,17},{10,2},{18,10},{26,18},{... | collective-permute-start | bytes 49160 | tf_op jit(solution)/shard_map/ppermute | solution.py:46
  93.8 8.1 %collective-permute-start.14 = (bf16[2,64,64]{2,1,0:T(8,128)(2,1)S(1)}, bf16[2,64,64]{2,1,0:T(8,128)(2,1)S(1)}, u32[]{:S(2)}, u32[]{:S(2)}) collective-permute-start(bf16[2,64,64]{2,1,0:T(8,128)(2,1)S(1)} %get-tuple-element.71), channel_id=1, source_target_pairs={{16,0},{24,8},{17,1},{25,9},{18,2},{26,10},{19,3},{27,11},{20,4},{... | collective-permute-start | bytes 49160 | tf_op jit(solution)/shard_map/ppermute | solution.py:46
  95.1 9.6 %collective-permute-start.15 = (bf16[2,64,64]{2,1,0:T(8,128)(2,1)S(1)}, bf16[2,64,64]{2,1,0:T(8,128)(2,1)S(1)}, u32[]{:S(2)}, u32[]{:S(2)}) collective-permute-start(bf16[2,64,64]{2,1,0:T(8,128)(2,1)S(1)} %get-tuple-element.70), channel_id=1, source_target_pairs={{24,0},{25,1},{26,2},{27,3},{28,4},{29,5},{30,6},{31,7}} | collective-permute-start | bytes 49160 | tf_op jit(solution)/shard_map/ppermute | solution.py:46
  96.4 10.0 %collective-permute-start.11 = (bf16[2,64,1024]{2,1,0:T(8,128)(2,1)}, bf16[2,64,1024]{2,1,0:T(8,128)(2,1)S(1)}, u32[]{:S(2)}, u32[]{:S(2)}) collective-permute-start(bf16[2,64,1024]{2,1,0:T(8,128)(2,1)} %copy-done.13), channel_id=1, source_target_pairs={{24,16},{25,17},{26,18},{27,19},{28,20},{29,21},{30,22},{31,23}} | collective-permute-start | bytes 786440 | tf_op jit(solution)/shard_map/ppermute | solution.py:46
  106.4 0.7 copy-start.22
  107.1 2.6 %collective-permute-start.16 = (bf16[8,2,208,128]{3,2,1,0:T(8,128)(2,1)}, bf16[8,2,208,128]{3,2,1,0:T(8,128)(2,1)S(1)}, u32[]{:S(2)}, u32[]{:S(2)}) collective-permute-start(bf16[8,2,208,128]{3,2,1,0:T(8,128)(2,1)} %get-tuple-element.47), channel_id=1, source_target_pairs={{0,1},{1,0},{2,3},{3,2},{4,5},{5,4},{6,7},{7,6},{8,9},{9,8},{10,11... | collective-permute-start | bytes 2555912 | tf_op jit(solution)/shard_map/ppermute | solution.py:51
  107.2 1.0 copy-start.23
  108.2 8.7 %collective-permute-start.12 = (bf16[2,64,1024]{2,1,0:T(8,128)(2,1)S(1)}, bf16[2,64,1024]{2,1,0:T(8,128)(2,1)S(1)}, u32[]{:S(2)}, u32[]{:S(2)}) collective-permute-start(bf16[2,64,1024]{2,1,0:T(8,128)(2,1)S(1)} %add_convert_fusion.2), channel_id=1, source_target_pairs={{16,8},{24,16},{17,9},{25,17},{18,10},{26,18},{19,11},{27,19},{20,... | collective-permute-start | bytes 786440 | tf_op jit(solution)/shard_map/ppermute | solution.py:46
  109.8 7.0 %collective-permute-start.18 = (bf16[4,2,96,128]{3,2,0,1:T(8,128)(2,1)S(1)}, bf16[4,2,96,128]{3,2,0,1:T(8,128)(2,1)S(1)}, u32[]{:S(2)}, u32[]{:S(2)}) collective-permute-start(bf16[4,2,96,128]{3,2,0,1:T(8,128)(2,1)S(1)} %fusion.4), channel_id=1, source_target_pairs={{0,4},{4,0},{1,5},{5,1},{2,6},{6,2},{3,7},{7,3},{8,12},{12,8},{9,1... | collective-permute-start | bytes 589832 | tf_op jit(solution)/shard_map/ppermute | solution.py:51
  111.5 7.4 %collective-permute-start.17 = (bf16[4,2,112,128]{3,2,0,1:T(8,128)(2,1)S(1)}, bf16[4,2,112,128]{3,2,0,1:T(8,128)(2,1)S(1)}, u32[]{:S(2)}, u32[]{:S(2)}) collective-permute-start(bf16[4,2,112,128]{3,2,0,1:T(8,128)(2,1)S(1)} %fusion), channel_id=1, source_target_pairs={{0,2},{1,3},{2,0},{3,1},{4,6},{5,7},{6,4},{7,5},{8,10},{9,11},{10,... | collective-permute-start | bytes 688136 | tf_op jit(solution)/shard_map/ppermute | solution.py:51
  116.9 4.7 %collective-permute-start.20 = (bf16[4,96,128]{2,1,0:T(8,128)(2,1)S(1)}, bf16[4,96,128]{2,1,0:T(8,128)(2,1)S(1)}, u32[]{:S(2)}, u32[]{:S(2)}) collective-permute-start(bf16[4,96,128]{2,1,0:T(8,128)(2,1)S(1)} %fusion.14), channel_id=1, source_target_pairs={{0,2},{1,3},{2,0},{3,1},{4,6},{5,7},{6,4},{7,5},{8,10},{9,11},{10,... | collective-permute-start | bytes 294920 | tf_op jit(solution)/shard_map/ppermute | solution.py:51
  119.0 13.4 %copy-start.8 = (bf16[4096,128]{1,0:T(8,128)(2,1)S(1)}, bf16[4096,128]{1,0:T(8,128)(2,1)}, u32[]{:S(2)}) copy-start(bf16[4096,128]{1,0:T(8,128)(2,1)} %copy-done.7) | copy-start | bytes 3145732
  119.0 4.9 %collective-permute-start.21 = (bf16[4,112,128]{2,1,0:T(8,128)(2,1)S(1)}, bf16[4,112,128]{2,1,0:T(8,128)(2,1)S(1)}, u32[]{:S(2)}, u32[]{:S(2)}) collective-permute-start(bf16[4,112,128]{2,1,0:T(8,128)(2,1)S(1)} %fusion.9), channel_id=1, source_target_pairs={{0,4},{4,0},{1,5},{5,1},{2,6},{6,2},{3,7},{7,3},{8,12},{12,8},{9,1... | collective-permute-start | bytes 344072 | tf_op jit(solution)/shard_map/ppermute | solution.py:51
  119.7 17.8 %collective-permute-start.19 = (bf16[2,64,1024]{2,1,0:T(8,128)(2,1)S(1)}, bf16[2,64,1024]{2,1,0:T(8,128)(2,1)S(1)}, u32[]{:S(2)}, u32[]{:S(2)}) collective-permute-start(bf16[2,64,1024]{2,1,0:T(8,128)(2,1)S(1)} %add_convert_fusion.1), channel_id=1, source_target_pairs={{8,0},{16,8},{24,16},{9,1},{17,9},{25,17},{10,2},{18,10},{26,18},{... | collective-permute-start | bytes 786440 | tf_op jit(solution)/shard_map/ppermute | solution.py:46
  124.0 12.8 %collective-permute-start.22 = (bf16[208,128]{1,0:T(8,128)(2,1)S(1)}, bf16[208,128]{1,0:T(8,128)(2,1)S(1)}, u32[]{:S(2)}, u32[]{:S(2)}) collective-permute-start(bf16[208,128]{1,0:T(8,128)(2,1)S(1)} %get-tuple-element.66), channel_id=1, source_target_pairs={{0,8},{8,16},{16,24},{24,0},{1,9},{9,17},{17,25},{25,1},{2,10},{10... | collective-permute-start | bytes 159752 | tf_op jit(solution)/shard_map/ppermute | solution.py:41
  127.9 9.5 %collective-permute-start.23 = (bf16[208,128]{1,0:T(8,128)(2,1)S(1)}, bf16[208,128]{1,0:T(8,128)(2,1)S(1)}, u32[]{:S(2)}, u32[]{:S(2)}) collective-permute-start(bf16[208,128]{1,0:T(8,128)(2,1)S(1)} %get-tuple-element.67), channel_id=1, source_target_pairs={{0,16},{8,24},{16,0},{24,8},{1,17},{9,25},{17,1},{25,9},{2,18},{10... | collective-permute-start | bytes 159752 | tf_op jit(solution)/shard_map/ppermute | solution.py:41
  131.3 6.2 %collective-permute-start.24 = (bf16[208,128]{1,0:T(8,128)(2,1)S(1)}, bf16[208,128]{1,0:T(8,128)(2,1)S(1)}, u32[]{:S(2)}, u32[]{:S(2)}) collective-permute-start(bf16[208,128]{1,0:T(8,128)(2,1)S(1)} %get-tuple-element.68), channel_id=1, source_target_pairs={{0,24},{8,0},{16,8},{24,16},{1,25},{9,1},{17,9},{25,17},{2,26},{10... | collective-permute-start | bytes 159752 | tf_op jit(solution)/shard_map/ppermute | solution.py:41
  137.5 4.1 %collective-permute-start.25 = (bf16[208,128]{1,0:T(8,128)(2,1)S(1)}, bf16[208,128]{1,0:T(8,128)(2,1)S(1)}, u32[]{:S(2)}, u32[]{:S(2)}) collective-permute-start(bf16[208,128]{1,0:T(8,128)(2,1)S(1)} %fusion.12), channel_id=1, source_target_pairs={{0,3},{1,2},{2,1},{3,0},{4,7},{5,6},{6,5},{7,4},{8,11},{9,10},{10,... | collective-permute-start | bytes 159752 | tf_op jit(solution)/shard_map/ppermute | solution.py:51
  137.5 5.1 %collective-permute-start.26 = (bf16[208,128]{1,0:T(8,128)(2,1)S(1)}, bf16[208,128]{1,0:T(8,128)(2,1)S(1)}, u32[]{:S(2)}, u32[]{:S(2)}) collective-permute-start(bf16[208,128]{1,0:T(8,128)(2,1)S(1)} %fusion.12), channel_id=1, source_target_pairs={{0,2},{1,3},{2,0},{3,1},{4,6},{5,7},{6,4},{7,5},{8,10},{9,11},{10,... | collective-permute-start | bytes 159752 | tf_op jit(solution)/shard_map/ppermute | solution.py:51
  139.1 3.6 %collective-permute-start.27 = (bf16[208,128]{1,0:T(8,128)(2,1)S(1)}, bf16[208,128]{1,0:T(8,128)(2,1)S(1)}, u32[]{:S(2)}, u32[]{:S(2)}) collective-permute-start(bf16[208,128]{1,0:T(8,128)(2,1)S(1)} %fusion.12), channel_id=1, source_target_pairs={{0,1},{1,0},{2,3},{3,2},{4,5},{5,4},{6,7},{7,6},{8,9},{9,8},{10,11... | collective-permute-start | bytes 159752 | tf_op jit(solution)/shard_map/ppermute | solution.py:51
